TPU v7x, 32 devices: a whole 2x2x4 slice. The times are simulated.
32 devices in a mesh: dp: 16 (over z, x, core), fsdp: 2 (over y).
Axes of the slice: x: 2, y: 2, z: 4, core: 2. Of those that a mesh axis runs over, the one named last changes fastest.
Arguments:
- inputs: bfloat16 [2, 2, 1024, 1024], P(None, 'fsdp', 'dp'), may hold values from -6 to 6
- encoded: bfloat16 [2, 2, 512, 1024], P(None, 'fsdp', 'dp'), may hold values from -6 to 6
- cotangent: bfloat16 [2, 2, 1024, 1024], P(None, 'fsdp', 'dp'), may hold values from -6 to 6
- doc_ids: int32 [2, 2, 16], P(None, 'fsdp'), may hold values from 0 to 2, never falling along the last dimension, each value on 1 to 12 neighbouring positions
- buckets: int32 [1024], replicated, may hold values from 0 to 31, as said below
- gain_self: bfloat16 [1024], P('fsdp'), may hold values from 0.5 to 1.5
- query_self: bfloat16 [1024, 1024], P('fsdp'), may hold values from -0.09375 to 0.09375
- key_self: bfloat16 [1024, 1024], P('fsdp'), may hold values from -0.09375 to 0.09375
- value_self: bfloat16 [1024, 1024], P('fsdp'), may hold values from -0.1875 to 0.1875
- output_self: bfloat16 [1024, 1024], P('fsdp'), may hold values from -0.75 to 0.75
- position_bias: bfloat16 [32, 16], P('fsdp'), may hold values from -4 to 4
- gain_cross: bfloat16 [1024], P('fsdp'), may hold values from 0.5 to 1.5
- query_cross: bfloat16 [1024, 1024], P('fsdp'), may hold values from -0.09375 to 0.09375
- key_cross: bfloat16 [1024, 1024], P('fsdp'), may hold values from -0.09375 to 0.09375
- value_cross: bfloat16 [1024, 1024], P('fsdp'), may hold values from -0.1875 to 0.1875
- output_cross: bfloat16 [1024, 1024], P('fsdp'), may hold values from -0.75 to 0.75
- gain_dense: bfloat16 [1024], P('fsdp'), may hold values from 0.5 to 1.5
- dense_gate: bfloat16 [1024, 2816], P('fsdp'), may hold values from -0.1875 to 0.1875
- dense_up: bfloat16 [1024, 2816], P('fsdp'), may hold values from -0.1875 to 0.1875
- dense_down: bfloat16 [2816, 1024], P('fsdp'), may hold values from -0.15625 to 0.15625
Outputs:
- outputs: bfloat16 [2, 2, 1024, 1024], P(None, 'fsdp', 'dp')
- grad_inputs: float32 [2, 2, 1024, 1024], P(None, 'fsdp', 'dp')
- grad_encoded: float32 [2, 2, 512, 1024], P(None, 'fsdp', 'dp')
- grad_gain_self: float32 [1024], P('fsdp')
- grad_query_self: float32 [1024, 1024], P('fsdp')
- grad_key_self: float32 [1024, 1024], P('fsdp')
- grad_value_self: float32 [1024, 1024], P('fsdp')
- grad_output_self: float32 [1024, 1024], P('fsdp')
- grad_position_bias: float32 [32, 16], P('fsdp')
- grad_gain_cross: float32 [1024], P('fsdp')
- grad_query_cross: float32 [1024, 1024], P('fsdp')
- grad_key_cross: float32 [1024, 1024], P('fsdp')
- grad_value_cross: float32 [1024, 1024], P('fsdp')
- grad_output_cross: float32 [1024, 1024], P('fsdp')
- grad_gain_dense: float32 [1024], P('fsdp')
- grad_dense_gate: float32 [1024, 2816], P('fsdp')
- grad_dense_up: float32 [1024, 2816], P('fsdp')
- grad_dense_down: float32 [2816, 1024], P('fsdp')
Inputs may be any that keep to these rules, and one draw needn't show every extreme that they name: Along the last dimension doc_ids never fall; each document covers 1 to 12 blocks, one exactly 12. buckets[d] = d for d < 16; buckets never falls as d grows, and buckets[1023] = 31.
All inputs are finite; a program needn't handle non-finite values.
Results may differ from a plain program's by a relative error of at most 0.03.
The roundings to bfloat16 on the way count: a program that leaves them out, or rounds other values in their place, can miss the bound.
Values may be sent and summed in bfloat16 or wider, within the bound.
No kernel may reach another device: no remote copies, remote signals or barrier semaphores. Data moves between devices by JAX's collectives and lax.ppermute only.
A program may use at most 256 MiB of HBM per device.

v0:
```python
import jax
import jax.numpy as jnp
from jax import lax
from jax.sharding import PartitionSpec as P

EPS = 1e-06
NEGATIVE = -1e30


def norm_rows(values, gain):
    return values * lax.rsqrt(jnp.mean(values * values, axis=-1, keepdims=True) + EPS) * gain


def gated(gate_pre, upper_pre):
    return jax.nn.gelu(gate_pre, approximate=True) * upper_pre


def bucket_table(apart, edges):
    lower = apart[:, :, None] >= edges[None, None, :-1]
    upper = apart[:, :, None] < edges[None, None, 1:]
    return (lower & upper).astype(jnp.bfloat16)


def scores_of(queries, key_rows, bias_part, allowed):
    scores = jnp.einsum("qhd,khd->hqk", queries, key_rows, preferred_element_type=jnp.float32)
    if bias_part is None:
        return scores
    return jnp.where(allowed[None], scores + bias_part, NEGATIVE)


def bias_slice(bias_full):
    if bias_full is None:
        return None
    return bias_full


def attend(queries, key_rows, value_rows, head_count, bias_full, allowed):
    row_count = queries.shape[0]
    key_count = key_rows.shape[0]
    queries = queries.reshape(row_count, head_count, -1)
    key_rows = key_rows.reshape(key_count, head_count, -1)
    value_rows = value_rows.reshape(key_count, head_count, -1)
    scores = scores_of(queries, key_rows, bias_slice(bias_full), allowed)
    probability = jax.nn.softmax(scores, axis=-1).astype(jnp.bfloat16)
    pieces = [
        jnp.einsum("hqk,khd->qhd", probability, value_rows, preferred_element_type=jnp.float32)
    ]
    return jnp.concatenate(pieces, axis=1).reshape(row_count, -1).astype(jnp.bfloat16)


def attend_back(queries, key_rows, value_rows, grad_out, head_count, bias_full, bias_hot, allowed):
    row_count = queries.shape[0]
    key_count = key_rows.shape[0]
    queries = queries.reshape(row_count, head_count, -1)
    key_rows = key_rows.reshape(key_count, head_count, -1)
    value_rows = value_rows.reshape(key_count, head_count, -1)
    grad_out = grad_out.reshape(row_count, head_count, -1)
    grad_query, grad_key, grad_value, grad_table, log_totals, inner_sums = ([], [], [], [], [], [])
    scores = scores_of(queries, key_rows, bias_slice(bias_full), allowed)
    probability = jax.nn.softmax(scores, axis=-1)
    log_totals.append(jax.nn.logsumexp(scores, axis=-1).T)
    grad_probability = jnp.einsum(
        "qhd,khd->hqk", grad_out, value_rows, preferred_element_type=jnp.float32
    )
    inner_sum = jnp.sum(probability * grad_probability, axis=-1, keepdims=True)
    inner_sums.append(inner_sum[:, :, 0].T)
    grad_scores = (probability * (grad_probability - inner_sum)).astype(jnp.bfloat16)
    grad_query.append(
        jnp.einsum("hqk,khd->qhd", grad_scores, key_rows, preferred_element_type=jnp.float32)
    )
    grad_key.append(
        jnp.einsum("hqk,qhd->khd", grad_scores, queries, preferred_element_type=jnp.float32)
    )
    grad_value.append(
        jnp.einsum(
            "hqk,qhd->khd",
            probability.astype(jnp.bfloat16),
            grad_out,
            preferred_element_type=jnp.float32,
        )
    )
    if bias_hot is not None:
        grad_table.append(
            jnp.einsum("qkc,hqk->ch", bias_hot, grad_scores, preferred_element_type=jnp.float32)
        )
    grad_query = jnp.concatenate(grad_query, axis=1).reshape(row_count, -1)
    grad_key = jnp.concatenate(grad_key, axis=1).reshape(key_count, -1)
    grad_value = jnp.concatenate(grad_value, axis=1).reshape(key_count, -1)
    table_grad = None if bias_hot is None else jnp.concatenate(grad_table, axis=1)
    log_rows = jnp.concatenate(log_totals, axis=1)
    inner_rows = jnp.concatenate(inner_sums, axis=1)
    return (grad_query, grad_key, grad_value, table_grad, log_rows, inner_rows)


def matmul(left, right):
    return jnp.dot(left, right, preferred_element_type=jnp.float32)


def outer_sum(left, right):
    return jnp.einsum("rd,re->de", left, right, preferred_element_type=jnp.float32)


def times_transposed(left, right):
    return jnp.einsum("re,de->rd", left, right, preferred_element_type=jnp.float32)


def per_device(
    inputs,
    encoded,
    cotangent,
    doc_ids,
    buckets,
    gain_self,
    query_self,
    key_self,
    value_self,
    output_self,
    position_bias,
    gain_cross,
    query_cross,
    key_cross,
    value_cross,
    output_cross,
    gain_dense,
    dense_gate,
    dense_up,
    dense_down,
):
    micro_count = inputs.shape[0]
    row_count = inputs.shape[2]
    head_count = position_bias.shape[1]
    block_count = lax.axis_size("dp")
    length = row_count * block_count
    row_start = lax.axis_index("dp") * row_count
    query_place = row_start + jnp.arange(row_count, dtype=jnp.int32)
    key_place = jnp.arange(length, dtype=jnp.int32)
    apart = query_place[:, None] - key_place[None, :]
    bucket_count = position_bias.shape[0] * lax.axis_size("fsdp")
    bucket_marks = jnp.arange(bucket_count + 1, dtype=jnp.int32)
    edges = jnp.sum((buckets[:, None] < bucket_marks[None, :]).astype(jnp.int32), axis=0)
    self_hot = bucket_table(apart, edges)
    outputs, grad_inputs, grad_encoded = ([], [], [])
    totals = None
    for micro_index in range(micro_count):
        gathered = (
            lax.all_gather(gain_self, "fsdp", axis=0, tiled=True),
            lax.all_gather(query_self, "fsdp", axis=0, tiled=True),
            lax.all_gather(key_self, "fsdp", axis=0, tiled=True),
            lax.all_gather(value_self, "fsdp", axis=0, tiled=True),
            lax.all_gather(output_self, "fsdp", axis=0, tiled=True),
            lax.all_gather(position_bias, "fsdp", axis=0, tiled=True),
            lax.all_gather(gain_cross, "fsdp", axis=0, tiled=True),
            lax.all_gather(query_cross, "fsdp", axis=0, tiled=True),
            lax.all_gather(key_cross, "fsdp", axis=0, tiled=True),
            lax.all_gather(value_cross, "fsdp", axis=0, tiled=True),
            lax.all_gather(output_cross, "fsdp", axis=0, tiled=True),
            lax.all_gather(gain_dense, "fsdp", axis=0, tiled=True),
            lax.all_gather(dense_gate, "fsdp", axis=0, tiled=True),
            lax.all_gather(dense_up, "fsdp", axis=0, tiled=True),
            lax.all_gather(dense_down, "fsdp", axis=0, tiled=True),
        )
        (
            norm_self,
            self_query,
            self_key,
            self_value,
            self_output,
            bias_table,
            norm_cross,
            cross_query,
            cross_key,
            cross_value,
            cross_output,
            norm_dense,
            gate_full,
            upper_full,
            down_full,
        ) = gathered
        norm_self = norm_self.astype(jnp.float32)
        norm_cross = norm_cross.astype(jnp.float32)
        norm_dense = norm_dense.astype(jnp.float32)
        tokens = inputs[micro_index, 0]
        states = encoded[micro_index, 0]
        grad_top = cotangent[micro_index, 0]
        key_docs = jnp.repeat(doc_ids[micro_index, 0], row_count, total_repeat_length=length)
        query_docs = lax.dynamic_slice_in_dim(key_docs, row_start, row_count)
        allowed = (apart >= 0) & (query_docs[:, None] == key_docs[None, :])
        self_bias = jnp.einsum(
            "qkc,ch->hqk", self_hot, bias_table, preferred_element_type=jnp.float32
        )
        residual = tokens.astype(jnp.float32)
        normed_one = norm_rows(residual, norm_self).astype(jnp.bfloat16)
        queries = matmul(normed_one, self_query).astype(jnp.bfloat16)
        own_keys = matmul(normed_one, self_key).astype(jnp.bfloat16)
        own_values = matmul(normed_one, self_value).astype(jnp.bfloat16)
        all_keys, all_values = (
            lax.all_gather(own_keys, "dp", axis=0, tiled=True),
            lax.all_gather(own_values, "dp", axis=0, tiled=True),
        )
        mixed_self = attend(queries, all_keys, all_values, head_count, self_bias, allowed)
        after_self = residual + matmul(mixed_self, self_output)
        normed_two = norm_rows(after_self, norm_cross).astype(jnp.bfloat16)
        cross_queries = matmul(normed_two, cross_query).astype(jnp.bfloat16)
        enc_keys = matmul(states, cross_key).astype(jnp.bfloat16)
        enc_values = matmul(states, cross_value).astype(jnp.bfloat16)
        all_enc_keys, all_enc_values = (
            lax.all_gather(enc_keys, "dp", axis=0, tiled=True),
            lax.all_gather(enc_values, "dp", axis=0, tiled=True),
        )
        mixed_cross = attend(cross_queries, all_enc_keys, all_enc_values, head_count, None, None)
        after_cross = after_self + matmul(mixed_cross, cross_output)
        normed_three = norm_rows(after_cross, norm_dense).astype(jnp.bfloat16)
        gate_pre = matmul(normed_three, gate_full)
        upper_pre = matmul(normed_three, upper_full)
        hidden, gated_back = jax.vjp(gated, gate_pre, upper_pre)
        hidden_low = hidden.astype(jnp.bfloat16)
        outputs.append((after_cross + matmul(hidden_low, down_full)).astype(jnp.bfloat16))
        grad_dense_down = outer_sum(hidden_low, grad_top)
        grad_hidden = times_transposed(grad_top, down_full)
        grad_gate_pre, grad_upper_pre = gated_back(grad_hidden)
        grad_gate_low = grad_gate_pre.astype(jnp.bfloat16)
        grad_upper_low = grad_upper_pre.astype(jnp.bfloat16)
        grad_dense_gate = outer_sum(normed_three, grad_gate_low)
        grad_dense_up = outer_sum(normed_three, grad_upper_low)
        grad_normed_three = times_transposed(grad_gate_low, gate_full) + times_transposed(
            grad_upper_low, upper_full
        )
        _, dense_norm_back = jax.vjp(norm_rows, after_cross, norm_dense)
        grad_from_dense, grad_gain_dense = dense_norm_back(grad_normed_three)
        grad_after_cross = grad_top.astype(jnp.float32) + grad_from_dense
        grad_cross_low = grad_after_cross.astype(jnp.bfloat16)
        grad_output_cross = outer_sum(mixed_cross, grad_cross_low)
        grad_mixed_cross = times_transposed(grad_cross_low, cross_output).astype(jnp.bfloat16)
        grad_cross_queries, grad_enc_keys, grad_enc_values, _, _, _ = attend_back(
            cross_queries,
            all_enc_keys,
            all_enc_values,
            grad_mixed_cross,
            head_count,
            None,
            None,
            None,
        )
        own_enc_keys, own_enc_values = (
            lax.psum_scatter(
                grad_enc_keys.astype(jnp.bfloat16), "dp", scatter_dimension=0, tiled=True
            ).astype(jnp.float32),
            lax.psum_scatter(
                grad_enc_values.astype(jnp.bfloat16), "dp", scatter_dimension=0, tiled=True
            ).astype(jnp.float32),
        )
        enc_keys_low = own_enc_keys.astype(jnp.bfloat16)
        enc_values_low = own_enc_values.astype(jnp.bfloat16)
        grad_key_cross = outer_sum(states, enc_keys_low)
        grad_value_cross = outer_sum(states, enc_values_low)
        grad_encoded.append(
            times_transposed(enc_keys_low, cross_key)
            + times_transposed(enc_values_low, cross_value)
        )
        cross_queries_low = grad_cross_queries.astype(jnp.bfloat16)
        grad_query_cross = outer_sum(normed_two, cross_queries_low)
        grad_normed_two = times_transposed(cross_queries_low, cross_query)
        _, cross_norm_back = jax.vjp(norm_rows, after_self, norm_cross)
        grad_from_cross, grad_gain_cross = cross_norm_back(grad_normed_two)
        grad_after_self = grad_after_cross + grad_from_cross
        grad_self_low = grad_after_self.astype(jnp.bfloat16)
        grad_output_self = outer_sum(mixed_self, grad_self_low)
        grad_mixed_self = times_transposed(grad_self_low, self_output).astype(jnp.bfloat16)
        grad_queries, grad_all_keys, grad_all_values, grad_position_bias, _, _ = attend_back(
            queries, all_keys, all_values, grad_mixed_self, head_count, self_bias, self_hot, allowed
        )
        own_grad_keys, own_grad_values = (
            lax.psum_scatter(
                grad_all_keys.astype(jnp.bfloat16), "dp", scatter_dimension=0, tiled=True
            ).astype(jnp.float32),
            lax.psum_scatter(
                grad_all_values.astype(jnp.bfloat16), "dp", scatter_dimension=0, tiled=True
            ).astype(jnp.float32),
        )
        queries_low = grad_queries.astype(jnp.bfloat16)
        keys_low = own_grad_keys.astype(jnp.bfloat16)
        values_low = own_grad_values.astype(jnp.bfloat16)
        grad_query_self = outer_sum(normed_one, queries_low)
        grad_key_self = outer_sum(normed_one, keys_low)
        grad_value_self = outer_sum(normed_one, values_low)
        grad_normed_one = (
            times_transposed(queries_low, self_query)
            + times_transposed(keys_low, self_key)
            + times_transposed(values_low, self_value)
        )
        _, self_norm_back = jax.vjp(norm_rows, residual, norm_self)
        grad_from_self, grad_gain_self = self_norm_back(grad_normed_one)
        grad_inputs.append(grad_after_self + grad_from_self)
        grads = (
            grad_gain_self,
            grad_query_self,
            grad_key_self,
            grad_value_self,
            grad_output_self,
            grad_position_bias,
            grad_gain_cross,
            grad_query_cross,
            grad_key_cross,
            grad_value_cross,
            grad_output_cross,
            grad_gain_dense,
            grad_dense_gate,
            grad_dense_up,
            grad_dense_down,
        )
        totals = grads if totals is None else jax.tree.map(jnp.add, totals, grads)
    totals = (
        lax.psum_scatter(
            totals[0].astype(jnp.bfloat16), "fsdp", scatter_dimension=0, tiled=True
        ).astype(jnp.float32),
        lax.psum_scatter(
            totals[1].astype(jnp.bfloat16), "fsdp", scatter_dimension=0, tiled=True
        ).astype(jnp.float32),
        lax.psum_scatter(
            totals[2].astype(jnp.bfloat16), "fsdp", scatter_dimension=0, tiled=True
        ).astype(jnp.float32),
        lax.psum_scatter(
            totals[3].astype(jnp.bfloat16), "fsdp", scatter_dimension=0, tiled=True
        ).astype(jnp.float32),
        lax.psum_scatter(
            totals[4].astype(jnp.bfloat16), "fsdp", scatter_dimension=0, tiled=True
        ).astype(jnp.float32),
        lax.psum_scatter(
            totals[5].astype(jnp.bfloat16), "fsdp", scatter_dimension=0, tiled=True
        ).astype(jnp.float32),
        lax.psum_scatter(
            totals[6].astype(jnp.bfloat16), "fsdp", scatter_dimension=0, tiled=True
        ).astype(jnp.float32),
        lax.psum_scatter(
            totals[7].astype(jnp.bfloat16), "fsdp", scatter_dimension=0, tiled=True
        ).astype(jnp.float32),
        lax.psum_scatter(
            totals[8].astype(jnp.bfloat16), "fsdp", scatter_dimension=0, tiled=True
        ).astype(jnp.float32),
        lax.psum_scatter(
            totals[9].astype(jnp.bfloat16), "fsdp", scatter_dimension=0, tiled=True
        ).astype(jnp.float32),
        lax.psum_scatter(
            totals[10].astype(jnp.bfloat16), "fsdp", scatter_dimension=0, tiled=True
        ).astype(jnp.float32),
        lax.psum_scatter(
            totals[11].astype(jnp.bfloat16), "fsdp", scatter_dimension=0, tiled=True
        ).astype(jnp.float32),
        lax.psum_scatter(
            totals[12].astype(jnp.bfloat16), "fsdp", scatter_dimension=0, tiled=True
        ).astype(jnp.float32),
        lax.psum_scatter(
            totals[13].astype(jnp.bfloat16), "fsdp", scatter_dimension=0, tiled=True
        ).astype(jnp.float32),
        lax.psum_scatter(
            totals[14].astype(jnp.bfloat16), "fsdp", scatter_dimension=0, tiled=True
        ).astype(jnp.float32),
    )
    totals = (
        lax.psum(totals[0].astype(jnp.bfloat16), "dp").astype(jnp.float32),
        lax.psum(totals[1].astype(jnp.bfloat16), "dp").astype(jnp.float32),
        lax.psum(totals[2].astype(jnp.bfloat16), "dp").astype(jnp.float32),
        lax.psum(totals[3].astype(jnp.bfloat16), "dp").astype(jnp.float32),
        lax.psum(totals[4].astype(jnp.bfloat16), "dp").astype(jnp.float32),
        lax.psum(totals[5].astype(jnp.bfloat16), "dp").astype(jnp.float32),
        lax.psum(totals[6].astype(jnp.bfloat16), "dp").astype(jnp.float32),
        lax.psum(totals[7].astype(jnp.bfloat16), "dp").astype(jnp.float32),
        lax.psum(totals[8].astype(jnp.bfloat16), "dp").astype(jnp.float32),
        lax.psum(totals[9].astype(jnp.bfloat16), "dp").astype(jnp.float32),
        lax.psum(totals[10].astype(jnp.bfloat16), "dp").astype(jnp.float32),
        lax.psum(totals[11].astype(jnp.bfloat16), "dp").astype(jnp.float32),
        lax.psum(totals[12].astype(jnp.bfloat16), "dp").astype(jnp.float32),
        lax.psum(totals[13].astype(jnp.bfloat16), "dp").astype(jnp.float32),
        lax.psum(totals[14].astype(jnp.bfloat16), "dp").astype(jnp.float32),
    )
    return (
        jnp.stack(outputs)[:, None],
        jnp.stack(grad_inputs)[:, None],
        jnp.stack(grad_encoded)[:, None],
        totals[0],
        totals[1],
        totals[2],
        totals[3],
        totals[4],
        totals[5],
        totals[6],
        totals[7],
        totals[8],
        totals[9],
        totals[10],
        totals[11],
        totals[12],
        totals[13],
        totals[14],
    )


def solution(mesh):
    placed = (
        P(None, "fsdp", "dp", None),
        P(None, "fsdp", "dp", None),
        P(None, "fsdp", "dp", None),
        P(None, "fsdp", None),
        P(),
        P("fsdp"),
        P("fsdp", None),
        P("fsdp", None),
        P("fsdp", None),
        P("fsdp", None),
        P("fsdp", None),
        P("fsdp"),
        P("fsdp", None),
        P("fsdp", None),
        P("fsdp", None),
        P("fsdp", None),
        P("fsdp"),
        P("fsdp", None),
        P("fsdp", None),
        P("fsdp", None),
    )
    return jax.shard_map(
        per_device,
        mesh=mesh,
        in_specs=placed,
        out_specs=(
            P(None, "fsdp", "dp", None),
            P(None, "fsdp", "dp", None),
            P(None, "fsdp", "dp", None),
            P("fsdp"),
            P("fsdp", None),
            P("fsdp", None),
            P("fsdp", None),
            P("fsdp", None),
            P("fsdp", None),
            P("fsdp"),
            P("fsdp", None),
            P("fsdp", None),
            P("fsdp", None),
            P("fsdp", None),
            P("fsdp"),
            P("fsdp", None),
            P("fsdp", None),
            P("fsdp", None),
        ),
        check_vma=False,
    )
```

profile of v0, /device:TPU:0, one launch (start us, length us, event | category | flops | bytes accessed | tf_op | source)
XLA Modules:
  0.0 2235.3 jit_solution(10223681469726987293)
XLA Ops:
  10.6 34.8 %all-gather.35.cloned.1.call-done = bf16[1024,1024]{1,0:T(8,128)(2,1)} async-done(((bf16[512,1024]{1,0:T(8,128)(2,1)}), bf16[1024,1024]{1,0:T(8,128)(2,1)}) %all-gather.35.cloned.1.call-update) | async-done | bytes 2097168 | tf_op jit(solution)/shard_map/all_gather | solution.py:155
  48.3 31.8 %all-gather.41.cloned.1.call-done = bf16[1024,1024]{1,0:T(8,128)(2,1)} async-done(((bf16[512,1024]{1,0:T(8,128)(2,1)}), bf16[1024,1024]{1,0:T(8,128)(2,1)}) %all-gather.41.cloned.1.call-update) | async-done | bytes 2097168 | tf_op jit(solution)/shard_map/all_gather | solution.py:154
  91.4 23.4 %all-gather.29.cloned.1.call-done = bf16[1024,1024]{1,0:T(8,128)(2,1)} async-done(((bf16[512,1024]{1,0:T(8,128)(2,1)}), bf16[1024,1024]{1,0:T(8,128)(2,1)}) %all-gather.29.cloned.1.call-update) | async-done | bytes 2097168 | tf_op jit(solution)/shard_map/all_gather | solution.py:148
  117.7 31.7 %all-gather.23.cloned.1.call-done = bf16[1024,1024]{1,0:T(8,128)(2,1)} async-done(((bf16[512,1024]{1,0:T(8,128)(2,1)}), bf16[1024,1024]{1,0:T(8,128)(2,1)}) %all-gather.23.cloned.1.call-update) | async-done | bytes 2097168 | tf_op jit(solution)/shard_map/all_gather | solution.py:149
  166.6 10.2 select_select_fusion.1
  176.9 9.9 select_select_fusion
  203.9 20.7 all-gather.57.cloned.1.call-done
  226.9 37.3 %all-gather.59.cloned.1.call-done = bf16[512,1024]{1,0:T(8,128)(2,1)} async-done(((bf16[32,1024]{1,0:T(8,128)(2,1)}), bf16[512,1024]{1,0:T(8,128)(2,1)}) %all-gather.59.cloned.1.call-update) | async-done | bytes 1048592 | tf_op jit(solution)/shard_map/all_gather | solution.py:207
  266.5 37.3 %all-gather.37.cloned.1.call-done = bf16[512,1024]{1,0:T(8,128)(2,1)} async-done(((bf16[32,1024]{1,0:T(8,128)(2,1)}), bf16[512,1024]{1,0:T(8,128)(2,1)}) %all-gather.37.cloned.1.call-update) | async-done | bytes 1048592 | tf_op jit(solution)/shard_map/all_gather | solution.py:208
  306.1 37.3 %all-gather.43.cloned.1.call-done = bf16[512,1024]{1,0:T(8,128)(2,1)} async-done(((bf16[32,1024]{1,0:T(8,128)(2,1)}), bf16[512,1024]{1,0:T(8,128)(2,1)}) %all-gather.43.cloned.1.call-update) | async-done | bytes 1048592 | tf_op jit(solution)/shard_map/all_gather | solution.py:207
  345.7 40.7 %all-gather.55.cloned.1.call-done = bf16[1024,1024]{1,0:T(8,128)(2,1)} async-done(((bf16[64,1024]{1,0:T(8,128)(2,1)}), bf16[1024,1024]{1,0:T(8,128)(2,1)}) %all-gather.55.cloned.1.call-update) | async-done | bytes 2097168 | tf_op jit(solution)/shard_map/all_gather | solution.py:197
  389.3 6.3 fusion.8
  400.4 29.0 %all-gather.53.cloned.1.call-done = bf16[1024,1024]{1,0:T(8,128)(2,1)} async-done(((bf16[64,1024]{1,0:T(8,128)(2,1)}), bf16[1024,1024]{1,0:T(8,128)(2,1)}) %all-gather.53.cloned.1.call-update) | async-done | bytes 2097168 | tf_op jit(solution)/shard_map/all_gather | solution.py:198
  432.2 6.5 convolution_convert_fusion.13
  438.7 23.9 %all-gather.33.cloned.1.call-done = bf16[1024,1024]{1,0:T(8,128)(2,1)} async-done(((bf16[512,1024]{1,0:T(8,128)(2,1)}), bf16[1024,1024]{1,0:T(8,128)(2,1)}) %all-gather.33.cloned.1.call-update) | async-done | bytes 2097168 | tf_op jit(solution)/shard_map/all_gather | solution.py:150
  464.9 32.5 %all-gather.39.cloned.1.call-done = bf16[1024,1024]{1,0:T(8,128)(2,1)} async-done(((bf16[512,1024]{1,0:T(8,128)(2,1)}), bf16[1024,1024]{1,0:T(8,128)(2,1)}) %all-gather.39.cloned.1.call-update) | async-done | bytes 2097168 | tf_op jit(solution)/shard_map/all_gather | solution.py:153
  499.7 41.7 %all-gather.25.cloned.1.call-done = bf16[1024,1024]{1,0:T(8,128)(2,1)} async-done(((bf16[64,1024]{1,0:T(8,128)(2,1)}), bf16[1024,1024]{1,0:T(8,128)(2,1)}) %all-gather.25.cloned.1.call-update) | async-done | bytes 2097168 | tf_op jit(solution)/shard_map/all_gather | solution.py:198
  545.3 38.9 %all-gather.31.cloned.1.call-done = bf16[1024,1024]{1,0:T(8,128)(2,1)} async-done(((bf16[64,1024]{1,0:T(8,128)(2,1)}), bf16[1024,1024]{1,0:T(8,128)(2,1)}) %all-gather.31.cloned.1.call-update) | async-done | bytes 2097168 | tf_op jit(solution)/shard_map/all_gather | solution.py:197
  587.5 6.4 fusion.7
  597.1 6.0 convolution_convert_fusion.15
  611.1 5.1 convolution_convert_fusion.14
  631.0 62.4 %all-gather.47.cloned.1.call-done = bf16[1024,2816]{1,0:T(8,128)(2,1)} async-done(((bf16[512,2816]{1,0:T(8,128)(2,1)}), bf16[1024,2816]{1,0:T(8,128)(2,1)}) %all-gather.47.cloned.1.call-update) | async-done | bytes 5767184 | tf_op jit(solution)/shard_map/all_gather | solution.py:158
  698.2 71.1 %all-gather.49.cloned.1.call-done = bf16[1024,2816]{1,0:T(8,128)(2,1)} async-done(((bf16[512,2816]{1,0:T(8,128)(2,1)}), bf16[1024,2816]{1,0:T(8,128)(2,1)}) %all-gather.49.cloned.1.call-update) | async-done | bytes 5767184 | tf_op jit(solution)/shard_map/all_gather | solution.py:159
  773.9 71.4 %all-gather.51.cloned.1.call-done = bf16[2816,1024]{1,0:T(8,128)(2,1)} async-done(((bf16[1408,1024]{1,0:T(8,128)(2,1)}), bf16[2816,1024]{1,0:T(8,128)(2,1)}) %all-gather.51.cloned.1.call-update) | async-done | bytes 5767184 | tf_op jit(solution)/shard_map/all_gather | solution.py:160
  845.3 5.8 multiply_convert_fusion.5
  890.1 5.4 convolution_convert_fusion.6
  908.3 5.2 convolution_convert_fusion.4
  938.5 5.7 convolution_convert_fusion.2
  946.9 5.8 convolution_convert_fusion
  979.1 16.1 reduce-scatter.73.cloned.1.call-done
  999.6 55.8 %reduce-scatter.71.cloned.1.call-done = bf16[32,1024]{1,0:T(8,128)(2,1)} async-done(((bf16[512,1024]{1,0:T(8,128)(2,1)}), bf16[32,1024]{1,0:T(8,128)(2,1)}) %reduce-scatter.71.cloned.1.call-update) | async-done | bytes 65552
  1059.0 56.9 %reduce-scatter.75.cloned.1.call-done = bf16[32,1024]{1,0:T(8,128)(2,1)} async-done(((bf16[512,1024]{1,0:T(8,128)(2,1)}), bf16[32,1024]{1,0:T(8,128)(2,1)}) %reduce-scatter.75.cloned.1.call-update) | async-done | bytes 65552
  1120.2 60.5 %reduce-scatter.61.cloned.1.call-done = bf16[64,1024]{1,0:T(8,128)(2,1)} async-done(((bf16[1024,1024]{1,0:T(8,128)(2,1)}), bf16[64,1024]{1,0:T(8,128)(2,1)}) %reduce-scatter.61.cloned.1.call-update) | async-done | bytes 131088
  1184.4 61.7 %reduce-scatter.65.cloned.1.call-done = bf16[64,1024]{1,0:T(8,128)(2,1)} async-done(((bf16[1024,1024]{1,0:T(8,128)(2,1)}), bf16[64,1024]{1,0:T(8,128)(2,1)}) %reduce-scatter.65.cloned.1.call-update) | async-done | bytes 131088
  1250.6 60.3 %reduce-scatter.63.cloned.1.call-done = bf16[64,1024]{1,0:T(8,128)(2,1)} async-done(((bf16[1024,1024]{1,0:T(8,128)(2,1)}), bf16[64,1024]{1,0:T(8,128)(2,1)}) %reduce-scatter.63.cloned.1.call-update) | async-done | bytes 131088
  1314.6 61.6 %reduce-scatter.67.cloned.1.call-done = bf16[64,1024]{1,0:T(8,128)(2,1)} async-done(((bf16[1024,1024]{1,0:T(8,128)(2,1)}), bf16[64,1024]{1,0:T(8,128)(2,1)}) %reduce-scatter.67.cloned.1.call-update) | async-done | bytes 131088
  1411.3 32.7 %reduce-scatter.43.cloned.1.call-done = bf16[512,1024]{1,0:T(8,128)(2,1)} async-done(((bf16[1024,1024]{1,0:T(8,128)(2,1)}), bf16[512,1024]{1,0:T(8,128)(2,1)}) %reduce-scatter.43.cloned.1.call-update) | async-done | bytes 1048592 | tf_op jit(solution)/shard_map/reduce_scatter | solution.py:325
  1444.0 34.0 %reduce-scatter.47.cloned.1.call-done = bf16[512,1024]{1,0:T(8,128)(2,1)} async-done(((bf16[1024,1024]{1,0:T(8,128)(2,1)}), bf16[512,1024]{1,0:T(8,128)(2,1)}) %reduce-scatter.47.cloned.1.call-update) | async-done | bytes 1048592 | tf_op jit(solution)/shard_map/reduce_scatter | solution.py:334
  1478.0 34.2 %reduce-scatter.53.cloned.1.call-done = bf16[512,1024]{1,0:T(8,128)(2,1)} async-done(((bf16[1024,1024]{1,0:T(8,128)(2,1)}), bf16[512,1024]{1,0:T(8,128)(2,1)}) %reduce-scatter.53.cloned.1.call-update) | async-done | bytes 1048592 | tf_op jit(solution)/shard_map/reduce_scatter | solution.py:343
  1512.2 34.7 %reduce-scatter.49.cloned.1.call-done = bf16[512,1024]{0,1:T(8,128)(2,1)} async-done(((bf16[1024,1024]{0,1:T(8,128)(2,1)}), bf16[512,1024]{0,1:T(8,128)(2,1)}) %reduce-scatter.49.cloned.1.call-update) | async-done | bytes 1048592 | tf_op jit(solution)/shard_map/reduce_scatter | solution.py:337
  1546.9 34.6 %reduce-scatter.51.cloned.1.call-done = bf16[512,1024]{0,1:T(8,128)(2,1)} async-done(((bf16[1024,1024]{0,1:T(8,128)(2,1)}), bf16[512,1024]{0,1:T(8,128)(2,1)}) %reduce-scatter.51.cloned.1.call-update) | async-done | bytes 1048592 | tf_op jit(solution)/shard_map/reduce_scatter | solution.py:340
  1581.5 34.7 %reduce-scatter.39.cloned.1.call-done = bf16[512,1024]{1,0:T(8,128)(2,1)} async-done(((bf16[1024,1024]{1,0:T(8,128)(2,1)}), bf16[512,1024]{1,0:T(8,128)(2,1)}) %reduce-scatter.39.cloned.1.call-update) | async-done | bytes 1048592 | tf_op jit(solution)/shard_map/reduce_scatter | solution.py:319
  1616.2 34.8 %reduce-scatter.41.cloned.1.call-done = bf16[512,1024]{1,0:T(8,128)(2,1)} async-done(((bf16[1024,1024]{1,0:T(8,128)(2,1)}), bf16[512,1024]{1,0:T(8,128)(2,1)}) %reduce-scatter.41.cloned.1.call-update) | async-done | bytes 1048592 | tf_op jit(solution)/shard_map/reduce_scatter | solution.py:322
  1651.0 74.1 %reduce-scatter.55.cloned.1.call-done = bf16[512,2816]{1,0:T(8,128)(2,1)} async-done(((bf16[1024,2816]{1,0:T(8,128)(2,1)}), bf16[512,2816]{1,0:T(8,128)(2,1)}) %reduce-scatter.55.cloned.1.call-update) | async-done | bytes 2883600 | tf_op jit(solution)/shard_map/reduce_scatter | solution.py:349
  1725.1 74.2 %reduce-scatter.57.cloned.1.call-done = bf16[512,2816]{1,0:T(8,128)(2,1)} async-done(((bf16[1024,2816]{1,0:T(8,128)(2,1)}), bf16[512,2816]{1,0:T(8,128)(2,1)}) %reduce-scatter.57.cloned.1.call-update) | async-done | bytes 2883600 | tf_op jit(solution)/shard_map/reduce_scatter | solution.py:352
  1799.3 74.3 %reduce-scatter.59.cloned.1.call-done = bf16[1408,1024]{1,0:T(8,128)(2,1)} async-done(((bf16[2816,1024]{1,0:T(8,128)(2,1)}), bf16[1408,1024]{1,0:T(8,128)(2,1)}) %reduce-scatter.59.cloned.1.call-update) | async-done | bytes 2883600 | tf_op jit(solution)/shard_map/reduce_scatter | solution.py:355
  1898.4 34.9 %all-reduce.3 = (bf16[512]{0:T(512)(128)(2,1)S(1)}, bf16[16,16]{1,0:T(8,128)(2,1)S(1)}, bf16[512]{0:T(512)(128)(2,1)S(1)}, bf16[512]{0:T(512)(128)(2,1)S(1)}) all-reduce(bf16[512]{0:T(512)(128)(2,1)S(1)} %dynamic-slice.10, bf16[16,16]{1,0:T(8,128)(2,1)} %reduce-scatter.45.cloned.1.call-done, ...), channel_id=1, replica_groups=mesh['dp'=16,'fsdp'=2] {'dp'}, use_global_device_ids=true, to_apply=%region_36.38 | all-reduce | flops 1792 | bytes 7168 | tf_op jit(solution)/shard_map/psum | solution.py:360
  1936.7 267.2 %all-reduce.8.cloned.1.call-done = (bf16[512,1024]{0,1:T(8,128)(2,1)}, bf16[512,1024]{0,1:T(8,128)(2,1)}, bf16[512,1024]{1,0:T(8,128)(2,1)}, bf16[512,1024]{1,0:...) async-done(((bf16[512,1024]{0,1:T(8,128)(2,1)}, ...) | async-done | bytes 17039376 | tf_op jit(solution)/shard_map/psum | solution.py:368
  (582 shorter events, 336.0 us)
Async XLA Ops:
  7.2 38.2 %all-gather.35.cloned.1.call-start = ((), (), s32[]{:S(2)}) async-start(), calls=%async_computation.26 | async-start | bytes 3145728 | tf_op jit(solution)/shard_map/all_gather | solution.py:155
  7.9 72.2 %all-gather.41.cloned.1.call-start = ((), (), s32[]{:S(2)}) async-start(), calls=%async_computation.29 | async-start | bytes 3145728 | tf_op jit(solution)/shard_map/all_gather | solution.py:154
  8.7 106.1 %all-gather.29.cloned.1.call-start = ((), (), s32[]{:S(2)}) async-start(), calls=%async_computation.23 | async-start | bytes 3145728 | tf_op jit(solution)/shard_map/all_gather | solution.py:148
  9.4 140.0 %all-gather.23.cloned.1.call-start = ((), (), s32[]{:S(2)}) async-start(), calls=%async_computation.20 | async-start | bytes 3145728 | tf_op jit(solution)/shard_map/all_gather | solution.py:149
  10.0 190.6 %all-gather.27.cloned.1.call-start = ((), (), s32[]{:S(2)}) async-start(), calls=%async_computation.22 | async-start | bytes 3145728 | tf_op jit(solution)/shard_map/all_gather | solution.py:147
  10.6 214.0 %all-gather.57.cloned.1.call-start = ((), (), s32[]{:S(2)}) async-start(), calls=%async_computation.37 | async-start | bytes 1114112 | tf_op jit(solution)/shard_map/all_gather | solution.py:208
  48.3 215.9 %all-gather.59.cloned.1.call-start = ((), (), s32[]{:S(2)}) async-start(), calls=%async_computation.38 | async-start | bytes 1114112 | tf_op jit(solution)/shard_map/all_gather | solution.py:207
  82.9 221.0 %all-gather.37.cloned.1.call-start = ((), (), s32[]{:S(2)}) async-start(), calls=%async_computation.27 | async-start | bytes 1114112 | tf_op jit(solution)/shard_map/all_gather | solution.py:208
  84.0 259.4 %all-gather.43.cloned.1.call-start = ((), (), s32[]{:S(2)}) async-start(), calls=%async_computation.30 | async-start | bytes 1114112 | tf_op jit(solution)/shard_map/all_gather | solution.py:207
  86.8 299.6 %all-gather.55.cloned.1.call-start = ((), (), s32[]{:S(2)}) async-start(), calls=%async_computation.36 | async-start | bytes 2228224 | tf_op jit(solution)/shard_map/all_gather | solution.py:197
  117.6 311.7 %all-gather.53.cloned.1.call-start = ((), (), s32[]{:S(2)}) async-start(), calls=%async_computation.35 | async-start | bytes 2228224 | tf_op jit(solution)/shard_map/all_gather | solution.py:198
  152.3 310.3 %all-gather.33.cloned.1.call-start = ((), (), s32[]{:S(2)}) async-start(), calls=%async_computation.25 | async-start | bytes 3145728 | tf_op jit(solution)/shard_map/all_gather | solution.py:150
  152.9 344.5 %all-gather.39.cloned.1.call-start = ((), (), s32[]{:S(2)}) async-start(), calls=%async_computation.28 | async-start | bytes 3145728 | tf_op jit(solution)/shard_map/all_gather | solution.py:153
  153.7 387.7 %all-gather.25.cloned.1.call-start = ((), (), s32[]{:S(2)}) async-start(), calls=%async_computation.21 | async-start | bytes 2228224 | tf_op jit(solution)/shard_map/all_gather | solution.py:198
  154.9 429.2 %all-gather.31.cloned.1.call-start = ((), (), s32[]{:S(2)}) async-start(), calls=%async_computation.24 | async-start | bytes 2228224 | tf_op jit(solution)/shard_map/all_gather | solution.py:197
  157.8 459.7 %all-gather.45.cloned.1.call-start = ((), (), s32[]{:S(2)}) async-start(), calls=%async_computation.31 | async-start | bytes 3145728 | tf_op jit(solution)/shard_map/all_gather | solution.py:156
  158.4 535.0 %all-gather.47.cloned.1.call-start = ((), (), s32[]{:S(2)}) async-start(), calls=%async_computation.32 | async-start | bytes 8650752 | tf_op jit(solution)/shard_map/all_gather | solution.py:158
  159.0 610.3 %all-gather.49.cloned.1.call-start = ((), (), s32[]{:S(2)}) async-start(), calls=%async_computation.33 | async-start | bytes 8650752 | tf_op jit(solution)/shard_map/all_gather | solution.py:159
  159.6 685.7 %all-gather.51.cloned.1.call-start = ((), (), s32[]{:S(2)}) async-start(), calls=%async_computation.34 | async-start | bytes 8650752 | tf_op jit(solution)/shard_map/all_gather | solution.py:160
  160.4 814.4 %reduce-scatter.69.cloned.1.call-start = ((), (), s32[]{:S(2)}) async-start(), calls=%async_computation.55 | async-start | bytes 1114112
  203.1 186.1 %copy-start.61 = (bf16[64,1024]{0,1:T(8,128)(2,1)}, bf16[64,1024]{0,1:T(8,128)(2,1)S(1)}, u32[]{:S(2)}) copy-start(bf16[64,1024]{0,1:T(8,128)(2,1)S(1)} %copy.198) | copy-start | bytes 393220
  203.9 383.6 %copy-start.63 = (bf16[64,1024]{0,1:T(8,128)(2,1)}, bf16[64,1024]{0,1:T(8,128)(2,1)S(1)}, u32[]{:S(2)}) copy-start(bf16[64,1024]{0,1:T(8,128)(2,1)S(1)} %copy.196) | copy-start | bytes 393220
  464.9 162.9 %copy-start.26 = (f32[64,1024]{1,0:T(8,128)}, f32[64,1024]{1,0:T(8,128)S(1)}, u32[]{:S(2)}) copy-start(f32[64,1024]{1,0:T(8,128)S(1)} %get-tuple-element.201) | copy-start | bytes 786436
  499.7 120.2 %copy-start.57 = (bf16[64,1024]{0,1:T(8,128)(2,1)}, bf16[64,1024]{0,1:T(8,128)(2,1)S(1)}, u32[]{:S(2)}) copy-start(bf16[64,1024]{0,1:T(8,128)(2,1)S(1)} %copy.199) | copy-start | bytes 393220
  619.9 248.1 %copy-start.38 = (f32[64,1024]{1,0:T(8,128)}, f32[64,1024]{1,0:T(8,128)S(1)}, u32[]{:S(2)}) copy-start(f32[64,1024]{1,0:T(8,128)S(1)} %get-tuple-element.211) | copy-start | bytes 786436
  630.4 237.6 %copy-start.36 = (f32[64,1024]{1,0:T(8,128)}, f32[64,1024]{1,0:T(8,128)S(1)}, u32[]{:S(2)}) copy-start(f32[64,1024]{1,0:T(8,128)S(1)} %get-tuple-element.213) | copy-start | bytes 786436
  630.4 225.6 %copy-start.130 = (f32[64]{0:T(128)}, f32[64]{0:T(128)S(1)}, u32[]{:S(2)}) copy-start(f32[64]{0:T(128)S(1)} %fusion.168) | copy-start | bytes 772
  698.2 147.2 %copy-start.79 = (bf16[2,1,64,1024]{3,2,1,0:T(8,128)(2,1)S(1)}, bf16[2,1,64,1024]{3,2,1,0:T(8,128)(2,1)}, u32[]{:S(2)}) copy-start(bf16[2,1,64,1024]{3,2,1,0:T(8,128)(2,1)} %param.28) | copy-start | bytes 786436
  877.1 118.1 %reduce-scatter.73.cloned.1.call-start = ((), (), s32[]{:S(2)}) async-start(), calls=%async_computation.57 | async-start | bytes 1114112
  890.1 165.3 %reduce-scatter.71.cloned.1.call-start = ((), (), s32[]{:S(2)}) async-start(), calls=%async_computation.56 | async-start | bytes 1114112
  901.7 214.2 %reduce-scatter.75.cloned.1.call-start = ((), (), s32[]{:S(2)}) async-start(), calls=%async_computation.58 | async-start | bytes 1114112
  916.0 264.7 %reduce-scatter.61.cloned.1.call-start = ((), (), s32[]{:S(2)}) async-start(), calls=%async_computation.51 | async-start | bytes 2228224
  924.4 321.6 %reduce-scatter.65.cloned.1.call-start = ((), (), s32[]{:S(2)}) async-start(), calls=%async_computation.53 | async-start | bytes 2228224
  938.5 372.4 %reduce-scatter.63.cloned.1.call-start = ((), (), s32[]{:S(2)}) async-start(), calls=%async_computation.52 | async-start | bytes 2228224
  946.8 429.3 %reduce-scatter.67.cloned.1.call-start = ((), (), s32[]{:S(2)}) async-start(), calls=%async_computation.54 | async-start | bytes 2228224
  955.3 456.0 %reduce-scatter.37.cloned.1.call-start = ((), (), s32[]{:S(2)}) async-start(), calls=%async_computation.39 | async-start | bytes 3145728 | tf_op jit(solution)/shard_map/reduce_scatter | solution.py:316
  962.6 481.4 %reduce-scatter.43.cloned.1.call-start = ((), (), s32[]{:S(2)}) async-start(), calls=%async_computation.42 | async-start | bytes 3145728 | tf_op jit(solution)/shard_map/reduce_scatter | solution.py:325
  966.5 511.6 %reduce-scatter.47.cloned.1.call-start = ((), (), s32[]{:S(2)}) async-start(), calls=%async_computation.44 | async-start | bytes 3145728 | tf_op jit(solution)/shard_map/reduce_scatter | solution.py:334
  970.7 541.5 %reduce-scatter.53.cloned.1.call-start = ((), (), s32[]{:S(2)}) async-start(), calls=%async_computation.47 | async-start | bytes 3145728 | tf_op jit(solution)/shard_map/reduce_scatter | solution.py:343
  974.7 572.2 %reduce-scatter.49.cloned.1.call-start = ((), (), s32[]{:S(2)}) async-start(), calls=%async_computation.45 | async-start | bytes 3145728 | tf_op jit(solution)/shard_map/reduce_scatter | solution.py:337
  999.6 581.9 %reduce-scatter.51.cloned.1.call-start = ((), (), s32[]{:S(2)}) async-start(), calls=%async_computation.46 | async-start | bytes 3145728 | tf_op jit(solution)/shard_map/reduce_scatter | solution.py:340
  1120.2 496.0 %reduce-scatter.39.cloned.1.call-start = ((), (), s32[]{:S(2)}) async-start(), calls=%async_computation.40 | async-start | bytes 3145728 | tf_op jit(solution)/shard_map/reduce_scatter | solution.py:319
  1250.5 400.5 %reduce-scatter.41.cloned.1.call-start = ((), (), s32[]{:S(2)}) async-start(), calls=%async_computation.41 | async-start | bytes 3145728 | tf_op jit(solution)/shard_map/reduce_scatter | solution.py:322
  1380.6 344.5 %reduce-scatter.55.cloned.1.call-start = ((), (), s32[]{:S(2)}) async-start(), calls=%async_computation.48 | async-start | bytes 8650752 | tf_op jit(solution)/shard_map/reduce_scatter | solution.py:349
  1387.5 411.8 %reduce-scatter.57.cloned.1.call-start = ((), (), s32[]{:S(2)}) async-start(), calls=%async_computation.49 | async-start | bytes 8650752 | tf_op jit(solution)/shard_map/reduce_scatter | solution.py:352
  1394.4 479.2 %reduce-scatter.59.cloned.1.call-start = ((), (), s32[]{:S(2)}) async-start(), calls=%async_computation.50 | async-start | bytes 8650752 | tf_op jit(solution)/shard_map/reduce_scatter | solution.py:355
  1402.3 496.1 %reduce-scatter.45.cloned.1.call-start = ((), (), s32[]{:S(2)}) async-start(), calls=%async_computation.43 | async-start | bytes 12288 | tf_op jit(solution)/shard_map/reduce_scatter | solution.py:328
  1411.0 792.9 %all-reduce.8.cloned.1.call-start = ((), (), s32[]{:S(2)}) async-start(), calls=%async_computation.59 | async-start | bytes 34078720 | tf_op jit(solution)/shard_map/psum | solution.py:368
  (151 other events, 1293.9 us)
Sparse Core Ops, SparseCore 0:
  9.6 35.8 all-gather.34
  47.0 33.1 all-gather.40
  81.7 33.1 all-gather.28
  116.2 33.1 all-gather.22
  150.8 33.1 all-gather.26
  186.6 37.9 all-gather.56
  227.3 36.8 all-gather.58
  266.9 36.8 all-gather.36
  306.6 36.8 all-gather.42
  346.0 40.3 all-gather.54
  389.1 40.1 all-gather.52
  430.7 31.8 all-gather.32
  464.2 33.1 all-gather.38
  500.0 41.3 all-gather.24
  544.0 40.1 all-gather.30
  585.6 31.8 all-gather.44
  618.9 74.4 all-gather.46
  694.8 74.4 all-gather.48
  770.8 74.4 all-gather.50
  877.3 57.3 reduce-scatter.68
  938.8 56.4 reduce-scatter.72
  998.9 56.4 reduce-scatter.70
  1059.5 56.3 reduce-scatter.74
  1120.0 60.6 reduce-scatter.60
  1185.5 60.5 reduce-scatter.64
  1250.3 60.5 reduce-scatter.62
  1315.5 60.6 reduce-scatter.66
  1379.0 30.8 reduce-scatter.36
  1412.2 31.8 reduce-scatter.42
  1446.1 31.8 reduce-scatter.46
  1480.3 31.8 reduce-scatter.52
  1515.0 31.8 reduce-scatter.48
  1549.7 31.8 reduce-scatter.50
  1584.3 31.8 reduce-scatter.38
  1619.1 31.8 reduce-scatter.40
  1653.7 71.3 reduce-scatter.54
  1727.9 71.3 reduce-scatter.56
  1802.2 71.3 reduce-scatter.58
  1876.3 9.7 reduce-scatter.44
  1893.7 310.1 all-reduce.7
where the time goes:
time: 2240 us
  waiting for transfers between devices  1780 us (79%)
  matrix products  252 us (11%)
  local copies, waits for them, and re-layouts  68.3 us (3%)
  other arithmetic  60 us (3%)
  blocking collectives  57.5 us (3%)
    unnamed x48, waiting for transfers between devices  380 us
    psum x1, waiting for transfers between devices, per_device(): lax.psum(totals[8].astype(jnp.bfloat16), 'dp').astype(jnp.float32)  267 us
    all_gather x2, waiting for transfers between devices, per_device(): lax.all_gather(own_keys, 'dp', axis=0, tiled=True)  79.5 us
    all_gather x2, waiting for transfers between devices, per_device(): lax.all_gather(enc_keys, 'dp', axis=0, tiled=True)  74.7 us
    reduce_scatter x1, waiting for transfers between devices, per_device(): lax.psum_scatter(totals[14].astype(jnp.bfloat16), 'fsdp', scatter_dimensi...  74.3 us
    reduce_scatter x1, waiting for transfers between devices, per_device(): lax.psum_scatter(totals[13].astype(jnp.bfloat16), 'fsdp', scatter_dimensi...  74.2 us
    reduce_scatter x1, waiting for transfers between devices, per_device(): lax.psum_scatter(totals[12].astype(jnp.bfloat16), 'fsdp', scatter_dimensi...  74.1 us
    all_gather x1, waiting for transfers between devices, per_device(): lax.all_gather(dense_down, 'fsdp', axis=0, tiled=True)  71.4 us
  transfers between devices with their start and end apart: 40, of which 36 were waited for; matrix products, arithmetic and copies ran while one was open for 14% of the time, Pallas kernels for 0%

commit v1 on v0

v1 whole, which is shorter than its diff:
```python
import functools

import jax
import jax.numpy as jnp
from jax import lax
from jax.experimental import pallas as pl
from jax.experimental.pallas import tpu as pltpu
from jax.sharding import PartitionSpec as P

EPS = 1e-06
NEGATIVE = -1e30
TILE = 256
F32 = jnp.float32
BF16 = jnp.bfloat16
VMEM_LIMIT = 56 * 1024 * 1024


def vmem():
    return pl.BlockSpec(memory_space=pltpu.VMEM)


def smem():
    return pl.BlockSpec(memory_space=pltpu.SMEM)


def params(limit=VMEM_LIMIT):
    return pltpu.CompilerParams(vmem_limit_bytes=limit)


def dot(left, right):
    return jnp.dot(left, right, preferred_element_type=F32)


def dot_t(left, right):
    return lax.dot_general(left, right, (((1,), (1,)), ((), ())), preferred_element_type=F32)


def t_dot(left, right):
    return lax.dot_general(left, right, (((0,), (0,)), ((), ())), preferred_element_type=F32)


def norm_rows(values, gain):
    return values * lax.rsqrt(jnp.mean(values * values, axis=-1, keepdims=True) + EPS) * gain


def norm_back(values, gain, grad):
    r = lax.rsqrt(jnp.mean(values * values, axis=-1, keepdims=True) + EPS)
    scaled = grad * gain
    inner = jnp.mean(scaled * values, axis=-1, keepdims=True)
    back = r * scaled - values * (r * r * r * inner)
    return back, jnp.sum(grad * (values * r), axis=0, keepdims=True)


def low_lanes(rows):
    return lax.broadcasted_iota(jnp.int32, (rows, 128), 1) < 64


def pair_up(first, second):
    lane = low_lanes(first.shape[0])
    low = jnp.where(lane, first, pltpu.roll(second, 64, 1))
    high = jnp.where(lane, pltpu.roll(first, 64, 1), second)
    return low, high


def keep_half(values, half):
    lane = low_lanes(values.shape[0])
    return jnp.where(lane if half == 0 else ~lane, values, jnp.zeros_like(values))


def softmax_rows(scores):
    top = jnp.max(scores, axis=-1, keepdims=True)
    raised = jnp.exp(scores - top)
    return raised * (1.0 / jnp.sum(raised, axis=-1, keepdims=True))


def table_kernel(edge_ref, value_ref, out_ref):
    rows, length = out_ref.shape
    bucket_count = value_ref.shape[0]
    for start in range(0, length, TILE):
        place = (rows, TILE)
        apart = (
            lax.broadcasted_iota(jnp.int32, place, 0)
            - lax.broadcasted_iota(jnp.int32, place, 1)
            + (length - rows - start)
        )
        value = jnp.full(place, value_ref[0], F32)
        for bucket in range(1, bucket_count):
            value = jnp.where(apart >= edge_ref[bucket], value_ref[bucket], value)
        out_ref[:, start : start + TILE] = jnp.where(apart >= 0, value, NEGATIVE)


def bias_table(edges, values, length):
    return pl.pallas_call(
        table_kernel,
        out_shape=jax.ShapeDtypeStruct((TILE, length), F32),
        in_specs=[smem(), smem()],
        out_specs=vmem(),
        name="bias_table",
    )(edges, values)


def bucket_kernel(edge_ref, grad_ref, out_ref):
    rows, length = grad_ref.shape
    bucket_count = out_ref.shape[0]
    above = [jnp.zeros((8, TILE), F32) for _ in range(bucket_count)]
    for start in range(0, length, TILE):
        for row in range(0, rows, 8):
            place = (8, TILE)
            apart = (
                lax.broadcasted_iota(jnp.int32, place, 0)
                - lax.broadcasted_iota(jnp.int32, place, 1)
                + (length - rows - start + row)
            )
            tile = grad_ref[row : row + 8, start : start + TILE]
            for bucket in range(bucket_count):
                above[bucket] = above[bucket] + jnp.where(apart >= edge_ref[bucket], tile, 0.0)
    for bucket in range(bucket_count):
        rest = above[bucket + 1] if bucket + 1 < bucket_count else 0.0
        part = jnp.sum(above[bucket] - rest, axis=0, keepdims=True)
        out_ref[bucket : bucket + 1, :] = part[:, :128] + part[:, 128:]


def bucket_sums(edges, grad, bucket_count):
    return pl.pallas_call(
        bucket_kernel,
        out_shape=jax.ShapeDtypeStruct((bucket_count, 128), F32),
        in_specs=[smem(), vmem()],
        out_specs=vmem(),
        name="bucket_sums",
    )(edges, grad)


def self_scores(q, k, table, doc_col, doc_row):
    scores = dot_t(q, k) + table
    return jnp.where(doc_col == doc_row, scores, NEGATIVE)


def self_forward_kernel(
    pos_ref, x_ref, gain_ref, w_ref, table_ref, doc_row_ref, doc_col_ref, n_ref, qkv_ref, o_ref
):
    blocks, _, rows, width = x_ref.shape
    length = blocks * rows
    group = TILE // rows
    lane = lax.broadcasted_iota(jnp.int32, (TILE, 384), 1) % 128 < 64

    def project(step, carry):
        parts = []
        for inner in range(group):
            own = step * group + inner
            x = x_ref[pos_ref[own]].astype(F32).reshape(2 * rows, width)
            n = norm_rows(x, gain_ref[...]).astype(BF16).reshape(2, rows, width)
            n_ref[own] = n
            parts.append(n)
        first = jnp.concatenate([part[0] for part in parts], axis=0)
        second = jnp.concatenate([part[1] for part in parts], axis=0)
        made = dot(jnp.concatenate([first, second], axis=0), w_ref[...])
        picked = jnp.where(lane, made[:TILE], made[TILE:])
        qkv_ref[pl.ds(pl.multiple_of(step * TILE, TILE), TILE), :] = picked.astype(BF16)
        return carry

    lax.fori_loop(0, blocks // group, project, 0)
    for block in range(length // TILE):
        start, count = block * TILE, (block + 1) * TILE
        table = table_ref[:, length - count :]
        q = qkv_ref[start:count, 0:128]
        k = qkv_ref[:count, 128:256]
        v = qkv_ref[:count, 256:384]
        mixed = []
        for half in range(2):
            scores = self_scores(
                keep_half(q, half),
                k,
                table,
                doc_col_ref[half, start:count, :],
                doc_row_ref[half : half + 1, :count],
            )
            mixed.append(dot(softmax_rows(scores).astype(BF16), v))
        o_ref[start:count, :] = jnp.where(low_lanes(TILE), mixed[0], mixed[1]).astype(BF16)


def self_backward_kernel(
    qkv_ref, do_ref, table_ref, doc_row_ref, doc_col_ref, dqkv_ref, grad_ref, dk_ref, dv_ref
):
    length = qkv_ref.shape[0]
    grad_ref[...] = jnp.zeros_like(grad_ref)
    dk_ref[...] = jnp.zeros_like(dk_ref)
    dv_ref[...] = jnp.zeros_like(dv_ref)
    for block in range(length // TILE):
        start, count = block * TILE, (block + 1) * TILE
        table = table_ref[:, length - count :]
        k = qkv_ref[:count, 128:256]
        v = qkv_ref[:count, 256:384]
        made = []
        for half in range(2):
            q = keep_half(qkv_ref[start:count, 0:128], half)
            do = keep_half(do_ref[start:count, :], half)
            p = softmax_rows(
                self_scores(
                    q,
                    k,
                    table,
                    doc_col_ref[half, start:count, :],
                    doc_row_ref[half : half + 1, :count],
                )
            )
            dp = dot_t(do, v)
            ds = (p * (dp - jnp.sum(p * dp, axis=-1, keepdims=True))).astype(BF16)
            grad_ref[:, length - count :] += ds.astype(F32)
            made.append(dot(ds, k))
            dk_ref[:count, :] += t_dot(ds, q)
            dv_ref[:count, :] += t_dot(p.astype(BF16), do)
        dq = jnp.where(low_lanes(TILE), made[0], made[1])
        dqkv_ref[start:count, 0:128] = dq.astype(BF16)
    dqkv_ref[:, 128:256] = dk_ref[...].astype(BF16)
    dqkv_ref[:, 256:384] = dv_ref[...].astype(BF16)


def head_weight_kernel(n_ref, d_ref, out_ref):
    blocks, _, rows, width = n_ref.shape
    shards = out_ref.shape[0]
    span = width // shards
    lane = lax.broadcasted_iota(jnp.int32, (blocks * rows, 384), 1) % 128 < 64
    d = d_ref[...]
    zero = jnp.zeros_like(d)
    right = [jnp.where(lane, d, zero), jnp.where(lane, zero, d)]
    half = span // 2
    for shard in range(shards):
        total = jnp.zeros((span, 384), F32)
        for micro in range(2):
            left = n_ref[:, micro, :, shard * span : (shard + 1) * span]
            total = total + t_dot(left.reshape(blocks * rows, span), right[micro])
        q, k, v = (
            total[:, at : at + 128] + pltpu.roll(total[:, at : at + 128], 64, 1)
            for at in (0, 128, 256)
        )
        out_ref[shard, :span, :] = jnp.where(low_lanes(span), q, k).astype(BF16)
        out_ref[shard, span:, :] = jnp.where(low_lanes(half), v[:half], v[half:]).astype(BF16)


def mid_forward_kernel(
    o1_ref,
    x_ref,
    wo_ref,
    gain_cross_ref,
    wq_ref,
    ke_ref,
    ve_ref,
    wc_ref,
    gain_dense_ref,
    o1c_ref,
    x1_ref,
    n2_ref,
    q2_ref,
    o2_ref,
    x2_ref,
    n3_ref,
):
    heads, rows, _ = o1_ref.shape
    width = x_ref.shape[-1]
    for pair in range(heads // 2):
        at = pair * 128
        low, high = pair_up(o1_ref[2 * pair].astype(F32), o1_ref[2 * pair + 1].astype(F32))
        o1c_ref[0:rows, at : at + 128] = low.astype(BF16)
        o1c_ref[rows : 2 * rows, at : at + 128] = high.astype(BF16)
    x = x_ref[...].astype(F32).reshape(2 * rows, width)
    x1 = x + dot(o1c_ref[...], wo_ref[...])
    x1_ref[...] = x1
    n2 = norm_rows(x1, gain_cross_ref[...]).astype(BF16)
    n2_ref[...] = n2
    q2_ref[...] = dot(n2, wq_ref[...]).astype(BF16)
    for micro in range(2):
        for pair in range(heads // 2):
            at = pair * 128
            span = slice(micro * rows, (micro + 1) * rows)
            q = q2_ref[span, at : at + 128]
            both = jnp.concatenate([keep_half(q, 0), keep_half(q, 1)], axis=0)
            p = softmax_rows(dot_t(both, ke_ref[micro, :, at : at + 128]))
            o = dot(p.astype(BF16), ve_ref[micro, :, at : at + 128])
            o2_ref[span, at : at + 128] = jnp.where(
                low_lanes(rows), o[:rows], o[rows:]
            ).astype(BF16)
    x2 = x1 + dot(o2_ref[...], wc_ref[...])
    x2_ref[...] = x2
    n3_ref[...] = norm_rows(x2, gain_dense_ref[...]).astype(BF16)


def mid_backward_kernel(
    g_ref,
    dn3_ref,
    dn3_more_ref,
    x2_ref,
    gain_dense_ref,
    wc_ref,
    q2_ref,
    ke_ref,
    ve_ref,
    wq_ref,
    x1_ref,
    gain_cross_ref,
    wo_ref,
    gx2b_ref,
    dq2_ref,
    gx1_ref,
    gx1b_ref,
    do1_ref,
    dkv_ref,
    dc_ref,
    do2_ref,
):
    heads, rows, _ = do1_ref.shape
    blocks, _, part, _ = dkv_ref.shape
    width = x1_ref.shape[-1]
    dn3 = dn3_ref[...] + dn3_more_ref[...].astype(F32)
    back, dc = norm_back(x2_ref[...], gain_dense_ref[...], dn3)
    dc_ref[0:1, :] = dc
    gx2 = g_ref[...].astype(F32).reshape(2 * rows, width) + back
    gx2b = gx2.astype(BF16)
    gx2b_ref[...] = gx2b
    do2_ref[...] = dot_t(gx2b, wc_ref[...]).astype(BF16)
    for micro in range(2):
        for pair in range(heads // 2):
            at = pair * 128
            span = slice(micro * rows, (micro + 1) * rows)
            q = q2_ref[span, at : at + 128]
            do = do2_ref[span, at : at + 128]
            q = jnp.concatenate([keep_half(q, 0), keep_half(q, 1)], axis=0)
            do = jnp.concatenate([keep_half(do, 0), keep_half(do, 1)], axis=0)
            k = ke_ref[micro, :, at : at + 128]
            v = ve_ref[micro, :, at : at + 128]
            p = softmax_rows(dot_t(q, k))
            dp = dot_t(do, v)
            ds = (p * (dp - jnp.sum(p * dp, axis=-1, keepdims=True))).astype(BF16)
            dq = dot(ds, k)
            dq2_ref[span, at : at + 128] = jnp.where(
                low_lanes(rows), dq[:rows], dq[rows:]
            ).astype(BF16)
            dk = t_dot(ds, q).astype(BF16).reshape(blocks, part, 128)
            dv = t_dot(p.astype(BF16), do).astype(BF16).reshape(blocks, part, 128)
            dkv_ref[:, micro, :, at : at + 128] = dk
            dkv_ref[:, micro, :, width + at : width + at + 128] = dv
    dn2 = dot_t(dq2_ref[...], wq_ref[...])
    back, dc = norm_back(x1_ref[...], gain_cross_ref[...], dn2)
    dc_ref[1:2, :] = dc
    gx1 = gx2 + back
    gx1_ref[...] = gx1
    gx1b = gx1.astype(BF16)
    gx1b_ref[...] = gx1b
    do1 = dot_t(gx1b, wo_ref[...]).astype(BF16).astype(F32)
    for pair in range(heads // 2):
        at = pair * 128
        low, high = pair_up(do1[:rows, at : at + 128], do1[rows:, at : at + 128])
        do1_ref[2 * pair] = low.astype(BF16)
        do1_ref[2 * pair + 1] = high.astype(BF16)


def dense_kernel(
    n_ref, g_ref, wg_ref, wu_ref, wd_ref, hid_ref, da_ref, db_ref, y_ref, ylow_ref, d_ref, dlow_ref
):
    n = n_ref[...]
    a = dot(n, wg_ref[...])
    b = dot(n, wu_ref[...])
    scale = 0.7978845608028654
    cubed = 0.044715
    inner = jnp.tanh(scale * (a + cubed * (a * a * a)))
    gelu = 0.5 * a * (1.0 + inner)
    slope = 0.5 * (1.0 + inner) + 0.5 * a * (1.0 - inner * inner) * (
        scale * (1.0 + 3.0 * cubed * (a * a))
    )
    hid = (gelu * b).astype(BF16)
    hid_ref[...] = hid
    dh = dot_t(g_ref[...], wd_ref[...])
    da = (dh * b * slope).astype(BF16)
    db = (dh * gelu).astype(BF16)
    da_ref[...] = da
    db_ref[...] = db
    d = dot_t(da, wg_ref[...]) + dot_t(db, wu_ref[...])
    d_ref[...] = d
    dlow_ref[...] = d.astype(BF16)
    y = dot(hid, wd_ref[...])
    y_ref[...] = y
    ylow_ref[...] = y.astype(BF16)


def dense_layer(n, g, wg, wu, wd, step):
    count, width = n.shape
    hidden = wg.shape[1]
    row = lambda size: pl.BlockSpec((step, size), lambda i: (i, 0))
    whole = lambda array: pl.BlockSpec(array.shape, lambda i: (0, 0))
    made = lambda size, kind: jax.ShapeDtypeStruct((count, size), kind)
    return pl.pallas_call(
        dense_kernel,
        grid=(count // step,),
        in_specs=[row(width), row(width), whole(wg), whole(wu), whole(wd)],
        out_specs=[row(hidden)] * 3 + [row(width)] * 4,
        out_shape=[made(hidden, BF16)] * 3
        + [made(width, F32), made(width, BF16), made(width, F32), made(width, BF16)],
        compiler_params=params(),
        name="dense_layer",
    )(n, g, wg, wu, wd)


def spread_kernel(counts, where_ref, in_ref, *out_refs):
    for place, out_ref in enumerate(out_refs):
        out_ref[...] = in_ref[0, 0, place].astype(F32)


def spread(where, pieces, shapes, index):
    count, halves, kinds, rows, cols = pieces.shape
    return pl.pallas_call(
        functools.partial(spread_kernel, kinds),
        grid_spec=pltpu.PrefetchScalarGridSpec(
            num_scalar_prefetch=1,
            grid=(count, halves),
            in_specs=[
                pl.BlockSpec((1, 1, kinds, rows, cols), lambda t, h, where: (t, h, 0, 0, 0))
            ],
            out_specs=[pl.BlockSpec((rows, cols), index)] * kinds,
        ),
        out_shape=[jax.ShapeDtypeStruct(shape, F32) for shape in shapes],
        compiler_params=params(),
        name="spread",
    )(where, pieces)


def head_spread_kernel(pos_ref, in_ref, q_ref, k_ref, v_ref):
    span, width = q_ref.shape
    half = span // 2
    for pair in range(width // 128):
        at = pair * 128
        first, second = in_ref[pos_ref[2 * pair]], in_ref[pos_ref[2 * pair + 1]]
        low, high = pair_up(first.astype(F32), second.astype(F32))
        q_ref[:, at : at + 128] = low[:span]
        k_ref[:, at : at + 128] = high[:span]
        v_ref[:half, at : at + 128] = low[span:]
        v_ref[half:, at : at + 128] = high[span:]


def per_device(
    inputs,
    encoded,
    cotangent,
    doc_ids,
    buckets,
    gain_self,
    query_self,
    key_self,
    value_self,
    output_self,
    position_bias,
    gain_cross,
    query_cross,
    key_cross,
    value_cross,
    output_cross,
    gain_dense,
    dense_gate,
    dense_up,
    dense_down,
):
    micro_count, _, rows, width = inputs.shape
    part = encoded.shape[2]
    heads = position_bias.shape[1]
    dp, fs = lax.axis_size("dp"), lax.axis_size("fsdp")
    me, shard = lax.axis_index("dp"), lax.axis_index("fsdp")
    core = me % 2
    length = rows * dp
    tokens = micro_count * rows
    copies = dp // heads
    head = me // copies
    span = width // fs
    hidden = dense_down.shape[0]
    bits = [1 << place for place in reversed(range(dp.bit_length() - 1))]

    def swap_dp(values, bit):
        return lax.ppermute(values, "dp", [(j, j ^ bit) for j in range(dp)])

    def swap_fs(values):
        return lax.ppermute(values, "fsdp", [(j, 1 - j) for j in range(2)])

    def two(first, second, which):
        return jnp.where(
            which == 0,
            jnp.concatenate([first, second], axis=-2),
            jnp.concatenate([second, first], axis=-2),
        )

    def other_rows(values):
        half = values.shape[-2] // 2
        sent = lax.dynamic_slice_in_dim(values, core * half, half, axis=values.ndim - 2)
        got = swap_fs(sent)
        return two(got, swap_dp(got, 1), core)

    def whole_rows(values):
        if fs == 2:
            return two(values, other_rows(values), shard)
        return lax.all_gather(values, "fsdp", axis=1, tiled=True)

    def gather_small(values):
        if fs == 2:
            got = swap_fs(values)
            return jnp.where(
                shard == 0,
                jnp.concatenate([values, got], axis=-1),
                jnp.concatenate([got, values], axis=-1),
            )
        return lax.all_gather(values, "fsdp", axis=1, tiled=True)

    def both_tokens(values):
        if fs == 2:
            return jnp.concatenate([values, swap_fs(values)], axis=0)
        return lax.all_gather(values, "fsdp", axis=0, tiled=True)

    def gather_all(values):
        for bit in bits:
            values = jnp.concatenate([values, swap_dp(values, bit)], axis=0)
        return values

    def sum_chips(values):
        chip, size = me // 2, values.shape[0]
        for bit in reversed(bits[:-1]):
            values = values.reshape((size // 2, 2) + values.shape[1:])
            size = size // 2
            mine = (me // bit) % 2
            kept = lax.dynamic_index_in_dim(values, mine, 1, keepdims=False)
            sent = lax.dynamic_index_in_dim(values, 1 - mine, 1, keepdims=False)
            got = swap_dp(sent, bit)
            values = (kept.astype(F32) + got.astype(F32)).astype(BF16)
        return values

    turned = [
        sum(((t >> place) & 1) << (len(bits) - 1 - place) for place in range(len(bits)))
        for t in range(dp)
    ]
    source = me ^ jnp.array(turned, jnp.int32)
    place_of = jnp.zeros((dp,), jnp.int32).at[source].set(jnp.arange(dp, dtype=jnp.int32))

    x = inputs[:, 0]
    g = cotangent[:, 0]
    e = encoded[:, 0]

    pieces = {0: x}
    for bit in bits:
        for known in list(pieces):
            pieces[known | bit] = swap_dp(pieces[known], bit)
    x_all = jnp.stack([pieces[turn] for turn in turned])
    e_all = lax.all_gather(e, "dp", axis=0)

    gains = gather_small(jnp.stack([gain_self, gain_cross, gain_dense])).astype(F32)
    gain_one, gain_two, gain_three = gains[0:1], gains[1:2], gains[2:3]
    bias_all = gather_small(position_bias.T).T.astype(F32)
    own_head = lambda w: lax.dynamic_slice_in_dim(w, head * 64, 64, axis=1)
    head_pack = jnp.concatenate([own_head(query_self), own_head(key_self), own_head(value_self)], axis=1)
    if fs == 2:
        head_whole = two(head_pack, swap_fs(head_pack), shard)
    else:
        picked = jnp.concatenate(
            [w.reshape(span, heads, 64) for w in (query_self, key_self, value_self)], axis=2
        )
        whole = lax.all_gather(picked.reshape(span, heads * 192), "fsdp", axis=0, tiled=True)
        head_whole = lax.dynamic_slice_in_dim(whole, head * 192, 192, axis=1)
    head_w = jnp.concatenate(
        [head_whole[:, at : at + 64] for at in (0, 0, 64, 64, 128, 128)], axis=1
    )

    cross_kv = whole_rows(jnp.stack([key_cross, value_cross]))
    near = whole_rows(jnp.stack([output_self, query_cross, output_cross]))
    wo, wq2, wc = near[0], near[1], near[2]

    slab = jnp.stack([dense_gate, dense_up])
    if fs == 2:
        mine = lax.dynamic_slice_in_dim(slab, shard * hidden, hidden, axis=2)
        theirs = lax.dynamic_slice_in_dim(slab, (1 - shard) * hidden, hidden, axis=2)
        gate_up = two(mine, other_rows(theirs), shard)
    else:
        gate_up = lax.all_to_all(slab, "fsdp", 2, 1, tiled=True)

    g_group = both_tokens(g.reshape(tokens, width))

    marks = jnp.arange(bias_all.shape[0], dtype=jnp.int32)
    edges = jnp.sum((buckets[:, None] < marks[None, :]).astype(jnp.int32), axis=0)
    bias_values = lax.dynamic_slice_in_dim(bias_all, head, 1, axis=1)[:, 0]
    table = bias_table(edges, bias_values, length)
    doc_row = jnp.repeat(doc_ids[:, 0], rows, axis=1, total_repeat_length=length)
    doc_col = doc_row[:, :, None]

    n_all, qkv, mixed = pl.pallas_call(
        self_forward_kernel,
        out_shape=[
            jax.ShapeDtypeStruct((dp, micro_count, rows, width), BF16),
            jax.ShapeDtypeStruct((length, 384), BF16),
            jax.ShapeDtypeStruct((length, 128), BF16),
        ],
        in_specs=[smem()] + [vmem()] * 6,
        out_specs=[vmem()] * 3,
        compiler_params=params(),
        name="self_forward",
    )(place_of, x_all, gain_one, head_w, table, doc_row, doc_col)
    o1_heads = lax.all_to_all(mixed.reshape(dp, rows, 128), "dp", 0, 0, tiled=True)[::copies]

    states = jnp.swapaxes(e_all, 0, 1).reshape(micro_count, dp * part, width)
    ke = dot(states, cross_kv[0]).astype(BF16)
    ve = dot(states, cross_kv[1]).astype(BF16)

    row32 = jax.ShapeDtypeStruct((tokens, width), F32)
    row16 = jax.ShapeDtypeStruct((tokens, width), BF16)
    o1, x1, n2, q2, o2, x2, n3 = pl.pallas_call(
        mid_forward_kernel,
        out_shape=[row16, row32, row16, row16, row16, row32, row16],
        in_specs=[vmem()] * 9,
        out_specs=[vmem()] * 7,
        compiler_params=params(),
        name="mid_forward",
    )(o1_heads, x, wo, gain_two, wq2, ke, ve, wc, gain_three)

    n_group = both_tokens(n3)
    hid, da, db, y32, y16, d32, d16 = dense_layer(
        n_group, g_group, gate_up[0], gate_up[1], dense_down, tokens
    )
    if fs == 2:
        dn3, dn3_more = d32[:tokens], swap_fs(d16[tokens:])
        dense_out = y32[:tokens] + swap_fs(y16[tokens:]).astype(F32)
    else:
        dn3 = jnp.zeros((tokens, width), F32)
        dn3_more = lax.psum_scatter(d16, "fsdp", scatter_dimension=0, tiled=True)
        dense_out = lax.psum_scatter(y16, "fsdp", scatter_dimension=0, tiled=True).astype(F32)
    outputs = (x2 + dense_out).astype(BF16)

    gx2b, dq2, gx1, gx1b, do1_heads, dkv, dc_two = pl.pallas_call(
        mid_backward_kernel,
        out_shape=[
            row16,
            row16,
            row32,
            row16,
            jax.ShapeDtypeStruct((heads, rows, 128), BF16),
            jax.ShapeDtypeStruct((dp, micro_count, part, 2 * width), BF16),
            jax.ShapeDtypeStruct((2, width), F32),
        ],
        in_specs=[vmem()] * 13,
        out_specs=[vmem()] * 7,
        scratch_shapes=[pltpu.VMEM((tokens, width), BF16)],
        compiler_params=params(),
        name="mid_backward",
    )(g, dn3, dn3_more, x2, gain_three, wc, q2, ke, ve, wq2, x1, gain_two, wo)
    do1 = lax.all_to_all(
        jnp.repeat(do1_heads, copies, axis=0) if copies > 1 else do1_heads, "dp", 0, 0, tiled=True
    ).reshape(length, 128)

    dqkv, table_grad = pl.pallas_call(
        self_backward_kernel,
        out_shape=[
            jax.ShapeDtypeStruct((length, 384), BF16),
            jax.ShapeDtypeStruct((TILE, length), F32),
        ],
        in_specs=[vmem()] * 5,
        out_specs=[vmem()] * 2,
        scratch_shapes=[pltpu.VMEM((length, 128), F32), pltpu.VMEM((length, 128), F32)],
        compiler_params=params(),
        name="self_backward",
    )(qkv, do1, table, doc_row, doc_col)
    head_grad = pl.pallas_call(
        head_weight_kernel,
        out_shape=jax.ShapeDtypeStruct((fs, span * 3 // 2, 128), BF16),
        in_specs=[vmem()] * 2,
        out_specs=vmem(),
        compiler_params=params(),
        name="head_weight",
    )(n_all, dqkv)
    if fs == 2:
        kept = lax.dynamic_index_in_dim(head_grad, shard, 0, keepdims=False)
        sent = lax.dynamic_index_in_dim(head_grad, 1 - shard, 0, keepdims=False)
        head_sum = (kept.astype(F32) + swap_fs(sent).astype(F32)).astype(BF16)
    else:
        head_sum = lax.psum_scatter(head_grad, "fsdp", scatter_dimension=0, tiled=False)
    head_pieces = gather_all(head_sum[None])
    head_places = place_of[jnp.arange(heads) * copies]
    grad_query_self, grad_key_self, grad_value_self = pl.pallas_call(
        head_spread_kernel,
        out_shape=[jax.ShapeDtypeStruct((span, width), F32)] * 3,
        in_specs=[smem(), vmem()],
        out_specs=[vmem()] * 3,
        compiler_params=params(),
        name="head_spread",
    )(head_places, head_pieces)

    table_sums = jnp.sum(bucket_sums(edges, table_grad, bias_all.shape[0]), axis=1)

    own_d = lax.all_to_all(dqkv.reshape(dp, rows, 384), "dp", 0, 0, tiled=True)[::copies]
    own_d = own_d.reshape(heads, rows, 3, 2, 64).transpose(2, 3, 1, 0, 4).reshape(3, tokens, width)
    first = whole_rows(jnp.stack([query_self, key_self, value_self]))
    dn1 = sum(dot_t(own_d[at], first[at]) for at in range(3))
    back, dc_one = norm_back(x.astype(F32).reshape(tokens, width), gain_one, dn1)
    grad_inputs = gx1 + back

    own_dkv = lax.psum_scatter(dkv, "dp", scatter_dimension=0, tiled=False)
    own_dkv = own_dkv.reshape(micro_count * part, 2 * width)
    grad_encoded = dot_t(own_dkv[:, :width], cross_kv[0]) + dot_t(own_dkv[:, width:], cross_kv[1])

    chips = dp // 2
    half = span // 2

    def group_left(values):
        if fs == 2:
            kept = lax.dynamic_slice_in_dim(values, shard * span, span, axis=1)
            sent = lax.dynamic_slice_in_dim(values, (1 - shard) * span, span, axis=1)
            return jnp.concatenate([kept, swap_fs(sent)], axis=0)
        return lax.all_to_all(values, "fsdp", 1, 0, tiled=True)

    def chip_left(values, size):
        kept = lax.dynamic_slice_in_dim(values, core * size, size, axis=1)
        sent = lax.dynamic_slice_in_dim(values, (1 - core) * size, size, axis=1)
        return jnp.concatenate([kept, swap_dp(sent, 1)], axis=0)

    def chip_all(values):
        return jnp.concatenate([values, swap_dp(values, 1)], axis=0)

    def in_order(values):
        values = lax.all_gather(values, "dp", axis=0, tiled=True)
        return values.reshape((chips, 2) + values.shape[1:]).astype(F32)

    def row_block(j):
        return (j % 2) * chips + j // 2

    def token_weights(lefts, rights):
        left = jnp.concatenate([group_left(v) for v in lefts], axis=0)
        left = chip_left(left, half)
        right = chip_all(both_tokens(jnp.concatenate(rights, axis=1)))
        group = left.shape[0] // 2 // len(lefts)
        totals = []
        at = 0
        for place, value in enumerate(rights):
            low = left[place * group : (place + 1) * group]
            high = left[(len(lefts) + place) * group : (len(lefts) + place + 1) * group]
            totals.append(
                t_dot(jnp.concatenate([low, high], axis=0), right[:, at : at + value.shape[1]])
            )
            at += value.shape[1]
        made = jnp.stack([total.astype(BF16).reshape(chips, -1, total.shape[1]) for total in totals], axis=1)
        made = sum_chips(made)
        if made.shape[2] % 8:
            pieces = in_order(made).transpose(2, 1, 0, 3, 4)
            return [piece.reshape(span, -1) for piece in pieces]
        pieces = gather_all(made)
        return spread(
            source,
            pieces[:, None],
            [(span, pieces.shape[-1])] * len(lefts),
            lambda t, h, where: (row_block(where[t]), 0),
        )

    grad_query_cross, grad_output_cross, grad_output_self = token_weights(
        [n2, o2, o1], [dq2, gx2b, gx1b]
    )
    (grad_kv_cross,) = token_weights([e.reshape(micro_count * part, width)], [own_dkv])
    grad_key_cross, grad_value_cross = grad_kv_cross[:, :width], grad_kv_cross[:, width:]

    picked = n_group.reshape(n_group.shape[0], fs, 2, half)
    n_mine = lax.dynamic_index_in_dim(picked, core, 2, keepdims=False)
    n_sent = lax.dynamic_index_in_dim(picked, 1 - core, 2, keepdims=False)
    n_chip = jnp.concatenate([n_mine, swap_dp(n_sent, 1)], axis=0)
    back_chip = chip_all(jnp.concatenate([da, db, hid], axis=1))
    g_chip = chip_left(g_group, width // 2)
    n_chip = n_chip.reshape(n_chip.shape[0], fs * half)
    made = t_dot(n_chip, back_chip[:, : 2 * hidden]).astype(BF16)
    made = made.reshape(fs, half, 2, hidden).transpose(0, 2, 1, 3)
    if fs == 2:
        kept = lax.dynamic_index_in_dim(made, shard, 0, keepdims=False)
        sent = lax.dynamic_index_in_dim(made, 1 - shard, 0, keepdims=False)
        halves = jnp.stack([kept, swap_fs(sent)])
    else:
        halves = lax.all_to_all(made, "fsdp", 0, 0, tiled=True)
    halves = halves.reshape(fs, 2, chips, half // chips, hidden).transpose(2, 0, 1, 3, 4)
    halves = sum_chips(halves)
    dense_where = jnp.concatenate([source, jnp.where(fs == 2, shard, 0)[None].astype(jnp.int32)])
    if halves.shape[3] % 8 or hidden % 128:
        ordered = in_order(halves).transpose(3, 1, 0, 4, 2, 5).reshape(2, span, fs * hidden)
        grad_dense_gate, grad_dense_up = ordered[0], ordered[1]
    else:
        grad_dense_gate, grad_dense_up = spread(
            dense_where,
            gather_all(halves),
            [(span, fs * hidden)] * 2,
            lambda t, h, where: (row_block(where[t]), h ^ where[dp]),
        )
    down = t_dot(back_chip[:, 2 * hidden :], g_chip).astype(BF16)
    down = down.reshape(chips, hidden // chips, width // 2)
    down = sum_chips(down)
    if down.shape[1] % 8:
        grad_dense_down = in_order(down).transpose(0, 2, 1, 3).reshape(hidden, width)
    else:
        (grad_dense_down,) = spread(
            source,
            gather_all(down)[:, None, None],
            [(hidden, width)],
            lambda t, h, where: (where[t] // 2, where[t] % 2),
        )

    column = (jnp.arange(heads) == head) & (me % copies == 0)
    bias_row = jnp.where(column[None, :], table_sums[:, None], 0.0).reshape(1, -1)
    bias_row = jnp.pad(bias_row, ((0, 0), (0, width - bias_row.shape[1])))
    sums = lax.psum(jnp.concatenate([dc_one, dc_two, bias_row], axis=0), ("dp", "fsdp"))
    own = lax.dynamic_slice_in_dim(sums[:3], shard * span, span, axis=1)
    grad_bias = sums[3, : bias_all.size].reshape(bias_all.shape)
    grad_bias = lax.dynamic_slice_in_dim(
        grad_bias, shard * position_bias.shape[0], position_bias.shape[0], axis=0
    )
    shape = (micro_count, 1, rows, width)
    return (
        outputs.reshape(shape),
        grad_inputs.reshape(shape),
        grad_encoded.reshape(micro_count, 1, part, width),
        own[0],
        grad_query_self,
        grad_key_self,
        grad_value_self,
        grad_output_self,
        grad_bias,
        own[2],
        grad_query_cross,
        grad_key_cross,
        grad_value_cross,
        grad_output_cross,
        own[1],
        grad_dense_gate,
        grad_dense_up,
        grad_dense_down,
    )


def solution(mesh):
    matrix = P("fsdp", None)
    token = P(None, "fsdp", "dp", None)
    weights = (
        (P("fsdp"),)
        + (matrix,) * 5
        + (P("fsdp"),)
        + (matrix,) * 4
        + (P("fsdp"),)
        + (matrix,) * 3
    )
    return jax.shard_map(
        per_device,
        mesh=mesh,
        in_specs=(token,) * 3 + (P(None, "fsdp", None), P()) + weights,
        out_specs=(token,) * 3 + weights,
        check_vma=False,
    )
```

time: 2240 us -> 775 us (0.35)
  waiting for transfers between devices: 1780 us -> 267 us
  matrix products: 252 us -> 27.3 us
  Pallas kernels: 0 us -> 139 us
  starting transfers between devices: 2.88 us -> 83.5 us
  local copies, waits for them, and re-layouts: 68.3 us -> 106 us
  other arithmetic: 60 us -> 89.1 us
    all_gather x19 -> x1, waiting for transfers between devices: 667 us -> 0.01 us  [per_device(): e_all = lax.all_gather(e, 'dp', axis=0)]
    reduce_scatter x12 -> x1, waiting for transfers between devices: 462 us -> 0.01 us  [per_device(): own_dkv = lax.psum_scatter(dkv, 'dp', scatter_dimension=0, tiled=False)]
    unnamed x48 -> x2, waiting for transfers between devices: 380 us -> 0.49 us
    psum x1 -> x0, waiting for transfers between devices: 267 us -> none  [per_device(): lax.psum(totals[8].astype(jnp.bfloat16), 'dp').astype(jnp.float32)]
    ppermute x0 -> x77, waiting for transfers between devices: none -> 263 us  [the longest x58 156 us: swap_dp(): return lax.ppermute(values, 'dp', [(j, j ^ bit) for j in range(dp)])]
    dot_general x93 -> x13, matrix products: 252 us -> 27.3 us  [the longest x6 10 us: t_dot(): lax.dot_general(left, right, (((0,), (0,)), ((), ())), preferred_element_...]
    pallas_call x0 -> x13, Pallas kernels: none -> 139 us  [the longest x4 52.4 us: spread(): pl.pallas_call(functools.partial(spread_kernel, kinds), grid_spec=pltpu.P...]
    ppermute x0 -> x77, starting transfers between devices: none -> 70.3 us  [the longest x58 50.8 us: swap_dp(): return lax.ppermute(values, 'dp', [(j, j ^ bit) for j in range(dp)])]
  transfers between devices with their start and end apart: 40 -> 82, of which waited for: 36 -> 29; matrix products, arithmetic and copies ran while one was open for 14% -> 27% of each run, Pallas kernels for 0% -> 16%
where the time goes in v1:
time: 775 us; the launch traced here: 768 us
  waiting for transfers between devices  267 us (34%)
  Pallas kernels  139 us (18%)
  local copies, waits for them, and re-layouts  106 us (14%)
  other arithmetic  89.1 us (11%)
  starting transfers between devices  83.5 us (11%)
  blocking collectives  40.7 us (5%)
  matrix products  27.3 us (4%)
  between operations  15.9 us (2%)
    ppermute x58, waiting for transfers between devices, swap_dp(): return lax.ppermute(values, 'dp', [(j, j ^ bit) for j in range(dp)])  156 us
    ppermute x19, waiting for transfers between devices, swap_fs(): return lax.ppermute(values, 'fsdp', [(j, 1 - j) for j in range(2)])  106 us
    pallas_call x4, Pallas kernels, spread(): pl.pallas_call(functools.partial(spread_kernel, kinds), grid_spec=pltpu.P...  52.4 us
    ppermute x58, starting transfers between devices, swap_dp(): return lax.ppermute(values, 'dp', [(j, j ^ bit) for j in range(dp)])  50.8 us
    psum x1, blocking collectives, per_device(): lax.psum(jnp.concatenate([dc_one, dc_two, bias_row], axis=0), ('dp', 'fsd...  40.7 us
    unnamed x210, local copies, waits for them, and re-layouts  36.9 us
    select_n x9, other arithmetic, two(): jnp.where(which == 0, jnp.concatenate([first, second], axis=-2), jnp.conc...  30.9 us
    ppermute x19, starting transfers between devices, swap_fs(): return lax.ppermute(values, 'fsdp', [(j, 1 - j) for j in range(2)])  19.5 us
  transfers between devices with their start and end apart: 82, of which 29 were waited for; matrix products, arithmetic and copies ran while one was open for 27% of the time, Pallas kernels for 16%

profile of v1, /device:TPU:0, one launch (start us, length us, event | category | flops | bytes accessed | tf_op | source)
XLA Modules:
  0.0 767.7 jit_solution(17541788282554249121)
XLA Ops:
  7.2 4.1 collective-permute-start
  59.1 4.4 bias_table.1.table_ref
  76.4 23.5 %collective-permute-done.23 = bf16[128,1024]{1,0:T(8,128)(2,1)S(1)} collective-permute-done((bf16[128,1024]{1,0:T(8,128)(2,1)S(1)}, bf16[128,1024]{1,0:T(8,128)(2,1)S(1)}, u32[]{:S(2)}, u32[]{:S(2)}) %collective-permute-start.23) | collective-permute-done | bytes 262176 | tf_op jit(solution)/shard_map/ppermute | solution.py:478
  104.7 4.6 collective-permute-done.4
  110.1 4.9 collective-permute-done.5
  124.7 24.9 %collective-permute-done.24 = bf16[2,256,1408]{2,1,0:T(8,128)(2,1)} collective-permute-done((bf16[2,256,1408]{2,1,0:T(8,128)(2,1)S(1)}, bf16[2,256,1408]{2,1,0:T(8,128)(2,1)}, u32[]{:S(2)}, u32[]{:S(2)}) %collective-permute-start.24) | collective-permute-done | bytes 1441824 | tf_op jit(solution)/shard_map/ppermute | solution.py:478
  152.3 11.7 %self_forward.1 = (bf16[16,2,64,1024]{3,2,1,0:T(8,128)(2,1)}, bf16[1024,384]{1,0:T(8,128)(2,1)}, bf16[1024,128]{1,0:T(8,128)(2,1)}) custom-call(s32[16]{0:T(128)} %copy-done, bf16[16,2,64,1024]{3,2,1,0:T(8,128)(2,1)} %copy-done.19, f32[1,1024]{1,0:T(1,128)} %get-tuple-element.261.gain_ref, bf16[1024,384]{1,0:T(8,128)(2,1)} %pad_maximum_fusion.11.w_ref, ...), custom_call_target="tpu_custom_call" | custom-call | tf_op jit(solution)/shard_map/self_forward/pallas_call | solution.py:586
  163.9 4.5 all-to-all-start
  168.5 14.8 %collective-permute-done.18 = bf16[3,256,1024]{2,1,0:T(8,128)(2,1)} collective-permute-done((bf16[3,256,1024]{2,1,0:T(8,128)(2,1)}, bf16[3,256,1024]{2,1,0:T(8,128)(2,1)}, u32[]{:S(2)}, u32[]{:S(2)}) %collective-permute-start.18) | collective-permute-done | bytes 1572896 | tf_op jit(solution)/shard_map/ppermute | solution.py:478
  183.3 30.2 %collective-permute-done.28 = bf16[3,256,1024]{2,1,0:T(8,128)(2,1)} collective-permute-done((bf16[3,256,1024]{2,1,0:T(8,128)(2,1)}, bf16[3,256,1024]{2,1,0:T(8,128)(2,1)}, u32[]{:S(2)}, u32[]{:S(2)}) %collective-permute-start.28) | collective-permute-done | bytes 1572896 | tf_op jit(solution)/shard_map/ppermute | solution.py:478
  221.7 6.5 maximum_select_fusion.2
  236.9 4.0 maximum_select_fusion
  246.5 3.7 convert_bitcast_fusion.1.ke_ref
  250.2 3.7 convert_bitcast_fusion.ve_ref
  253.9 12.0 %mid_forward.1 = (bf16[128,1024]{1,0:T(8,128)(2,1)}, f32[128,1024]{1,0:T(8,128)}, bf16[128,1024]{1,0:T(8,128)(2,1)}, bf16[128,1024]{1,0:T(8,128)(2,1)}, bf16[128...) custom-call(bf16[16,64,128]{2,1,0:T(8,128)(2,1)} %all-to-all-done.o1_ref, ...), custom_call_target="tpu_custom_call" | custom-call | tf_op jit(solution)/shard_map/mid_forward/pallas_call | solution.py:606
  267.5 5.3 maximum_select_fusion.1
  275.0 7.0 collective-permute-done.22
  282.8 13.4 %dense_layer.1 = (bf16[256,1408]{1,0:T(8,128)(2,1)}, bf16[256,1408]{1,0:T(8,128)(2,1)}, bf16[256,1408]{1,0:T(8,128)(2,1)}, f32[256,1024]{1,0:T(8,128)}, bf16[256...) custom-call(bf16[256,1024]{1,0:T(8,128)(2,1)} %copy-done.25, ...), custom_call_target="tpu_custom_call" | custom-call | tf_op jit(solution)/shard_map/dense_layer/pallas_call | solution.py:390
  309.8 3.8 collective-permute-done.37
  315.1 16.6 %mid_backward.1 = (bf16[128,1024]{1,0:T(8,128)(2,1)}, bf16[128,1024]{1,0:T(8,128)(2,1)}, f32[128,1024]{1,0:T(8,128)}, bf16[128,1024]{1,0:T(8,128)(2,1)}, bf16[16...) custom-call(bf16[2,64,1024]{2,1,0:T(8,128)(2,1)} %bitcast.288, ...), custom_call_target="tpu_custom_call" | custom-call | tf_op jit(solution)/shard_map/mid_backward/pallas_call | solution.py:628
  331.7 3.7 all-to-all-start.1
  346.1 9.8 %self_backward.1 = (bf16[1024,384]{1,0:T(8,128)(2,1)}, f32[256,1024]{1,0:T(8,128)}) custom-call(bf16[1024,384]{1,0:T(8,128)(2,1)} %get-tuple-element.74.qkv_ref, bf16[1024,128]{1,0:T(8,128)(2,1)} %bitcast.299, f32[256,1024]{1,0:T(8,128)} %bias_table.1.table_ref, s32[2,1024]{1,0:T(2,128)} %bitcast_select_fusion.doc_row_ref, ...), custom_call_target="tpu_custom_call" | custom-call | tf_op jit(solution)/shard_map/self_backward/pallas_call | solution.py:649
  355.8 5.9 head_weight.1
  365.1 4.7 all-to-all-start.2
  369.8 7.4 bucket_sums.1
  381.7 34.1 %collective-permute-done.31 = bf16[1,768,128]{2,1,0:T(8,128)(2,1)S(1)} collective-permute-done((bf16[1,768,128]{2,1,0:T(8,128)(2,1)S(1)}, bf16[1,768,128]{2,1,0:T(8,128)(2,1)S(1)}, u32[]{:S(2)}, u32[]{:S(2)}) %collective-permute-start.31) | collective-permute-done | bytes 196640 | tf_op jit(solution)/shard_map/ppermute | solution.py:475
  418.0 17.1 %collective-permute-done.32 = bf16[2,768,128]{2,1,0:T(8,128)(2,1)S(1)} collective-permute-done((bf16[2,768,128]{2,1,0:T(8,128)(2,1)S(1)}, bf16[2,768,128]{2,1,0:T(8,128)(2,1)S(1)}, u32[]{:S(2)}, u32[]{:S(2)}) %collective-permute-start.32) | collective-permute-done | bytes 393248 | tf_op jit(solution)/shard_map/ppermute | solution.py:475
  438.3 5.0 convolution_convert_fusion
  443.3 5.7 reshape.356
  475.5 40.7 %psum.7 = f32[4,1024]{1,0:T(4,128)S(1)} all-reduce(f32[4,1024]{1,0:T(4,128)S(1)} %select_maximum_fusion), channel_id=1, replica_groups=mesh['dp'=16,'fsdp'=2] {'dp','fsdp'}, use_global_device_ids=true, to_apply=%region_7.8 | all-reduce | flops 4096 | bytes 32768 | tf_op jit(solution)/shard_map/psum | solution.py:801
  527.8 6.3 collective-permute-done.71
  535.4 4.9 collective-permute-done.41
  548.3 6.8 collective-permute-done.42
  560.7 4.5 collective-permute-done.43
  571.2 4.9 collective-permute-done.44
  582.1 5.7 head_spread.1
  594.8 7.2 collective-permute-done.63
  604.6 15.9 %collective-permute-done.64 = bf16[1,2,2,32,1408]{4,3,2,1,0:T(8,128)(2,1)S(1)} collective-permute-done((bf16[1,2,2,32,1408]{4,3,2,1,0:T(8,128)(2,1)S(1)}, bf16[1,2,2,32,1408]{4,3,2,1,0:T(8,128)(2,1)S(1)}, u32[]{:S(2)}, u32[]{:S(2)}) %collective-permute-start.64) | collective-permute-done | bytes 360480 | tf_op jit(solution)/shard_map/ppermute | solution.py:475
  626.9 11.0 %collective-permute-done.65 = bf16[1,2,2,32,1408]{4,3,2,1,0:T(8,128)(2,1)S(1)} collective-permute-done((bf16[1,2,2,32,1408]{4,3,2,1,0:T(8,128)(2,1)S(1)}, bf16[1,2,2,32,1408]{4,3,2,1,0:T(8,128)(2,1)S(1)}, u32[]{:S(2)}, u32[]{:S(2)}) %collective-permute-start.65) | collective-permute-done | bytes 360480 | tf_op jit(solution)/shard_map/ppermute | solution.py:475
  642.3 14.7 %collective-permute-done.66 = bf16[2,2,2,32,1408]{4,3,2,1,0:T(8,128)(2,1)S(1)} collective-permute-done((bf16[2,2,2,32,1408]{4,3,2,1,0:T(8,128)(2,1)S(1)}, bf16[2,2,2,32,1408]{4,3,2,1,0:T(8,128)(2,1)S(1)}, u32[]{:S(2)}, u32[]{:S(2)}) %collective-permute-start.66) | collective-permute-done | bytes 720928 | tf_op jit(solution)/shard_map/ppermute | solution.py:475
  666.9 10.9 %spread.7 = f32[1408,1024]{1,0:T(8,128)} custom-call(s32[16]{0:T(128)} %copy-done.79, bf16[16,1,1,176,512]{4,3,2,1,0:T(8,128)(2,1)} %bitcast.115.in_ref), custom_call_target="tpu_custom_call" | custom-call | tf_op jit(solution)/shard_map/spread/pallas_call | solution.py:409
  682.3 5.1 collective-permute-done.55
  687.5 4.3 collective-permute-done.67
  695.5 3.6 collective-permute-start.57
  703.6 11.1 %spread.4 = (f32[512,1024]{1,0:T(8,128)}, f32[512,1024]{1,0:T(8,128)}, f32[512,1024]{1,0:T(8,128)}) custom-call(s32[16]{0:T(128)} %copy-done.79, bf16[16,1,3,32,1024]{4,3,2,1,0:T(8,128)(2,1)} %bitcast.82.in_ref), custom_call_target="tpu_custom_call" | custom-call | tf_op jit(solution)/shard_map/spread/pallas_call | solution.py:409
  720.6 10.5 %spread.5 = f32[512,2048]{1,0:T(8,128)} custom-call(s32[16]{0:T(128)} %copy-done.79, bf16[16,1,1,32,2048]{4,3,2,1,0:T(8,128)(2,1)} %bitcast.91.in_ref), custom_call_target="tpu_custom_call" | custom-call | tf_op jit(solution)/shard_map/spread/pallas_call | solution.py:409
  731.1 4.8 fusion.96
  740.7 19.9 %spread.6 = (f32[512,2816]{1,0:T(8,128)}, f32[512,2816]{1,0:T(8,128)}) custom-call(s32[17]{0:T(128)} %pad_add_fusion.where_ref, bf16[16,2,2,32,1408]{4,3,2,1,0:T(8,128)(2,1)} %copy-done.10), custom_call_target="tpu_custom_call" | custom-call | tf_op jit(solution)/shard_map/spread/pallas_call | solution.py:409
  (503 shorter events, 262.3 us)
Async XLA Ops:
  7.2 236.5 %all-gather.3.cloned.1.call-start = ((), (), s32[]{:S(2)}) async-start(), calls=%async_computation.5 | async-start | bytes 2228224 | tf_op jit(solution)/shard_map/all_gather | solution.py:546
  7.2 64.8 %collective-permute-start = (bf16[2,64,1024]{2,1,0:T(8,128)(2,1)}, bf16[2,64,1024]{2,1,0:T(8,128)(2,1)}, u32[]{:S(2)}, u32[]{:S(2)}) collective-permute-start(bf16[2,64,1024]{2,1,0:T(8,128)(2,1)} %bitcast.263), channel_id=1, source_target_pairs={{0,16},{2,18},{4,20},{6,22},{8,24},{10,26},{12,28},{14,30},{16,0},... | collective-permute-start | bytes 786440 | tf_op jit(solution)/shard_map/ppermute | solution.py:475
  11.3 63.3 %collective-permute-start.1 = (bf16[2,64,1024]{2,1,0:T(8,128)(2,1)}, bf16[2,64,1024]{2,1,0:T(8,128)(2,1)}, u32[]{:S(2)}, u32[]{:S(2)}) collective-permute-start(bf16[2,64,1024]{2,1,0:T(8,128)(2,1)} %bitcast.264), channel_id=1, source_target_pairs={{0,8},{2,10},{4,12},{6,14},{8,0},{10,2},{12,4},{14,6},{16,24},{18,... | collective-permute-start | bytes 786440 | tf_op jit(solution)/shard_map/ppermute | solution.py:475
  12.9 90.7 %collective-permute-start.3 = (bf16[2,64,1024]{2,1,0:T(8,128)(2,1)}, bf16[2,64,1024]{2,1,0:T(8,128)(2,1)}, u32[]{:S(2)}, u32[]{:S(2)}) collective-permute-start(bf16[2,64,1024]{2,1,0:T(8,128)(2,1)} %bitcast.265), channel_id=1, source_target_pairs={{0,4},{2,6},{4,0},{6,2},{8,12},{10,14},{12,8},{14,10},{16,20},{18,... | collective-permute-start | bytes 786440 | tf_op jit(solution)/shard_map/ppermute | solution.py:475
  17.1 46.5 %collective-permute-start.15 = (bf16[3,512]{1,0:T(4,128)(2,1)}, bf16[3,512]{1,0:T(4,128)(2,1)}, u32[]{:S(2)}, u32[]{:S(2)}) collective-permute-start(bf16[3,512]{1,0:T(4,128)(2,1)} %pad_maximum_fusion.24), channel_id=1, source_target_pairs={{0,1},{1,0},{2,3},{3,2},{4,5},{5,4},{6,7},{7,6},{8,9},{9,8},{10,11... | collective-permute-start | bytes 9224 | tf_op jit(solution)/shard_map/ppermute | solution.py:478
  18.6 37.5 %collective-permute-start.17 = (bf16[16,16]{0,1:T(8,128)(2,1)}, bf16[16,16]{0,1:T(8,128)(2,1)}, u32[]{:S(2)}, u32[]{:S(2)}) collective-permute-start(bf16[16,16]{0,1:T(8,128)(2,1)} %bitcast.327), channel_id=1, source_target_pairs={{0,1},{1,0},{2,3},{3,2},{4,5},{5,4},{6,7},{7,6},{8,9},{9,8},{10,11... | collective-permute-start | bytes 1544 | tf_op jit(solution)/shard_map/ppermute | solution.py:478
  67.9 47.6 %collective-permute-start.7 = (bf16[2,64,1024]{2,1,0:T(8,128)(2,1)S(1)}, bf16[2,64,1024]{2,1,0:T(8,128)(2,1)S(1)}, u32[]{:S(2)}, u32[]{:S(2)}) collective-permute-start(bf16[2,64,1024]{2,1,0:T(8,128)(2,1)S(1)} %bitcast.267), channel_id=1, source_target_pairs={{0,2},{2,0},{4,6},{6,4},{8,10},{10,8},{12,14},{14,12},{16,18},{18,... | collective-permute-start | bytes 786440 | tf_op jit(solution)/shard_map/ppermute | solution.py:475
  68.5 54.6 %collective-permute-start.20 = (bf16[2,256,1024]{1,2,0:T(8,128)(2,1)}, bf16[2,256,1024]{1,2,0:T(8,128)(2,1)}, u32[]{:S(2)}, u32[]{:S(2)}) collective-permute-start(bf16[2,256,1024]{1,2,0:T(8,128)(2,1)} %fusion.37), channel_id=1, source_target_pairs={{0,1},{1,0},{2,3},{3,2},{4,5},{5,4},{6,7},{7,6},{8,9},{9,8},{10,11... | collective-permute-start | bytes 3145736 | tf_op jit(solution)/shard_map/ppermute | solution.py:478
  72.1 27.9 %collective-permute-start.23 = (bf16[128,1024]{1,0:T(8,128)(2,1)S(1)}, bf16[128,1024]{1,0:T(8,128)(2,1)S(1)}, u32[]{:S(2)}, u32[]{:S(2)}) collective-permute-start(bf16[128,1024]{1,0:T(8,128)(2,1)S(1)} %bitcast.289), channel_id=1, source_target_pairs={{0,1},{1,0},{2,3},{3,2},{4,5},{5,4},{6,7},{7,6},{8,9},{9,8},{10,11... | collective-permute-start | bytes 786440 | tf_op jit(solution)/shard_map/ppermute | solution.py:478
  74.7 27.7 %collective-permute-start.2 = (bf16[2,64,1024]{2,1,0:T(8,128)(2,1)}, bf16[2,64,1024]{2,1,0:T(8,128)(2,1)S(1)}, u32[]{:S(2)}, u32[]{:S(2)}) collective-permute-start(bf16[2,64,1024]{2,1,0:T(8,128)(2,1)} %collective-permute-done), channel_id=1, source_target_pairs={{0,8},{2,10},{4,12},{6,14},{8,0},{10,2},{12,4},{14,6},{16,24},{18,... | collective-permute-start | bytes 786440 | tf_op jit(solution)/shard_map/ppermute | solution.py:475
  115.0 34.6 %collective-permute-start.24 = (bf16[2,256,1408]{2,1,0:T(8,128)(2,1)S(1)}, bf16[2,256,1408]{2,1,0:T(8,128)(2,1)}, u32[]{:S(2)}, u32[]{:S(2)}) collective-permute-start(bf16[2,256,1408]{2,1,0:T(8,128)(2,1)S(1)} %copy-done.46), channel_id=1, source_target_pairs={{0,1},{1,0},{2,3},{3,2},{4,5},{5,4},{6,7},{7,6},{8,9},{9,8},{10,11... | collective-permute-start | bytes 4325384 | tf_op jit(solution)/shard_map/ppermute | solution.py:478
  119.4 63.9 %collective-permute-start.18 = (bf16[3,256,1024]{2,1,0:T(8,128)(2,1)}, bf16[3,256,1024]{2,1,0:T(8,128)(2,1)}, u32[]{:S(2)}, u32[]{:S(2)}) collective-permute-start(bf16[3,256,1024]{2,1,0:T(8,128)(2,1)} %fusion.26), channel_id=1, source_target_pairs={{0,1},{1,0},{2,3},{3,2},{4,5},{5,4},{6,7},{7,6},{8,9},{9,8},{10,11... | collective-permute-start | bytes 4718600 | tf_op jit(solution)/shard_map/ppermute | solution.py:478
  119.9 93.6 %collective-permute-start.28 = (bf16[3,256,1024]{2,1,0:T(8,128)(2,1)}, bf16[3,256,1024]{2,1,0:T(8,128)(2,1)}, u32[]{:S(2)}, u32[]{:S(2)}) collective-permute-start(bf16[3,256,1024]{2,1,0:T(8,128)(2,1)} %fusion.24), channel_id=1, source_target_pairs={{0,1},{1,0},{2,3},{3,2},{4,5},{5,4},{6,7},{7,6},{8,9},{9,8},{10,11... | collective-permute-start | bytes 4718600 | tf_op jit(solution)/shard_map/ppermute | solution.py:478
  123.2 90.4 %collective-permute-start.21 = (bf16[2,256,1024]{1,2,0:T(8,128)(2,1)}, bf16[2,256,1024]{1,2,0:T(8,128)(2,1)}, u32[]{:S(2)}, u32[]{:S(2)}) collective-permute-start(bf16[2,256,1024]{1,2,0:T(8,128)(2,1)} %collective-permute-done.20), channel_id=1, source_target_pairs={{0,2},{2,0},{4,6},{6,4},{8,10},{10,8},{12,14},{14,12},{16,18},{18,... | collective-permute-start | bytes 3145736 | tf_op jit(solution)/shard_map/ppermute | solution.py:475
  124.6 25.1 %collective-permute-start.14 = (bf16[2,64,1024]{2,1,0:T(8,128)(2,1)S(1)}, bf16[2,64,1024]{2,1,0:T(8,128)(2,1)S(1)}, u32[]{:S(2)}, u32[]{:S(2)}) collective-permute-start(bf16[2,64,1024]{2,1,0:T(8,128)(2,1)S(1)} %collective-permute-done.6), channel_id=1, source_target_pairs={{0,2},{2,0},{4,6},{6,4},{8,10},{10,8},{12,14},{14,12},{16,18},{18,... | collective-permute-start | bytes 786440 | tf_op jit(solution)/shard_map/ppermute | solution.py:475
  149.6 69.4 %collective-permute-start.25 = (bf16[2,256,1408]{2,1,0:T(8,128)(2,1)}, bf16[2,256,1408]{2,1,0:T(8,128)(2,1)S(1)}, u32[]{:S(2)}, u32[]{:S(2)}) collective-permute-start(bf16[2,256,1408]{2,1,0:T(8,128)(2,1)} %collective-permute-done.24), channel_id=1, source_target_pairs={{0,2},{2,0},{4,6},{6,4},{8,10},{10,8},{12,14},{14,12},{16,18},{18,... | collective-permute-start | bytes 4325384 | tf_op jit(solution)/shard_map/ppermute | solution.py:475
  149.7 471.1 %collective-permute-start.49 = (bf16[128,256]{1,0:T(8,128)(2,1)}, bf16[128,256]{1,0:T(8,128)(2,1)}, u32[]{:S(2)}, u32[]{:S(2)}) collective-permute-start(bf16[128,256]{1,0:T(8,128)(2,1)} %get-tuple-element.253), channel_id=1, source_target_pairs={{0,2},{2,0},{4,6},{6,4},{8,10},{10,8},{12,14},{14,12},{16,18},{18,... | collective-permute-start | bytes 196616 | tf_op jit(solution)/shard_map/ppermute | solution.py:475
  163.9 90.0 %all-to-all-start = ((bf16[16,64,128]{2,1,0:T(8,128)(2,1)}), bf16[16,64,128]{2,1,0:T(8,128)(2,1)}, u32[]{:S(2)}, u32[]{:S(2)}) async-start(bf16[16,64,128]{2,1,0:T(8,128)(2,1)} %bitcast.316), calls=%async_computation | async-start | bytes 524288 | tf_op jit(solution)/shard_map/all_to_all | solution.py:598
  183.3 47.8 %collective-permute-start.19 = (bf16[3,256,1024]{2,1,0:T(8,128)(2,1)}, bf16[3,256,1024]{2,1,0:T(8,128)(2,1)S(1)}, u32[]{:S(2)}, u32[]{:S(2)}) collective-permute-start(bf16[3,256,1024]{2,1,0:T(8,128)(2,1)} %collective-permute-done.18), channel_id=1, source_target_pairs={{0,2},{2,0},{4,6},{6,4},{8,10},{10,8},{12,14},{14,12},{16,18},{18,... | collective-permute-start | bytes 4718600 | tf_op jit(solution)/shard_map/ppermute | solution.py:475
  213.6 20.3 %collective-permute-start.29 = (bf16[3,256,1024]{2,1,0:T(8,128)(2,1)}, bf16[3,256,1024]{2,1,0:T(8,128)(2,1)S(1)}, u32[]{:S(2)}, u32[]{:S(2)}) collective-permute-start(bf16[3,256,1024]{2,1,0:T(8,128)(2,1)} %collective-permute-done.28), channel_id=1, source_target_pairs={{0,2},{2,0},{4,6},{6,4},{8,10},{10,8},{12,14},{14,12},{16,18},{18,... | collective-permute-start | bytes 4718600 | tf_op jit(solution)/shard_map/ppermute | solution.py:475
  274.4 28.5 %collective-permute-start.36 = (bf16[128,512]{1,0:T(8,128)(2,1)S(1)}, bf16[128,512]{1,0:T(8,128)(2,1)S(1)}, u32[]{:S(2)}, u32[]{:S(2)}) collective-permute-start(bf16[128,512]{1,0:T(8,128)(2,1)S(1)} %get-tuple-element.248), channel_id=1, source_target_pairs={{0,1},{1,0},{2,3},{3,2},{4,5},{5,4},{6,7},{7,6},{8,9},{9,8},{10,11... | collective-permute-start | bytes 393224 | tf_op jit(solution)/shard_map/ppermute | solution.py:478
  298.0 40.5 %collective-permute-start.26 = (bf16[128,1024]{1,0:T(8,128)(2,1)}, bf16[128,1024]{1,0:T(8,128)(2,1)}, u32[]{:S(2)}, u32[]{:S(2)}) collective-permute-start(bf16[128,1024]{1,0:T(8,128)(2,1)} %slice.172), channel_id=1, source_target_pairs={{0,1},{1,0},{2,3},{3,2},{4,5},{5,4},{6,7},{7,6},{8,9},{9,8},{10,11... | collective-permute-start | bytes 786440 | tf_op jit(solution)/shard_map/ppermute | solution.py:478
  307.5 130.8 %collective-permute-start.60 = (bf16[256,4224]{1,0:T(8,128)(2,1)}, bf16[256,4224]{1,0:T(8,128)(2,1)}, u32[]{:S(2)}, u32[]{:S(2)}) collective-permute-start(bf16[256,4224]{1,0:T(8,128)(2,1)} %constant_dynamic-update-slice_fusion.23), channel_id=1, source_target_pairs={{0,2},{2,0},{4,6},{6,4},{8,10},{10,8},{12,14},{14,12},{16,18},{18,... | collective-permute-start | bytes 6488072 | tf_op jit(solution)/shard_map/ppermute | solution.py:475
  313.6 23.6 %collective-permute-start.59 = (bf16[256,2,256]{2,0,1:T(8,128)(2,1)S(1)}, bf16[256,2,256]{2,0,1:T(8,128)(2,1)S(1)}, u32[]{:S(2)}, u32[]{:S(2)}) collective-permute-start(bf16[256,2,256]{2,0,1:T(8,128)(2,1)S(1)} %bitcast.314), channel_id=1, source_target_pairs={{0,2},{2,0},{4,6},{6,4},{8,10},{10,8},{12,14},{14,12},{16,18},{18,... | collective-permute-start | bytes 786440 | tf_op jit(solution)/shard_map/ppermute | solution.py:475
  314.4 48.4 %collective-permute-start.38 = (bf16[768,256]{1,0:T(8,128)(2,1)S(1)}, bf16[768,256]{1,0:T(8,128)(2,1)S(1)}, u32[]{:S(2)}, u32[]{:S(2)}) collective-permute-start(bf16[768,256]{1,0:T(8,128)(2,1)S(1)} %constant_dynamic-slice_fusion.17), channel_id=1, source_target_pairs={{0,2},{2,0},{4,6},{6,4},{8,10},{10,8},{12,14},{14,12},{16,18},{18,... | collective-permute-start | bytes 1179656 | tf_op jit(solution)/shard_map/ppermute | solution.py:475
  335.4 258.6 %reduce-scatter.2.cloned.1.call-start = ((), (), s32[]{:S(2)}) async-start(), calls=%async_computation.4 | async-start | bytes 4456448 | tf_op jit(solution)/shard_map/reduce_scatter | solution.py:695
  337.2 115.8 %collective-permute-start.69 = (bf16[256,512]{1,0:T(8,128)(2,1)}, bf16[256,512]{1,0:T(8,128)(2,1)}, u32[]{:S(2)}, u32[]{:S(2)}) collective-permute-start(bf16[256,512]{1,0:T(8,128)(2,1)} %get-tuple-element.236), channel_id=1, source_target_pairs={{0,2},{2,0},{4,6},{6,4},{8,10},{10,8},{12,14},{14,12},{16,18},{18,... | collective-permute-start | bytes 786440 | tf_op jit(solution)/shard_map/ppermute | solution.py:475
  338.5 77.5 %collective-permute-start.39 = (bf16[128,3072]{1,0:T(8,128)(2,1)S(1)}, bf16[128,3072]{1,0:T(8,128)(2,1)S(1)}, u32[]{:S(2)}, u32[]{:S(2)}) collective-permute-start(bf16[128,3072]{1,0:T(8,128)(2,1)S(1)} %constant_dynamic-update-slice_fusion.10), channel_id=1, source_target_pairs={{0,1},{1,0},{2,3},{3,2},{4,5},{5,4},{6,7},{7,6},{8,9},{9,8},{10,11... | collective-permute-start | bytes 2359304 | tf_op jit(solution)/shard_map/ppermute | solution.py:478
  365.1 92.9 %all-to-all-start.2 = ((bf16[16,64,384]{2,1,0:T(8,128)(2,1)}), bf16[16,64,384]{2,1,0:T(8,128)(2,1)}, u32[]{:S(2)}, u32[]{:S(2)}) async-start(bf16[16,64,384]{2,1,0:T(8,128)(2,1)} %bitcast.54), calls=%async_computation.2 | async-start | bytes 1572864 | tf_op jit(solution)/shard_map/all_to_all | solution.py:688
  378.7 37.1 %collective-permute-start.31 = (bf16[1,768,128]{2,1,0:T(8,128)(2,1)S(1)}, bf16[1,768,128]{2,1,0:T(8,128)(2,1)S(1)}, u32[]{:S(2)}, u32[]{:S(2)}) collective-permute-start(bf16[1,768,128]{2,1,0:T(8,128)(2,1)S(1)} %get-tuple-element.217), channel_id=1, source_target_pairs={{0,16},{2,18},{4,20},{6,22},{8,24},{10,26},{12,28},{14,30},{16,0},... | collective-permute-start | bytes 589832 | tf_op jit(solution)/shard_map/ppermute | solution.py:475
  415.9 19.1 %collective-permute-start.32 = (bf16[2,768,128]{2,1,0:T(8,128)(2,1)S(1)}, bf16[2,768,128]{2,1,0:T(8,128)(2,1)S(1)}, u32[]{:S(2)}, u32[]{:S(2)}) collective-permute-start(bf16[2,768,128]{2,1,0:T(8,128)(2,1)S(1)} %pad_maximum_fusion.19), channel_id=1, source_target_pairs={{0,8},{2,10},{4,12},{6,14},{8,0},{10,2},{12,4},{14,6},{16,24},{18,... | collective-permute-start | bytes 1179656 | tf_op jit(solution)/shard_map/ppermute | solution.py:475
  417.3 100.3 %collective-permute-start.40 = (bf16[256,3072]{1,0:T(8,128)(2,1)}, bf16[256,3072]{1,0:T(8,128)(2,1)}, u32[]{:S(2)}, u32[]{:S(2)}) collective-permute-start(bf16[256,3072]{1,0:T(8,128)(2,1)} %pad_maximum_fusion.3), channel_id=1, source_target_pairs={{0,2},{2,0},{4,6},{6,4},{8,10},{10,8},{12,14},{14,12},{16,18},{18,... | collective-permute-start | bytes 4718600 | tf_op jit(solution)/shard_map/ppermute | solution.py:475
  436.0 90.4 %collective-permute-start.33 = (bf16[4,768,128]{2,1,0:T(8,128)(2,1)}, bf16[4,768,128]{2,1,0:T(8,128)(2,1)}, u32[]{:S(2)}, u32[]{:S(2)}) collective-permute-start(bf16[4,768,128]{2,1,0:T(8,128)(2,1)} %pad_maximum_fusion.12), channel_id=1, source_target_pairs={{0,4},{2,6},{4,0},{6,2},{8,12},{10,14},{12,8},{14,10},{16,20},{18,... | collective-permute-start | bytes 2359304 | tf_op jit(solution)/shard_map/ppermute | solution.py:475
  452.3 88.5 %collective-permute-start.61 = (bf16[2,256,1408]{2,1,0:T(8,128)(2,1)}, bf16[2,256,1408]{2,1,0:T(8,128)(2,1)}, u32[]{:S(2)}, u32[]{:S(2)}) collective-permute-start(bf16[2,256,1408]{2,1,0:T(8,128)(2,1)} %bitcast.249), channel_id=1, source_target_pairs={{0,1},{1,0},{2,3},{3,2},{4,5},{5,4},{6,7},{7,6},{8,9},{9,8},{10,11... | collective-permute-start | bytes 4325384 | tf_op jit(solution)/shard_map/ppermute | solution.py:478
  457.4 66.4 %collective-permute-start.70 = (bf16[4,176,512]{2,1,0:T(8,128)(2,1)}, bf16[4,176,512]{2,1,0:T(8,128)(2,1)}, u32[]{:S(2)}, u32[]{:S(2)}) collective-permute-start(bf16[4,176,512]{2,1,0:T(8,128)(2,1)} %dynamic-slice_bitcast_fusion.1), channel_id=1, source_target_pairs={{0,4},{2,6},{4,0},{6,2},{8,12},{10,14},{12,8},{14,10},{16,20},{18,... | collective-permute-start | bytes 2162696 | tf_op jit(solution)/shard_map/ppermute | solution.py:475
  521.4 18.9 %collective-permute-start.41 = (bf16[4,3,32,1024]{3,2,1,0:T(8,128)(2,1)S(1)}, bf16[4,3,32,1024]{3,2,1,0:T(8,128)(2,1)S(1)}, u32[]{:S(2)}, u32[]{:S(2)}) collective-permute-start(bf16[4,3,32,1024]{3,2,1,0:T(8,128)(2,1)S(1)} %bitcast.302), channel_id=1, source_target_pairs={{0,4},{2,6},{4,0},{6,2},{8,12},{10,14},{12,8},{14,10},{16,20},{18,... | collective-permute-start | bytes 2359304 | tf_op jit(solution)/shard_map/ppermute | solution.py:475
  527.7 53.1 %collective-permute-start.34 = (bf16[8,768,128]{2,1,0:T(8,128)(2,1)S(1)}, bf16[8,768,128]{2,1,0:T(8,128)(2,1)S(1)}, u32[]{:S(2)}, u32[]{:S(2)}) collective-permute-start(bf16[8,768,128]{2,1,0:T(8,128)(2,1)S(1)} %pad_maximum_fusion.2), channel_id=1, source_target_pairs={{0,2},{2,0},{4,6},{6,4},{8,10},{10,8},{12,14},{14,12},{16,18},{18,... | collective-permute-start | bytes 4718600 | tf_op jit(solution)/shard_map/ppermute | solution.py:475
  542.9 34.6 %collective-permute-start.62 = (bf16[4,2,2,32,1408]{4,3,2,1,0:T(8,128)(2,1)S(1)}, bf16[4,2,2,32,1408]{4,3,2,1,0:T(8,128)(2,1)S(1)}, u32[]{:S(2)}, u32[]{:S(2)}) collective-permute-start(bf16[4,2,2,32,1408]{4,3,2,1,0:T(8,128)(2,1)S(1)} %dynamic-slice_bitcast_fusion), channel_id=1, source_target_pairs={{0,4},{2,6},{4,0},{6,2},{8,12},{10,14},{12,8},{14,10},{16,20},{18,... | collective-permute-start | bytes 4325384 | tf_op jit(solution)/shard_map/ppermute | solution.py:475
  569.6 23.1 %collective-permute-start.75 = (bf16[4,176,512]{2,1,0:T(8,128)(2,1)S(1)}, bf16[4,176,512]{2,1,0:T(8,128)(2,1)S(1)}, u32[]{:S(2)}, u32[]{:S(2)}) collective-permute-start(bf16[4,176,512]{2,1,0:T(8,128)(2,1)S(1)} %pad_maximum_fusion.15), channel_id=1, source_target_pairs={{0,4},{2,6},{4,0},{6,2},{8,12},{10,14},{12,8},{14,10},{16,20},{18,... | collective-permute-start | bytes 2162696 | tf_op jit(solution)/shard_map/ppermute | solution.py:475
  578.8 23.2 %collective-permute-start.63 = (bf16[2,2,2,32,1408]{4,3,2,1,0:T(8,128)(2,1)}, bf16[2,2,2,32,1408]{4,3,2,1,0:T(8,128)(2,1)}, u32[]{:S(2)}, u32[]{:S(2)}) collective-permute-start(bf16[2,2,2,32,1408]{4,3,2,1,0:T(8,128)(2,1)} %dynamic-slice_bitcast_fusion.2), channel_id=1, source_target_pairs={{0,8},{2,10},{4,12},{6,14},{8,0},{10,2},{12,4},{14,6},{16,24},{18,... | collective-permute-start | bytes 2162696 | tf_op jit(solution)/shard_map/ppermute | solution.py:475
  590.1 34.3 %collective-permute-start.46 = (bf16[4,3,32,1024]{3,2,1,0:T(8,128)(2,1)}, bf16[4,3,32,1024]{3,2,1,0:T(8,128)(2,1)}, u32[]{:S(2)}, u32[]{:S(2)}) collective-permute-start(bf16[4,3,32,1024]{3,2,1,0:T(8,128)(2,1)} %pad_maximum_fusion.13), channel_id=1, source_target_pairs={{0,4},{2,6},{4,0},{6,2},{8,12},{10,14},{12,8},{14,10},{16,20},{18,... | collective-permute-start | bytes 2359304 | tf_op jit(solution)/shard_map/ppermute | solution.py:475
  594.0 70.2 %collective-permute-start.76 = (bf16[8,176,512]{2,1,0:T(8,128)(2,1)}, bf16[8,176,512]{2,1,0:T(8,128)(2,1)}, u32[]{:S(2)}, u32[]{:S(2)}) collective-permute-start(bf16[8,176,512]{2,1,0:T(8,128)(2,1)} %pad_maximum_fusion.9), channel_id=1, source_target_pairs={{0,2},{2,0},{4,6},{6,4},{8,10},{10,8},{12,14},{14,12},{16,18},{18,... | collective-permute-start | bytes 4325384 | tf_op jit(solution)/shard_map/ppermute | solution.py:475
  626.9 73.8 %collective-permute-start.47 = (bf16[8,3,32,1024]{3,2,1,0:T(8,128)(2,1)}, bf16[8,3,32,1024]{3,2,1,0:T(8,128)(2,1)}, u32[]{:S(2)}, u32[]{:S(2)}) collective-permute-start(bf16[8,3,32,1024]{3,2,1,0:T(8,128)(2,1)} %pad_maximum_fusion.5), channel_id=1, source_target_pairs={{0,2},{2,0},{4,6},{6,4},{8,10},{10,8},{12,14},{14,12},{16,18},{18,... | collective-permute-start | bytes 4718600 | tf_op jit(solution)/shard_map/ppermute | solution.py:475
  638.0 19.1 %collective-permute-start.66 = (bf16[2,2,2,32,1408]{4,3,2,1,0:T(8,128)(2,1)S(1)}, bf16[2,2,2,32,1408]{4,3,2,1,0:T(8,128)(2,1)S(1)}, u32[]{:S(2)}, u32[]{:S(2)}) collective-permute-start(bf16[2,2,2,32,1408]{4,3,2,1,0:T(8,128)(2,1)S(1)} %pad_maximum_fusion.14), channel_id=1, source_target_pairs={{0,8},{2,10},{4,12},{6,14},{8,0},{10,2},{12,4},{14,6},{16,24},{18,... | collective-permute-start | bytes 2162696 | tf_op jit(solution)/shard_map/ppermute | solution.py:475
  640.3 21.4 %collective-permute-start.53 = (bf16[2,1,32,2048]{3,2,0,1:T(8,128)(2,1)S(1)}, bf16[2,1,32,2048]{3,2,0,1:T(8,128)(2,1)S(1)}, u32[]{:S(2)}, u32[]{:S(2)}) collective-permute-start(bf16[2,1,32,2048]{3,2,0,1:T(8,128)(2,1)S(1)} %dynamic-slice_bitcast_fusion.6), channel_id=1, source_target_pairs={{0,8},{2,10},{4,12},{6,14},{8,0},{10,2},{12,4},{14,6},{16,24},{18,... | collective-permute-start | bytes 786440 | tf_op jit(solution)/shard_map/ppermute | solution.py:475
  658.3 33.5 %collective-permute-start.67 = (bf16[4,2,2,32,1408]{4,3,2,1,0:T(8,128)(2,1)}, bf16[4,2,2,32,1408]{4,3,2,1,0:T(8,128)(2,1)S(1)}, u32[]{:S(2)}, u32[]{:S(2)}) collective-permute-start(bf16[4,2,2,32,1408]{4,3,2,1,0:T(8,128)(2,1)} %pad_maximum_fusion.8), channel_id=1, source_target_pairs={{0,4},{2,6},{4,0},{6,2},{8,12},{10,14},{12,8},{14,10},{16,20},{18,... | collective-permute-start | bytes 4325384 | tf_op jit(solution)/shard_map/ppermute | solution.py:475
  694.6 41.4 %collective-permute-start.68 = (bf16[8,2,2,32,1408]{4,3,2,1,0:T(8,128)(2,1)}, bf16[8,2,2,32,1408]{4,3,2,1,0:T(8,128)(2,1)}, u32[]{:S(2)}, u32[]{:S(2)}) collective-permute-start(bf16[8,2,2,32,1408]{4,3,2,1,0:T(8,128)(2,1)} %pad_maximum_fusion.1), channel_id=1, source_target_pairs={{0,2},{2,0},{4,6},{6,4},{8,10},{10,8},{12,14},{14,12},{16,18},{18,... | collective-permute-start | bytes 8650760 | tf_op jit(solution)/shard_map/ppermute | solution.py:475
  695.5 19.2 %collective-permute-start.57 = (bf16[4,1,32,2048]{3,2,0,1:T(8,128)(2,1)}, bf16[4,1,32,2048]{3,2,0,1:T(8,128)(2,1)}, u32[]{:S(2)}, u32[]{:S(2)}) collective-permute-start(bf16[4,1,32,2048]{3,2,0,1:T(8,128)(2,1)} %pad_maximum_fusion.18), channel_id=1, source_target_pairs={{0,4},{2,6},{4,0},{6,2},{8,12},{10,14},{12,8},{14,10},{16,20},{18,... | collective-permute-start | bytes 1572872 | tf_op jit(solution)/shard_map/ppermute | solution.py:475
  (117 other events, 1324.4 us)
Sparse Core Ops, SparseCore 0:
  19.2 38.6 all-gather.2
  340.6 94.7 reduce-scatter.1

commit v2 on v1

v2 whole, which is shorter than its diff:
```python
import functools

import jax
import jax.numpy as jnp
from jax import lax
from jax.experimental import pallas as pl
from jax.experimental.pallas import tpu as pltpu
from jax.sharding import PartitionSpec as P

EPS = 1e-06
NEGATIVE = -1e30
TILE = 256
F32 = jnp.float32
BF16 = jnp.bfloat16
VMEM_LIMIT = 56 * 1024 * 1024


def vmem():
    return pl.BlockSpec(memory_space=pltpu.VMEM)


def smem():
    return pl.BlockSpec(memory_space=pltpu.SMEM)


def params(limit=VMEM_LIMIT):
    return pltpu.CompilerParams(vmem_limit_bytes=limit)


def cost(microseconds):
    return pl.CostEstimate(
        flops=int(microseconds * 1.15e9),
        bytes_accessed=int(microseconds * 3.69e6),
        transcendentals=0,
    )


def aligned(start, size):
    return pl.ds(pl.multiple_of(start, size), size)


def dot(left, right):
    return jnp.dot(left, right, preferred_element_type=F32)


def dot_t(left, right):
    return lax.dot_general(left, right, (((1,), (1,)), ((), ())), preferred_element_type=F32)


def t_dot(left, right):
    return lax.dot_general(left, right, (((0,), (0,)), ((), ())), preferred_element_type=F32)


def norm_rows(values, gain):
    return values * lax.rsqrt(jnp.mean(values * values, axis=-1, keepdims=True) + EPS) * gain


def norm_back(values, gain, grad):
    r = lax.rsqrt(jnp.mean(values * values, axis=-1, keepdims=True) + EPS)
    scaled = grad * gain
    inner = jnp.mean(scaled * values, axis=-1, keepdims=True)
    back = r * scaled - values * (r * r * r * inner)
    return back, jnp.sum(grad * (values * r), axis=0, keepdims=True)


def low_lanes(rows):
    return lax.broadcasted_iota(jnp.int32, (rows, 128), 1) < 64


def pair_up(first, second):
    lane = low_lanes(first.shape[0])
    low = jnp.where(lane, first, pltpu.roll(second, 64, 1))
    high = jnp.where(lane, pltpu.roll(first, 64, 1), second)
    return low, high


def keep_half(values, half):
    lane = low_lanes(values.shape[0])
    return jnp.where(lane if half == 0 else ~lane, values, jnp.zeros_like(values))


def softmax_rows(scores):
    top = jnp.max(scores, axis=-1, keepdims=True)
    raised = jnp.exp(scores - top)
    return raised * (1.0 / jnp.sum(raised, axis=-1, keepdims=True))


def table_kernel(edge_ref, value_ref, out_ref):
    rows, length = out_ref.shape
    bucket_count = value_ref.shape[0]
    for start in range(0, length, TILE):
        place = (rows, TILE)
        apart = (
            lax.broadcasted_iota(jnp.int32, place, 0)
            - lax.broadcasted_iota(jnp.int32, place, 1)
            + (length - rows - start)
        )
        value = jnp.full(place, value_ref[0], F32)
        for bucket in range(1, bucket_count):
            value = jnp.where(apart >= edge_ref[bucket], value_ref[bucket], value)
        out_ref[:, start : start + TILE] = jnp.where(apart >= 0, value, NEGATIVE)


def bias_table(edges, values, length):
    return pl.pallas_call(
        table_kernel,
        out_shape=jax.ShapeDtypeStruct((TILE, length), F32),
        in_specs=[smem(), smem()],
        out_specs=vmem(),
        cost_estimate=cost(4),
        name="bias_table",
    )(edges, values)


def bucket_kernel(edge_ref, grad_ref, out_ref):
    rows, length = grad_ref.shape
    bucket_count = out_ref.shape[0]
    above = [jnp.zeros((8, TILE), F32) for _ in range(bucket_count)]
    for start in range(0, length, TILE):
        for row in range(0, rows, 8):
            place = (8, TILE)
            apart = (
                lax.broadcasted_iota(jnp.int32, place, 0)
                - lax.broadcasted_iota(jnp.int32, place, 1)
                + (length - rows - start + row)
            )
            tile = grad_ref[row : row + 8, start : start + TILE]
            for bucket in range(bucket_count):
                above[bucket] = above[bucket] + jnp.where(apart >= edge_ref[bucket], tile, 0.0)
    for bucket in range(bucket_count):
        rest = above[bucket + 1] if bucket + 1 < bucket_count else 0.0
        part = jnp.sum(above[bucket] - rest, axis=0, keepdims=True)
        out_ref[bucket : bucket + 1, :] = part[:, :128] + part[:, 128:]


def bucket_sums(edges, grad, bucket_count):
    return pl.pallas_call(
        bucket_kernel,
        out_shape=jax.ShapeDtypeStruct((bucket_count, 128), F32),
        in_specs=[smem(), vmem()],
        out_specs=vmem(),
        cost_estimate=cost(7),
        name="bucket_sums",
    )(edges, grad)


def times(x_ref, starts_ref, pieces):
    if len(pieces) == 1:
        return dot(x_ref[...], pieces[0])
    total = None
    for place, piece in enumerate(pieces):
        rows = piece.shape[0]
        part = dot(x_ref[:, aligned(starts_ref[place], rows)], piece)
        total = part if total is None else total + part
    return total


def times_back(out_ref, starts_ref, terms):
    for place in range(len(terms[0][1])):
        total = sum(dot_t(d, pieces[place]) for d, pieces in terms)
        rows = terms[0][1][place].shape[0]
        if len(terms[0][1]) == 1:
            out_ref[...] = total
        else:
            out_ref[:, aligned(starts_ref[place], rows)] = total


def pieces_of(own_ref, more, index):
    return [own_ref[...]] + [ref[index] for ref in more]


def self_scores(q, k, table, doc_col, doc_row):
    scores = dot_t(q, k) + table
    return jnp.where(doc_col == doc_row, scores, NEGATIVE)


def self_forward_kernel(groups, source_ref, *refs):
    x_refs = refs[:groups]
    gain_ref, w_ref, table_ref, doc_row_ref, doc_col_ref, n_ref, qkv_ref, o_ref = refs[groups:]
    count, _, rows, width = x_refs[0].shape
    length = groups * count * rows
    lane = lax.broadcasted_iota(jnp.int32, (rows, 384), 1) % 128 < 64
    together = min(TILE // rows, count)
    for place, x_ref in enumerate(x_refs):
        for first in range(0, count, together):
            parts = []
            for inner in range(first, first + together):
                x = x_ref[inner].astype(F32).reshape(2 * rows, width)
                n = norm_rows(x, gain_ref[...]).astype(BF16)
                n_ref[source_ref[place * count + inner]] = n.reshape(2, rows, width)
                parts.append(n)
            made = dot(jnp.concatenate(parts, axis=0), w_ref[...])
            for inner in range(together):
                at = 2 * rows * inner
                picked = jnp.where(lane, made[at : at + rows], made[at + rows : at + 2 * rows])
                own = source_ref[place * count + first + inner]
                qkv_ref[aligned(own * rows, rows), :] = picked.astype(BF16)
    for block in range(length // TILE):
        start, stop = block * TILE, (block + 1) * TILE
        table = table_ref[:, length - stop :]
        q = qkv_ref[start:stop, 0:128]
        k = qkv_ref[:stop, 128:256]
        v = qkv_ref[:stop, 256:384]
        mixed = []
        for half in range(2):
            scores = self_scores(
                keep_half(q, half),
                k,
                table,
                doc_col_ref[half, start:stop, :],
                doc_row_ref[half : half + 1, :stop],
            )
            mixed.append(dot(softmax_rows(scores).astype(BF16), v))
        o_ref[start:stop, :] = jnp.where(low_lanes(TILE), mixed[0], mixed[1]).astype(BF16)


def self_backward_kernel(
    qkv_ref, do_ref, table_ref, doc_row_ref, doc_col_ref, dqkv_ref, grad_ref, dk_ref, dv_ref
):
    length = qkv_ref.shape[0]
    grad_ref[...] = jnp.zeros_like(grad_ref)
    dk_ref[...] = jnp.zeros_like(dk_ref)
    dv_ref[...] = jnp.zeros_like(dv_ref)
    for block in range(length // TILE):
        start, count = block * TILE, (block + 1) * TILE
        table = table_ref[:, length - count :]
        k = qkv_ref[:count, 128:256]
        v = qkv_ref[:count, 256:384]
        made = []
        for half in range(2):
            q = keep_half(qkv_ref[start:count, 0:128], half)
            do = keep_half(do_ref[start:count, :], half)
            p = softmax_rows(
                self_scores(
                    q,
                    k,
                    table,
                    doc_col_ref[half, start:count, :],
                    doc_row_ref[half : half + 1, :count],
                )
            )
            dp = dot_t(do, v)
            ds = (p * (dp - jnp.sum(p * dp, axis=-1, keepdims=True))).astype(BF16)
            grad_ref[:, length - count :] += ds.astype(F32)
            made.append(dot(ds, k))
            dk_ref[:count, :] += t_dot(ds, q)
            dv_ref[:count, :] += t_dot(p.astype(BF16), do)
        dq = jnp.where(low_lanes(TILE), made[0], made[1])
        dqkv_ref[start:count, 0:128] = dq.astype(BF16)
    dqkv_ref[:, 128:256] = dk_ref[...].astype(BF16)
    dqkv_ref[:, 256:384] = dv_ref[...].astype(BF16)


def head_weight_kernel(n_ref, d_ref, out_ref):
    blocks, _, rows, width = n_ref.shape
    shards = out_ref.shape[0]
    span = width // shards
    lane = lax.broadcasted_iota(jnp.int32, (blocks * rows, 384), 1) % 128 < 64
    d = d_ref[...]
    zero = jnp.zeros_like(d)
    right = [jnp.where(lane, d, zero), jnp.where(lane, zero, d)]
    half = span // 2
    for shard in range(shards):
        total = jnp.zeros((span, 384), F32)
        for micro in range(2):
            left = n_ref[:, micro, :, shard * span : (shard + 1) * span]
            total = total + t_dot(left.reshape(blocks * rows, span), right[micro])
        q, k, v = (
            total[:, at : at + 128] + pltpu.roll(total[:, at : at + 128], 64, 1)
            for at in (0, 128, 256)
        )
        out_ref[shard, :span, :] = jnp.where(low_lanes(span), q, k).astype(BF16)
        out_ref[shard, span:, :] = jnp.where(low_lanes(half), v[:half], v[half:]).astype(BF16)


def cross_kv_kernel(split, starts_ref, e_ref, wk_ref, wv_ref, *refs):
    more, (ke_ref, ve_ref) = refs[:split], refs[split:]
    blocks, _, part, _ = e_ref.shape
    for index, (own_ref, out_ref) in enumerate(((wk_ref, ke_ref), (wv_ref, ve_ref)), 3):
        total = None
        pieces = pieces_of(own_ref, more, index)
        for place, piece in enumerate(pieces):
            rows = piece.shape[0]
            if split:
                left = e_ref[:, 0, :, aligned(starts_ref[place], rows)]
            else:
                left = e_ref[:, 0]
            made = dot(left.reshape(blocks * part, rows), piece)
            total = made if total is None else total + made
        out_ref[0] = total.astype(BF16)


def cross_kv(starts, e_all, wk, wv, more):
    blocks, micro, part, width = e_all.shape
    whole = lambda array: pl.BlockSpec(array.shape, lambda m, s: (0,) * array.ndim)
    out = pl.BlockSpec((1, blocks * part, width), lambda m, s: (m, 0, 0))
    return pl.pallas_call(
        functools.partial(cross_kv_kernel, len(more)),
        grid_spec=pltpu.PrefetchScalarGridSpec(
            num_scalar_prefetch=1,
            grid=(micro,),
            in_specs=[pl.BlockSpec((blocks, 1, part, width), lambda m, s: (0, m, 0, 0))]
            + [whole(array) for array in (wk, wv, *more)],
            out_specs=[out, out],
        ),
        out_shape=[jax.ShapeDtypeStruct((micro, blocks * part, width), BF16)] * 2,
        compiler_params=params(),
        cost_estimate=cost(8),
        name="cross_kv",
    )(starts, e_all, wk, wv, *more)


def mid_forward_kernel(split, starts_ref, o1_ref, x_ref, gain_ref, ke_ref, ve_ref, wo, wq, wc, *refs):
    more = refs[:split]
    left_ref, x1_ref, q2_ref, x2_ref, n3_ref, o1c_ref, n2_ref, o2_ref = refs[split:]
    heads, rows, _ = o1_ref.shape
    width = x_ref.shape[-1]
    for pair in range(heads // 2):
        at = pair * 128
        low, high = pair_up(o1_ref[2 * pair].astype(F32), o1_ref[2 * pair + 1].astype(F32))
        o1c_ref[0:rows, at : at + 128] = low.astype(BF16)
        o1c_ref[rows : 2 * rows, at : at + 128] = high.astype(BF16)
    x = x_ref[...].astype(F32).reshape(2 * rows, width)
    x1 = x + times(o1c_ref, starts_ref, pieces_of(wo, more, 0))
    x1_ref[...] = x1
    n2_ref[...] = norm_rows(x1, gain_ref[1:2]).astype(BF16)
    q2_ref[...] = times(n2_ref, starts_ref, pieces_of(wq, more, 1)).astype(BF16)
    for micro in range(2):
        for pair in range(heads // 2):
            at = pair * 128
            span = slice(micro * rows, (micro + 1) * rows)
            q = q2_ref[span, at : at + 128]
            both = jnp.concatenate([keep_half(q, 0), keep_half(q, 1)], axis=0)
            p = softmax_rows(dot_t(both, ke_ref[micro, :, at : at + 128]))
            o = dot(p.astype(BF16), ve_ref[micro, :, at : at + 128])
            o2_ref[span, at : at + 128] = jnp.where(
                low_lanes(rows), o[:rows], o[rows:]
            ).astype(BF16)
    x2 = x1 + times(o2_ref, starts_ref, pieces_of(wc, more, 2))
    x2_ref[...] = x2
    n3_ref[...] = norm_rows(x2, gain_ref[2:3]).astype(BF16)
    left_ref[0] = o2_ref[...]
    left_ref[1] = n2_ref[...]
    left_ref[2] = o1c_ref[...]


def mid_backward_kernel(
    split, starts_ref, g_ref, dn3_ref, more_ref, x1_ref, x2_ref, gain_ref, q2_ref, ke_ref, ve_ref,
    wo, wq, wc, *refs
):
    more = refs[:split]
    right_ref, gx1_ref, do1_ref, dkv_ref, dc_ref, back_ref, do2_ref, dq2_ref = refs[split:]
    heads, rows, _ = do1_ref.shape
    blocks, micros, part = dkv_ref.shape[1:4]
    width = x1_ref.shape[-1]
    dn3 = dn3_ref[...] + more_ref[...].astype(F32)
    back, dc = norm_back(x2_ref[...], gain_ref[2:3], dn3)
    dc_ref[0:1, :] = dc
    gx2 = g_ref[...].astype(F32).reshape(2 * rows, width) + back
    gx2b = gx2.astype(BF16)
    right_ref[:, 0:width] = gx2b
    times_back(back_ref, starts_ref, [(gx2b, pieces_of(wc, more, 2))])
    do2_ref[...] = back_ref[...].astype(BF16)
    for micro in range(2):
        for pair in range(heads // 2):
            at = pair * 128
            span = slice(micro * rows, (micro + 1) * rows)
            q = q2_ref[span, at : at + 128]
            do = do2_ref[span, at : at + 128]
            q = jnp.concatenate([keep_half(q, 0), keep_half(q, 1)], axis=0)
            do = jnp.concatenate([keep_half(do, 0), keep_half(do, 1)], axis=0)
            k = ke_ref[micro, :, at : at + 128]
            v = ve_ref[micro, :, at : at + 128]
            p = softmax_rows(dot_t(q, k))
            dp = dot_t(do, v)
            ds = (p * (dp - jnp.sum(p * dp, axis=-1, keepdims=True))).astype(BF16)
            dq = dot(ds, k)
            dq2_ref[span, at : at + 128] = jnp.where(
                low_lanes(rows), dq[:rows], dq[rows:]
            ).astype(BF16)
            low, high = pair_up(t_dot(ds, q), t_dot(p.astype(BF16), do))
            dkv_ref[2 * pair, :, micro] = low.astype(BF16).reshape(blocks, part, 128)
            dkv_ref[2 * pair + 1, :, micro] = high.astype(BF16).reshape(blocks, part, 128)
    right_ref[:, width : 2 * width] = dq2_ref[...]
    times_back(back_ref, starts_ref, [(dq2_ref[...], pieces_of(wq, more, 1))])
    back, dc = norm_back(x1_ref[...], gain_ref[1:2], back_ref[...])
    dc_ref[1:2, :] = dc
    gx1 = gx2 + back
    gx1_ref[...] = gx1
    gx1b = gx1.astype(BF16)
    right_ref[:, 2 * width :] = gx1b
    times_back(back_ref, starts_ref, [(gx1b, pieces_of(wo, more, 0))])
    for pair in range(heads // 2):
        at = pair * 128
        do1 = back_ref[:, at : at + 128].astype(BF16).astype(F32)
        low, high = pair_up(do1[:rows], do1[rows:])
        do1_ref[2 * pair] = low.astype(BF16)
        do1_ref[2 * pair + 1] = high.astype(BF16)


def input_grad_kernel(split, starts_ref, d_ref, x_ref, gain_ref, gx1_ref, wq, wk, wv, *refs):
    more = refs[:split]
    out_ref, dc_ref, all_ref, back_ref = refs[split:]
    heads, rows, _ = d_ref.shape
    width = x_ref.shape[-1]
    for kind in range(3):
        for pair in range(heads // 2):
            lanes = slice(kind * 128, (kind + 1) * 128)
            low, high = pair_up(
                d_ref[2 * pair, :, lanes].astype(F32), d_ref[2 * pair + 1, :, lanes].astype(F32)
            )
            at = kind * width + pair * 128
            all_ref[0:rows, at : at + 128] = low.astype(BF16)
            all_ref[rows : 2 * rows, at : at + 128] = high.astype(BF16)
    terms = [
        (all_ref[:, kind * width : (kind + 1) * width], pieces_of(own, more, kind))
        for kind, own in enumerate((wq, wk, wv))
    ]
    times_back(back_ref, starts_ref, terms)
    x = x_ref[...].astype(F32).reshape(2 * rows, width)
    back, dc = norm_back(x, gain_ref[0:1], back_ref[...])
    dc_ref[...] = dc
    out_ref[...] = gx1_ref[...] + back


def encoder_grad_kernel(split, starts_ref, d_ref, wk, wv, *refs):
    more = refs[:split]
    out_ref, k_ref, v_ref = refs[split:]
    for pair in range(d_ref.shape[0] // 2):
        at = pair * 128
        low, high = pair_up(d_ref[2 * pair].astype(F32), d_ref[2 * pair + 1].astype(F32))
        k_ref[:, at : at + 128] = low.astype(BF16)
        v_ref[:, at : at + 128] = high.astype(BF16)
    terms = [(k_ref[...], pieces_of(wk, more, 3)), (v_ref[...], pieces_of(wv, more, 4))]
    times_back(out_ref, starts_ref, terms)


def cross_head_weight_kernel(e_ref, d_ref, out_ref):
    blocks, micro, part, width = e_ref.shape
    shards, span, _ = out_ref.shape
    for shard in range(shards):
        left = e_ref[:, :, :, shard * span : (shard + 1) * span]
        left = left.reshape(blocks * micro * part, span)
        out_ref[shard] = t_dot(left, d_ref[...]).astype(BF16)


def dense_kernel(split, starts_ref, n_ref, g_ref, wg, wu, wd_ref, *refs):
    more = refs[:split]
    back_ref, y_ref, ylow_ref, d_ref, dlow_ref = refs[split:]
    hidden = wd_ref.shape[0]
    gate, up = pieces_of(wg, more, 0), pieces_of(wu, more, 1)
    a = times(n_ref, starts_ref, gate)
    b = times(n_ref, starts_ref, up)
    scale = 0.7978845608028654
    cubed = 0.044715
    inner = jnp.tanh(scale * (a + cubed * (a * a * a)))
    gelu = 0.5 * a * (1.0 + inner)
    slope = 0.5 * (1.0 + inner) + 0.5 * a * (1.0 - inner * inner) * (
        scale * (1.0 + 3.0 * cubed * (a * a))
    )
    hid = (gelu * b).astype(BF16)
    dh = dot_t(g_ref[...], wd_ref[...])
    da = (dh * b * slope).astype(BF16)
    db = (dh * gelu).astype(BF16)
    times_back(d_ref, starts_ref, [(da, gate), (db, up)])
    dlow_ref[...] = d_ref[...].astype(BF16)
    y = dot(hid, wd_ref[...])
    y_ref[...] = y
    ylow_ref[...] = y.astype(BF16)
    back_ref[:, 0:hidden] = da
    back_ref[:, hidden : 2 * hidden] = db
    back_ref[:, 2 * hidden : 3 * hidden] = hid
    if more:
        shard, other = starts_ref[len(more) + 1], 1 - starts_ref[len(more) + 2]
        put_features(back_ref, 3 * hidden, n_ref, g_ref, shard, other)


def put_features(out_ref, at, n_ref, g_ref, shard, core):
    quarter = n_ref.shape[1] // 4
    for side, place in enumerate((2 * shard + core, 2 * (1 - shard) + core)):
        lanes = slice(at + side * quarter, at + (side + 1) * quarter)
        out_ref[:, lanes] = n_ref[:, aligned(place * quarter, quarter)]
    lanes = slice(at + 2 * quarter, at + 4 * quarter)
    out_ref[:, lanes] = g_ref[:, aligned(core * 2 * quarter, 2 * quarter)]


def dense_layer(starts, n, g, wg, wu, wd, more, step):
    count, width = n.shape
    hidden = wd.shape[0]
    which = starts.shape[0] - 2
    back = 3 * hidden + (width if more else 0)
    row = lambda size: pl.BlockSpec((step, size), lambda i, s: (i, 0))
    whole = lambda array: pl.BlockSpec(array.shape, lambda i, s: (0,) * array.ndim)
    column = pl.BlockSpec((wg.shape[0], hidden), lambda i, s: (0, s[which]))
    made = lambda size, kind: jax.ShapeDtypeStruct((count, size), kind)
    return pl.pallas_call(
        functools.partial(dense_kernel, len(more)),
        grid_spec=pltpu.PrefetchScalarGridSpec(
            num_scalar_prefetch=1,
            grid=(count // step,),
            in_specs=[row(width), row(width), column, column, whole(wd)]
            + [whole(array) for array in more],
            out_specs=[row(back)] + [row(width)] * 4,
        ),
        out_shape=[made(back, BF16)]
        + [made(width, F32), made(width, BF16), made(width, F32), made(width, BF16)],
        compiler_params=params(),
        cost_estimate=cost(13),
        name="dense_layer",
    )(starts, n, g, wg, wu, wd, *more)


def put_chunk(ref, slot, at, value):
    rows, width = value.shape
    for block in range(width // 128):
        ref[slot, at + block * rows : at + (block + 1) * rows, :] = value[
            :, block * 128 : (block + 1) * 128
        ].astype(BF16)


def take_chunk(ref, slot, at, rows, width):
    return jnp.concatenate(
        [
            ref[slot, at + block * rows : at + (block + 1) * rows, :].astype(F32)
            for block in range(width // 128)
        ],
        axis=1,
    )


def put_all(scratch_ref, value, chip, chunk_refs, at):
    count = 2 * chunk_refs[0].shape[0]
    rows = value.shape[0] // count
    scratch_ref[: value.shape[0], : value.shape[1]] = value
    for r in range(count):
        chunk = scratch_ref[aligned((chip ^ r) * rows, rows), : value.shape[1]]
        put_chunk(chunk_refs[r // (count // 2)], r % (count // 2), at, chunk)


def dense_weight_kernel(
    where_ref, n0_ref, n1_ref, g0_ref, g1_ref, own0_ref, own1_ref, mate0_ref, mate1_ref, keep_ref,
    send_ref, down_keep_ref, down_send_ref, far_keep_ref, far_send_ref, scratch_ref, left_ref
):
    tokens, width = n0_ref.shape
    hidden = (own0_ref.shape[1] - width) // 3
    quarter = width // 4
    at = keep_ref.shape[1] // 2
    x_chip, core, shard, z_chip = where_ref[0], where_ref[1], where_ref[2], where_ref[3]
    put_features(left_ref.at[:tokens], 0, n0_ref, g0_ref, shard, core)
    put_features(left_ref.at[tokens : 2 * tokens], 0, n1_ref, g1_ref, shard, core)
    left_ref[2 * tokens : 3 * tokens, :] = mate0_ref[:, 3 * hidden :]
    left_ref[3 * tokens :, :] = mate1_ref[:, 3 * hidden :]

    def whole(kind):
        span = slice(kind * hidden, (kind + 1) * hidden)
        refs = (own0_ref, own1_ref, mate0_ref, mate1_ref)
        return jnp.concatenate([ref[:, span] for ref in refs], axis=0)

    for kind in range(2):
        right = whole(kind)
        for side, (chip, refs) in enumerate(
            ((z_chip, (keep_ref, send_ref)), (x_chip, (far_keep_ref, far_send_ref)))
        ):
            value = t_dot(left_ref[:, side * quarter : (side + 1) * quarter], right)
            put_all(scratch_ref, value, chip, refs, kind * at)
    value = t_dot(whole(2), left_ref[:, 2 * quarter :])
    put_all(scratch_ref, value, x_chip, (down_keep_ref, down_send_ref), 0)


def token_weight_kernel(
    where_ref, left_ref, left_mate_ref, r0_ref, r1_ref, r2_ref, r3_ref, keep_ref, send_ref,
    scratch_ref
):
    width = r0_ref.shape[1] // 3
    tokens = r0_ref.shape[0]
    half = left_ref.shape[1] // 3
    rows = half // (2 * keep_ref.shape[0])
    for kind in range(3):
        span = slice(kind * width, (kind + 1) * width)
        lanes = slice(kind * half, (kind + 1) * half)
        value = t_dot(left_ref[:tokens, lanes], r0_ref[:, span])
        value = value + t_dot(left_ref[tokens:, lanes], r1_ref[:, span])
        value = value + t_dot(left_mate_ref[:tokens, lanes], r2_ref[:, span])
        value = value + t_dot(left_mate_ref[tokens:, lanes], r3_ref[:, span])
        put_all(scratch_ref, value, where_ref[0], (keep_ref, send_ref), kind * rows * width // 128)


def chunk_weights(kernel, where, operands, counts, chips, scratches, length, name):
    shapes = []
    for count in counts:
        shapes += [jax.ShapeDtypeStruct((chips // 2, count, 128), BF16)] * 2
    return pl.pallas_call(
        kernel,
        out_shape=shapes,
        in_specs=[smem()] + [vmem()] * len(operands),
        out_specs=[vmem()] * len(shapes),
        scratch_shapes=scratches,
        compiler_params=params(),
        cost_estimate=cost(length),
        name=name,
    )(where, *operands)


def spread_gate_kernel(where_ref, low, high, far_low, far_high, out_ref, other_ref):
    x_chip, core, shard, z_chip = where_ref[0], where_ref[1], where_ref[2], where_ref[3]
    rows = out_ref.shape[2] // low.shape[0]
    hidden = out_ref.shape[3] // 2
    at = rows * hidden // 128
    count = low.shape[0]
    for side, (chip, refs) in enumerate(((z_chip, (low, high)), (x_chip, (far_low, far_high)))):
        for cores, ref in enumerate(refs):
            for r in range(count):
                place = aligned(((chip ^ r) % count) * rows, rows)
                lanes = aligned((shard ^ side) * hidden, hidden)
                out_ref[core ^ cores, 0, place, lanes] = take_chunk(ref, r, 0, rows, hidden)
                other_ref[core ^ cores, 0, place, lanes] = take_chunk(ref, r, at, rows, hidden)


def spread_gate(where, low, high, far_low, far_high, hidden, span):
    chips, total, _ = low.shape
    count = chips // 2
    rows = span // (2 * chips)
    into = lambda at: pl.BlockSpec(
        (count, total, 128), lambda b, where: (b ^ (where[at] // count), 0, 0)
    )
    out = pl.BlockSpec((2, 1, count * rows, 2 * hidden), lambda b, where: (0, b, 0, 0))
    made = pl.pallas_call(
        spread_gate_kernel,
        grid_spec=pltpu.PrefetchScalarGridSpec(
            num_scalar_prefetch=1,
            grid=(2,),
            in_specs=[into(3), into(3), into(0), into(0)],
            out_specs=[out, out],
        ),
        out_shape=[jax.ShapeDtypeStruct((2, 2, count * rows, 2 * hidden), F32)] * 2,
        compiler_params=params(),
        cost_estimate=cost(8),
        name="spread_gate",
    )(where, low, high, far_low, far_high)
    return [array.reshape(span, 2 * hidden) for array in made]


def spread_down_kernel(where_ref, low, high, out_ref):
    chip, core = where_ref[0], where_ref[1]
    count = low.shape[0]
    rows = out_ref.shape[0] // count
    width = out_ref.shape[1] // 2
    for cores, ref in enumerate((low, high)):
        for r in range(count):
            place = aligned(((chip ^ r) % count) * rows, rows)
            lanes = aligned((core ^ cores) * width, width)
            out_ref[place, lanes] = take_chunk(ref, r, 0, rows, width)


def spread_down(where, low, high, hidden, width):
    chips, total, _ = low.shape
    count = chips // 2
    into = pl.BlockSpec((count, total, 128), lambda b, where: (b ^ (where[0] // count), 0, 0))
    return pl.pallas_call(
        spread_down_kernel,
        grid_spec=pltpu.PrefetchScalarGridSpec(
            num_scalar_prefetch=1,
            grid=(2,),
            in_specs=[into] * 2,
            out_specs=pl.BlockSpec((hidden // 2, width), lambda b, where: (b, 0)),
        ),
        out_shape=jax.ShapeDtypeStruct((hidden, width), F32),
        compiler_params=params(),
        cost_estimate=cost(5),
        name="spread_down",
    )(where, low, high)


def spread_token_kernel(where_ref, low, high, *out_refs):
    chip, core = where_ref[0], where_ref[1]
    count = low.shape[0]
    rows = out_refs[0].shape[2] // count
    width = out_refs[0].shape[3]
    for cores, ref in enumerate((low, high)):
        for r in range(count):
            place = aligned(((chip ^ r) % count) * rows, rows)
            for kind, out_ref in enumerate(out_refs):
                at = kind * rows * width // 128
                out_ref[core ^ cores, 0, place, :] = take_chunk(ref, r, at, rows, width)


def spread_token(where, low, high, span, width, kinds):
    chips, total, _ = low.shape
    count = chips // 2
    rows = span // (2 * chips)
    into = pl.BlockSpec((count, total, 128), lambda b, where: (b ^ (where[0] // count), 0, 0))
    out = pl.BlockSpec((2, 1, count * rows, width), lambda b, where: (0, b, 0, 0))
    made = pl.pallas_call(
        spread_token_kernel,
        grid_spec=pltpu.PrefetchScalarGridSpec(
            num_scalar_prefetch=1, grid=(2,), in_specs=[into] * 2, out_specs=[out] * kinds
        ),
        out_shape=[jax.ShapeDtypeStruct((2, 2, count * rows, width), F32)] * kinds,
        compiler_params=params(),
        cost_estimate=cost(5),
        name="spread_token",
    )(where, low, high)
    return [array.reshape(span, width) for array in made]


def picked_head(pos_ref, low, high, head):
    place = pos_ref[head]
    count = low.shape[0]
    return jnp.where(
        place < count, low[place % count].astype(F32), high[place % count].astype(F32)
    )


def head_spread_kernel(pos_ref, low_ref, high_ref, q_ref, k_ref, v_ref):
    span, width = q_ref.shape
    half = span // 2
    for pair in range(width // 128):
        at = pair * 128
        first = picked_head(pos_ref, low_ref, high_ref, 2 * pair)
        second = picked_head(pos_ref, low_ref, high_ref, 2 * pair + 1)
        low, high = pair_up(first, second)
        q_ref[:, at : at + 128] = low[:span]
        k_ref[:, at : at + 128] = high[:span]
        v_ref[:half, at : at + 128] = low[span:]
        v_ref[half:, at : at + 128] = high[span:]


def cross_head_spread_kernel(pos_ref, low_ref, high_ref, k_ref, v_ref):
    for pair in range(k_ref.shape[1] // 128):
        at = pair * 128
        first = picked_head(pos_ref, low_ref, high_ref, 2 * pair)
        second = picked_head(pos_ref, low_ref, high_ref, 2 * pair + 1)
        k_ref[:, at : at + 128], v_ref[:, at : at + 128] = pair_up(first, second)


def per_device(
    inputs,
    encoded,
    cotangent,
    doc_ids,
    buckets,
    gain_self,
    query_self,
    key_self,
    value_self,
    output_self,
    position_bias,
    gain_cross,
    query_cross,
    key_cross,
    value_cross,
    output_cross,
    gain_dense,
    dense_gate,
    dense_up,
    dense_down,
):
    micro_count, _, rows, width = inputs.shape
    part = encoded.shape[2]
    heads = position_bias.shape[1]
    dp, fs = lax.axis_size("dp"), lax.axis_size("fsdp")
    me, shard = lax.axis_index("dp"), lax.axis_index("fsdp")
    core, chips = me % 2, dp // 2
    length = rows * dp
    tokens = micro_count * rows
    copies = dp // heads
    head = me // copies
    span = width // fs
    half = span // 2
    hidden = dense_down.shape[0]
    chip_bits = [1 << place for place in range(1, dp.bit_length() - 1)]
    x_order, z_order = chip_bits, chip_bits[1:] + chip_bits[:1]
    paired = fs == 2
    chunked = paired and half % (16 * chips) == 0 and hidden % (16 * chips) == 0
    chunked = chunked and hidden % 128 == 0

    def chip_of(j, order=x_order):
        last = len(order) - 1
        return sum(((j // bit) % 2) << (last - place) for place, bit in enumerate(order))

    def swap_dp(values, bit):
        return lax.ppermute(values, "dp", [(j, j ^ bit) for j in range(dp)])

    def swap_fs(values):
        return lax.ppermute(values, "fsdp", [(j, 1 - j) for j in range(2)])

    def after(values, *others):
        return lax.optimization_barrier((values, *others))[0]

    def half_rows(values):
        return jnp.stack([lax.dynamic_slice_in_dim(w, core * half, half, axis=0) for w in values])

    def both_halves(sent):
        got = swap_fs(sent)
        return got, swap_dp(got, 1)

    def gather_rows(values):
        return [lax.all_gather(w, "fsdp", axis=0, tiled=True) for w in values]

    def both_tokens(values):
        if paired:
            return jnp.concatenate([values, swap_fs(values)], axis=0)
        return lax.all_gather(values, "fsdp", axis=0, tiled=True)

    def reduce_chips(kept, got, order=x_order):
        total = kept.astype(F32) + got.astype(F32)
        for bit in order[1:]:
            count = total.shape[0] // 2
            sent, total = total[count:].astype(BF16), total[:count]
            total = total + swap_dp(sent, bit).astype(F32)
        return total.astype(BF16)

    def gather_chips(values, order=x_order):
        for bit in reversed(order):
            values = jnp.concatenate([values, swap_dp(values, bit)], axis=0)
        return values, swap_dp(values, 1)

    x, g, e = inputs[:, 0], cotangent[:, 0], encoded[:, 0]

    low, offsets = [x], [0]
    for bit in reversed(chip_bits[1:]):
        low = low + [swap_dp(piece, bit) for piece in low]
        offsets = offsets + [offset | bit for offset in offsets]
    high = [swap_dp(piece, 2) for piece in low]
    near, far = jnp.stack(low), jnp.stack(high)
    offsets = [offset ^ more for more in (0, 2, 1, 3) for offset in offsets]
    source = me ^ jnp.array(offsets, jnp.int32)
    e_all = lax.all_gather(e, "dp", axis=0)

    gains = jnp.stack([gain_self, gain_cross, gain_dense])
    own_head = lambda w: lax.dynamic_slice_in_dim(w, head * 64, 64, axis=1)
    if paired:
        pad = jnp.pad(position_bias.reshape(1, -1), ((0, 0), (0, span - position_bias.size)))
        small = jnp.concatenate([gains, pad], axis=0)
        small_got = swap_fs(small)
        head_pack = jnp.concatenate([own_head(w) for w in (query_self, key_self, value_self)], 1)
        head_got = swap_fs(head_pack)
        first, second = (
            jnp.where(shard == which, mine, got)
            for which, mine, got in ((0, small, small_got), (1, small, small_got))
        )
        gains = jnp.concatenate([first[:3], second[:3]], axis=1)
        bias_all = jnp.concatenate(
            [piece[3, : position_bias.size].reshape(position_bias.shape) for piece in (first, second)]
        )
        head_whole = jnp.where(
            shard == 0,
            jnp.concatenate([head_pack, head_got]),
            jnp.concatenate([head_got, head_pack]),
        )
        other = (1 - shard) * span
        starts = jnp.stack([shard * span, other + core * half, other + (1 - core) * half])
        starts = starts.astype(jnp.int32)
        kv_own = (key_cross, value_cross)
        near_own = (output_self, query_cross, output_cross)
        near_got = swap_fs(half_rows(near_own + kv_own))
        theirs = jnp.stack(
            [
                lax.dynamic_slice(w, (core * half, (1 - shard) * hidden), (half, hidden))
                for w in (dense_gate, dense_up)
            ]
        )
        dense_own = (dense_gate, dense_up)
        which = jnp.stack([shard, core]).astype(jnp.int32)
        dense_starts = jnp.concatenate([starts, which])
    else:
        gains = lax.all_gather(gains, "fsdp", axis=1, tiled=True)
        bias_all = lax.all_gather(position_bias, "fsdp", axis=0, tiled=True)
        kv_own, kv_more = gather_rows((key_cross, value_cross)), ()
        near_own, near_more = gather_rows((output_self, query_cross, output_cross)), ()
        first_own, first_more = gather_rows((query_self, key_self, value_self)), ()
        head_whole = jnp.concatenate([own_head(w) for w in first_own], axis=1)
        dense_own = [
            lax.all_to_all(w, "fsdp", 1, 0, tiled=True) for w in (dense_gate, dense_up)
        ]
        dense_more = ()
        starts = jnp.zeros((1,), jnp.int32)
        dense_starts = jnp.zeros((3,), jnp.int32)
        g_group = both_tokens(g.reshape(tokens, width))
    gains, bias_all = gains.astype(F32), bias_all.astype(F32)
    head_w = jnp.concatenate(
        [head_whole[:, at : at + 64] for at in (0, 0, 64, 64, 128, 128)], axis=1
    )

    marks = jnp.arange(bias_all.shape[0], dtype=jnp.int32)
    edges = jnp.sum((buckets[:, None] < marks[None, :]).astype(jnp.int32), axis=0)
    bias_values = lax.dynamic_slice_in_dim(bias_all, head, 1, axis=1)[:, 0]
    table = bias_table(edges, bias_values, length)
    x_groups = [near, far, swap_dp(near, 1), swap_dp(after(far, table), 1)]
    doc_row = jnp.broadcast_to(doc_ids[:, 0, :, None], (micro_count, dp, rows))
    doc_row = doc_row.reshape(micro_count, length)
    doc_col = doc_row[:, :, None]

    n_all, qkv, mixed = pl.pallas_call(
        functools.partial(self_forward_kernel, len(x_groups)),
        out_shape=[
            jax.ShapeDtypeStruct((dp, micro_count, rows, width), BF16),
            jax.ShapeDtypeStruct((length, 384), BF16),
            jax.ShapeDtypeStruct((length, 128), BF16),
        ],
        in_specs=[smem()] + [vmem()] * (len(x_groups) + 5),
        out_specs=[vmem()] * 3,
        compiler_params=params(),
        cost_estimate=cost(12),
        name="self_forward",
    )(source, *x_groups, gains[0:1], head_w, table, doc_row, doc_col)
    o1_heads = lax.all_to_all(mixed.reshape(dp, rows, 128), "dp", 0, 0, tiled=True)[::copies]

    if paired:
        near_more = kv_more = (near_got, swap_dp(after(near_got, mixed), 1))
        dense_got = swap_fs(after(theirs, near_got, mixed))
    ke, ve = cross_kv(starts, e_all, *kv_own, kv_more)

    row32 = jax.ShapeDtypeStruct((tokens, width), F32)
    row16 = jax.ShapeDtypeStruct((tokens, width), BF16)
    left, x1, q2, x2, n3 = pl.pallas_call(
        functools.partial(mid_forward_kernel, len(near_more)),
        out_shape=[
            jax.ShapeDtypeStruct((3, tokens, width), BF16), row32, row16, row32, row16
        ],
        in_specs=[smem()] + [vmem()] * (8 + len(near_more)),
        out_specs=[vmem()] * 5,
        scratch_shapes=[pltpu.VMEM((tokens, width), BF16)] * 3,
        compiler_params=params(),
        cost_estimate=cost(12),
        name="mid_forward",
    )(starts, o1_heads, x, gains, ke, ve, *near_own, *near_more)

    if paired:
        dense_more = (dense_got, swap_dp(after(dense_got, n3), 1))
        g_rows = g.reshape(tokens, width)
        g_got = swap_fs(after(g_rows, dense_got))
        n_got = swap_fs(n3)
        back, y32, _, dn3, _ = dense_layer(
            dense_starts, n3, g_rows, *dense_own, dense_down, dense_more, tokens
        )
        back_mate = swap_dp(back, 1)
        back_got, _, y16, _, d16 = dense_layer(
            dense_starts,
            after(n_got, dn3),
            g_got,
            *dense_own,
            dense_down,
            dense_more,
            tokens,
        )
        back_got_mate = swap_dp(back_got, 1)
        dn3_more = swap_fs(d16)
    else:
        n_group = both_tokens(n3)
        back, _, y16, _, d16 = dense_layer(
            dense_starts, n_group, g_group, *dense_own, dense_down, dense_more, tokens
        )
        dn3 = jnp.zeros((tokens, width), F32)
        dn3_more = lax.psum_scatter(d16, "fsdp", scatter_dimension=0, tiled=True)
        dense_out = lax.psum_scatter(y16, "fsdp", scatter_dimension=0, tiled=True).astype(F32)
        outputs = (x2 + dense_out).astype(BF16)

    if chunked:
        where = jnp.stack([chip_of(me), core, shard, chip_of(me, z_order)]).astype(jnp.int32)
        own_kept, own_sent, down_kept, down_sent, far_kept, far_sent = chunk_weights(
            dense_weight_kernel,
            where,
            (n3, n_got, g_rows, g_got, back, back_got, back_mate, back_got_mate),
            (
                span // chips * hidden // 128,
                hidden // chips * width // 256,
                span // chips * hidden // 128,
            ),
            chips,
            [
                pltpu.VMEM((max(hidden, half), max(hidden, width // 2)), F32),
                pltpu.VMEM((4 * tokens, width), BF16),
            ],
            7,
            "dense_weight",
        )
        dn3_more = after(dn3_more, own_sent)
        own_got, down_got = swap_dp(own_sent, z_order[0]), swap_dp(down_sent, x_order[0])
        far_got = swap_fs(far_sent)

    right, gx1, do1_heads, dkv, dc_two = pl.pallas_call(
        functools.partial(mid_backward_kernel, len(near_more)),
        out_shape=[
            jax.ShapeDtypeStruct((tokens, 3 * width), BF16),
            row32,
            jax.ShapeDtypeStruct((heads, rows, 128), BF16),
            jax.ShapeDtypeStruct((heads, dp, micro_count, part, 128), BF16),
            jax.ShapeDtypeStruct((2, width), F32),
        ],
        in_specs=[smem()] + [vmem()] * (12 + len(near_more)),
        out_specs=[vmem()] * 5,
        scratch_shapes=[
            pltpu.VMEM((tokens, width), F32),
            pltpu.VMEM((tokens, width), BF16),
            pltpu.VMEM((tokens, width), BF16),
        ],
        compiler_params=params(),
        cost_estimate=cost(16),
        name="mid_backward",
    )(starts, g, dn3, dn3_more, x1, x2, gains, q2, ke, ve, *near_own, *near_more)
    do1 = lax.all_to_all(
        jnp.repeat(do1_heads, copies, axis=0) if copies > 1 else do1_heads, "dp", 0, 0, tiled=True
    ).reshape(length, 128)

    if chunked:
        views = left.reshape(3, tokens, 2, 2 * half)
        own = lax.dynamic_index_in_dim(views, shard, 2, keepdims=False)
        sent = lax.dynamic_index_in_dim(views, 1 - shard, 2, keepdims=False)
        got = swap_fs(after(sent, dn3_more))
        left_views = jnp.concatenate([own, got], axis=1).reshape(3, 2 * tokens, 2, half)

        def left_features(which):
            picked = lax.dynamic_index_in_dim(left_views, which, 2, keepdims=False)
            return picked.transpose(1, 0, 2).reshape(2 * tokens, 3 * half)

        left_mate = swap_dp(left_features(1 - core), 1)
        right_got = swap_fs(right)
        far_kept = swap_fs(after(far_kept, right_got))
        do1 = after(do1, left_mate, own_got, down_got, far_got)

    dqkv, table_grad = pl.pallas_call(
        self_backward_kernel,
        out_shape=[
            jax.ShapeDtypeStruct((length, 384), BF16),
            jax.ShapeDtypeStruct((TILE, length), F32),
        ],
        in_specs=[vmem()] * 5,
        out_specs=[vmem()] * 2,
        scratch_shapes=[pltpu.VMEM((length, 128), F32), pltpu.VMEM((length, 128), F32)],
        compiler_params=params(),
        cost_estimate=cost(10),
        name="self_backward",
    )(qkv, do1, table, doc_row, doc_col)
    if chunked:
        dqkv = after(dqkv, right_got)
    head_grad = pl.pallas_call(
        head_weight_kernel,
        out_shape=jax.ShapeDtypeStruct((fs, span * 3 // 2, 128), BF16),
        in_specs=[vmem()] * 2,
        out_specs=vmem(),
        compiler_params=params(),
        cost_estimate=cost(6),
        name="head_weight",
    )(n_all, dqkv)
    def sum_shards(values):
        if paired:
            kept = lax.dynamic_index_in_dim(values, shard, 0)
            sent = lax.dynamic_index_in_dim(values, 1 - shard, 0)
            return (kept.astype(F32) + swap_fs(sent).astype(F32)).astype(BF16)
        return lax.psum_scatter(values, "fsdp", scatter_dimension=0, tiled=True)

    head_sum = sum_shards(head_grad)
    if chunked:
        token_kept, token_sent = chunk_weights(
            token_weight_kernel,
            where,
            (
                left_features(core),
                left_mate,
                right,
                right_got,
                swap_dp(right, 1),
                swap_dp(right_got, 1),
            ),
            (3 * half // chips * width // 128,),
            chips,
            [pltpu.VMEM((half, width), F32)],
            5,
            "token_weight",
        )
        head_sum = after(head_sum, token_kept)

    relative = me ^ (jnp.arange(heads, dtype=jnp.int32) * copies)
    head_places = (relative % 2) * chips + chip_of(relative)
    grad_query_self, grad_key_self, grad_value_self = pl.pallas_call(
        head_spread_kernel,
        out_shape=[jax.ShapeDtypeStruct((span, width), F32)] * 3,
        in_specs=[smem(), vmem(), vmem()],
        out_specs=[vmem()] * 3,
        compiler_params=params(),
        cost_estimate=cost(6),
        name="head_spread",
    )(head_places, *gather_chips(head_sum))

    if paired:
        first_own = (query_self, key_self, value_self)
        first_more = both_halves(after(half_rows(first_own), head_sum))
        y16 = swap_fs(after(y16, first_more[0]))
        outputs = (x2 + (y32 + y16.astype(F32))).astype(BF16)
    own_d = lax.all_to_all(dqkv.reshape(dp, rows, 384), "dp", 0, 0, tiled=True)[::copies]
    grad_inputs, dc_one = pl.pallas_call(
        functools.partial(input_grad_kernel, len(first_more)),
        out_shape=[row32, jax.ShapeDtypeStruct((1, width), F32)],
        in_specs=[smem()] + [vmem()] * (7 + len(first_more)),
        out_specs=[vmem()] * 2,
        scratch_shapes=[
            pltpu.VMEM((tokens, 3 * width), BF16),
            pltpu.VMEM((tokens, width), F32),
        ],
        compiler_params=params(),
        cost_estimate=cost(7),
        name="input_grad",
    )(starts, own_d, x, gains, gx1, *first_own, *first_more)

    dkv = dkv.reshape(heads * copies, -1, 128)
    dkv = lax.psum_scatter(dkv, "dp", scatter_dimension=0, tiled=True)[0]
    bit = 1
    while bit < copies:
        got = swap_dp(dkv, bit)
        dkv = jnp.where(
            (me // bit) % 2 == 0, jnp.concatenate([dkv, got]), jnp.concatenate([got, dkv])
        )
        bit *= 2
    cross_grad = pl.pallas_call(
        cross_head_weight_kernel,
        out_shape=jax.ShapeDtypeStruct((fs, span, 128), BF16),
        in_specs=[vmem()] * 2,
        out_specs=vmem(),
        compiler_params=params(),
        cost_estimate=cost(3),
        name="cross_head_weight",
    )(e_all, dkv)
    cross_sum = sum_shards(cross_grad)
    grad_key_cross, grad_value_cross = pl.pallas_call(
        cross_head_spread_kernel,
        out_shape=[jax.ShapeDtypeStruct((span, width), F32)] * 2,
        in_specs=[smem(), vmem(), vmem()],
        out_specs=[vmem()] * 2,
        compiler_params=params(),
        cost_estimate=cost(4),
        name="cross_head_spread",
    )(head_places, *gather_chips(cross_sum))
    own_dkv = dkv.reshape(dp, micro_count * part, 128)
    own_dkv = lax.all_to_all(own_dkv, "dp", 0, 0, tiled=True)[::copies]
    grad_encoded = pl.pallas_call(
        functools.partial(encoder_grad_kernel, len(kv_more)),
        out_shape=jax.ShapeDtypeStruct((micro_count * part, width), F32),
        in_specs=[smem()] + [vmem()] * (3 + len(kv_more)),
        out_specs=vmem(),
        scratch_shapes=[pltpu.VMEM((micro_count * part, width), BF16)] * 2,
        compiler_params=params(),
        cost_estimate=cost(4),
        name="encoder_grad",
    )(starts, own_dkv, *kv_own, *kv_more)

    if chunked:
        dense_low, dense_high = gather_chips(reduce_chips(own_kept, own_got, z_order), z_order)
        down_low, down_high = gather_chips(reduce_chips(down_kept, down_got))
        far_low, far_high = gather_chips(reduce_chips(far_kept, swap_dp(far_got, 2)))
        grad_dense_down = spread_down(where, down_low, down_high, hidden, width)
        grad_dense_gate, grad_dense_up = spread_gate(
            where, dense_low, dense_high, far_low, far_high, hidden, span
        )

        token_sum = after(reduce_chips(token_kept, swap_dp(token_sent, 2)), cross_grad)
        token_low, token_high = gather_chips(token_sum)
        grad_output_cross, grad_query_cross, grad_output_self = spread_token(
            where, token_low, token_high, span, width, 3
        )
    else:

        def over_dp(values):
            return lax.psum(values.astype(BF16), "dp").astype(F32)

        def over_all(a, b):
            made = t_dot(a, b).astype(BF16)
            return over_dp(lax.psum_scatter(made, "fsdp", scatter_dimension=0, tiled=True))

        grad_output_cross, grad_query_cross, grad_output_self = (
            over_all(left[kind], right[:, kind * width : (kind + 1) * width]) for kind in range(3)
        )
        grad_dense_gate, grad_dense_up = (
            over_dp(
                lax.all_to_all(
                    t_dot(n_group, back[:, kind * hidden : (kind + 1) * hidden]).astype(BF16),
                    "fsdp",
                    0,
                    1,
                    tiled=True,
                )
            )
            for kind in range(2)
        )
        grad_dense_down = over_dp(t_dot(back[:, 2 * hidden :], g_group))

    if chunked:
        table_grad = after(table_grad, first_more[1])
    table_sums = jnp.sum(bucket_sums(edges, table_grad, bias_all.shape[0]), axis=1)
    column = (jnp.arange(heads) == head) & (me % copies == 0)
    bias_row = jnp.where(column[None, :], table_sums[:, None], 0.0).reshape(1, -1)
    bias_row = jnp.pad(bias_row, ((0, 0), (0, width - bias_row.shape[1])))
    sums = jnp.concatenate([dc_one, dc_two, bias_row], axis=0)
    if paired:
        sums = sums + swap_fs(sums)
        for bit in [1] + chip_bits:
            sums = sums + swap_dp(sums, bit)
    else:
        sums = lax.psum(sums, ("dp", "fsdp"))
    own = lax.dynamic_slice_in_dim(sums[:3], shard * span, span, axis=1)
    grad_bias = sums[3, : bias_all.size].reshape(bias_all.shape)
    grad_bias = lax.dynamic_slice_in_dim(
        grad_bias, shard * position_bias.shape[0], position_bias.shape[0], axis=0
    )
    shape = (micro_count, 1, rows, width)
    return (
        outputs.reshape(shape),
        grad_inputs.reshape(shape),
        grad_encoded.reshape(micro_count, 1, part, width),
        own[0],
        grad_query_self,
        grad_key_self,
        grad_value_self,
        grad_output_self,
        grad_bias,
        own[2],
        grad_query_cross,
        grad_key_cross,
        grad_value_cross,
        grad_output_cross,
        own[1],
        grad_dense_gate,
        grad_dense_up,
        grad_dense_down,
    )


def solution(mesh):
    matrix = P("fsdp", None)
    token = P(None, "fsdp", "dp", None)
    weights = (
        (P("fsdp"),)
        + (matrix,) * 5
        + (P("fsdp"),)
        + (matrix,) * 4
        + (P("fsdp"),)
        + (matrix,) * 3
    )
    return jax.shard_map(
        per_device,
        mesh=mesh,
        in_specs=(token,) * 3 + (P(None, "fsdp", None), P()) + weights,
        out_specs=(token,) * 3 + weights,
        check_vma=False,
    )
```

time: 775 us -> 553 us (0.71)
  other arithmetic: 89.1 us -> 27.1 us
  local copies, waits for them, and re-layouts: 106 us -> 50.6 us
  waiting for transfers between devices: 267 us -> 215 us
  blocking collectives: 40.7 us -> 0 us
  matrix products: 27.3 us -> 0 us
  Pallas kernels: 139 us -> 155 us
    ppermute x19 -> x16, waiting for transfers between devices: 106 us -> 45.9 us  [swap_fs(): return lax.ppermute(values, 'fsdp', [(j, 1 - j) for j in range(2)])]
    psum x1 -> x0, blocking collectives: 40.7 us -> none  [per_device(): lax.psum(jnp.concatenate([dc_one, dc_two, bias_row], axis=0), ('dp', 'fsd...]
    select_n x12 -> x2, other arithmetic: 32.7 us -> 1.43 us  [the longest x1 1.42 us: per_device(): jnp.where(shard == 0, jnp.concatenate([head_pack, head_got]), jnp.concate...]
    dot_general x13 -> x0, matrix products: 27.3 us -> none  [the longest x6 10 us: t_dot(): lax.dot_general(left, right, (((0,), (0,)), ((), ())), preferred_element_...]
    unnamed x210 -> x104, local copies, waits for them, and re-layouts: 36.9 us -> 17.3 us
    pallas_call x8 -> x15, Pallas kernels: 106 us -> 122 us  [the longest x2 19.7 us: dense_layer(): pl.pallas_call(functools.partial(dense_kernel, len(more)), grid_spec=pltp...]
    concatenate x24 -> x20, other arithmetic: 20.4 us -> 6.96 us  [the longest x16 5.28 us: gather_chips(): values = jnp.concatenate([values, swap_dp(values, bit)], axis=0)]
    slice x11 -> x10, local copies, waits for them, and re-layouts: 15.7 us -> 2.37 us  [the longest x8 1.75 us: reduce_chips(): sent, total = (total[count:].astype(BF16), total[:count])]
  transfers between devices with their start and end apart: 82 -> 79, of which waited for: 29 -> 27; matrix products, arithmetic and copies ran while one was open for 27% -> 13% of each run, Pallas kernels for 16% -> 27%
where the time goes in v2:
time: 553 us; the launch traced here: 546 us
  waiting for transfers between devices  215 us (39%)
  Pallas kernels  155 us (28%)
  starting transfers between devices  83.5 us (15%)
  local copies, waits for them, and re-layouts  50.6 us (9%)
  other arithmetic  27.1 us (5%)
  between operations  15.3 us (3%)
    ppermute x57, waiting for transfers between devices, swap_dp(): return lax.ppermute(values, 'dp', [(j, j ^ bit) for j in range(dp)])  169 us
    ppermute x16, waiting for transfers between devices, swap_fs(): return lax.ppermute(values, 'fsdp', [(j, 1 - j) for j in range(2)])  45.9 us
    ppermute x57, starting transfers between devices, swap_dp(): return lax.ppermute(values, 'dp', [(j, j ^ bit) for j in range(dp)])  45.1 us
    ppermute x16, starting transfers between devices, swap_fs(): return lax.ppermute(values, 'fsdp', [(j, 1 - j) for j in range(2)])  22.2 us
    pallas_call x2, Pallas kernels, dense_layer(): pl.pallas_call(functools.partial(dense_kernel, len(more)), grid_spec=pltp...  19.7 us
    pallas_call x1, Pallas kernels, per_device(): pl.pallas_call(functools.partial(mid_backward_kernel, len(near_more)), ou...  18.5 us
    unnamed x104, local copies, waits for them, and re-layouts  17.3 us
    pallas_call x1, Pallas kernels, per_device(): pl.pallas_call(functools.partial(mid_forward_kernel, len(near_more)), out...  12.9 us
  transfers between devices with their start and end apart: 79, of which 27 were waited for; matrix products, arithmetic and copies ran while one was open for 13% of the time, Pallas kernels for 27%

profile of v2, /device:TPU:0, one launch (start us, length us, event | category | flops | bytes accessed | tf_op | source)
XLA Modules:
  0.0 546.5 jit_solution(11154274799875727485)
XLA Ops:
  7.3 4.1 collective-permute-start
  31.8 6.2 %collective-permute-done.2 = bf16[2,64,1024]{2,1,0:T(8,128)(2,1)S(1)} collective-permute-done((bf16[2,64,1024]{2,1,0:T(8,128)(2,1)}, bf16[2,64,1024]{2,1,0:T(8,128)(2,1)S(1)}, u32[]{:S(2)}, u32[]{:S(2)}) %collective-permute-start.2) | collective-permute-done | bytes 262176 | tf_op jit(solution)/shard_map/ppermute | solution.py:782
  38.5 4.4 bias_table.1.refs_6_.table_ref
  45.7 7.6 %collective-permute-done.6 = bf16[2,64,1024]{2,1,0:T(8,128)(2,1)} collective-permute-done((bf16[2,64,1024]{2,1,0:T(8,128)(2,1)S(1)}, bf16[2,64,1024]{2,1,0:T(8,128)(2,1)}, u32[]{:S(2)}, u32[]{:S(2)}) %collective-permute-start.6) | collective-permute-done | bytes 262176 | tf_op jit(solution)/shard_map/ppermute | solution.py:782
  59.4 28.2 %collective-permute-done.10 = bf16[512,192]{1,0:T(8,128)(2,1)} collective-permute-done((bf16[512,192]{1,0:T(8,128)(2,1)}, bf16[512,192]{1,0:T(8,128)(2,1)}, u32[]{:S(2)}, u32[]{:S(2)}) %collective-permute-start.10) | collective-permute-done | bytes 196640 | tf_op jit(solution)/shard_map/ppermute | solution.py:785
  90.7 11.6 %self_forward.1 = (bf16[16,2,64,1024]{3,2,1,0:T(8,128)(2,1)}, bf16[1024,384]{1,0:T(8,128)(2,1)}, bf16[1024,128]{1,0:T(8,128)(2,1)}) custom-call(s32[16]{0:T(128)} %broadcast_xor_fusion.source_ref, bf16[4,2,64,1024]{3,2,1,0:T(8,128)(2,1)} %copy-done.2, bf16[4,2,64,1024]{3,2,1,0:T(8,128)(2,1)} %copy-done.4, ...), custom_call_target="tpu_custom_call" | custom-call | flops 13799999488 | bytes 44280000 | tf_op jit(solution)/shard_map/self_forward/pallas_call | solution.py:894
  104.5 3.5 all-to-all-start
  108.7 9.9 %cross_kv.1 = (bf16[2,512,1024]{2,1,0:T(8,128)(2,1)}, bf16[2,512,1024]{2,1,0:T(8,128)(2,1)}) custom-call(s32[3]{0:T(128)} %pad_add_fusion.starts_ref, bf16[16,2,32,1024]{3,2,1,0:T(8,128)(2,1)} %bitcast.106, bf16[512,1024]{1,0:T(8,128)(2,1)} %wk.3, bf16[512,1024]{1,0:T(8,128)(2,1)} %wv.3, bf16[5,256,1024]{2,1,0:T(8,128)(2,1)} %collective-permute-done.11.refs_0_, ...), custom_call_target="tpu_custom_call" | custom-call | flops 9200000000 | bytes 29520000 | tf_op jit(solution)/shard_map/cross_kv/pallas_call | solution.py:297
  119.2 12.9 %mid_forward.1 = (bf16[3,128,1024]{2,1,0:T(8,128)(2,1)}, f32[128,1024]{1,0:T(8,128)}, bf16[128,1024]{1,0:T(8,128)(2,1)}, f32[128,1024]{1,0:T(8,128)}, bf16[128,1024]{1,0:T(8,128)(2,1)}) custom-call(s32[3]{0:T(128)} %pad_add_fusion.starts_ref, bf16[16,64,128]{2,1,0:T(8,128)(2,1)} %copy-done.20, bf16[2,64,1024]{2,1,0:T(8,128)(2,1)} %bitcast.94, ...), custom_call_target="tpu_custom_call" | custom-call | flops 13799999488 | bytes 44280000 | tf_op jit(solution)/shard_map/mid_forward/pallas_call | solution.py:916
  132.1 10.0 %collective-permute-done.13.refs_0_ = bf16[2,256,1408]{2,1,0:T(8,128)(2,1)} collective-permute-done((bf16[2,256,1408]{2,1,0:T(8,128)(2,1)S(1)}, bf16[2,256,1408]{2,1,0:T(8,128)(2,1)}, u32[]{:S(2)}, u32[]{:S(2)}) %collective-permute-start.13) | collective-permute-done | bytes 1441824 | tf_op jit(solution)/shard_map/ppermute | solution.py:785
  146.6 9.8 %dense_layer.2 = (bf16[128,5248]{1,0:T(8,128)(2,1)}, f32[128,1024]{1,0:T(8,128)}, bf16[128,1024]{1,0:T(8,128)(2,1)}, f32[128,1024]{1,0:T(8,128)}, bf16[128,1024]{1,0:T(8,128)(2,1)}) custom-call(s32[5]{0:T(128)} %concatenate.109.starts_ref, bf16[128,1024]{1,0:T(8,128)(2,1)} %get-tuple-element.83.n_ref.n0_ref, bf16[128,1024]{1,0:T(8,128)(2,1)} %bitcast.108, ...), custom_call_target="tpu_custom_call" | custom-call | flops 14949999616 | bytes 47970000 | tf_op jit(solution)/shard_map/dense_layer/pallas_call | solution.py:496
  158.5 9.8 %dense_layer.3 = (bf16[128,5248]{1,0:T(8,128)(2,1)}, f32[128,1024]{1,0:T(8,128)}, bf16[128,1024]{1,0:T(8,128)(2,1)}, f32[128,1024]{1,0:T(8,128)}, bf16[128,1024]{1,0:T(8,128)(2,1)}) custom-call(s32[5]{0:T(128)} %concatenate.109.starts_ref, bf16[128,1024]{1,0:T(8,128)(2,1)} %copy-done.42, bf16[128,1024]{1,0:T(8,128)(2,1)} %copy-done.41, ...), custom_call_target="tpu_custom_call" | custom-call | flops 14949999616 | bytes 47970000 | tf_op jit(solution)/shard_map/dense_layer/pallas_call | solution.py:496
  171.0 10.5 %reshape.126 = bf16[3,128,2,512]{3,2,1,0:T(2,128)(2,1)S(1)} reshape(bf16[3,128,1024]{2,1,0:T(8,128)(2,1)S(1)} %copy-done.7) | data formatting | bytes 1572864 | tf_op jit(solution)/shard_map/reshape | solution.py:1007
  184.6 7.3 %dense_weight.1 = (bf16[4,704,128]{2,1,0:T(8,128)(2,1)}, bf16[4,704,128]{2,1,0:T(8,128)(2,1)}, bf16[4,704,128]{2,1,0:T(8,128)(2,1)}, bf16[4,704,128]{2,1,0:T(8,1...) custom-call(s32[4]{0:T(128)} %pad_add_fusion.1.where_ref, ...), custom_call_target="tpu_custom_call" | custom-call | flops 8049999872 | bytes 25830000 | tf_op jit(solution)/shard_map/dense_weight/pallas_call | solution.py:592
  197.0 18.5 %mid_backward.1 = (bf16[128,3072]{1,0:T(8,128)(2,1)}, f32[128,1024]{1,0:T(8,128)}, bf16[16,64,128]{2,1,0:T(8,128)(2,1)}, bf16[16,16,2,32,128]{4,3,2,1,0:T(8,128)(2,1)}, f32[2,1024]{1,0:T(2,128)}) custom-call(s32[3]{0:T(128)} %pad_add_fusion.starts_ref, bf16[2,64,1024]{2,1,0:T(8,128)(2,1)} %bitcast.110, f32[128,1024]{1,0:T(8,128)} %get-tuple-element.87.dn3_ref, ...), custom_call_target="tpu_custom_call" | custom-call | flops 18400000000 | bytes 59040000 | tf_op jit(solution)/shard_map/mid_backward/pallas_call | solution.py:982
  215.5 4.2 all-to-all-start.1
  229.8 9.6 %self_backward.1 = (bf16[1024,384]{1,0:T(8,128)(2,1)}, f32[256,1024]{1,0:T(8,128)}) custom-call(bf16[1024,384]{1,0:T(8,128)(2,1)} %get-tuple-element.92.qkv_ref, bf16[1024,128]{1,0:T(8,128)(2,1)} %bitcast.32.do_ref, f32[256,1024]{1,0:T(8,128)} %bias_table.1.refs_6_.table_ref, s32[2,1024]{1,0:T(2,128)} %reshape.123.refs_7_.doc_row_ref, ...), custom_call_target="tpu_custom_call" | custom-call | flops 11500000256 | bytes 36900000 | tf_op jit(solution)/shard_map/self_backward/pallas_call | solution.py:1022
  241.6 6.0 %head_weight.1 = bf16[2,768,128]{2,1,0:T(8,128)(2,1)} custom-call(bf16[16,2,64,1024]{3,2,1,0:T(8,128)(2,1)} %get-tuple-element.91.n_ref, bf16[1024,384]{1,0:T(8,128)(2,1)} %get-tuple-element.108.d_ref), custom_call_target="tpu_custom_call" | custom-call | flops 6899999744 | bytes 22140000 | tf_op jit(solution)/shard_map/head_weight/pallas_call | solution.py:1037
  254.3 4.5 all-to-all-start.2
  261.5 14.0 %collective-permute-done.67 = bf16[2,704,128]{2,1,0:T(8,128)(2,1)} collective-permute-done((bf16[2,704,128]{2,1,0:T(8,128)(2,1)}, bf16[2,704,128]{2,1,0:T(8,128)(2,1)}, u32[]{:S(2)}, u32[]{:S(2)}) %collective-permute-start.67) | collective-permute-done | bytes 360480 | tf_op jit(solution)/shard_map/ppermute | solution.py:782
  277.7 15.9 %collective-permute-done.54 = bf16[1,704,128]{2,1,0:T(8,128)(2,1)S(1)} collective-permute-done((bf16[1,704,128]{2,1,0:T(8,128)(2,1)S(1)}, bf16[1,704,128]{2,1,0:T(8,128)(2,1)S(1)}, u32[]{:S(2)}, u32[]{:S(2)}) %collective-permute-start.54) | collective-permute-done | bytes 180256 | tf_op jit(solution)/shard_map/ppermute | solution.py:782
  296.0 9.2 %collective-permute-done.68 = bf16[1,704,128]{2,1,0:T(8,128)(2,1)S(1)} collective-permute-done((bf16[1,704,128]{2,1,0:T(8,128)(2,1)S(1)}, bf16[1,704,128]{2,1,0:T(8,128)(2,1)S(1)}, u32[]{:S(2)}, u32[]{:S(2)}) %collective-permute-start.68) | collective-permute-done | bytes 180256 | tf_op jit(solution)/shard_map/ppermute | solution.py:782
  305.8 8.6 %collective-permute-done.55 = bf16[1,704,128]{2,1,0:T(8,128)(2,1)S(1)} collective-permute-done((bf16[1,704,128]{2,1,0:T(8,128)(2,1)S(1)}, bf16[1,704,128]{2,1,0:T(8,128)(2,1)S(1)}, u32[]{:S(2)}, u32[]{:S(2)}) %collective-permute-start.55) | collective-permute-done | bytes 180256 | tf_op jit(solution)/shard_map/ppermute | solution.py:782
  318.4 5.1 token_weight.1
  326.7 8.0 %collective-permute-done.69 = bf16[1,704,128]{2,1,0:T(8,128)(2,1)S(1)} collective-permute-done((bf16[1,704,128]{2,1,0:T(8,128)(2,1)S(1)}, bf16[1,704,128]{2,1,0:T(8,128)(2,1)S(1)}, u32[]{:S(2)}, u32[]{:S(2)}) %collective-permute-start.69) | collective-permute-done | bytes 180256 | tf_op jit(solution)/shard_map/ppermute | solution.py:782
  335.4 15.2 %collective-permute-done.37 = bf16[1,768,128]{2,1,0:T(8,128)(2,1)S(1)} collective-permute-done((bf16[1,768,128]{2,1,0:T(8,128)(2,1)S(1)}, bf16[1,768,128]{2,1,0:T(8,128)(2,1)S(1)}, u32[]{:S(2)}, u32[]{:S(2)}) %collective-permute-start.37) | collective-permute-done | bytes 196640 | tf_op jit(solution)/shard_map/ppermute | solution.py:782
  352.9 8.6 %collective-permute-done.70 = bf16[2,704,128]{2,1,0:T(8,128)(2,1)S(1)} collective-permute-done((bf16[2,704,128]{2,1,0:T(8,128)(2,1)S(1)}, bf16[2,704,128]{2,1,0:T(8,128)(2,1)S(1)}, u32[]{:S(2)}, u32[]{:S(2)}) %collective-permute-start.70) | collective-permute-done | bytes 360480 | tf_op jit(solution)/shard_map/ppermute | solution.py:782
  363.3 12.7 %collective-permute-done.38 = bf16[2,768,128]{2,1,0:T(8,128)(2,1)S(1)} collective-permute-done((bf16[2,768,128]{2,1,0:T(8,128)(2,1)S(1)}, bf16[2,768,128]{2,1,0:T(8,128)(2,1)S(1)}, u32[]{:S(2)}, u32[]{:S(2)}) %collective-permute-start.38) | collective-permute-done | bytes 393248 | tf_op jit(solution)/shard_map/ppermute | solution.py:782
  379.6 7.0 %collective-permute-done.71 = bf16[4,704,128]{2,1,0:T(8,128)(2,1)S(1)} collective-permute-done((bf16[4,704,128]{2,1,0:T(8,128)(2,1)S(1)}, bf16[4,704,128]{2,1,0:T(8,128)(2,1)S(1)}, u32[]{:S(2)}, u32[]{:S(2)}) %collective-permute-start.71) | collective-permute-done | bytes 720928 | tf_op jit(solution)/shard_map/ppermute | solution.py:782
  388.5 12.0 %collective-permute-done.64 = bf16[2,704,128]{2,1,0:T(8,128)(2,1)S(1)} collective-permute-done((bf16[2,704,128]{2,1,0:T(8,128)(2,1)S(1)}, bf16[2,704,128]{2,1,0:T(8,128)(2,1)S(1)}, u32[]{:S(2)}, u32[]{:S(2)}) %collective-permute-start.64) | collective-permute-done | bytes 360480 | tf_op jit(solution)/shard_map/ppermute | solution.py:782
  400.6 4.1 collective-permute-done.42
  408.3 6.8 %collective-permute-done.43 = bf16[1,768,128]{2,1,0:T(8,128)(2,1)S(1)} collective-permute-done((bf16[1,768,128]{2,1,0:T(8,128)(2,1)S(1)}, bf16[1,768,128]{2,1,0:T(8,128)(2,1)S(1)}, u32[]{:S(2)}, u32[]{:S(2)}) %collective-permute-start.43) | collective-permute-done | bytes 196640 | tf_op jit(solution)/shard_map/ppermute | solution.py:782
  421.7 7.4 %bucket_sums.1 = f32[32,128]{1,0:T(8,128)} custom-call(s32[32]{0:T(128)} %convert_reduce_fusion.edge_ref, f32[256,1024]{1,0:T(8,128)} %get-tuple-element.119.grad_ref), custom_call_target="tpu_custom_call" | custom-call | flops 8049999872 | bytes 25830000 | tf_op jit(solution)/shard_map/bucket_sums/pallas_call | solution.py:137
  430.0 6.8 %input_grad.1 = (f32[128,1024]{1,0:T(8,128)}, f32[1,1024]{1,0:T(1,128)}) custom-call(s32[3]{0:T(128)} %pad_add_fusion.starts_ref, bf16[16,64,384]{2,1,0:T(8,128)(2,1)} %all-to-all-done.2.d_ref, bf16[2,64,1024]{2,1,0:T(8,128)(2,1)} %bitcast.95, f32[3,1024]{1,0:T(4,128)} %copy-done.28, f32[128,1024]{1,0:T(8,128)} %get-tuple-element.113.gx1_ref, ...), custom_call_target="tpu_custom_call" | custom-call | flops 8049999872 | bytes 25830000 | tf_op jit(solution)/shard_map/input_grad/pallas_call | solution.py:1092
  437.5 5.4 collective-permute-start.32
  442.9 3.2 cross_head_weight.1
  447.2 4.8 collective-permute-done.48
  453.0 3.0 collective-permute-start.49
  456.8 8.0 %collective-permute-done.44 = bf16[1,768,128]{2,1,0:T(8,128)(2,1)S(1)} collective-permute-done((bf16[1,768,128]{2,1,0:T(8,128)(2,1)S(1)}, bf16[1,768,128]{2,1,0:T(8,128)(2,1)S(1)}, u32[]{:S(2)}, u32[]{:S(2)}) %collective-permute-start.44) | collective-permute-done | bytes 196640 | tf_op jit(solution)/shard_map/ppermute | solution.py:782
  468.4 4.7 spread_down.1
  473.2 8.6 %collective-permute-done.50 = bf16[2,512,128]{2,1,0:T(8,128)(2,1)S(1)} collective-permute-done((bf16[2,512,128]{2,1,0:T(8,128)(2,1)S(1)}, bf16[2,512,128]{2,1,0:T(8,128)(2,1)S(1)}, u32[]{:S(2)}, u32[]{:S(2)}) %collective-permute-start.50) | collective-permute-done | bytes 262176 | tf_op jit(solution)/shard_map/ppermute | solution.py:782
  485.1 5.8 %head_spread.1 = (f32[512,1024]{1,0:T(8,128)}, f32[512,1024]{1,0:T(8,128)}, f32[512,1024]{1,0:T(8,128)}) custom-call(s32[16]{0:T(128)} %fusion.9.pos_ref, bf16[8,768,128]{2,1,0:T(8,128)(2,1)} %constant_dynamic-update-slice_fusion.low_ref, bf16[8,768,128]{2,1,0:T(8,128)(2,1)} %collective-permute-done.40.high_ref), custom_call_target="tpu_custom_call" | custom-call | flops 6899999744 | bytes 22140000 | tf_op jit(solution)/shard_map/head_spread/pallas_call | solution.py:1076
  493.8 3.5 all-to-all-start.3
  501.0 12.3 %collective-permute-done.46 = bf16[4,768,128]{2,1,0:T(8,128)(2,1)} collective-permute-done((bf16[4,768,128]{2,1,0:T(8,128)(2,1)}, bf16[4,768,128]{2,1,0:T(8,128)(2,1)}, u32[]{:S(2)}, u32[]{:S(2)}) %collective-permute-start.46) | collective-permute-done | bytes 786464 | tf_op jit(solution)/shard_map/ppermute | solution.py:782
  515.4 7.2 %spread_gate.1 = (f32[2,2,128,2816]{3,2,1,0:T(8,128)}, f32[2,2,128,2816]{3,2,1,0:T(8,128)}) custom-call(s32[4]{0:T(128)} %pad_add_fusion.1.where_ref, bf16[8,704,128]{2,1,0:T(8,128)(2,1)} %copy-done.1, bf16[8,704,128]{2,1,0:T(8,128)(2,1)} %collective-permute-done.58.high, bf16[8,704,128]{2,1,0:T(8,128)(2,1)} %pad_maximum_fusion.3.far_low, ...), custom_call_target="tpu_custom_call" | custom-call | flops 9200000000 | bytes 29520000 | tf_op jit(solution)/shard_map/spread_gate/pallas_call | solution.py:627
  524.7 5.4 encoder_grad.1
  530.1 4.4 cross_head_spread.1
  534.5 4.9 spread_token.1
  (337 shorter events, 130.0 us)
Async XLA Ops:
  7.2 101.5 %all-gather.3.cloned.1.call-start = ((), (), s32[]{:S(2)}) async-start(), calls=%async_computation.6 | async-start | bytes 2228224 | tf_op jit(solution)/shard_map/all_gather | solution.py:828
  7.3 21.0 %collective-permute-start = (bf16[2,64,1024]{2,1,0:T(8,128)(2,1)}, bf16[2,64,1024]{2,1,0:T(8,128)(2,1)}, u32[]{:S(2)}, u32[]{:S(2)}) collective-permute-start(bf16[2,64,1024]{2,1,0:T(8,128)(2,1)} %bitcast.91), channel_id=1, source_target_pairs={{0,16},{2,18},{4,20},{6,22},{8,24},{10,26},{12,28},{14,30},{16,0},... | collective-permute-start | bytes 786440 | tf_op jit(solution)/shard_map/ppermute | solution.py:782
  11.4 18.9 %collective-permute-start.1 = (bf16[2,64,1024]{2,1,0:T(8,128)(2,1)}, bf16[2,64,1024]{2,1,0:T(8,128)(2,1)}, u32[]{:S(2)}, u32[]{:S(2)}) collective-permute-start(bf16[2,64,1024]{2,1,0:T(8,128)(2,1)} %bitcast.92), channel_id=1, source_target_pairs={{0,8},{2,10},{4,12},{6,14},{8,0},{10,2},{12,4},{14,6},{16,24},{18,... | collective-permute-start | bytes 786440 | tf_op jit(solution)/shard_map/ppermute | solution.py:782
  12.9 31.1 %collective-permute-start.3 = (bf16[2,64,1024]{2,1,0:T(8,128)(2,1)}, bf16[2,64,1024]{2,1,0:T(8,128)(2,1)S(1)}, u32[]{:S(2)}, u32[]{:S(2)}) collective-permute-start(bf16[2,64,1024]{2,1,0:T(8,128)(2,1)} %bitcast.93), channel_id=1, source_target_pairs={{0,4},{2,6},{4,0},{6,2},{8,12},{10,14},{12,8},{14,10},{16,20},{18,... | collective-permute-start | bytes 786440 | tf_op jit(solution)/shard_map/ppermute | solution.py:782
  24.2 78.0 %collective-permute-start.11 = (bf16[5,256,1024]{2,1,0:T(8,128)(2,1)}, bf16[5,256,1024]{2,1,0:T(8,128)(2,1)}, u32[]{:S(2)}, u32[]{:S(2)}) collective-permute-start(bf16[5,256,1024]{2,1,0:T(8,128)(2,1)} %bitcast_dynamic-update-slice_fusion), channel_id=1, source_target_pairs={{0,1},{1,0},{2,3},{3,2},{4,5},{5,4},{6,7},{7,6},{8,9},{9,8},{10,11... | collective-permute-start | bytes 7864328 | tf_op jit(solution)/shard_map/ppermute | solution.py:785
  44.1 43.5 %collective-permute-start.10 = (bf16[512,192]{1,0:T(8,128)(2,1)}, bf16[512,192]{1,0:T(8,128)(2,1)}, u32[]{:S(2)}, u32[]{:S(2)}) collective-permute-start(bf16[512,192]{1,0:T(8,128)(2,1)} %pad_maximum_fusion.20), channel_id=1, source_target_pairs={{0,1},{1,0},{2,3},{3,2},{4,5},{5,4},{6,7},{7,6},{8,9},{9,8},{10,11... | collective-permute-start | bytes 589832 | tf_op jit(solution)/shard_map/ppermute | solution.py:785
  45.7 45.0 %collective-permute-start.7 = (bf16[4,2,64,1024]{3,2,1,0:T(8,128)(2,1)S(1)}, bf16[4,2,64,1024]{3,2,1,0:T(8,128)(2,1)}, u32[]{:S(2)}, u32[]{:S(2)}) collective-permute-start(bf16[4,2,64,1024]{3,2,1,0:T(8,128)(2,1)S(1)} %pad_maximum_fusion.5.refs_0_), channel_id=1, source_target_pairs={{0,2},{2,0},{4,6},{6,4},{8,10},{10,8},{12,14},{14,12},{16,18},{18,... | collective-permute-start | bytes 3145736 | tf_op jit(solution)/shard_map/ppermute | solution.py:782
  54.6 36.0 %collective-permute-start.9 = (bf16[4,2,64,1024]{3,2,1,0:T(8,128)(2,1)S(1)}, bf16[4,2,64,1024]{3,2,1,0:T(8,128)(2,1)}, u32[]{:S(2)}, u32[]{:S(2)}) collective-permute-start(bf16[4,2,64,1024]{3,2,1,0:T(8,128)(2,1)S(1)} %pad_maximum_fusion.6.refs_1_), channel_id=1, source_target_pairs={{0,2},{2,0},{4,6},{6,4},{8,10},{10,8},{12,14},{14,12},{16,18},{18,... | collective-permute-start | bytes 3145736 | tf_op jit(solution)/shard_map/ppermute | solution.py:782
  108.1 34.0 %collective-permute-start.13 = (bf16[2,256,1408]{2,1,0:T(8,128)(2,1)S(1)}, bf16[2,256,1408]{2,1,0:T(8,128)(2,1)}, u32[]{:S(2)}, u32[]{:S(2)}) collective-permute-start(bf16[2,256,1408]{2,1,0:T(8,128)(2,1)S(1)} %pad_maximum_fusion.1), channel_id=1, source_target_pairs={{0,1},{1,0},{2,3},{3,2},{4,5},{5,4},{6,7},{7,6},{8,9},{9,8},{10,11... | collective-permute-start | bytes 4325384 | tf_op jit(solution)/shard_map/ppermute | solution.py:785
  157.1 27.5 %collective-permute-start.18 = (bf16[128,5248]{1,0:T(8,128)(2,1)}, bf16[128,5248]{1,0:T(8,128)(2,1)}, u32[]{:S(2)}, u32[]{:S(2)}) collective-permute-start(bf16[128,5248]{1,0:T(8,128)(2,1)} %get-tuple-element.94.own0_ref), channel_id=1, source_target_pairs={{0,2},{2,0},{4,6},{6,4},{8,10},{10,8},{12,14},{14,12},{16,18},{18,... | collective-permute-start | bytes 4030472 | tf_op jit(solution)/shard_map/ppermute | solution.py:782
  191.9 32.0 %collective-permute-start.22 = (bf16[4,704,128]{2,1,0:T(8,128)(2,1)}, bf16[4,704,128]{2,1,0:T(8,128)(2,1)}, u32[]{:S(2)}, u32[]{:S(2)}) collective-permute-start(bf16[4,704,128]{2,1,0:T(8,128)(2,1)} %get-tuple-element.96), channel_id=1, source_target_pairs={{0,8},{2,10},{4,12},{6,14},{8,0},{10,2},{12,4},{14,6},{16,24},{18,... | collective-permute-start | bytes 2162696 | tf_op jit(solution)/shard_map/ppermute | solution.py:782
  193.4 26.7 %collective-permute-start.20 = (bf16[3,128,512]{2,1,0:T(8,128)(2,1)S(1)}, bf16[3,128,512]{2,1,0:T(8,128)(2,1)S(1)}, u32[]{:S(2)}, u32[]{:S(2)}) collective-permute-start(bf16[3,128,512]{2,1,0:T(8,128)(2,1)S(1)} %bitcast.89), channel_id=1, source_target_pairs={{0,1},{1,0},{2,3},{3,2},{4,5},{5,4},{6,7},{7,6},{8,9},{9,8},{10,11... | collective-permute-start | bytes 1179656 | tf_op jit(solution)/shard_map/ppermute | solution.py:785
  195.0 31.2 %collective-permute-start.23 = (bf16[4,704,128]{2,1,0:T(8,128)(2,1)}, bf16[4,704,128]{2,1,0:T(8,128)(2,1)S(1)}, u32[]{:S(2)}, u32[]{:S(2)}) collective-permute-start(bf16[4,704,128]{2,1,0:T(8,128)(2,1)} %get-tuple-element.103), channel_id=1, source_target_pairs={{0,4},{2,6},{4,0},{6,2},{8,12},{10,14},{12,8},{14,10},{16,20},{18,... | collective-permute-start | bytes 2162696 | tf_op jit(solution)/shard_map/ppermute | solution.py:782
  196.4 33.3 %collective-permute-start.24 = (bf16[4,704,128]{2,1,0:T(8,128)(2,1)}, bf16[4,704,128]{2,1,0:T(8,128)(2,1)}, u32[]{:S(2)}, u32[]{:S(2)}) collective-permute-start(bf16[4,704,128]{2,1,0:T(8,128)(2,1)} %get-tuple-element.104), channel_id=1, source_target_pairs={{0,1},{1,0},{2,3},{3,2},{4,5},{5,4},{6,7},{7,6},{8,9},{9,8},{10,11... | collective-permute-start | bytes 2162696 | tf_op jit(solution)/shard_map/ppermute | solution.py:785
  219.7 223.2 %reduce-scatter.2.cloned.1.call-start = ((), (), s32[]{:S(2)}) async-start(), calls=%async_computation.5 | async-start | bytes 4456448 | tf_op jit(solution)/shard_map/reduce_scatter | solution.py:1107
  221.5 20.0 %collective-permute-start.25 = (bf16[128,3072]{1,0:T(8,128)(2,1)}, bf16[128,3072]{1,0:T(8,128)(2,1)}, u32[]{:S(2)}, u32[]{:S(2)}) collective-permute-start(bf16[128,3072]{1,0:T(8,128)(2,1)} %get-tuple-element.107.r0_ref), channel_id=1, source_target_pairs={{0,1},{1,0},{2,3},{3,2},{4,5},{5,4},{6,7},{7,6},{8,9},{9,8},{10,11... | collective-permute-start | bytes 2359304 | tf_op jit(solution)/shard_map/ppermute | solution.py:785
  224.0 90.6 %collective-permute-start.27 = (bf16[128,3072]{1,0:T(8,128)(2,1)}, bf16[128,3072]{1,0:T(8,128)(2,1)}, u32[]{:S(2)}, u32[]{:S(2)}) collective-permute-start(bf16[128,3072]{1,0:T(8,128)(2,1)} %get-tuple-element.107.r0_ref), channel_id=1, source_target_pairs={{0,2},{2,0},{4,6},{6,4},{8,10},{10,8},{12,14},{14,12},{16,18},{18,... | collective-permute-start | bytes 2359304 | tf_op jit(solution)/shard_map/ppermute | solution.py:782
  226.2 34.1 %collective-permute-start.53 = (bf16[2,704,128]{2,1,0:T(8,128)(2,1)}, bf16[2,704,128]{2,1,0:T(8,128)(2,1)}, u32[]{:S(2)}, u32[]{:S(2)}) collective-permute-start(bf16[2,704,128]{2,1,0:T(8,128)(2,1)} %slice.189), channel_id=1, source_target_pairs={{0,16},{2,18},{4,20},{6,22},{8,24},{10,26},{12,28},{14,30},{16,0},... | collective-permute-start | bytes 1081352 | tf_op jit(solution)/shard_map/ppermute | solution.py:782
  251.1 24.4 %collective-permute-start.67 = (bf16[2,704,128]{2,1,0:T(8,128)(2,1)}, bf16[2,704,128]{2,1,0:T(8,128)(2,1)}, u32[]{:S(2)}, u32[]{:S(2)}) collective-permute-start(bf16[2,704,128]{2,1,0:T(8,128)(2,1)} %slice.187), channel_id=1, source_target_pairs={{0,8},{2,10},{4,12},{6,14},{8,0},{10,2},{12,4},{14,6},{16,24},{18,... | collective-permute-start | bytes 1081352 | tf_op jit(solution)/shard_map/ppermute | solution.py:782
  252.8 72.1 %collective-permute-start.60 = (bf16[4,704,128]{2,1,0:T(8,128)(2,1)}, bf16[4,704,128]{2,1,0:T(8,128)(2,1)}, u32[]{:S(2)}, u32[]{:S(2)}) collective-permute-start(bf16[4,704,128]{2,1,0:T(8,128)(2,1)} %collective-permute-done.24), channel_id=1, source_target_pairs={{0,4},{2,6},{4,0},{6,2},{8,12},{10,14},{12,8},{14,10},{16,20},{18,... | collective-permute-start | bytes 2162696 | tf_op jit(solution)/shard_map/ppermute | solution.py:782
  254.3 175.7 %all-to-all-start.2 = ((bf16[16,64,384]{2,1,0:T(8,128)(2,1)}), bf16[16,64,384]{2,1,0:T(8,128)(2,1)}, u32[]{:S(2)}, u32[]{:S(2)}) async-start(bf16[16,64,384]{2,1,0:T(8,128)(2,1)} %bitcast.88), calls=%async_computation.2 | async-start | bytes 1572864 | tf_op jit(solution)/shard_map/all_to_all | solution.py:1091
  258.8 66.2 %collective-permute-start.59 = (bf16[4,704,128]{2,1,0:T(8,128)(2,1)}, bf16[4,704,128]{2,1,0:T(8,128)(2,1)S(1)}, u32[]{:S(2)}, u32[]{:S(2)}) collective-permute-start(bf16[4,704,128]{2,1,0:T(8,128)(2,1)} %get-tuple-element.132), channel_id=1, source_target_pairs={{0,1},{1,0},{2,3},{3,2},{4,5},{5,4},{6,7},{7,6},{8,9},{9,8},{10,11... | collective-permute-start | bytes 2162696 | tf_op jit(solution)/shard_map/ppermute | solution.py:785
  260.3 57.2 %collective-permute-start.28 = (bf16[128,3072]{1,0:T(8,128)(2,1)}, bf16[128,3072]{1,0:T(8,128)(2,1)S(1)}, u32[]{:S(2)}, u32[]{:S(2)}) collective-permute-start(bf16[128,3072]{1,0:T(8,128)(2,1)} %collective-permute-done.25.r1_ref), channel_id=1, source_target_pairs={{0,2},{2,0},{4,6},{6,4},{8,10},{10,8},{12,14},{14,12},{16,18},{18,... | collective-permute-start | bytes 2359304 | tf_op jit(solution)/shard_map/ppermute | solution.py:782
  275.5 18.1 %collective-permute-start.54 = (bf16[1,704,128]{2,1,0:T(8,128)(2,1)S(1)}, bf16[1,704,128]{2,1,0:T(8,128)(2,1)S(1)}, u32[]{:S(2)}, u32[]{:S(2)}) collective-permute-start(bf16[1,704,128]{2,1,0:T(8,128)(2,1)S(1)} %slice.193), channel_id=1, source_target_pairs={{0,4},{2,6},{4,0},{6,2},{8,12},{10,14},{12,8},{14,10},{16,20},{18,... | collective-permute-start | bytes 540680 | tf_op jit(solution)/shard_map/ppermute | solution.py:782
  314.5 20.1 %collective-permute-start.69 = (bf16[1,704,128]{2,1,0:T(8,128)(2,1)S(1)}, bf16[1,704,128]{2,1,0:T(8,128)(2,1)S(1)}, u32[]{:S(2)}, u32[]{:S(2)}) collective-permute-start(bf16[1,704,128]{2,1,0:T(8,128)(2,1)S(1)} %fusion.3), channel_id=1, source_target_pairs={{0,16},{2,18},{4,20},{6,22},{8,24},{10,26},{12,28},{14,30},{16,0},... | collective-permute-start | bytes 540680 | tf_op jit(solution)/shard_map/ppermute | solution.py:782
  314.5 48.5 %collective-permute-start.56 = (bf16[2,704,128]{2,1,0:T(8,128)(2,1)S(1)}, bf16[2,704,128]{2,1,0:T(8,128)(2,1)S(1)}, u32[]{:S(2)}, u32[]{:S(2)}) collective-permute-start(bf16[2,704,128]{2,1,0:T(8,128)(2,1)S(1)} %pad_maximum_fusion.17), channel_id=1, source_target_pairs={{0,16},{2,18},{4,20},{6,22},{8,24},{10,26},{12,28},{14,30},{16,0},... | collective-permute-start | bytes 1081352 | tf_op jit(solution)/shard_map/ppermute | solution.py:782
  323.5 54.9 %collective-permute-start.29 = (bf16[3,256,1024]{2,1,0:T(8,128)(2,1)S(1)}, bf16[3,256,1024]{2,1,0:T(8,128)(2,1)S(1)}, u32[]{:S(2)}, u32[]{:S(2)}) collective-permute-start(bf16[3,256,1024]{2,1,0:T(8,128)(2,1)S(1)} %copy-done), channel_id=1, source_target_pairs={{0,1},{1,0},{2,3},{3,2},{4,5},{5,4},{6,7},{7,6},{8,9},{9,8},{10,11... | collective-permute-start | bytes 4718600 | tf_op jit(solution)/shard_map/ppermute | solution.py:785
  326.3 25.8 %collective-permute-start.61 = (bf16[2,704,128]{2,1,0:T(8,128)(2,1)S(1)}, bf16[2,704,128]{2,1,0:T(8,128)(2,1)S(1)}, u32[]{:S(2)}, u32[]{:S(2)}) collective-permute-start(bf16[2,704,128]{2,1,0:T(8,128)(2,1)S(1)} %slice.188), channel_id=1, source_target_pairs={{0,8},{2,10},{4,12},{6,14},{8,0},{10,2},{12,4},{14,6},{16,24},{18,... | collective-permute-start | bytes 1081352 | tf_op jit(solution)/shard_map/ppermute | solution.py:782
  326.3 24.3 %collective-permute-start.37 = (bf16[1,768,128]{2,1,0:T(8,128)(2,1)S(1)}, bf16[1,768,128]{2,1,0:T(8,128)(2,1)S(1)}, u32[]{:S(2)}, u32[]{:S(2)}) collective-permute-start(bf16[1,768,128]{2,1,0:T(8,128)(2,1)S(1)} %add_convert_fusion.1), channel_id=1, source_target_pairs={{0,16},{2,18},{4,20},{6,22},{8,24},{10,26},{12,28},{14,30},{16,0},... | collective-permute-start | bytes 589832 | tf_op jit(solution)/shard_map/ppermute | solution.py:782
  334.7 26.9 %collective-permute-start.70 = (bf16[2,704,128]{2,1,0:T(8,128)(2,1)S(1)}, bf16[2,704,128]{2,1,0:T(8,128)(2,1)S(1)}, u32[]{:S(2)}, u32[]{:S(2)}) collective-permute-start(bf16[2,704,128]{2,1,0:T(8,128)(2,1)S(1)} %pad_maximum_fusion.19), channel_id=1, source_target_pairs={{0,8},{2,10},{4,12},{6,14},{8,0},{10,2},{12,4},{14,6},{16,24},{18,... | collective-permute-start | bytes 1081352 | tf_op jit(solution)/shard_map/ppermute | solution.py:782
  350.6 25.6 %collective-permute-start.41 = (bf16[4,768,128]{2,1,0:T(8,128)(2,1)S(1)}, bf16[4,768,128]{2,1,0:T(8,128)(2,1)S(1)}, u32[]{:S(2)}, u32[]{:S(2)}) collective-permute-start(bf16[4,768,128]{2,1,0:T(8,128)(2,1)S(1)} %copy-done.37), channel_id=1, source_target_pairs={{0,4},{2,6},{4,0},{6,2},{8,12},{10,14},{12,8},{14,10},{16,20},{18,... | collective-permute-start | bytes 2359304 | tf_op jit(solution)/shard_map/ppermute | solution.py:782
  361.7 24.9 %collective-permute-start.71 = (bf16[4,704,128]{2,1,0:T(8,128)(2,1)S(1)}, bf16[4,704,128]{2,1,0:T(8,128)(2,1)S(1)}, u32[]{:S(2)}, u32[]{:S(2)}) collective-permute-start(bf16[4,704,128]{2,1,0:T(8,128)(2,1)S(1)} %pad_maximum_fusion.13), channel_id=1, source_target_pairs={{0,4},{2,6},{4,0},{6,2},{8,12},{10,14},{12,8},{14,10},{16,20},{18,... | collective-permute-start | bytes 2162696 | tf_op jit(solution)/shard_map/ppermute | solution.py:782
  376.0 30.2 %collective-permute-start.57 = (bf16[4,704,128]{2,1,0:T(8,128)(2,1)S(1)}, bf16[4,704,128]{2,1,0:T(8,128)(2,1)S(1)}, u32[]{:S(2)}, u32[]{:S(2)}) collective-permute-start(bf16[4,704,128]{2,1,0:T(8,128)(2,1)S(1)} %pad_maximum_fusion.11), channel_id=1, source_target_pairs={{0,8},{2,10},{4,12},{6,14},{8,0},{10,2},{12,4},{14,6},{16,24},{18,... | collective-permute-start | bytes 2162696 | tf_op jit(solution)/shard_map/ppermute | solution.py:782
  376.1 31.2 %collective-permute-start.39 = (bf16[4,768,128]{2,1,0:T(8,128)(2,1)S(1)}, bf16[4,768,128]{2,1,0:T(8,128)(2,1)S(1)}, u32[]{:S(2)}, u32[]{:S(2)}) collective-permute-start(bf16[4,768,128]{2,1,0:T(8,128)(2,1)S(1)} %pad_maximum_fusion.9), channel_id=1, source_target_pairs={{0,4},{2,6},{4,0},{6,2},{8,12},{10,14},{12,8},{14,10},{16,20},{18,... | collective-permute-start | bytes 2359304 | tf_op jit(solution)/shard_map/ppermute | solution.py:782
  376.3 24.3 %collective-permute-start.64 = (bf16[2,704,128]{2,1,0:T(8,128)(2,1)S(1)}, bf16[2,704,128]{2,1,0:T(8,128)(2,1)S(1)}, u32[]{:S(2)}, u32[]{:S(2)}) collective-permute-start(bf16[2,704,128]{2,1,0:T(8,128)(2,1)S(1)} %pad_maximum_fusion.18), channel_id=1, source_target_pairs={{0,8},{2,10},{4,12},{6,14},{8,0},{10,2},{12,4},{14,6},{16,24},{18,... | collective-permute-start | bytes 1081352 | tf_op jit(solution)/shard_map/ppermute | solution.py:782
  378.4 42.1 %collective-permute-start.31 = (bf16[3,256,1024]{2,1,0:T(8,128)(2,1)S(1)}, bf16[3,256,1024]{2,1,0:T(8,128)(2,1)S(1)}, u32[]{:S(2)}, u32[]{:S(2)}) collective-permute-start(bf16[3,256,1024]{2,1,0:T(8,128)(2,1)S(1)} %collective-permute-done.29.refs_0_), channel_id=1, source_target_pairs={{0,2},{2,0},{4,6},{6,4},{8,10},{10,8},{12,14},{14,12},{16,18},{18,... | collective-permute-start | bytes 4718600 | tf_op jit(solution)/shard_map/ppermute | solution.py:782
  386.5 18.3 %collective-permute-start.42 = (bf16[2,768,128]{2,1,0:T(8,128)(2,1)S(1)}, bf16[2,768,128]{2,1,0:T(8,128)(2,1)S(1)}, u32[]{:S(2)}, u32[]{:S(2)}) collective-permute-start(bf16[2,768,128]{2,1,0:T(8,128)(2,1)S(1)} %slice.186), channel_id=1, source_target_pairs={{0,8},{2,10},{4,12},{6,14},{8,0},{10,2},{12,4},{14,6},{16,24},{18,... | collective-permute-start | bytes 1179656 | tf_op jit(solution)/shard_map/ppermute | solution.py:782
  400.6 65.7 %collective-permute-start.72 = (bf16[8,704,128]{2,1,0:T(8,128)(2,1)}, bf16[8,704,128]{2,1,0:T(8,128)(2,1)}, u32[]{:S(2)}, u32[]{:S(2)}) collective-permute-start(bf16[8,704,128]{2,1,0:T(8,128)(2,1)} %pad_maximum_fusion.4.low), channel_id=1, source_target_pairs={{0,2},{2,0},{4,6},{6,4},{8,10},{10,8},{12,14},{14,12},{16,18},{18,... | collective-permute-start | bytes 4325384 | tf_op jit(solution)/shard_map/ppermute | solution.py:782
  408.3 74.9 %collective-permute-start.40 = (bf16[8,768,128]{2,1,0:T(8,128)(2,1)}, bf16[8,768,128]{2,1,0:T(8,128)(2,1)}, u32[]{:S(2)}, u32[]{:S(2)}) collective-permute-start(bf16[8,768,128]{2,1,0:T(8,128)(2,1)} %constant_dynamic-update-slice_fusion.low_ref), channel_id=1, source_target_pairs={{0,2},{2,0},{4,6},{6,4},{8,10},{10,8},{12,14},{14,12},{16,18},{18,... | collective-permute-start | bytes 4718600 | tf_op jit(solution)/shard_map/ppermute | solution.py:782
  415.1 37.8 %collective-permute-start.30 = (bf16[128,1024]{1,0:T(8,128)(2,1)S(1)}, bf16[128,1024]{1,0:T(8,128)(2,1)S(1)}, u32[]{:S(2)}, u32[]{:S(2)}) collective-permute-start(bf16[128,1024]{1,0:T(8,128)(2,1)S(1)} %copy-done.40), channel_id=1, source_target_pairs={{0,1},{1,0},{2,3},{3,2},{4,5},{5,4},{6,7},{7,6},{8,9},{9,8},{10,11... | collective-permute-start | bytes 786440 | tf_op jit(solution)/shard_map/ppermute | solution.py:785
  456.8 58.6 %collective-permute-start.58 = (bf16[8,704,128]{2,1,0:T(8,128)(2,1)S(1)}, bf16[8,704,128]{2,1,0:T(8,128)(2,1)}, u32[]{:S(2)}, u32[]{:S(2)}) collective-permute-start(bf16[8,704,128]{2,1,0:T(8,128)(2,1)S(1)} %pad_maximum_fusion.2.low), channel_id=1, source_target_pairs={{0,2},{2,0},{4,6},{6,4},{8,10},{10,8},{12,14},{14,12},{16,18},{18,... | collective-permute-start | bytes 4325384 | tf_op jit(solution)/shard_map/ppermute | solution.py:782
  473.1 42.2 %collective-permute-start.66 = (bf16[8,704,128]{2,1,0:T(8,128)(2,1)}, bf16[8,704,128]{2,1,0:T(8,128)(2,1)}, u32[]{:S(2)}, u32[]{:S(2)}) collective-permute-start(bf16[8,704,128]{2,1,0:T(8,128)(2,1)} %pad_maximum_fusion.3.far_low), channel_id=1, source_target_pairs={{0,2},{2,0},{4,6},{6,4},{8,10},{10,8},{12,14},{14,12},{16,18},{18,... | collective-permute-start | bytes 4325384 | tf_op jit(solution)/shard_map/ppermute | solution.py:782
  482.1 17.4 %collective-permute-start.51 = (bf16[4,512,128]{2,1,0:T(8,128)(2,1)S(1)}, bf16[4,512,128]{2,1,0:T(8,128)(2,1)}, u32[]{:S(2)}, u32[]{:S(2)}) collective-permute-start(bf16[4,512,128]{2,1,0:T(8,128)(2,1)S(1)} %pad_maximum_fusion.14), channel_id=1, source_target_pairs={{0,4},{2,6},{4,0},{6,2},{8,12},{10,14},{12,8},{14,10},{16,20},{18,... | collective-permute-start | bytes 1572872 | tf_op jit(solution)/shard_map/ppermute | solution.py:782
  483.1 30.2 %collective-permute-start.46 = (bf16[4,768,128]{2,1,0:T(8,128)(2,1)}, bf16[4,768,128]{2,1,0:T(8,128)(2,1)}, u32[]{:S(2)}, u32[]{:S(2)}) collective-permute-start(bf16[4,768,128]{2,1,0:T(8,128)(2,1)} %pad_maximum_fusion.10), channel_id=1, source_target_pairs={{0,4},{2,6},{4,0},{6,2},{8,12},{10,14},{12,8},{14,10},{16,20},{18,... | collective-permute-start | bytes 2359304 | tf_op jit(solution)/shard_map/ppermute | solution.py:782
  490.9 31.6 %collective-permute-start.36 = (f32[4,1024]{1,0:T(4,128)S(1)}, f32[4,1024]{1,0:T(4,128)S(1)}, u32[]{:S(2)}, u32[]{:S(2)}) collective-permute-start(f32[4,1024]{1,0:T(4,128)S(1)} %add.214), channel_id=1, source_target_pairs={{0,16},{2,18},{4,20},{6,22},{8,24},{10,26},{12,28},{14,30},{16,0},... | collective-permute-start | bytes 49160 | tf_op jit(solution)/shard_map/ppermute | solution.py:782
  493.8 30.2 %all-to-all-start.3 = ((bf16[16,64,128]{2,1,0:T(8,128)(2,1)}), bf16[16,64,128]{2,1,0:T(8,128)(2,1)S(1)}, u32[]{:S(2)}, u32[]{:S(2)}) async-start(bf16[16,64,128]{2,1,0:T(8,128)(2,1)} %bitcast.48), calls=%async_computation.4 | async-start | bytes 524288 | tf_op jit(solution)/shard_map/all_to_all | solution.py:1135
  500.7 29.4 %collective-permute-start.52 = (bf16[8,512,128]{2,1,0:T(8,128)(2,1)S(1)}, bf16[8,512,128]{2,1,0:T(8,128)(2,1)}, u32[]{:S(2)}, u32[]{:S(2)}) collective-permute-start(bf16[8,512,128]{2,1,0:T(8,128)(2,1)S(1)} %pad_maximum_fusion.7.low_ref), channel_id=1, source_target_pairs={{0,2},{2,0},{4,6},{6,4},{8,10},{10,8},{12,14},{14,12},{16,18},{18,... | collective-permute-start | bytes 3145736 | tf_op jit(solution)/shard_map/ppermute | solution.py:782
  515.4 19.1 %collective-permute-start.47 = (bf16[8,768,128]{2,1,0:T(8,128)(2,1)}, bf16[8,768,128]{2,1,0:T(8,128)(2,1)}, u32[]{:S(2)}, u32[]{:S(2)}) collective-permute-start(bf16[8,768,128]{2,1,0:T(8,128)(2,1)} %constant_dynamic-update-slice_fusion.4.low), channel_id=1, source_target_pairs={{0,2},{2,0},{4,6},{6,4},{8,10},{10,8},{12,14},{14,12},{16,18},{18,... | collective-permute-start | bytes 4718600 | tf_op jit(solution)/shard_map/ppermute | solution.py:782
  (77 other events, 819.9 us)
Sparse Core Ops, SparseCore 0:
  19.0 40.7 all-gather.2
  225.0 108.6 reduce-scatter.1

commit v3 on v2

--- a/solution.py
+++ b/solution.py
@@ -345,13 +345,14 @@
 
 
 def mid_backward_kernel(
-    split, starts_ref, g_ref, dn3_ref, more_ref, x1_ref, x2_ref, gain_ref, q2_ref, ke_ref, ve_ref,
+    split, starts_ref, slots_ref, g_ref, dn3_ref, more_ref, x1_ref, x2_ref, gain_ref, q2_ref, ke_ref, ve_ref,
     wo, wq, wc, *refs
 ):
     more = refs[:split]
-    right_ref, gx1_ref, do1_ref, dkv_ref, dc_ref, back_ref, do2_ref, dq2_ref = refs[split:]
+    right_ref, gx1_ref, do1_ref, keep_ref, send_ref, dc_ref, back_ref, do2_ref, dq2_ref = refs[split:]
     heads, rows, _ = do1_ref.shape
-    blocks, micros, part = dkv_ref.shape[1:4]
+    blocks, micros, part = keep_ref.shape[1:4]
+    even = slots_ref[heads // 2] == 0
     width = x1_ref.shape[-1]
     dn3 = dn3_ref[...] + more_ref[...].astype(F32)
     back, dc = norm_back(x2_ref[...], gain_ref[2:3], dn3)
@@ -379,8 +380,10 @@
                 low_lanes(rows), dq[:rows], dq[rows:]
             ).astype(BF16)
             low, high = pair_up(t_dot(ds, q), t_dot(p.astype(BF16), do))
-            dkv_ref[2 * pair, :, micro] = low.astype(BF16).reshape(blocks, part, 128)
-            dkv_ref[2 * pair + 1, :, micro] = high.astype(BF16).reshape(blocks, part, 128)
+            kept, sent = jnp.where(even, low, high), jnp.where(even, high, low)
+            slot = slots_ref[pair]
+            keep_ref[slot, :, micro] = kept.astype(BF16).reshape(blocks, part, 128)
+            send_ref[slot, :, micro] = sent.astype(BF16).reshape(blocks, part, 128)
     right_ref[:, width : 2 * width] = dq2_ref[...]
     times_back(back_ref, starts_ref, [(dq2_ref[...], pieces_of(wq, more, 1))])
     back, dc = norm_back(x1_ref[...], gain_ref[1:2], back_ref[...])
@@ -528,24 +531,23 @@
     )
 
 
-def put_all(scratch_ref, value, chip, chunk_refs, at):
-    count = 2 * chunk_refs[0].shape[0]
-    rows = value.shape[0] // count
-    scratch_ref[: value.shape[0], : value.shape[1]] = value
-    for r in range(count):
-        chunk = scratch_ref[aligned((chip ^ r) * rows, rows), : value.shape[1]]
-        put_chunk(chunk_refs[r // (count // 2)], r % (count // 2), at, chunk)
+def put_all(scratch_ref, first, count, chip, chunk_refs, at, width, masks):
+    slots = [(ref, slot) for ref in chunk_refs for slot in range(ref.shape[0])]
+    rows = count // len(slots)
+    for (ref, slot), mask in zip(slots, masks):
+        chunk = scratch_ref[aligned(first + (chip ^ mask) * rows, rows), :width]
+        put_chunk(ref, slot, at, chunk)
 
 
 def dense_weight_kernel(
-    where_ref, n0_ref, n1_ref, g0_ref, g1_ref, own0_ref, own1_ref, mate0_ref, mate1_ref, keep_ref,
+    x_masks, z_masks, where_ref, n0_ref, n1_ref, g0_ref, g1_ref, own0_ref, own1_ref, mate0_ref, mate1_ref, keep_ref,
     send_ref, down_keep_ref, down_send_ref, far_keep_ref, far_send_ref, scratch_ref, left_ref
 ):
     tokens, width = n0_ref.shape
     hidden = (own0_ref.shape[1] - width) // 3
     quarter = width // 4
     at = keep_ref.shape[1] // 2
-    x_chip, core, shard, z_chip = where_ref[0], where_ref[1], where_ref[2], where_ref[3]
+    core, shard, chip = where_ref[1], where_ref[2], where_ref[3]
     put_features(left_ref.at[:tokens], 0, n0_ref, g0_ref, shard, core)
     put_features(left_ref.at[tokens : 2 * tokens], 0, n1_ref, g1_ref, shard, core)
     left_ref[2 * tokens : 3 * tokens, :] = mate0_ref[:, 3 * hidden :]
@@ -558,37 +560,40 @@
 
     for kind in range(2):
         right = whole(kind)
-        for side, (chip, refs) in enumerate(
-            ((z_chip, (keep_ref, send_ref)), (x_chip, (far_keep_ref, far_send_ref)))
+        for side, (masks, refs) in enumerate(
+            ((z_masks, (keep_ref, send_ref)), (x_masks, (far_keep_ref, far_send_ref)))
         ):
             value = t_dot(left_ref[:, side * quarter : (side + 1) * quarter], right)
-            put_all(scratch_ref, value, chip, refs, kind * at)
+            scratch_ref[:quarter, :hidden] = value
+            put_all(scratch_ref, 0, quarter, chip, refs, kind * at, hidden, masks)
     value = t_dot(whole(2), left_ref[:, 2 * quarter :])
-    put_all(scratch_ref, value, x_chip, (down_keep_ref, down_send_ref), 0)
+    scratch_ref[:, : 2 * quarter] = value
+    refs = (down_keep_ref, down_send_ref)
+    put_all(scratch_ref, 0, hidden, chip, refs, 0, 2 * quarter, x_masks)
 
 
 def token_weight_kernel(
-    where_ref, left_ref, left_mate_ref, r0_ref, r1_ref, r2_ref, r3_ref, keep_ref, send_ref,
-    scratch_ref
+    where_ref, left_ref, left_more_ref, right_ref, right_more_ref, mine_ref, mate_ref, scratch_ref
 ):
-    width = r0_ref.shape[1] // 3
-    tokens = r0_ref.shape[0]
-    half = left_ref.shape[1] // 3
-    rows = half // (2 * keep_ref.shape[0])
-    for kind in range(3):
-        span = slice(kind * width, (kind + 1) * width)
-        lanes = slice(kind * half, (kind + 1) * half)
-        value = t_dot(left_ref[:tokens, lanes], r0_ref[:, span])
-        value = value + t_dot(left_ref[tokens:, lanes], r1_ref[:, span])
-        value = value + t_dot(left_mate_ref[:tokens, lanes], r2_ref[:, span])
-        value = value + t_dot(left_mate_ref[tokens:, lanes], r3_ref[:, span])
-        put_all(scratch_ref, value, where_ref[0], (keep_ref, send_ref), kind * rows * width // 128)
-
-
-def chunk_weights(kernel, where, operands, counts, chips, scratches, length, name):
+    kinds, _, span = left_more_ref.shape
+    width = right_ref.shape[1] // kinds
+    chip, core, shard = where_ref[0], where_ref[1], where_ref[2]
+    half = span // 2
+    masks = range(mine_ref.shape[0])
+    at = half // len(masks) * width // 128
+    for kind in range(kinds):
+        lanes = slice(kind * width, (kind + 1) * width)
+        left = [left_ref[kind, :, aligned(shard * span, span)], left_more_ref[kind]]
+        right = [right_ref[:, lanes], right_more_ref[:, lanes]]
+        scratch_ref[...] = t_dot(jnp.concatenate(left, axis=0), jnp.concatenate(right, axis=0))
+        for ref, own in ((mine_ref, core), (mate_ref, 1 - core)):
+            put_all(scratch_ref, own * half, half, chip, (ref,), kind * at, width, masks)
+
+
+def chunk_weights(kernel, where, operands, counts, slots, scratches, length, name):
     shapes = []
     for count in counts:
-        shapes += [jax.ShapeDtypeStruct((chips // 2, count, 128), BF16)] * 2
+        shapes += [jax.ShapeDtypeStruct((slots, count, 128), BF16)] * 2
     return pl.pallas_call(
         kernel,
         out_shape=shapes,
@@ -601,74 +606,45 @@
     )(where, *operands)
 
 
-def spread_gate_kernel(where_ref, low, high, far_low, far_high, out_ref, other_ref):
-    x_chip, core, shard, z_chip = where_ref[0], where_ref[1], where_ref[2], where_ref[3]
-    rows = out_ref.shape[2] // low.shape[0]
-    hidden = out_ref.shape[3] // 2
+def spread_dense_kernel(where_ref, in_ref, gate_ref, up_ref, down_ref):
+    shard = where_ref[2]
+    hidden = gate_ref.shape[3] // 2
+    rows = gate_ref.shape[2] // 2
     at = rows * hidden // 128
-    count = low.shape[0]
-    for side, (chip, refs) in enumerate(((z_chip, (low, high)), (x_chip, (far_low, far_high)))):
-        for cores, ref in enumerate(refs):
-            for r in range(count):
-                place = aligned(((chip ^ r) % count) * rows, rows)
-                lanes = aligned((shard ^ side) * hidden, hidden)
-                out_ref[core ^ cores, 0, place, lanes] = take_chunk(ref, r, 0, rows, hidden)
-                other_ref[core ^ cores, 0, place, lanes] = take_chunk(ref, r, at, rows, hidden)
-
-
-def spread_gate(where, low, high, far_low, far_high, hidden, span):
-    chips, total, _ = low.shape
-    count = chips // 2
-    rows = span // (2 * chips)
-    into = lambda at: pl.BlockSpec(
-        (count, total, 128), lambda b, where: (b ^ (where[at] // count), 0, 0)
-    )
-    out = pl.BlockSpec((2, 1, count * rows, 2 * hidden), lambda b, where: (0, b, 0, 0))
+    tall = down_ref.shape[0] // 2
+    half = down_ref.shape[1] // 2
+    for piece in range(4):
+        chip, core = piece // 2, piece % 2
+        place = slice(chip * rows, (chip + 1) * rows)
+        for side, start in enumerate((0, 4 * at)):
+            lanes = aligned((shard ^ side) * hidden, hidden)
+            for kind, out_ref in enumerate((gate_ref, up_ref)):
+                chunk = take_chunk(in_ref, piece, start + kind * at, rows, hidden)
+                out_ref[core, 0, place, lanes] = chunk
+        chunk = take_chunk(in_ref, piece, 2 * at, tall, half)
+        down_ref[chip * tall : (chip + 1) * tall, core * half : (core + 1) * half] = chunk
+
+
+def spread_dense(where, pieces, hidden, span, width):
+    count, total, _ = pieces.shape
+    steps = count // 4
+    rows = span // count
+    out = pl.BlockSpec((2, 1, 2 * rows, 2 * hidden), lambda q, where: (0, q, 0, 0))
     made = pl.pallas_call(
-        spread_gate_kernel,
+        spread_dense_kernel,
         grid_spec=pltpu.PrefetchScalarGridSpec(
             num_scalar_prefetch=1,
-            grid=(2,),
-            in_specs=[into(3), into(3), into(0), into(0)],
-            out_specs=[out, out],
+            grid=(steps,),
+            in_specs=[pl.BlockSpec((4, total, 128), lambda q, where: (q, 0, 0))],
+            out_specs=[out, out, pl.BlockSpec((hidden // steps, width), lambda q, where: (q, 0))],
         ),
-        out_shape=[jax.ShapeDtypeStruct((2, 2, count * rows, 2 * hidden), F32)] * 2,
-        compiler_params=params(),
-        cost_estimate=cost(8),
-        name="spread_gate",
-    )(where, low, high, far_low, far_high)
-    return [array.reshape(span, 2 * hidden) for array in made]
-
-
-def spread_down_kernel(where_ref, low, high, out_ref):
-    chip, core = where_ref[0], where_ref[1]
-    count = low.shape[0]
-    rows = out_ref.shape[0] // count
-    width = out_ref.shape[1] // 2
-    for cores, ref in enumerate((low, high)):
-        for r in range(count):
-            place = aligned(((chip ^ r) % count) * rows, rows)
-            lanes = aligned((core ^ cores) * width, width)
-            out_ref[place, lanes] = take_chunk(ref, r, 0, rows, width)
-
-
-def spread_down(where, low, high, hidden, width):
-    chips, total, _ = low.shape
-    count = chips // 2
-    into = pl.BlockSpec((count, total, 128), lambda b, where: (b ^ (where[0] // count), 0, 0))
-    return pl.pallas_call(
-        spread_down_kernel,
-        grid_spec=pltpu.PrefetchScalarGridSpec(
-            num_scalar_prefetch=1,
-            grid=(2,),
-            in_specs=[into] * 2,
-            out_specs=pl.BlockSpec((hidden // 2, width), lambda b, where: (b, 0)),
-        ),
-        out_shape=jax.ShapeDtypeStruct((hidden, width), F32),
-        compiler_params=params(),
-        cost_estimate=cost(5),
-        name="spread_down",
-    )(where, low, high)
+        out_shape=[jax.ShapeDtypeStruct((2, steps, 2 * rows, 2 * hidden), F32)] * 2
+        + [jax.ShapeDtypeStruct((hidden, width), F32)],
+        compiler_params=params(),
+        cost_estimate=cost(10),
+        name="spread_dense",
+    )(where, pieces)
+    return made[0].reshape(span, 2 * hidden), made[1].reshape(span, 2 * hidden), made[2]
 
 
 def spread_token_kernel(where_ref, low, high, *out_refs):
@@ -802,11 +778,13 @@
             return jnp.concatenate([values, swap_fs(values)], axis=0)
         return lax.all_gather(values, "fsdp", axis=0, tiled=True)
 
-    def reduce_chips(kept, got, order=x_order):
+    def reduce_chips(kept, got, order=x_order, marks=()):
         total = kept.astype(F32) + got.astype(F32)
-        for bit in order[1:]:
+        for place, bit in enumerate(order[1:]):
             count = total.shape[0] // 2
             sent, total = total[count:].astype(BF16), total[:count]
+            if place < len(marks):
+                sent = after(sent, marks[place])
             total = total + swap_dp(sent, bit).astype(F32)
         return total.astype(BF16)
 
@@ -853,7 +831,7 @@
         starts = starts.astype(jnp.int32)
         kv_own = (key_cross, value_cross)
         near_own = (output_self, query_cross, output_cross)
-        near_got = swap_fs(half_rows(near_own + kv_own))
+        near_got = swap_fs(after(half_rows(near_own + kv_own), small_got, head_got))
         theirs = jnp.stack(
             [
                 lax.dynamic_slice(w, (core * half, (1 - shard) * hidden), (half, hidden))
@@ -931,13 +909,15 @@
         g_rows = g.reshape(tokens, width)
         g_got = swap_fs(after(g_rows, dense_got))
         n_got = swap_fs(n3)
+        views = left.reshape(3, tokens, 2, span)
+        left_got = swap_fs(lax.dynamic_index_in_dim(views, 1 - shard, 2, keepdims=False))
         back, y32, _, dn3, _ = dense_layer(
             dense_starts, n3, g_rows, *dense_own, dense_down, dense_more, tokens
         )
         back_mate = swap_dp(back, 1)
         back_got, _, y16, _, d16 = dense_layer(
             dense_starts,
-            after(n_got, dn3),
+            after(n_got, dn3, left_got),
             g_got,
             *dense_own,
             dense_down,
@@ -957,17 +937,24 @@
         outputs = (x2 + dense_out).astype(BF16)
 
     if chunked:
-        where = jnp.stack([chip_of(me), core, shard, chip_of(me, z_order)]).astype(jnp.int32)
+        where = jnp.stack([chip_of(me), core, shard, me // 2]).astype(jnp.int32)
+        masks = [
+            [
+                sum(((slot >> (len(order) - 1 - at)) & 1) * (bit // 2) for at, bit in enumerate(order))
+                for slot in range(chips)
+            ]
+            for order in (x_order, z_order)
+        ]
         own_kept, own_sent, down_kept, down_sent, far_kept, far_sent = chunk_weights(
-            dense_weight_kernel,
+            functools.partial(dense_weight_kernel, *masks),
             where,
-            (n3, n_got, g_rows, g_got, back, back_got, back_mate, back_got_mate),
+            (after(n3, dn3_more), n_got, g_rows, g_got, back, back_got, back_mate, back_got_mate),
             (
                 span // chips * hidden // 128,
                 hidden // chips * width // 256,
                 span // chips * hidden // 128,
             ),
-            chips,
+            chips // 2,
             [
                 pltpu.VMEM((max(hidden, half), max(hidden, width // 2)), F32),
                 pltpu.VMEM((4 * tokens, width), BF16),
@@ -977,19 +964,25 @@
         )
         dn3_more = after(dn3_more, own_sent)
         own_got, down_got = swap_dp(own_sent, z_order[0]), swap_dp(down_sent, x_order[0])
-        far_got = swap_fs(far_sent)
-
-    right, gx1, do1_heads, dkv, dc_two = pl.pallas_call(
+        far_got, far_kept = swap_fs(far_sent), swap_fs(far_kept)
+
+    straight = chunked and copies == 1
+    if straight:
+        slots = jnp.append(chip_of(me ^ (2 * jnp.arange(heads // 2))), core).astype(jnp.int32)
+    else:
+        slots = jnp.append(jnp.arange(heads // 2), 0).astype(jnp.int32)
+    right, gx1, do1_heads, dkv_kept, dkv_sent, dc_two = pl.pallas_call(
         functools.partial(mid_backward_kernel, len(near_more)),
         out_shape=[
             jax.ShapeDtypeStruct((tokens, 3 * width), BF16),
             row32,
             jax.ShapeDtypeStruct((heads, rows, 128), BF16),
-            jax.ShapeDtypeStruct((heads, dp, micro_count, part, 128), BF16),
+            jax.ShapeDtypeStruct((heads // 2, dp, micro_count, part, 128), BF16),
+            jax.ShapeDtypeStruct((heads // 2, dp, micro_count, part, 128), BF16),
             jax.ShapeDtypeStruct((2, width), F32),
         ],
-        in_specs=[smem()] + [vmem()] * (12 + len(near_more)),
-        out_specs=[vmem()] * 5,
+        in_specs=[smem()] * 2 + [vmem()] * (12 + len(near_more)),
+        out_specs=[vmem()] * 6,
         scratch_shapes=[
             pltpu.VMEM((tokens, width), F32),
             pltpu.VMEM((tokens, width), BF16),
@@ -998,26 +991,17 @@
         compiler_params=params(),
         cost_estimate=cost(16),
         name="mid_backward",
-    )(starts, g, dn3, dn3_more, x1, x2, gains, q2, ke, ve, *near_own, *near_more)
+    )(starts, slots, g, dn3, dn3_more, x1, x2, gains, q2, ke, ve, *near_own, *near_more)
     do1 = lax.all_to_all(
         jnp.repeat(do1_heads, copies, axis=0) if copies > 1 else do1_heads, "dp", 0, 0, tiled=True
     ).reshape(length, 128)
 
     if chunked:
-        views = left.reshape(3, tokens, 2, 2 * half)
-        own = lax.dynamic_index_in_dim(views, shard, 2, keepdims=False)
-        sent = lax.dynamic_index_in_dim(views, 1 - shard, 2, keepdims=False)
-        got = swap_fs(after(sent, dn3_more))
-        left_views = jnp.concatenate([own, got], axis=1).reshape(3, 2 * tokens, 2, half)
-
-        def left_features(which):
-            picked = lax.dynamic_index_in_dim(left_views, which, 2, keepdims=False)
-            return picked.transpose(1, 0, 2).reshape(2 * tokens, 3 * half)
-
-        left_mate = swap_dp(left_features(1 - core), 1)
         right_got = swap_fs(right)
-        far_kept = swap_fs(after(far_kept, right_got))
-        do1 = after(do1, left_mate, own_got, down_got, far_got)
+        if straight:
+            dkv_got = swap_dp(dkv_sent, 1)
+            do1 = after(do1, dkv_got)
+        do1 = after(do1, own_got, down_got, far_got)
 
     dqkv, table_grad = pl.pallas_call(
         self_backward_kernel,
@@ -1033,7 +1017,7 @@
         name="self_backward",
     )(qkv, do1, table, doc_row, doc_col)
     if chunked:
-        dqkv = after(dqkv, right_got)
+        dqkv = after(dqkv, right_got, far_kept)
     head_grad = pl.pallas_call(
         head_weight_kernel,
         out_shape=jax.ShapeDtypeStruct((fs, span * 3 // 2, 128), BF16),
@@ -1055,20 +1039,14 @@
         token_kept, token_sent = chunk_weights(
             token_weight_kernel,
             where,
-            (
-                left_features(core),
-                left_mate,
-                right,
-                right_got,
-                swap_dp(right, 1),
-                swap_dp(right_got, 1),
-            ),
+            (after(left, head_grad), left_got, right, right_got),
             (3 * half // chips * width // 128,),
             chips,
-            [pltpu.VMEM((half, width), F32)],
-            5,
+            [pltpu.VMEM((span, width), F32)],
+            6,
             "token_weight",
         )
+        token_got = swap_dp(token_sent, 1)
         head_sum = after(head_sum, token_kept)
 
     relative = me ^ (jnp.arange(heads, dtype=jnp.int32) * copies)
@@ -1103,15 +1081,18 @@
         name="input_grad",
     )(starts, own_d, x, gains, gx1, *first_own, *first_more)
 
-    dkv = dkv.reshape(heads * copies, -1, 128)
-    dkv = lax.psum_scatter(dkv, "dp", scatter_dimension=0, tiled=True)[0]
-    bit = 1
-    while bit < copies:
-        got = swap_dp(dkv, bit)
-        dkv = jnp.where(
-            (me // bit) % 2 == 0, jnp.concatenate([dkv, got]), jnp.concatenate([got, dkv])
-        )
-        bit *= 2
+    if straight:
+        dkv = reduce_chips(dkv_kept, dkv_got, [1] + x_order).reshape(-1, 128)
+    else:
+        dkv = jnp.stack([dkv_kept, dkv_sent], axis=1).reshape(heads * copies, -1, 128)
+        dkv = lax.psum_scatter(dkv, "dp", scatter_dimension=0, tiled=True)[0]
+        bit = 1
+        while bit < copies:
+            got = swap_dp(dkv, bit)
+            dkv = jnp.where(
+                (me // bit) % 2 == 0, jnp.concatenate([dkv, got]), jnp.concatenate([got, dkv])
+            )
+            bit *= 2
     cross_grad = pl.pallas_call(
         cross_head_weight_kernel,
         out_shape=jax.ShapeDtypeStruct((fs, span, 128), BF16),
@@ -1145,15 +1126,18 @@
     )(starts, own_dkv, *kv_own, *kv_more)
 
     if chunked:
-        dense_low, dense_high = gather_chips(reduce_chips(own_kept, own_got, z_order), z_order)
-        down_low, down_high = gather_chips(reduce_chips(down_kept, down_got))
-        far_low, far_high = gather_chips(reduce_chips(far_kept, swap_dp(far_got, 2)))
-        grad_dense_down = spread_down(where, down_low, down_high, hidden, width)
-        grad_dense_gate, grad_dense_up = spread_gate(
-            where, dense_low, dense_high, far_low, far_high, hidden, span
-        )
-
-        token_sum = after(reduce_chips(token_kept, swap_dp(token_sent, 2)), cross_grad)
+        sums = (
+            reduce_chips(own_kept, own_got, z_order, (right, token_kept)),
+            reduce_chips(down_kept, down_got, x_order, (right, token_kept)),
+            reduce_chips(
+                far_kept, swap_dp(after(far_got, right), x_order[0]), x_order, (dqkv, token_kept)
+            ),
+        )
+        pieces = lax.all_gather(jnp.concatenate(sums, axis=1), "dp", axis=0, tiled=True)
+        grad_dense_gate, grad_dense_up, grad_dense_down = spread_dense(
+            where, pieces, hidden, span, width
+        )
+        token_sum = after(reduce_chips(token_kept, token_got, [1] + x_order), cross_grad)
         token_low, token_high = gather_chips(token_sum)
         grad_output_cross, grad_query_cross, grad_output_self = spread_token(
             where, token_low, token_high, span, width, 3

time: 553 us -> 554 us (level)
  starting transfers between devices: 83.5 us -> 93.6 us
  local copies, waits for them, and re-layouts: 50.6 us -> 43.1 us
    ppermute x16, waiting for transfers between devices: 45.9 us -> 65.9 us  [swap_fs(): return lax.ppermute(values, 'fsdp', [(j, 1 - j) for j in range(2)])]
    ppermute x57 -> x47, waiting for transfers between devices: 169 us -> 150 us  [swap_dp(): return lax.ppermute(values, 'dp', [(j, j ^ bit) for j in range(dp)])]
    ppermute x57 -> x47, starting transfers between devices: 45.1 us -> 55.9 us  [swap_dp(): return lax.ppermute(values, 'dp', [(j, j ^ bit) for j in range(dp)])]
    reshape x3 -> x1, local copies, waits for them, and re-layouts: 11.6 us -> 2.77 us  [per_device(): views = left.reshape(3, tokens, 2, span)]
    unnamed x104 -> x107, local copies, waits for them, and re-layouts: 17.3 us -> 15.8 us
    pallas_call x2 -> x1, Pallas kernels: 11.9 us -> 10.5 us  [spread_dense(): pl.pallas_call(spread_dense_kernel, grid_spec=pltpu.PrefetchScalarGridSpe...]
  transfers between devices with their start and end apart: 79 -> 69, of which waited for: 27 -> 24; matrix products, arithmetic and copies ran while one was open for 13% -> 10% of each run, Pallas kernels for 27% -> 19%
where the time goes in v3:
time: 554 us; the launch traced here: 545 us
  waiting for transfers between devices  216 us (39%)
  Pallas kernels  153 us (28%)
  starting transfers between devices  93.6 us (17%)
  local copies, waits for them, and re-layouts  43.1 us (8%)
  other arithmetic  23.8 us (4%)
  between operations  15.5 us (3%)
    ppermute x47, waiting for transfers between devices, swap_dp(): return lax.ppermute(values, 'dp', [(j, j ^ bit) for j in range(dp)])  150 us
    ppermute x16, waiting for transfers between devices, swap_fs(): return lax.ppermute(values, 'fsdp', [(j, 1 - j) for j in range(2)])  65.9 us
    ppermute x47, starting transfers between devices, swap_dp(): return lax.ppermute(values, 'dp', [(j, j ^ bit) for j in range(dp)])  55.9 us
    ppermute x16, starting transfers between devices, swap_fs(): return lax.ppermute(values, 'fsdp', [(j, 1 - j) for j in range(2)])  19.8 us
    pallas_call x2, Pallas kernels, dense_layer(): pl.pallas_call(functools.partial(dense_kernel, len(more)), grid_spec=pltp...  19.7 us
    pallas_call x1, Pallas kernels, per_device(): pl.pallas_call(functools.partial(mid_backward_kernel, len(near_more)), ou...  19.4 us
    unnamed x107, local copies, waits for them, and re-layouts  15.8 us
    pallas_call x1, Pallas kernels, per_device(): pl.pallas_call(functools.partial(mid_forward_kernel, len(near_more)), out...  12.8 us
  transfers between devices with their start and end apart: 69, of which 24 were waited for; matrix products, arithmetic and copies ran while one was open for 10% of the time, Pallas kernels for 19%

profile of v3, /device:TPU:0, one launch (start us, length us, event | category | flops | bytes accessed | tf_op | source)
XLA Modules:
  0.0 544.7 jit_solution(8237685248470912183)
XLA Ops:
  7.3 3.0 collective-permute-start.3
  33.2 4.0 collective-permute-done.2
  37.9 4.4 bias_table.1.refs_6_.table_ref
  44.9 6.6 %collective-permute-done.5 = bf16[2,64,1024]{2,1,0:T(8,128)(2,1)S(1)} collective-permute-done((bf16[2,64,1024]{2,1,0:T(8,128)(2,1)S(1)}, bf16[2,64,1024]{2,1,0:T(8,128)(2,1)S(1)}, u32[]{:S(2)}, u32[]{:S(2)}) %collective-permute-start.5) | collective-permute-done | bytes 262176 | tf_op jit(solution)/shard_map/ppermute | solution.py:758
  51.5 3.2 collective-permute-done.6
  60.1 11.5 %self_forward.1 = (bf16[16,2,64,1024]{3,2,1,0:T(8,128)(2,1)}, bf16[1024,384]{1,0:T(8,128)(2,1)}, bf16[1024,128]{1,0:T(8,128)(2,1)}) custom-call(s32[16]{0:T(128)} %broadcast_xor_fusion.source_ref, bf16[4,2,64,1024]{3,2,1,0:T(8,128)(2,1)} %copy-done.7, bf16[4,2,64,1024]{3,2,1,0:T(8,128)(2,1)} %copy-done.8, bf16[4,2,64,1024]{3,2,1,0:T(8,128)(2,1)} %copy-done.37, ...), custom_call_target="tpu_custom_call" | custom-call | flops 13799999488 | bytes 44280000 | tf_op jit(solution)/shard_map/self_forward/pallas_call | solution.py:872
  71.5 27.7 %collective-permute-done.11.refs_0_ = bf16[5,256,1024]{2,1,0:T(8,128)(2,1)} collective-permute-done((bf16[5,256,1024]{2,1,0:T(8,128)(2,1)}, bf16[5,256,1024]{2,1,0:T(8,128)(2,1)}, u32[]{:S(2)}, u32[]{:S(2)}) %collective-permute-start.11) | collective-permute-done | bytes 2621472 | tf_op jit(solution)/shard_map/ppermute | solution.py:761
  101.4 4.8 all-to-all-start
  107.9 9.9 %cross_kv.1 = (bf16[2,512,1024]{2,1,0:T(8,128)(2,1)}, bf16[2,512,1024]{2,1,0:T(8,128)(2,1)}) custom-call(s32[3]{0:T(128)} %pad_add_fusion.starts_ref, bf16[16,2,32,1024]{3,2,1,0:T(8,128)(2,1)} %bitcast.92, bf16[512,1024]{1,0:T(8,128)(2,1)} %wk.3, bf16[512,1024]{1,0:T(8,128)(2,1)} %wv.3, bf16[5,256,1024]{2,1,0:T(8,128)(2,1)} %collective-permute-done.11.refs_0_, ...), custom_call_target="tpu_custom_call" | custom-call | flops 9200000000 | bytes 29520000 | tf_op jit(solution)/shard_map/cross_kv/pallas_call | solution.py:297
  118.5 12.8 %mid_forward.1 = (bf16[3,128,1024]{2,1,0:T(8,128)(2,1)}, f32[128,1024]{1,0:T(8,128)}, bf16[128,1024]{1,0:T(8,128)(2,1)}, f32[128,1024]{1,0:T(8,128)}, bf16[128,1024]{1,0:T(8,128)(2,1)}) custom-call(s32[3]{0:T(128)} %pad_add_fusion.starts_ref, bf16[16,64,128]{2,1,0:T(8,128)(2,1)} %copy-done.19, bf16[2,64,1024]{2,1,0:T(8,128)(2,1)} %bitcast.76, ...), custom_call_target="tpu_custom_call" | custom-call | flops 13799999488 | bytes 44280000 | tf_op jit(solution)/shard_map/mid_forward/pallas_call | solution.py:894
  131.3 8.9 %collective-permute-done.13.refs_0_ = bf16[2,256,1408]{2,1,0:T(8,128)(2,1)S(1)} collective-permute-done((bf16[2,256,1408]{2,1,0:T(8,128)(2,1)S(1)}, bf16[2,256,1408]{2,1,0:T(8,128)(2,1)S(1)}, u32[]{:S(2)}, u32[]{:S(2)}) %collective-permute-start.13) | collective-permute-done | bytes 1441824 | tf_op jit(solution)/shard_map/ppermute | solution.py:761
  142.9 2.8 reshape.117
  148.2 9.8 %dense_layer.2 = (bf16[128,5248]{1,0:T(8,128)(2,1)}, f32[128,1024]{1,0:T(8,128)}, bf16[128,1024]{1,0:T(8,128)(2,1)}, f32[128,1024]{1,0:T(8,128)}, bf16[128,1024]{1,0:T(8,128)(2,1)}) custom-call(s32[5]{0:T(128)} %concatenate.75.starts_ref, bf16[128,1024]{1,0:T(8,128)(2,1)} %get-tuple-element.107.n_ref.n0_ref, bf16[128,1024]{1,0:T(8,128)(2,1)} %bitcast.94, ...), custom_call_target="tpu_custom_call" | custom-call | flops 14949999616 | bytes 47970000 | tf_op jit(solution)/shard_map/dense_layer/pallas_call | solution.py:499
  158.0 5.5 %collective-permute-done.16.left_more_ref = bf16[3,128,512]{2,1,0:T(8,128)(2,1)S(1)} collective-permute-done((bf16[3,128,512]{2,1,0:T(8,128)(2,1)S(1)}, bf16[3,128,512]{2,1,0:T(8,128)(2,1)S(1)}, u32[]{:S(2)}, u32[]{:S(2)}) %collective-permute-start.16) | collective-permute-done | bytes 393248 | tf_op jit(solution)/shard_map/ppermute | solution.py:761
  164.3 9.9 %dense_layer.3 = (bf16[128,5248]{1,0:T(8,128)(2,1)}, f32[128,1024]{1,0:T(8,128)}, bf16[128,1024]{1,0:T(8,128)(2,1)}, f32[128,1024]{1,0:T(8,128)}, bf16[128,1024]{1,0:T(8,128)(2,1)}) custom-call(s32[5]{0:T(128)} %concatenate.75.starts_ref, bf16[128,1024]{1,0:T(8,128)(2,1)} %copy-done.45, bf16[128,1024]{1,0:T(8,128)(2,1)} %copy-done.44, bf16[512,2816]{1,0:T(8,128)(2,1)} %wg.3, ...), custom_call_target="tpu_custom_call" | custom-call | flops 14949999616 | bytes 47970000 | tf_op jit(solution)/shard_map/dense_layer/pallas_call | solution.py:499
  177.5 5.7 %collective-permute-done.18.more_ref = bf16[128,1024]{1,0:T(8,128)(2,1)S(1)} collective-permute-done((bf16[128,1024]{1,0:T(8,128)(2,1)}, bf16[128,1024]{1,0:T(8,128)(2,1)S(1)}, u32[]{:S(2)}, u32[]{:S(2)}) %collective-permute-start.18) | collective-permute-done | bytes 262176 | tf_op jit(solution)/shard_map/ppermute | solution.py:761
  184.3 7.1 %dense_weight.1 = (bf16[4,704,128]{2,1,0:T(8,128)(2,1)}, bf16[4,704,128]{2,1,0:T(8,128)(2,1)}, bf16[4,704,128]{2,1,0:T(8,128)(2,1)}, bf16[4,704,128]{2,1,0:T(8,1...) custom-call(s32[4]{0:T(128)} %pad_add_fusion.2.where_ref, ...), custom_call_target="tpu_custom_call" | custom-call | flops 8049999872 | bytes 25830000 | tf_op jit(solution)/shard_map/dense_weight/pallas_call | solution.py:597
  191.4 19.4 %mid_backward.1 = (bf16[128,3072]{1,0:T(8,128)(2,1)}, f32[128,1024]{1,0:T(8,128)}, bf16[16,64,128]{2,1,0:T(8,128)(2,1)}, bf16[8,16,2,32,128]{4,3,2,1,0:T(8,128)(...) custom-call(s32[3]{0:T(128)} %pad_add_fusion.starts_ref, s32[9]{0:T(128)} %pad_add_fusion.1.slots_ref, ...), custom_call_target="tpu_custom_call" | custom-call | flops 18400000000 | bytes 59040000 | tf_op jit(solution)/shard_map/mid_backward/pallas_call | solution.py:974
  216.1 13.9 %collective-permute-done.24 = bf16[4,704,128]{2,1,0:T(8,128)(2,1)} collective-permute-done((bf16[4,704,128]{2,1,0:T(8,128)(2,1)S(1)}, bf16[4,704,128]{2,1,0:T(8,128)(2,1)}, u32[]{:S(2)}, u32[]{:S(2)}) %collective-permute-start.24) | collective-permute-done | bytes 720928 | tf_op jit(solution)/shard_map/ppermute | solution.py:761
  234.3 3.5 all-to-all-start.1
  242.0 11.8 %collective-permute-done.56 = bf16[2,704,128]{2,1,0:T(8,128)(2,1)} collective-permute-done((bf16[2,704,128]{2,1,0:T(8,128)(2,1)S(1)}, bf16[2,704,128]{2,1,0:T(8,128)(2,1)}, u32[]{:S(2)}, u32[]{:S(2)}) %collective-permute-start.56) | collective-permute-done | bytes 360480 | tf_op jit(solution)/shard_map/ppermute | solution.py:758
  258.7 9.6 %self_backward.1 = (bf16[1024,384]{1,0:T(8,128)(2,1)}, f32[256,1024]{1,0:T(8,128)}) custom-call(bf16[1024,384]{1,0:T(8,128)(2,1)} %get-tuple-element.105.qkv_ref, bf16[1024,128]{1,0:T(8,128)(2,1)} %bitcast.71, f32[256,1024]{1,0:T(8,128)} %bias_table.1.refs_6_.table_ref, s32[2,1024]{1,0:T(2,128)} %reshape.115.refs_7_.doc_row_ref, ...), custom_call_target="tpu_custom_call" | custom-call | flops 11500000256 | bytes 36900000 | tf_op jit(solution)/shard_map/self_backward/pallas_call | solution.py:1006
  268.3 5.7 %head_weight.1 = bf16[2,768,128]{2,1,0:T(8,128)(2,1)} custom-call(bf16[16,2,64,1024]{3,2,1,0:T(8,128)(2,1)} %get-tuple-element.104.n_ref, bf16[1024,384]{1,0:T(8,128)(2,1)} %get-tuple-element.123.d_ref), custom_call_target="tpu_custom_call" | custom-call | flops 6899999744 | bytes 22140000 | tf_op jit(solution)/shard_map/head_weight/pallas_call | solution.py:1021
  276.1 4.8 token_weight.1
  283.1 3.2 collective-permute-done.57
  288.4 8.5 %collective-permute-done.59 = bf16[1,704,128]{2,1,0:T(8,128)(2,1)S(1)} collective-permute-done((bf16[1,704,128]{2,1,0:T(8,128)(2,1)S(1)}, bf16[1,704,128]{2,1,0:T(8,128)(2,1)S(1)}, u32[]{:S(2)}, u32[]{:S(2)}) %collective-permute-start.59) | collective-permute-done | bytes 180256 | tf_op jit(solution)/shard_map/ppermute | solution.py:758
  312.0 22.8 %collective-permute-done.31 = bf16[4,16,2,32,128]{4,3,2,1,0:T(8,128)(2,1)S(1)} collective-permute-done((bf16[4,16,2,32,128]{4,3,2,1,0:T(8,128)(2,1)S(1)}, bf16[4,16,2,32,128]{4,3,2,1,0:T(8,128)(2,1)S(1)}, u32[]{:S(2)}, u32[]{:S(2)}) %collective-permute-start.31) | collective-permute-done | bytes 1048608 | tf_op jit(solution)/shard_map/ppermute | solution.py:758
  337.7 3.4 collective-permute-start.39
  341.1 4.3 all-to-all-start.2
  347.1 22.4 %collective-permute-done.39 = bf16[1,768,128]{2,1,0:T(8,128)(2,1)S(1)} collective-permute-done((bf16[1,768,128]{2,1,0:T(8,128)(2,1)S(1)}, bf16[1,768,128]{2,1,0:T(8,128)(2,1)S(1)}, u32[]{:S(2)}, u32[]{:S(2)}) %collective-permute-start.39) | collective-permute-done | bytes 196640 | tf_op jit(solution)/shard_map/ppermute | solution.py:758
  369.5 3.8 collective-permute-start.40
  373.4 12.8 %collective-permute-done.32 = bf16[2,16,2,32,128]{4,3,2,1,0:T(8,128)(2,1)S(1)} collective-permute-done((bf16[2,16,2,32,128]{4,3,2,1,0:T(8,128)(2,1)}, bf16[2,16,2,32,128]{4,3,2,1,0:T(8,128)(2,1)S(1)}, u32[]{:S(2)}, u32[]{:S(2)}) %collective-permute-start.32) | collective-permute-done | bytes 524320 | tf_op jit(solution)/shard_map/ppermute | solution.py:758
  390.3 24.5 %collective-permute-done.40 = bf16[2,768,128]{2,1,0:T(8,128)(2,1)S(1)} collective-permute-done((bf16[2,768,128]{2,1,0:T(8,128)(2,1)S(1)}, bf16[2,768,128]{2,1,0:T(8,128)(2,1)S(1)}, u32[]{:S(2)}, u32[]{:S(2)}) %collective-permute-start.40) | collective-permute-done | bytes 393248 | tf_op jit(solution)/shard_map/ppermute | solution.py:758
  416.5 3.1 cross_head_weight.1
  426.8 3.4 collective-permute-start.52
  430.2 5.4 collective-permute-done.45
  435.7 3.5 collective-permute-start.46
  444.2 3.5 collective-permute-done.46
  455.0 3.7 collective-permute-done.47
  458.9 7.4 %bucket_sums.1 = f32[32,128]{1,0:T(8,128)} custom-call(s32[32]{0:T(128)} %convert_reduce_fusion.edge_ref, f32[256,1024]{1,0:T(8,128)} %get-tuple-element.135.grad_ref), custom_call_target="tpu_custom_call" | custom-call | flops 8049999872 | bytes 25830000 | tf_op jit(solution)/shard_map/bucket_sums/pallas_call | solution.py:137
  466.2 5.0 all-to-all-start.3
  471.2 6.6 %input_grad.1 = (f32[128,1024]{1,0:T(8,128)}, f32[1,1024]{1,0:T(1,128)}) custom-call(s32[3]{0:T(128)} %pad_add_fusion.starts_ref, bf16[16,64,384]{2,1,0:T(8,128)(2,1)} %all-to-all-done.2.d_ref, bf16[2,64,1024]{2,1,0:T(8,128)(2,1)} %bitcast.77, f32[3,1024]{1,0:T(4,128)} %copy-done.29, f32[128,1024]{1,0:T(8,128)} %get-tuple-element.129.gx1_ref, ...), custom_call_target="tpu_custom_call" | custom-call | flops 8049999872 | bytes 25830000 | tf_op jit(solution)/shard_map/input_grad/pallas_call | solution.py:1070
  486.3 12.2 %collective-permute-done.36 = f32[4,1024]{1,0:T(4,128)S(1)} collective-permute-done((f32[4,1024]{1,0:T(4,128)S(1)}, f32[4,1024]{1,0:T(4,128)S(1)}, u32[]{:S(2)}, u32[]{:S(2)}) %collective-permute-start.36) | collective-permute-done | bytes 16416 | tf_op jit(solution)/shard_map/ppermute | solution.py:758
  502.6 5.4 encoder_grad.1
  510.5 5.8 %head_spread.1 = (f32[512,1024]{1,0:T(8,128)}, f32[512,1024]{1,0:T(8,128)}, f32[512,1024]{1,0:T(8,128)}) custom-call(s32[16]{0:T(128)} %fusion.13.pos_ref, bf16[8,768,128]{2,1,0:T(8,128)(2,1)} %constant_dynamic-update-slice_fusion.low_ref, bf16[8,768,128]{2,1,0:T(8,128)(2,1)} %collective-permute-done.42.high_ref), custom_call_target="tpu_custom_call" | custom-call | flops 6899999744 | bytes 22140000 | tf_op jit(solution)/shard_map/head_spread/pallas_call | solution.py:1054
  517.6 4.4 cross_head_spread.1
  522.1 4.9 spread_token.1
  527.0 10.5 %spread_dense.1 = (f32[2,4,64,2816]{3,2,1,0:T(8,128)}, f32[2,4,64,2816]{3,2,1,0:T(8,128)}, f32[1408,1024]{1,0:T(8,128)}) custom-call(s32[4]{0:T(128)} %pad_add_fusion.2.where_ref, bf16[16,2112,128]{2,1,0:T(8,128)(2,1)} %all-gather.4.cloned.1.call-done.in_ref), custom_call_target="tpu_custom_call" | custom-call | flops 11500000256 | bytes 36900000 | tf_op jit(solution)/shard_map/spread_dense/pallas_call | solution.py:633
  (318 shorter events, 132.8 us)
Async XLA Ops:
  7.2 100.7 %all-gather.6.cloned.1.call-start = ((), (), s32[]{:S(2)}) async-start(), calls=%async_computation.5 | async-start | bytes 2228224 | tf_op jit(solution)/shard_map/all_gather | solution.py:806
  7.3 37.6 %collective-permute-start.3 = (bf16[2,64,1024]{2,1,0:T(8,128)(2,1)}, bf16[2,64,1024]{2,1,0:T(8,128)(2,1)S(1)}, u32[]{:S(2)}, u32[]{:S(2)}) collective-permute-start(bf16[2,64,1024]{2,1,0:T(8,128)(2,1)} %bitcast.73), channel_id=1, source_target_pairs={{0,4},{2,6},{4,0},{6,2},{8,12},{10,14},{12,8},{14,10},{16,20},{18,... | collective-permute-start | bytes 786440 | tf_op jit(solution)/shard_map/ppermute | solution.py:758
  10.3 21.5 %collective-permute-start.1 = (bf16[2,64,1024]{2,1,0:T(8,128)(2,1)}, bf16[2,64,1024]{2,1,0:T(8,128)(2,1)S(1)}, u32[]{:S(2)}, u32[]{:S(2)}) collective-permute-start(bf16[2,64,1024]{2,1,0:T(8,128)(2,1)} %bitcast.74), channel_id=1, source_target_pairs={{0,8},{2,10},{4,12},{6,14},{8,0},{10,2},{12,4},{14,6},{16,24},{18,... | collective-permute-start | bytes 786440 | tf_op jit(solution)/shard_map/ppermute | solution.py:758
  11.8 17.2 %collective-permute-start = (bf16[2,64,1024]{2,1,0:T(8,128)(2,1)}, bf16[2,64,1024]{2,1,0:T(8,128)(2,1)}, u32[]{:S(2)}, u32[]{:S(2)}) collective-permute-start(bf16[2,64,1024]{2,1,0:T(8,128)(2,1)} %bitcast.75), channel_id=1, source_target_pairs={{0,16},{2,18},{4,20},{6,22},{8,24},{10,26},{12,28},{14,30},{16,0},... | collective-permute-start | bytes 786440 | tf_op jit(solution)/shard_map/ppermute | solution.py:758
  21.7 20.6 %collective-permute-start.10 = (bf16[512,192]{1,0:T(8,128)(2,1)S(1)}, bf16[512,192]{1,0:T(8,128)(2,1)S(1)}, u32[]{:S(2)}, u32[]{:S(2)}) collective-permute-start(bf16[512,192]{1,0:T(8,128)(2,1)S(1)} %pad_maximum_fusion.12), channel_id=1, source_target_pairs={{0,1},{1,0},{2,3},{3,2},{4,5},{5,4},{6,7},{7,6},{8,9},{9,8},{10,11... | collective-permute-start | bytes 589832 | tf_op jit(solution)/shard_map/ppermute | solution.py:761
  31.2 20.3 %collective-permute-start.4 = (bf16[2,64,1024]{2,1,0:T(8,128)(2,1)}, bf16[2,64,1024]{2,1,0:T(8,128)(2,1)S(1)}, u32[]{:S(2)}, u32[]{:S(2)}) collective-permute-start(bf16[2,64,1024]{2,1,0:T(8,128)(2,1)} %collective-permute-done), channel_id=1, source_target_pairs={{0,4},{2,6},{4,0},{6,2},{8,12},{10,14},{12,8},{14,10},{16,20},{18,... | collective-permute-start | bytes 786440 | tf_op jit(solution)/shard_map/ppermute | solution.py:758
  31.8 19.7 %collective-permute-start.5 = (bf16[2,64,1024]{2,1,0:T(8,128)(2,1)S(1)}, bf16[2,64,1024]{2,1,0:T(8,128)(2,1)S(1)}, u32[]{:S(2)}, u32[]{:S(2)}) collective-permute-start(bf16[2,64,1024]{2,1,0:T(8,128)(2,1)S(1)} %collective-permute-done.1), channel_id=1, source_target_pairs={{0,4},{2,6},{4,0},{6,2},{8,12},{10,14},{12,8},{14,10},{16,20},{18,... | collective-permute-start | bytes 786440 | tf_op jit(solution)/shard_map/ppermute | solution.py:758
  37.2 17.4 %collective-permute-start.6 = (bf16[2,64,1024]{2,1,0:T(8,128)(2,1)S(1)}, bf16[2,64,1024]{2,1,0:T(8,128)(2,1)S(1)}, u32[]{:S(2)}, u32[]{:S(2)}) collective-permute-start(bf16[2,64,1024]{2,1,0:T(8,128)(2,1)S(1)} %collective-permute-done.2), channel_id=1, source_target_pairs={{0,4},{2,6},{4,0},{6,2},{8,12},{10,14},{12,8},{14,10},{16,20},{18,... | collective-permute-start | bytes 786440 | tf_op jit(solution)/shard_map/ppermute | solution.py:758
  42.3 56.9 %collective-permute-start.11 = (bf16[5,256,1024]{2,1,0:T(8,128)(2,1)}, bf16[5,256,1024]{2,1,0:T(8,128)(2,1)}, u32[]{:S(2)}, u32[]{:S(2)}) collective-permute-start(bf16[5,256,1024]{2,1,0:T(8,128)(2,1)} %copy-done.27), channel_id=1, source_target_pairs={{0,1},{1,0},{2,3},{3,2},{4,5},{5,4},{6,7},{7,6},{8,9},{9,8},{10,11... | collective-permute-start | bytes 7864328 | tf_op jit(solution)/shard_map/ppermute | solution.py:761
  44.9 13.3 %collective-permute-start.7 = (bf16[4,2,64,1024]{3,2,1,0:T(8,128)(2,1)S(1)}, bf16[4,2,64,1024]{3,2,1,0:T(8,128)(2,1)S(1)}, u32[]{:S(2)}, u32[]{:S(2)}) collective-permute-start(bf16[4,2,64,1024]{3,2,1,0:T(8,128)(2,1)S(1)} %pad_maximum_fusion.2.refs_0_), channel_id=1, source_target_pairs={{0,2},{2,0},{4,6},{6,4},{8,10},{10,8},{12,14},{14,12},{16,18},{18,... | collective-permute-start | bytes 3145736 | tf_op jit(solution)/shard_map/ppermute | solution.py:758
  101.4 16.3 %all-to-all-start = ((bf16[16,64,128]{2,1,0:T(8,128)(2,1)}), bf16[16,64,128]{2,1,0:T(8,128)(2,1)S(1)}, u32[]{:S(2)}, u32[]{:S(2)}) async-start(bf16[16,64,128]{2,1,0:T(8,128)(2,1)} %bitcast.14), calls=%async_computation | async-start | bytes 524288 | tf_op jit(solution)/shard_map/all_to_all | solution.py:885
  106.3 33.9 %collective-permute-start.13 = (bf16[2,256,1408]{2,1,0:T(8,128)(2,1)S(1)}, bf16[2,256,1408]{2,1,0:T(8,128)(2,1)S(1)}, u32[]{:S(2)}, u32[]{:S(2)}) collective-permute-start(bf16[2,256,1408]{2,1,0:T(8,128)(2,1)S(1)} %pad_maximum_fusion.1), channel_id=1, source_target_pairs={{0,1},{1,0},{2,3},{3,2},{4,5},{5,4},{6,7},{7,6},{8,9},{9,8},{10,11... | collective-permute-start | bytes 4325384 | tf_op jit(solution)/shard_map/ppermute | solution.py:761
  140.9 22.7 %collective-permute-start.17 = (bf16[128,1024]{1,0:T(8,128)(2,1)S(1)}, bf16[128,1024]{1,0:T(8,128)(2,1)S(1)}, u32[]{:S(2)}, u32[]{:S(2)}) collective-permute-start(bf16[128,1024]{1,0:T(8,128)(2,1)S(1)} %bitcast.97), channel_id=1, source_target_pairs={{0,1},{1,0},{2,3},{3,2},{4,5},{5,4},{6,7},{7,6},{8,9},{9,8},{10,11... | collective-permute-start | bytes 786440 | tf_op jit(solution)/shard_map/ppermute | solution.py:761
  142.4 15.6 %collective-permute-start.15 = (bf16[128,1024]{1,0:T(8,128)(2,1)}, bf16[128,1024]{1,0:T(8,128)(2,1)S(1)}, u32[]{:S(2)}, u32[]{:S(2)}) collective-permute-start(bf16[128,1024]{1,0:T(8,128)(2,1)} %get-tuple-element.107.n_ref.n0_ref), channel_id=1, source_target_pairs={{0,1},{1,0},{2,3},{3,2},{4,5},{5,4},{6,7},{7,6},{8,9},{9,8},{10,11... | collective-permute-start | bytes 786440 | tf_op jit(solution)/shard_map/ppermute | solution.py:761
  146.6 17.0 %collective-permute-start.16 = (bf16[3,128,512]{2,1,0:T(8,128)(2,1)S(1)}, bf16[3,128,512]{2,1,0:T(8,128)(2,1)S(1)}, u32[]{:S(2)}, u32[]{:S(2)}) collective-permute-start(bf16[3,128,512]{2,1,0:T(8,128)(2,1)S(1)} %bitcast.70), channel_id=1, source_target_pairs={{0,1},{1,0},{2,3},{3,2},{4,5},{5,4},{6,7},{7,6},{8,9},{9,8},{10,11... | collective-permute-start | bytes 1179656 | tf_op jit(solution)/shard_map/ppermute | solution.py:761
  210.8 47.2 %collective-permute-start.21 = (bf16[8,16,2,32,128]{4,3,2,1,0:T(8,128)(2,1)}, bf16[8,16,2,32,128]{4,3,2,1,0:T(8,128)(2,1)}, u32[]{:S(2)}, u32[]{:S(2)}) collective-permute-start(bf16[8,16,2,32,128]{4,3,2,1,0:T(8,128)(2,1)} %get-tuple-element.115), channel_id=1, source_target_pairs={{0,2},{2,0},{4,6},{6,4},{8,10},{10,8},{12,14},{14,12},{16,18},{18,... | collective-permute-start | bytes 6291464 | tf_op jit(solution)/shard_map/ppermute | solution.py:758
  210.9 19.1 %collective-permute-start.24 = (bf16[4,704,128]{2,1,0:T(8,128)(2,1)S(1)}, bf16[4,704,128]{2,1,0:T(8,128)(2,1)}, u32[]{:S(2)}, u32[]{:S(2)}) collective-permute-start(bf16[4,704,128]{2,1,0:T(8,128)(2,1)S(1)} %copy-done.40), channel_id=1, source_target_pairs={{0,1},{1,0},{2,3},{3,2},{4,5},{5,4},{6,7},{7,6},{8,9},{9,8},{10,11... | collective-permute-start | bytes 2162696 | tf_op jit(solution)/shard_map/ppermute | solution.py:761
  212.5 19.2 %collective-permute-start.22 = (bf16[4,704,128]{2,1,0:T(8,128)(2,1)S(1)}, bf16[4,704,128]{2,1,0:T(8,128)(2,1)S(1)}, u32[]{:S(2)}, u32[]{:S(2)}) collective-permute-start(bf16[4,704,128]{2,1,0:T(8,128)(2,1)S(1)} %copy-done.39), channel_id=1, source_target_pairs={{0,8},{2,10},{4,12},{6,14},{8,0},{10,2},{12,4},{14,6},{16,24},{18,... | collective-permute-start | bytes 2162696 | tf_op jit(solution)/shard_map/ppermute | solution.py:758
  214.2 23.9 %collective-permute-start.23 = (bf16[4,704,128]{2,1,0:T(8,128)(2,1)}, bf16[4,704,128]{2,1,0:T(8,128)(2,1)S(1)}, u32[]{:S(2)}, u32[]{:S(2)}) collective-permute-start(bf16[4,704,128]{2,1,0:T(8,128)(2,1)} %get-tuple-element.117), channel_id=1, source_target_pairs={{0,4},{2,6},{4,0},{6,2},{8,12},{10,14},{12,8},{14,10},{16,20},{18,... | collective-permute-start | bytes 2162696 | tf_op jit(solution)/shard_map/ppermute | solution.py:758
  215.7 40.0 %collective-permute-start.26 = (bf16[4,704,128]{2,1,0:T(8,128)(2,1)}, bf16[4,704,128]{2,1,0:T(8,128)(2,1)}, u32[]{:S(2)}, u32[]{:S(2)}) collective-permute-start(bf16[4,704,128]{2,1,0:T(8,128)(2,1)} %get-tuple-element.122), channel_id=1, source_target_pairs={{0,1},{1,0},{2,3},{3,2},{4,5},{5,4},{6,7},{7,6},{8,9},{9,8},{10,11... | collective-permute-start | bytes 2162696 | tf_op jit(solution)/shard_map/ppermute | solution.py:761
  230.0 25.7 %collective-permute-start.60 = (bf16[4,704,128]{2,1,0:T(8,128)(2,1)}, bf16[4,704,128]{2,1,0:T(8,128)(2,1)}, u32[]{:S(2)}, u32[]{:S(2)}) collective-permute-start(bf16[4,704,128]{2,1,0:T(8,128)(2,1)} %collective-permute-done.24), channel_id=1, source_target_pairs={{0,4},{2,6},{4,0},{6,2},{8,12},{10,14},{12,8},{14,10},{16,20},{18,... | collective-permute-start | bytes 2162696 | tf_op jit(solution)/shard_map/ppermute | solution.py:758
  231.9 21.9 %collective-permute-start.56 = (bf16[2,704,128]{2,1,0:T(8,128)(2,1)S(1)}, bf16[2,704,128]{2,1,0:T(8,128)(2,1)}, u32[]{:S(2)}, u32[]{:S(2)}) collective-permute-start(bf16[2,704,128]{2,1,0:T(8,128)(2,1)S(1)} %slice.246), channel_id=1, source_target_pairs={{0,16},{2,18},{4,20},{6,22},{8,24},{10,26},{12,28},{14,30},{16,0},... | collective-permute-start | bytes 1081352 | tf_op jit(solution)/shard_map/ppermute | solution.py:758
  234.3 23.7 %all-to-all-start.1 = ((bf16[16,64,128]{2,1,0:T(8,128)(2,1)}), bf16[16,64,128]{2,1,0:T(8,128)(2,1)S(1)}, u32[]{:S(2)}, u32[]{:S(2)}) async-start(bf16[16,64,128]{2,1,0:T(8,128)(2,1)} %get-tuple-element.114), calls=%async_computation.1 | async-start | bytes 524288 | tf_op jit(solution)/shard_map/all_to_all | solution.py:995
  237.9 289.1 %all-gather.4.cloned.1.call-start = ((), (), s32[]{:S(2)}) async-start(), calls=%async_computation.4 | async-start | bytes 9191424 | tf_op jit(solution)/shard_map/all_gather | solution.py:1136
  238.1 30.2 %collective-permute-start.25 = (bf16[128,3072]{1,0:T(8,128)(2,1)}, bf16[128,3072]{1,0:T(8,128)(2,1)}, u32[]{:S(2)}, u32[]{:S(2)}) collective-permute-start(bf16[128,3072]{1,0:T(8,128)(2,1)} %get-tuple-element.121.right_ref), channel_id=1, source_target_pairs={{0,1},{1,0},{2,3},{3,2},{4,5},{5,4},{6,7},{7,6},{8,9},{9,8},{10,11... | collective-permute-start | bytes 2359304 | tf_op jit(solution)/shard_map/ppermute | solution.py:761
  253.8 28.3 %collective-permute-start.58 = (bf16[2,704,128]{2,1,0:T(8,128)(2,1)}, bf16[2,704,128]{2,1,0:T(8,128)(2,1)S(1)}, u32[]{:S(2)}, u32[]{:S(2)}) collective-permute-start(bf16[2,704,128]{2,1,0:T(8,128)(2,1)} %slice.245), channel_id=1, source_target_pairs={{0,8},{2,10},{4,12},{6,14},{8,0},{10,2},{12,4},{14,6},{16,24},{18,... | collective-permute-start | bytes 1081352 | tf_op jit(solution)/shard_map/ppermute | solution.py:758
  282.2 14.8 %collective-permute-start.59 = (bf16[1,704,128]{2,1,0:T(8,128)(2,1)S(1)}, bf16[1,704,128]{2,1,0:T(8,128)(2,1)S(1)}, u32[]{:S(2)}, u32[]{:S(2)}) collective-permute-start(bf16[1,704,128]{2,1,0:T(8,128)(2,1)S(1)} %slice.250), channel_id=1, source_target_pairs={{0,16},{2,18},{4,20},{6,22},{8,24},{10,26},{12,28},{14,30},{16,0},... | collective-permute-start | bytes 540680 | tf_op jit(solution)/shard_map/ppermute | solution.py:758
  305.2 29.5 %collective-permute-start.31 = (bf16[4,16,2,32,128]{4,3,2,1,0:T(8,128)(2,1)S(1)}, bf16[4,16,2,32,128]{4,3,2,1,0:T(8,128)(2,1)S(1)}, u32[]{:S(2)}, u32[]{:S(2)}) collective-permute-start(bf16[4,16,2,32,128]{4,3,2,1,0:T(8,128)(2,1)S(1)} %slice.240), channel_id=1, source_target_pairs={{0,4},{2,6},{4,0},{6,2},{8,12},{10,14},{12,8},{14,10},{16,20},{18,... | collective-permute-start | bytes 3145736 | tf_op jit(solution)/shard_map/ppermute | solution.py:758
  308.8 78.8 %collective-permute-start.43 = (bf16[8,768,128]{2,1,0:T(8,128)(2,1)}, bf16[8,768,128]{2,1,0:T(8,128)(2,1)}, u32[]{:S(2)}, u32[]{:S(2)}) collective-permute-start(bf16[8,768,128]{2,1,0:T(8,128)(2,1)} %get-tuple-element.139), channel_id=1, source_target_pairs={{0,2},{2,0},{4,6},{6,4},{8,10},{10,8},{12,14},{14,12},{16,18},{18,... | collective-permute-start | bytes 4718600 | tf_op jit(solution)/shard_map/ppermute | solution.py:758
  310.7 26.9 %collective-permute-start.27 = (bf16[1,768,128]{2,1,0:T(8,128)(2,1)S(1)}, bf16[1,768,128]{2,1,0:T(8,128)(2,1)S(1)}, u32[]{:S(2)}, u32[]{:S(2)}) collective-permute-start(bf16[1,768,128]{2,1,0:T(8,128)(2,1)S(1)} %constant_dynamic-slice_fusion.4), channel_id=1, source_target_pairs={{0,1},{1,0},{2,3},{3,2},{4,5},{5,4},{6,7},{7,6},{8,9},{9,8},{10,11... | collective-permute-start | bytes 589832 | tf_op jit(solution)/shard_map/ppermute | solution.py:761
  336.0 50.2 %collective-permute-start.32 = (bf16[2,16,2,32,128]{4,3,2,1,0:T(8,128)(2,1)}, bf16[2,16,2,32,128]{4,3,2,1,0:T(8,128)(2,1)S(1)}, u32[]{:S(2)}, u32[]{:S(2)}) collective-permute-start(bf16[2,16,2,32,128]{4,3,2,1,0:T(8,128)(2,1)} %slice.242), channel_id=1, source_target_pairs={{0,8},{2,10},{4,12},{6,14},{8,0},{10,2},{12,4},{14,6},{16,24},{18,... | collective-permute-start | bytes 1572872 | tf_op jit(solution)/shard_map/ppermute | solution.py:758
  337.7 31.8 %collective-permute-start.39 = (bf16[1,768,128]{2,1,0:T(8,128)(2,1)S(1)}, bf16[1,768,128]{2,1,0:T(8,128)(2,1)S(1)}, u32[]{:S(2)}, u32[]{:S(2)}) collective-permute-start(bf16[1,768,128]{2,1,0:T(8,128)(2,1)S(1)} %add_convert_fusion.1), channel_id=1, source_target_pairs={{0,16},{2,18},{4,20},{6,22},{8,24},{10,26},{12,28},{14,30},{16,0},... | collective-permute-start | bytes 589832 | tf_op jit(solution)/shard_map/ppermute | solution.py:758
  341.1 125.1 %all-to-all-start.2 = ((bf16[16,64,384]{2,1,0:T(8,128)(2,1)}), bf16[16,64,384]{2,1,0:T(8,128)(2,1)}, u32[]{:S(2)}, u32[]{:S(2)}) async-start(bf16[16,64,384]{2,1,0:T(8,128)(2,1)} %bitcast.36), calls=%async_computation.2 | async-start | bytes 1572864 | tf_op jit(solution)/shard_map/all_to_all | solution.py:1069
  345.4 80.5 %collective-permute-start.28 = (bf16[3,256,1024]{2,1,0:T(8,128)(2,1)}, bf16[3,256,1024]{2,1,0:T(8,128)(2,1)}, u32[]{:S(2)}, u32[]{:S(2)}) collective-permute-start(bf16[3,256,1024]{2,1,0:T(8,128)(2,1)} %pad_maximum_fusion), channel_id=1, source_target_pairs={{0,1},{1,0},{2,3},{3,2},{4,5},{5,4},{6,7},{7,6},{8,9},{9,8},{10,11... | collective-permute-start | bytes 4718600 | tf_op jit(solution)/shard_map/ppermute | solution.py:761
  369.5 45.2 %collective-permute-start.40 = (bf16[2,768,128]{2,1,0:T(8,128)(2,1)S(1)}, bf16[2,768,128]{2,1,0:T(8,128)(2,1)S(1)}, u32[]{:S(2)}, u32[]{:S(2)}) collective-permute-start(bf16[2,768,128]{2,1,0:T(8,128)(2,1)S(1)} %pad_maximum_fusion.10), channel_id=1, source_target_pairs={{0,8},{2,10},{4,12},{6,14},{8,0},{10,2},{12,4},{14,6},{16,24},{18,... | collective-permute-start | bytes 1179656 | tf_op jit(solution)/shard_map/ppermute | solution.py:758
  386.4 29.3 %collective-permute-start.33 = (bf16[1,16,2,32,128]{4,3,2,1,0:T(8,128)(2,1)S(1)}, bf16[1,16,2,32,128]{4,3,2,1,0:T(8,128)(2,1)S(1)}, u32[]{:S(2)}, u32[]{:S(2)}) collective-permute-start(bf16[1,16,2,32,128]{4,3,2,1,0:T(8,128)(2,1)S(1)} %slice.247), channel_id=1, source_target_pairs={{0,16},{2,18},{4,20},{6,22},{8,24},{10,26},{12,28},{14,30},{16,0},... | collective-permute-start | bytes 786440 | tf_op jit(solution)/shard_map/ppermute | solution.py:758
  390.3 31.8 %collective-permute-start.44 = (bf16[4,768,128]{2,1,0:T(8,128)(2,1)}, bf16[4,768,128]{2,1,0:T(8,128)(2,1)}, u32[]{:S(2)}, u32[]{:S(2)}) collective-permute-start(bf16[4,768,128]{2,1,0:T(8,128)(2,1)} %slice.241), channel_id=1, source_target_pairs={{0,4},{2,6},{4,0},{6,2},{8,12},{10,14},{12,8},{14,10},{16,20},{18,... | collective-permute-start | bytes 2359304 | tf_op jit(solution)/shard_map/ppermute | solution.py:758
  414.8 24.4 %collective-permute-start.41 = (bf16[4,768,128]{2,1,0:T(8,128)(2,1)S(1)}, bf16[4,768,128]{2,1,0:T(8,128)(2,1)}, u32[]{:S(2)}, u32[]{:S(2)}) collective-permute-start(bf16[4,768,128]{2,1,0:T(8,128)(2,1)S(1)} %pad_maximum_fusion.6), channel_id=1, source_target_pairs={{0,4},{2,6},{4,0},{6,2},{8,12},{10,14},{12,8},{14,10},{16,20},{18,... | collective-permute-start | bytes 2359304 | tf_op jit(solution)/shard_map/ppermute | solution.py:758
  426.0 32.9 %collective-permute-start.30 = (bf16[3,256,1024]{2,1,0:T(8,128)(2,1)}, bf16[3,256,1024]{2,1,0:T(8,128)(2,1)}, u32[]{:S(2)}, u32[]{:S(2)}) collective-permute-start(bf16[3,256,1024]{2,1,0:T(8,128)(2,1)} %collective-permute-done.28.refs_0_), channel_id=1, source_target_pairs={{0,2},{2,0},{4,6},{6,4},{8,10},{10,8},{12,14},{14,12},{16,18},{18,... | collective-permute-start | bytes 4718600 | tf_op jit(solution)/shard_map/ppermute | solution.py:758
  426.8 14.9 %collective-permute-start.52 = (bf16[1,512,128]{2,1,0:T(8,128)(2,1)S(1)}, bf16[1,512,128]{2,1,0:T(8,128)(2,1)S(1)}, u32[]{:S(2)}, u32[]{:S(2)}) collective-permute-start(bf16[1,512,128]{2,1,0:T(8,128)(2,1)S(1)} %add_convert_fusion.2), channel_id=1, source_target_pairs={{0,16},{2,18},{4,20},{6,22},{8,24},{10,26},{12,28},{14,30},{16,0},... | collective-permute-start | bytes 393224 | tf_op jit(solution)/shard_map/ppermute | solution.py:758
  441.3 69.2 %collective-permute-start.42 = (bf16[8,768,128]{2,1,0:T(8,128)(2,1)}, bf16[8,768,128]{2,1,0:T(8,128)(2,1)}, u32[]{:S(2)}, u32[]{:S(2)}) collective-permute-start(bf16[8,768,128]{2,1,0:T(8,128)(2,1)} %constant_dynamic-update-slice_fusion.low_ref), channel_id=1, source_target_pairs={{0,2},{2,0},{4,6},{6,4},{8,10},{10,8},{12,14},{14,12},{16,18},{18,... | collective-permute-start | bytes 4718600 | tf_op jit(solution)/shard_map/ppermute | solution.py:758
  453.6 28.2 %collective-permute-start.54 = (bf16[4,512,128]{2,1,0:T(8,128)(2,1)S(1)}, bf16[4,512,128]{2,1,0:T(8,128)(2,1)S(1)}, u32[]{:S(2)}, u32[]{:S(2)}) collective-permute-start(bf16[4,512,128]{2,1,0:T(8,128)(2,1)S(1)} %pad_maximum_fusion.9), channel_id=1, source_target_pairs={{0,4},{2,6},{4,0},{6,2},{8,12},{10,14},{12,8},{14,10},{16,20},{18,... | collective-permute-start | bytes 1572872 | tf_op jit(solution)/shard_map/ppermute | solution.py:758
  458.8 19.3 %collective-permute-start.48 = (bf16[2,768,128]{2,1,0:T(8,128)(2,1)S(1)}, bf16[2,768,128]{2,1,0:T(8,128)(2,1)S(1)}, u32[]{:S(2)}, u32[]{:S(2)}) collective-permute-start(bf16[2,768,128]{2,1,0:T(8,128)(2,1)S(1)} %pad_maximum_fusion.11), channel_id=1, source_target_pairs={{0,8},{2,10},{4,12},{6,14},{8,0},{10,2},{12,4},{14,6},{16,24},{18,... | collective-permute-start | bytes 1179656 | tf_op jit(solution)/shard_map/ppermute | solution.py:758
  466.2 35.7 %all-to-all-start.3 = ((bf16[16,64,128]{2,1,0:T(8,128)(2,1)}), bf16[16,64,128]{2,1,0:T(8,128)(2,1)S(1)}, u32[]{:S(2)}, u32[]{:S(2)}) async-start(bf16[16,64,128]{2,1,0:T(8,128)(2,1)} %bitcast.39), calls=%async_computation.3 | async-start | bytes 524288 | tf_op jit(solution)/shard_map/all_to_all | solution.py:1116
  478.2 22.8 %collective-permute-start.49 = (bf16[4,768,128]{2,1,0:T(8,128)(2,1)S(1)}, bf16[4,768,128]{2,1,0:T(8,128)(2,1)S(1)}, u32[]{:S(2)}, u32[]{:S(2)}) collective-permute-start(bf16[4,768,128]{2,1,0:T(8,128)(2,1)S(1)} %pad_maximum_fusion.7), channel_id=1, source_target_pairs={{0,4},{2,6},{4,0},{6,2},{8,12},{10,14},{12,8},{14,10},{16,20},{18,... | collective-permute-start | bytes 2359304 | tf_op jit(solution)/shard_map/ppermute | solution.py:758
  481.9 35.8 %collective-permute-start.55 = (bf16[8,512,128]{2,1,0:T(8,128)(2,1)S(1)}, bf16[8,512,128]{2,1,0:T(8,128)(2,1)}, u32[]{:S(2)}, u32[]{:S(2)}) collective-permute-start(bf16[8,512,128]{2,1,0:T(8,128)(2,1)S(1)} %pad_maximum_fusion.4.low_ref), channel_id=1, source_target_pairs={{0,2},{2,0},{4,6},{6,4},{8,10},{10,8},{12,14},{14,12},{16,18},{18,... | collective-permute-start | bytes 3145736 | tf_op jit(solution)/shard_map/ppermute | solution.py:758
  485.4 13.2 %collective-permute-start.36 = (f32[4,1024]{1,0:T(4,128)S(1)}, f32[4,1024]{1,0:T(4,128)S(1)}, u32[]{:S(2)}, u32[]{:S(2)}) collective-permute-start(f32[4,1024]{1,0:T(4,128)S(1)} %add.235), channel_id=1, source_target_pairs={{0,4},{2,6},{4,0},{6,2},{8,12},{10,14},{12,8},{14,10},{16,20},{18,... | collective-permute-start | bytes 49160 | tf_op jit(solution)/shard_map/ppermute | solution.py:758
  501.9 20.1 %collective-permute-start.50 = (bf16[8,768,128]{2,1,0:T(8,128)(2,1)}, bf16[8,768,128]{2,1,0:T(8,128)(2,1)}, u32[]{:S(2)}, u32[]{:S(2)}) collective-permute-start(bf16[8,768,128]{2,1,0:T(8,128)(2,1)} %constant_dynamic-update-slice_fusion.4.low), channel_id=1, source_target_pairs={{0,2},{2,0},{4,6},{6,4},{8,10},{10,8},{12,14},{14,12},{16,18},{18,... | collective-permute-start | bytes 4718600 | tf_op jit(solution)/shard_map/ppermute | solution.py:758
  (69 other events, 574.7 us)
Sparse Core Ops, SparseCore 0:
  14.6 44.2 all-gather.5
  300.3 111.9 all-gather.3

commit v4 on v3

--- a/solution.py
+++ b/solution.py
@@ -344,26 +344,27 @@
     left_ref[2] = o1c_ref[...]
 
 
-def mid_backward_kernel(
-    split, starts_ref, slots_ref, g_ref, dn3_ref, more_ref, x1_ref, x2_ref, gain_ref, q2_ref, ke_ref, ve_ref,
-    wo, wq, wc, *refs
+def cross_backward_kernel(
+    split, starts_ref, slots_ref, g_ref, dn3_ref, more_ref, x2_ref, gain_ref, q2_ref, ke_ref, ve_ref,
+    wc, *refs
 ):
     more = refs[:split]
-    right_ref, gx1_ref, do1_ref, keep_ref, send_ref, dc_ref, back_ref, do2_ref, dq2_ref = refs[split:]
-    heads, rows, _ = do1_ref.shape
+    right_ref, gx2_ref, keep_ref, send_ref, dc_ref, back_ref, do2_ref = refs[split:]
     blocks, micros, part = keep_ref.shape[1:4]
-    even = slots_ref[heads // 2] == 0
-    width = x1_ref.shape[-1]
+    tokens, width = x2_ref.shape
+    rows = tokens // micros
+    pairs = width // 128
+    even = slots_ref[pairs] == 0
     dn3 = dn3_ref[...] + more_ref[...].astype(F32)
-    back, dc = norm_back(x2_ref[...], gain_ref[2:3], dn3)
-    dc_ref[0:1, :] = dc
-    gx2 = g_ref[...].astype(F32).reshape(2 * rows, width) + back
+    back, dc_ref[...] = norm_back(x2_ref[...], gain_ref[2:3], dn3)
+    gx2 = g_ref[...].astype(F32) + back
+    gx2_ref[...] = gx2
     gx2b = gx2.astype(BF16)
     right_ref[:, 0:width] = gx2b
     times_back(back_ref, starts_ref, [(gx2b, pieces_of(wc, more, 2))])
     do2_ref[...] = back_ref[...].astype(BF16)
-    for micro in range(2):
-        for pair in range(heads // 2):
+    for micro in range(micros):
+        for pair in range(pairs):
             at = pair * 128
             span = slice(micro * rows, (micro + 1) * rows)
             q = q2_ref[span, at : at + 128]
@@ -376,7 +377,7 @@
             dp = dot_t(do, v)
             ds = (p * (dp - jnp.sum(p * dp, axis=-1, keepdims=True))).astype(BF16)
             dq = dot(ds, k)
-            dq2_ref[span, at : at + 128] = jnp.where(
+            right_ref[span, width + at : width + at + 128] = jnp.where(
                 low_lanes(rows), dq[:rows], dq[rows:]
             ).astype(BF16)
             low, high = pair_up(t_dot(ds, q), t_dot(p.astype(BF16), do))
@@ -384,14 +385,19 @@
             slot = slots_ref[pair]
             keep_ref[slot, :, micro] = kept.astype(BF16).reshape(blocks, part, 128)
             send_ref[slot, :, micro] = sent.astype(BF16).reshape(blocks, part, 128)
-    right_ref[:, width : 2 * width] = dq2_ref[...]
-    times_back(back_ref, starts_ref, [(dq2_ref[...], pieces_of(wq, more, 1))])
-    back, dc = norm_back(x1_ref[...], gain_ref[1:2], back_ref[...])
-    dc_ref[1:2, :] = dc
-    gx1 = gx2 + back
+
+
+def mid_backward_kernel(split, starts_ref, right_ref, gx2_ref, x1_ref, gain_ref, wo, wq, *refs):
+    more = refs[:split]
+    gx1_ref, low_ref, do1_ref, dc_ref, back_ref = refs[split:]
+    heads, rows, _ = do1_ref.shape
+    width = x1_ref.shape[-1]
+    times_back(back_ref, starts_ref, [(right_ref[:, width:], pieces_of(wq, more, 1))])
+    back, dc_ref[...] = norm_back(x1_ref[...], gain_ref[1:2], back_ref[...])
+    gx1 = gx2_ref[...] + back
     gx1_ref[...] = gx1
     gx1b = gx1.astype(BF16)
-    right_ref[:, 2 * width :] = gx1b
+    low_ref[...] = gx1b
     times_back(back_ref, starts_ref, [(gx1b, pieces_of(wo, more, 0))])
     for pair in range(heads // 2):
         at = pair * 128
@@ -547,7 +553,7 @@
     hidden = (own0_ref.shape[1] - width) // 3
     quarter = width // 4
     at = keep_ref.shape[1] // 2
-    core, shard, chip = where_ref[1], where_ref[2], where_ref[3]
+    core, shard, chip = where_ref[0], where_ref[1], where_ref[2]
     put_features(left_ref.at[:tokens], 0, n0_ref, g0_ref, shard, core)
     put_features(left_ref.at[tokens : 2 * tokens], 0, n1_ref, g1_ref, shard, core)
     left_ref[2 * tokens : 3 * tokens, :] = mate0_ref[:, 3 * hidden :]
@@ -573,18 +579,21 @@
 
 
 def token_weight_kernel(
-    where_ref, left_ref, left_more_ref, right_ref, right_more_ref, mine_ref, mate_ref, scratch_ref
+    masks, where_ref, left_ref, left_more_ref, right_ref, right_more_ref, last_ref, last_more_ref,
+    mine_ref, mate_ref, scratch_ref
 ):
     kinds, _, span = left_more_ref.shape
-    width = right_ref.shape[1] // kinds
-    chip, core, shard = where_ref[0], where_ref[1], where_ref[2]
+    width = last_ref.shape[1]
+    core, shard, chip = where_ref[0], where_ref[1], where_ref[2]
     half = span // 2
-    masks = range(mine_ref.shape[0])
     at = half // len(masks) * width // 128
     for kind in range(kinds):
         lanes = slice(kind * width, (kind + 1) * width)
         left = [left_ref[kind, :, aligned(shard * span, span)], left_more_ref[kind]]
-        right = [right_ref[:, lanes], right_more_ref[:, lanes]]
+        if kind < kinds - 1:
+            right = [right_ref[:, lanes], right_more_ref[:, lanes]]
+        else:
+            right = [last_ref[...], last_more_ref[...]]
         scratch_ref[...] = t_dot(jnp.concatenate(left, axis=0), jnp.concatenate(right, axis=0))
         for ref, own in ((mine_ref, core), (mate_ref, 1 - core)):
             put_all(scratch_ref, own * half, half, chip, (ref,), kind * at, width, masks)
@@ -606,8 +615,24 @@
     )(where, *operands)
 
 
-def spread_dense_kernel(where_ref, in_ref, gate_ref, up_ref, down_ref):
-    shard = where_ref[2]
+def head_rows(in_ref, at, rows, outs):
+    for pair in range(in_ref.shape[0] // 2):
+        lanes = slice(pair * 128, (pair + 1) * 128)
+        first = in_ref[2 * pair, at : at + rows, :].astype(F32)
+        second = in_ref[2 * pair + 1, at : at + rows, :].astype(F32)
+        for (out_ref, place), value in zip(outs, pair_up(first, second)):
+            out_ref[place, lanes] = value
+
+
+def head_spread(in_ref, at, q_ref, k_ref, v_ref):
+    span = q_ref.shape[0]
+    half = span // 2
+    head_rows(in_ref, at, span, ((q_ref, slice(None)), (k_ref, slice(None))))
+    head_rows(in_ref, at + span, half, ((v_ref, slice(0, half)), (v_ref, slice(half, span))))
+
+
+def first_spread_kernel(where_ref, in_ref, gate_ref, up_ref, down_ref, q_ref, k_ref, v_ref):
+    shard = where_ref[1]
     hidden = gate_ref.shape[3] // 2
     rows = gate_ref.shape[2] // 2
     at = rows * hidden // 128
@@ -623,90 +648,71 @@
                 out_ref[core, 0, place, lanes] = chunk
         chunk = take_chunk(in_ref, piece, 2 * at, tall, half)
         down_ref[chip * tall : (chip + 1) * tall, core * half : (core + 1) * half] = chunk
-
-
-def spread_dense(where, pieces, hidden, span, width):
+    head_spread(in_ref, 6 * at, q_ref, k_ref, v_ref)
+
+
+def second_spread_kernel(where_ref, in_ref, *out_refs):
+    kinds = len(out_refs) - 2
+    k_ref, v_ref = out_refs[kinds:]
+    rows, width = out_refs[0].shape[2] // 2, out_refs[0].shape[3]
+    at = rows * width // 128
+    for piece in range(4):
+        chip, core = piece // 2, piece % 2
+        for kind in range(kinds):
+            chunk = take_chunk(in_ref, piece, kind * at, rows, width)
+            out_refs[kind][core, 0, chip * rows : (chip + 1) * rows, :] = chunk
+    span = k_ref.shape[0]
+    head_rows(in_ref, kinds * at, span, ((k_ref, slice(None)), (v_ref, slice(None))))
+
+
+def spread(kernel, where, pieces, outs, length, name):
     count, total, _ = pieces.shape
     steps = count // 4
-    rows = span // count
-    out = pl.BlockSpec((2, 1, 2 * rows, 2 * hidden), lambda q, where: (0, q, 0, 0))
+    specs, shapes = [], []
+    for (rows, cols), kind in outs:
+        if kind == "core":
+            shapes.append((2, steps, rows // (2 * steps), cols))
+            block = (2, 1, rows // (2 * steps), cols)
+            specs.append(pl.BlockSpec(block, lambda q, where: (0, q, 0, 0)))
+        elif kind == "chip":
+            shapes.append((rows, cols))
+            specs.append(pl.BlockSpec((rows // steps, cols), lambda q, where: (q, 0)))
+        else:
+            shapes.append((rows, cols))
+            specs.append(pl.BlockSpec((rows, cols // steps), lambda q, where: (0, q)))
     made = pl.pallas_call(
-        spread_dense_kernel,
+        kernel,
         grid_spec=pltpu.PrefetchScalarGridSpec(
             num_scalar_prefetch=1,
             grid=(steps,),
             in_specs=[pl.BlockSpec((4, total, 128), lambda q, where: (q, 0, 0))],
-            out_specs=[out, out, pl.BlockSpec((hidden // steps, width), lambda q, where: (q, 0))],
+            out_specs=specs,
         ),
-        out_shape=[jax.ShapeDtypeStruct((2, steps, 2 * rows, 2 * hidden), F32)] * 2
-        + [jax.ShapeDtypeStruct((hidden, width), F32)],
-        compiler_params=params(),
-        cost_estimate=cost(10),
-        name="spread_dense",
+        out_shape=[jax.ShapeDtypeStruct(shape, F32) for shape in shapes],
+        compiler_params=params(),
+        cost_estimate=cost(length),
+        name=name,
     )(where, pieces)
-    return made[0].reshape(span, 2 * hidden), made[1].reshape(span, 2 * hidden), made[2]
-
-
-def spread_token_kernel(where_ref, low, high, *out_refs):
-    chip, core = where_ref[0], where_ref[1]
-    count = low.shape[0]
-    rows = out_refs[0].shape[2] // count
-    width = out_refs[0].shape[3]
-    for cores, ref in enumerate((low, high)):
-        for r in range(count):
-            place = aligned(((chip ^ r) % count) * rows, rows)
-            for kind, out_ref in enumerate(out_refs):
-                at = kind * rows * width // 128
-                out_ref[core ^ cores, 0, place, :] = take_chunk(ref, r, at, rows, width)
-
-
-def spread_token(where, low, high, span, width, kinds):
-    chips, total, _ = low.shape
-    count = chips // 2
-    rows = span // (2 * chips)
-    into = pl.BlockSpec((count, total, 128), lambda b, where: (b ^ (where[0] // count), 0, 0))
-    out = pl.BlockSpec((2, 1, count * rows, width), lambda b, where: (0, b, 0, 0))
-    made = pl.pallas_call(
-        spread_token_kernel,
-        grid_spec=pltpu.PrefetchScalarGridSpec(
-            num_scalar_prefetch=1, grid=(2,), in_specs=[into] * 2, out_specs=[out] * kinds
-        ),
-        out_shape=[jax.ShapeDtypeStruct((2, 2, count * rows, width), F32)] * kinds,
-        compiler_params=params(),
-        cost_estimate=cost(5),
-        name="spread_token",
-    )(where, low, high)
-    return [array.reshape(span, width) for array in made]
-
-
-def picked_head(pos_ref, low, high, head):
-    place = pos_ref[head]
-    count = low.shape[0]
-    return jnp.where(
-        place < count, low[place % count].astype(F32), high[place % count].astype(F32)
-    )
-
-
-def head_spread_kernel(pos_ref, low_ref, high_ref, q_ref, k_ref, v_ref):
-    span, width = q_ref.shape
-    half = span // 2
-    for pair in range(width // 128):
-        at = pair * 128
-        first = picked_head(pos_ref, low_ref, high_ref, 2 * pair)
-        second = picked_head(pos_ref, low_ref, high_ref, 2 * pair + 1)
-        low, high = pair_up(first, second)
-        q_ref[:, at : at + 128] = low[:span]
-        k_ref[:, at : at + 128] = high[:span]
-        v_ref[:half, at : at + 128] = low[span:]
-        v_ref[half:, at : at + 128] = high[span:]
-
-
-def cross_head_spread_kernel(pos_ref, low_ref, high_ref, k_ref, v_ref):
-    for pair in range(k_ref.shape[1] // 128):
-        at = pair * 128
-        first = picked_head(pos_ref, low_ref, high_ref, 2 * pair)
-        second = picked_head(pos_ref, low_ref, high_ref, 2 * pair + 1)
-        k_ref[:, at : at + 128], v_ref[:, at : at + 128] = pair_up(first, second)
+    return [array.reshape(shape) for array, (shape, _) in zip(made, outs)]
+
+
+def plain_head_kernel(in_ref, *out_refs):
+    span = out_refs[0].shape[0]
+    if len(out_refs) == 3:
+        head_spread(in_ref, 0, *out_refs)
+    else:
+        head_rows(in_ref, 0, span, [(out_ref, slice(None)) for out_ref in out_refs])
+
+
+def plain_head_spread(pieces, span, width, kinds):
+    return pl.pallas_call(
+        plain_head_kernel,
+        out_shape=[jax.ShapeDtypeStruct((span, width), F32)] * kinds,
+        in_specs=[vmem()],
+        out_specs=[vmem()] * kinds,
+        compiler_params=params(),
+        name="plain_head_spread",
+    )(pieces)
 
 
 def per_device(
@@ -748,11 +754,11 @@
     x_order, z_order = chip_bits, chip_bits[1:] + chip_bits[:1]
     paired = fs == 2
     chunked = paired and half % (16 * chips) == 0 and hidden % (16 * chips) == 0
-    chunked = chunked and hidden % 128 == 0
-
-    def chip_of(j, order=x_order):
-        last = len(order) - 1
-        return sum(((j // bit) % 2) << (last - place) for place, bit in enumerate(order))
+    chunked = chunked and hidden % 128 == 0 and dp == heads and dp % 4 == 0
+
+    def chip_of(j):
+        last = len(x_order) - 1
+        return sum(((j // bit) % 2) << (last - place) for place, bit in enumerate(x_order))
 
     def swap_dp(values, bit):
         return lax.ppermute(values, "dp", [(j, j ^ bit) for j in range(dp)])
@@ -769,6 +775,13 @@
     def both_halves(sent):
         got = swap_fs(sent)
         return got, swap_dp(got, 1)
+
+    def quarter(bit):
+        return 2 * ((me // bit) % 2) + core
+
+    def quarter_starts(bit):
+        rows = [(1 - shard) * span + (quarter(bit) ^ more) * (half // 2) for more in (0, 2, 1, 3)]
+        return jnp.stack([shard * span] + rows).astype(jnp.int32)
 
     def gather_rows(values):
         return [lax.all_gather(w, "fsdp", axis=0, tiled=True) for w in values]
@@ -787,11 +800,6 @@
                 sent = after(sent, marks[place])
             total = total + swap_dp(sent, bit).astype(F32)
         return total.astype(BF16)
-
-    def gather_chips(values, order=x_order):
-        for bit in reversed(order):
-            values = jnp.concatenate([values, swap_dp(values, bit)], axis=0)
-        return values, swap_dp(values, 1)
 
     x, g, e = inputs[:, 0], cotangent[:, 0], encoded[:, 0]
 
@@ -827,26 +835,41 @@
             jnp.concatenate([head_got, head_pack]),
         )
         other = (1 - shard) * span
-        starts = jnp.stack([shard * span, other + core * half, other + (1 - core) * half])
-        starts = starts.astype(jnp.int32)
+        half_starts = jnp.stack([shard * span, other + core * half, other + (1 - core) * half])
+        half_starts = half_starts.astype(jnp.int32)
+        near_bit, dense_bit = chip_bits[0], chip_bits[1]
+        starts = quarter_starts(near_bit)
         kv_own = (key_cross, value_cross)
         near_own = (output_self, query_cross, output_cross)
-        near_got = swap_fs(after(half_rows(near_own + kv_own), small_got, head_got))
+        near_sent = jnp.stack(
+            [
+                lax.dynamic_slice_in_dim(w, quarter(near_bit) * (half // 2), half // 2, axis=0)
+                for w in near_own + kv_own
+            ]
+        )
+        near_got = swap_fs(after(near_sent, small_got, head_got))
+        near_far = swap_dp(near_got, near_bit)
         theirs = jnp.stack(
             [
-                lax.dynamic_slice(w, (core * half, (1 - shard) * hidden), (half, hidden))
+                lax.dynamic_slice(
+                    w,
+                    (quarter(dense_bit) * (half // 2), (1 - shard) * hidden),
+                    (half // 2, hidden),
+                )
                 for w in (dense_gate, dense_up)
             ]
         )
+        dense_got = swap_fs(after(theirs, near_got))
         dense_own = (dense_gate, dense_up)
         which = jnp.stack([shard, core]).astype(jnp.int32)
-        dense_starts = jnp.concatenate([starts, which])
+        dense_starts = jnp.concatenate([quarter_starts(dense_bit), which])
     else:
         gains = lax.all_gather(gains, "fsdp", axis=1, tiled=True)
         bias_all = lax.all_gather(position_bias, "fsdp", axis=0, tiled=True)
         kv_own, kv_more = gather_rows((key_cross, value_cross)), ()
         near_own, near_more = gather_rows((output_self, query_cross, output_cross)), ()
         first_own, first_more = gather_rows((query_self, key_self, value_self)), ()
+        half_starts = jnp.zeros((1,), jnp.int32)
         head_whole = jnp.concatenate([own_head(w) for w in first_own], axis=1)
         dense_own = [
             lax.all_to_all(w, "fsdp", 1, 0, tiled=True) for w in (dense_gate, dense_up)
@@ -885,8 +908,9 @@
     o1_heads = lax.all_to_all(mixed.reshape(dp, rows, 128), "dp", 0, 0, tiled=True)[::copies]
 
     if paired:
-        near_more = kv_more = (near_got, swap_dp(after(near_got, mixed), 1))
-        dense_got = swap_fs(after(theirs, near_got, mixed))
+        near_more = (near_got, near_far, swap_dp(near_got, 1), swap_dp(after(near_far, mixed), 1))
+        kv_more = near_more
+        dense_far = swap_dp(after(dense_got, mixed), dense_bit)
     ke, ve = cross_kv(starts, e_all, *kv_own, kv_more)
 
     row32 = jax.ShapeDtypeStruct((tokens, width), F32)
@@ -905,7 +929,12 @@
     )(starts, o1_heads, x, gains, ke, ve, *near_own, *near_more)
 
     if paired:
-        dense_more = (dense_got, swap_dp(after(dense_got, n3), 1))
+        dense_more = (
+            dense_got,
+            dense_far,
+            swap_dp(after(dense_got, o1_heads), 1),
+            swap_dp(after(dense_far, o1_heads), 1),
+        )
         g_rows = g.reshape(tokens, width)
         g_got = swap_fs(after(g_rows, dense_got))
         n_got = swap_fs(n3)
@@ -937,7 +966,7 @@
         outputs = (x2 + dense_out).astype(BF16)
 
     if chunked:
-        where = jnp.stack([chip_of(me), core, shard, me // 2]).astype(jnp.int32)
+        where = jnp.stack([core, shard, me // 2]).astype(jnp.int32)
         masks = [
             [
                 sum(((slot >> (len(order) - 1 - at)) & 1) * (bit // 2) for at, bit in enumerate(order))
@@ -966,42 +995,53 @@
         own_got, down_got = swap_dp(own_sent, z_order[0]), swap_dp(down_sent, x_order[0])
         far_got, far_kept = swap_fs(far_sent), swap_fs(far_kept)
 
-    straight = chunked and copies == 1
+    straight = chunked
     if straight:
         slots = jnp.append(chip_of(me ^ (2 * jnp.arange(heads // 2))), core).astype(jnp.int32)
     else:
         slots = jnp.append(jnp.arange(heads // 2), 0).astype(jnp.int32)
-    right, gx1, do1_heads, dkv_kept, dkv_sent, dc_two = pl.pallas_call(
+    g_rows = g.reshape(tokens, width)
+    right, gx2, dkv_kept, dkv_sent, dc_dense = pl.pallas_call(
+        functools.partial(cross_backward_kernel, len(near_more)),
+        out_shape=[
+            jax.ShapeDtypeStruct((tokens, 2 * width), BF16),
+            row32,
+            jax.ShapeDtypeStruct((heads // 2, dp, micro_count, part, 128), BF16),
+            jax.ShapeDtypeStruct((heads // 2, dp, micro_count, part, 128), BF16),
+            jax.ShapeDtypeStruct((1, width), F32),
+        ],
+        in_specs=[smem()] * 2 + [vmem()] * (9 + len(near_more)),
+        out_specs=[vmem()] * 5,
+        scratch_shapes=[pltpu.VMEM((tokens, width), F32), pltpu.VMEM((tokens, width), BF16)],
+        compiler_params=params(),
+        cost_estimate=cost(15),
+        name="cross_backward",
+    )(starts, slots, g_rows, dn3, dn3_more, x2, gains, q2, ke, ve, near_own[2], *near_more)
+    if chunked:
+        gx2 = after(gx2, own_got, down_got, far_got)
+    gx1, last, do1_heads, dc_cross = pl.pallas_call(
         functools.partial(mid_backward_kernel, len(near_more)),
         out_shape=[
-            jax.ShapeDtypeStruct((tokens, 3 * width), BF16),
             row32,
+            row16,
             jax.ShapeDtypeStruct((heads, rows, 128), BF16),
-            jax.ShapeDtypeStruct((heads // 2, dp, micro_count, part, 128), BF16),
-            jax.ShapeDtypeStruct((heads // 2, dp, micro_count, part, 128), BF16),
-            jax.ShapeDtypeStruct((2, width), F32),
+            jax.ShapeDtypeStruct((1, width), F32),
         ],
-        in_specs=[smem()] * 2 + [vmem()] * (12 + len(near_more)),
-        out_specs=[vmem()] * 6,
-        scratch_shapes=[
-            pltpu.VMEM((tokens, width), F32),
-            pltpu.VMEM((tokens, width), BF16),
-            pltpu.VMEM((tokens, width), BF16),
-        ],
-        compiler_params=params(),
-        cost_estimate=cost(16),
+        in_specs=[smem()] + [vmem()] * (6 + len(near_more)),
+        out_specs=[vmem()] * 4,
+        scratch_shapes=[pltpu.VMEM((tokens, width), F32)],
+        compiler_params=params(),
+        cost_estimate=cost(6),
         name="mid_backward",
-    )(starts, slots, g, dn3, dn3_more, x1, x2, gains, q2, ke, ve, *near_own, *near_more)
+    )(starts, right, gx2, x1, gains, *near_own[:2], *near_more)
     do1 = lax.all_to_all(
         jnp.repeat(do1_heads, copies, axis=0) if copies > 1 else do1_heads, "dp", 0, 0, tiled=True
     ).reshape(length, 128)
 
     if chunked:
-        right_got = swap_fs(right)
+        right_got, last_got = swap_fs(right), swap_fs(last)
         if straight:
             dkv_got = swap_dp(dkv_sent, 1)
-            do1 = after(do1, dkv_got)
-        do1 = after(do1, own_got, down_got, far_got)
 
     dqkv, table_grad = pl.pallas_call(
         self_backward_kernel,
@@ -1017,7 +1057,7 @@
         name="self_backward",
     )(qkv, do1, table, doc_row, doc_col)
     if chunked:
-        dqkv = after(dqkv, right_got, far_kept)
+        dqkv = after(dqkv, right_got, last_got, far_kept, dkv_got)
     head_grad = pl.pallas_call(
         head_weight_kernel,
         out_shape=jax.ShapeDtypeStruct((fs, span * 3 // 2, 128), BF16),
@@ -1037,9 +1077,9 @@
     head_sum = sum_shards(head_grad)
     if chunked:
         token_kept, token_sent = chunk_weights(
-            token_weight_kernel,
+            functools.partial(token_weight_kernel, masks[0]),
             where,
-            (after(left, head_grad), left_got, right, right_got),
+            (after(left, head_grad), left_got, right, right_got, last, last_got),
             (3 * half // chips * width // 128,),
             chips,
             [pltpu.VMEM((span, width), F32)],
@@ -1047,20 +1087,6 @@
             "token_weight",
         )
         token_got = swap_dp(token_sent, 1)
-        head_sum = after(head_sum, token_kept)
-
-    relative = me ^ (jnp.arange(heads, dtype=jnp.int32) * copies)
-    head_places = (relative % 2) * chips + chip_of(relative)
-    grad_query_self, grad_key_self, grad_value_self = pl.pallas_call(
-        head_spread_kernel,
-        out_shape=[jax.ShapeDtypeStruct((span, width), F32)] * 3,
-        in_specs=[smem(), vmem(), vmem()],
-        out_specs=[vmem()] * 3,
-        compiler_params=params(),
-        cost_estimate=cost(6),
-        name="head_spread",
-    )(head_places, *gather_chips(head_sum))
-
     if paired:
         first_own = (query_self, key_self, value_self)
         first_more = both_halves(after(half_rows(first_own), head_sum))
@@ -1079,7 +1105,7 @@
         compiler_params=params(),
         cost_estimate=cost(7),
         name="input_grad",
-    )(starts, own_d, x, gains, gx1, *first_own, *first_more)
+    )(half_starts, own_d, x, gains, gx1, *first_own, *first_more)
 
     if straight:
         dkv = reduce_chips(dkv_kept, dkv_got, [1] + x_order).reshape(-1, 128)
@@ -1103,15 +1129,6 @@
         name="cross_head_weight",
     )(e_all, dkv)
     cross_sum = sum_shards(cross_grad)
-    grad_key_cross, grad_value_cross = pl.pallas_call(
-        cross_head_spread_kernel,
-        out_shape=[jax.ShapeDtypeStruct((span, width), F32)] * 2,
-        in_specs=[smem(), vmem(), vmem()],
-        out_specs=[vmem()] * 2,
-        compiler_params=params(),
-        cost_estimate=cost(4),
-        name="cross_head_spread",
-    )(head_places, *gather_chips(cross_sum))
     own_dkv = dkv.reshape(dp, micro_count * part, 128)
     own_dkv = lax.all_to_all(own_dkv, "dp", 0, 0, tiled=True)[::copies]
     grad_encoded = pl.pallas_call(
@@ -1126,23 +1143,55 @@
     )(starts, own_dkv, *kv_own, *kv_more)
 
     if chunked:
-        sums = (
-            reduce_chips(own_kept, own_got, z_order, (right, token_kept)),
-            reduce_chips(down_kept, down_got, x_order, (right, token_kept)),
-            reduce_chips(
-                far_kept, swap_dp(after(far_got, right), x_order[0]), x_order, (dqkv, token_kept)
-            ),
-        )
-        pieces = lax.all_gather(jnp.concatenate(sums, axis=1), "dp", axis=0, tiled=True)
-        grad_dense_gate, grad_dense_up, grad_dense_down = spread_dense(
-            where, pieces, hidden, span, width
-        )
-        token_sum = after(reduce_chips(token_kept, token_got, [1] + x_order), cross_grad)
-        token_low, token_high = gather_chips(token_sum)
-        grad_output_cross, grad_query_cross, grad_output_self = spread_token(
-            where, token_low, token_high, span, width, 3
+        own_sum = reduce_chips(own_kept, own_got, z_order, (do1_heads, dqkv))
+        down_sum = reduce_chips(down_kept, down_got, x_order, (do1_heads, dqkv))
+        far_got = swap_dp(after(far_got, do1_heads), x_order[0])
+        far_sum = reduce_chips(far_kept, far_got, x_order, (dqkv, head_grad))
+        token_sum = reduce_chips(token_kept, token_got, [1] + x_order)
+
+        def gather(*values):
+            return lax.all_gather(jnp.concatenate(values, axis=1), "dp", axis=0, tiled=True)
+
+        square, wide = (span, width), (span, fs * hidden)
+        first_pieces = gather(own_sum, down_sum, far_sum, head_sum)
+        (
+            grad_dense_gate,
+            grad_dense_up,
+            grad_dense_down,
+            grad_query_self,
+            grad_key_self,
+            grad_value_self,
+        ) = spread(
+            first_spread_kernel,
+            where,
+            first_pieces,
+            [(wide, "core"), (wide, "core"), ((hidden, width), "chip")] + [(square, "head")] * 3,
+            12,
+            "first_spread",
+        )
+        (
+            grad_output_cross,
+            grad_query_cross,
+            grad_output_self,
+            grad_key_cross,
+            grad_value_cross,
+        ) = spread(
+            second_spread_kernel,
+            where,
+            gather(after(token_sum, first_pieces), cross_sum),
+            [(square, "core")] * 3 + [(square, "head")] * 2,
+            8,
+            "second_spread",
         )
     else:
+
+        def all_heads(values, kinds):
+            pieces = lax.all_gather(values, "dp", axis=0, tiled=True)[::copies]
+            return plain_head_spread(pieces, span, width, kinds)
+
+        grad_query_self, grad_key_self, grad_value_self = all_heads(head_sum, 3)
+        grad_key_cross, grad_value_cross = all_heads(cross_sum, 2)
+        right = jnp.concatenate([right, last], axis=1)
 
         def over_dp(values):
             return lax.psum(values.astype(BF16), "dp").astype(F32)
@@ -1174,7 +1223,7 @@
     column = (jnp.arange(heads) == head) & (me % copies == 0)
     bias_row = jnp.where(column[None, :], table_sums[:, None], 0.0).reshape(1, -1)
     bias_row = jnp.pad(bias_row, ((0, 0), (0, width - bias_row.shape[1])))
-    sums = jnp.concatenate([dc_one, dc_two, bias_row], axis=0)
+    sums = jnp.concatenate([dc_one, dc_dense, dc_cross, bias_row], axis=0)
     if paired:
         sums = sums + swap_fs(sums)
         for bit in [1] + chip_bits:

time: 554 us -> 562 us (1.014)
  waiting for transfers between devices: 216 us -> 241 us
  starting transfers between devices: 93.6 us -> 85.3 us
  local copies, waits for them, and re-layouts: 43.1 us -> 37 us
    ppermute x16 -> x17, waiting for transfers between devices: 65.9 us -> 46.2 us  [swap_fs(): return lax.ppermute(values, 'fsdp', [(j, 1 - j) for j in range(2)])]
    all_to_all x1, waiting for transfers between devices: 0.01 us -> 16.7 us  [per_device(): lax.all_to_all(dqkv.reshape(dp, rows, 384), 'dp', 0, 0, tiled=True)]
    all_to_all x1, waiting for transfers between devices: 0.01 us -> 15.2 us  [per_device(): lax.all_to_all(mixed.reshape(dp, rows, 128), 'dp', 0, 0, tiled=True)]
    pallas_call x1, Pallas kernels: 19.4 us -> 6.12 us  [per_device(): pl.pallas_call(functools.partial(mid_backward_kernel, len(near_more)), ou...]
    pallas_call x4 -> x3, Pallas kernels: 25.6 us -> 38 us  [the longest x2 21.1 us: spread(): pl.pallas_call(kernel, grid_spec=pltpu.PrefetchScalarGridSpec(num_scalar_...]
    ppermute x47 -> x39, waiting for transfers between devices: 150 us -> 162 us  [swap_dp(): return lax.ppermute(values, 'dp', [(j, j ^ bit) for j in range(dp)])]
    ppermute x47 -> x39, starting transfers between devices: 55.9 us -> 47.2 us  [swap_dp(): return lax.ppermute(values, 'dp', [(j, j ^ bit) for j in range(dp)])]
    unnamed x107 -> x83, local copies, waits for them, and re-layouts: 15.8 us -> 14 us
  transfers between devices with their start and end apart: 69 -> 63, of which waited for: 24 -> 25; matrix products, arithmetic and copies ran while one was open for 10% -> 9% of each run, Pallas kernels for 19% -> 25%
where the time goes in v4:
time: 562 us; the launch traced here: 552 us
  waiting for transfers between devices  241 us (43%)
  Pallas kernels  155 us (28%)
  starting transfers between devices  85.3 us (15%)
  local copies, waits for them, and re-layouts  37 us (7%)
  other arithmetic  19.1 us (3%)
  between operations  15.2 us (3%)
    ppermute x39, waiting for transfers between devices, swap_dp(): return lax.ppermute(values, 'dp', [(j, j ^ bit) for j in range(dp)])  162 us
    ppermute x39, starting transfers between devices, swap_dp(): return lax.ppermute(values, 'dp', [(j, j ^ bit) for j in range(dp)])  47.2 us
    ppermute x17, waiting for transfers between devices, swap_fs(): return lax.ppermute(values, 'fsdp', [(j, 1 - j) for j in range(2)])  46.2 us
    pallas_call x2, Pallas kernels, spread(): pl.pallas_call(kernel, grid_spec=pltpu.PrefetchScalarGridSpec(num_scalar_...  21.1 us
    pallas_call x2, Pallas kernels, dense_layer(): pl.pallas_call(functools.partial(dense_kernel, len(more)), grid_spec=pltp...  19.9 us
    ppermute x17, starting transfers between devices, swap_fs(): return lax.ppermute(values, 'fsdp', [(j, 1 - j) for j in range(2)])  19.6 us
    pallas_call x1, Pallas kernels, per_device(): pl.pallas_call(functools.partial(cross_backward_kernel, len(near_more)),...  16.9 us
    all_to_all x1, waiting for transfers between devices, per_device(): lax.all_to_all(dqkv.reshape(dp, rows, 384), 'dp', 0, 0, tiled=True)  16.7 us
  transfers between devices with their start and end apart: 63, of which 25 were waited for; matrix products, arithmetic and copies ran while one was open for 9% of the time, Pallas kernels for 25%

profile of v4, /device:TPU:0, one launch (start us, length us, event | category | flops | bytes accessed | tf_op | source)
XLA Modules:
  0.0 552.3 jit_solution(4762284774892093650)
XLA Ops:
  7.2 4.1 collective-permute-start
  39.8 3.0 collective-permute-done.2
  43.9 4.4 bias_table.1.refs_6_.table_ref
  48.6 9.3 %collective-permute-done.5 = bf16[2,64,1024]{2,1,0:T(8,128)(2,1)S(1)} collective-permute-done((bf16[2,64,1024]{2,1,0:T(8,128)(2,1)S(1)}, bf16[2,64,1024]{2,1,0:T(8,128)(2,1)S(1)}, u32[]{:S(2)}, u32[]{:S(2)}) %collective-permute-start.5) | collective-permute-done | bytes 262176 | tf_op jit(solution)/shard_map/ppermute | solution.py:764
  57.9 2.8 collective-permute-done.6
  62.7 2.7 collective-permute-done.11.refs_0_
  70.8 11.4 %self_forward.1 = (bf16[16,2,64,1024]{3,2,1,0:T(8,128)(2,1)}, bf16[1024,384]{1,0:T(8,128)(2,1)}, bf16[1024,128]{1,0:T(8,128)(2,1)}) custom-call(s32[16]{0:T(128)} %broadcast_xor_fusion.source_ref, bf16[4,2,64,1024]{3,2,1,0:T(8,128)(2,1)} %copy-done.4, bf16[4,2,64,1024]{3,2,1,0:T(8,128)(2,1)} %copy-done.5, bf16[4,2,64,1024]{3,2,1,0:T(8,128)(2,1)} %copy-done.30, ...), custom_call_target="tpu_custom_call" | custom-call | flops 13799999488 | bytes 44280000 | tf_op jit(solution)/shard_map/self_forward/pallas_call | solution.py:895
  82.3 11.8 %collective-permute-done.12.refs_1_ = bf16[5,128,1024]{2,1,0:T(8,128)(2,1)S(1)} collective-permute-done((bf16[5,128,1024]{2,1,0:T(8,128)(2,1)}, bf16[5,128,1024]{2,1,0:T(8,128)(2,1)S(1)}, u32[]{:S(2)}, u32[]{:S(2)}) %collective-permute-start.12) | collective-permute-done | bytes 1310752 | tf_op jit(solution)/shard_map/ppermute | solution.py:764
  95.8 3.5 all-to-all-start
  101.6 15.2 %all-to-all-done.o1_ref = bf16[16,64,128]{2,1,0:T(8,128)(2,1)S(1)} async-done(((bf16[16,64,128]{2,1,0:T(8,128)(2,1)}), bf16[16,64,128]{2,1,0:T(8,128)(2,1)S(1)}, u32[]{:S(2)}, u32[]{:S(2)}) %all-to-all-start) | async-done | bytes 262176 | tf_op jit(solution)/shard_map/all_to_all | solution.py:908
  117.3 11.9 %cross_kv.1 = (bf16[2,512,1024]{2,1,0:T(8,128)(2,1)}, bf16[2,512,1024]{2,1,0:T(8,128)(2,1)}) custom-call(s32[5]{0:T(128)} %stack.135.starts_ref, bf16[16,2,32,1024]{3,2,1,0:T(8,128)(2,1)} %bitcast.100, bf16[512,1024]{1,0:T(8,128)(2,1)} %wk.3, bf16[512,1024]{1,0:T(8,128)(2,1)} %wv.3, bf16[5,128,1024]{2,1,0:T(8,128)(2,1)} %collective-permute-done.11.refs_0_, ...), custom_call_target="tpu_custom_call" | custom-call | flops 9200000000 | bytes 29520000 | tf_op jit(solution)/shard_map/cross_kv/pallas_call | solution.py:297
  129.2 13.2 %mid_forward.1 = (bf16[3,128,1024]{2,1,0:T(8,128)(2,1)}, f32[128,1024]{1,0:T(8,128)}, bf16[128,1024]{1,0:T(8,128)(2,1)}, f32[128,1024]{1,0:T(8,128)}, bf16[128,1024]{1,0:T(8,128)(2,1)}) custom-call(s32[5]{0:T(128)} %stack.135.starts_ref, bf16[16,64,128]{2,1,0:T(8,128)(2,1)} %copy-done.15, bf16[2,64,1024]{2,1,0:T(8,128)(2,1)} %bitcast.83, ...), custom_call_target="tpu_custom_call" | custom-call | flops 13799999488 | bytes 44280000 | tf_op jit(solution)/shard_map/mid_forward/pallas_call | solution.py:918
  143.4 2.8 reshape.117
  148.2 9.9 %dense_layer.2 = (bf16[128,5248]{1,0:T(8,128)(2,1)}, f32[128,1024]{1,0:T(8,128)}, bf16[128,1024]{1,0:T(8,128)(2,1)}, f32[128,1024]{1,0:T(8,128)}, bf16[128,1024]{1,0:T(8,128)(2,1)}) custom-call(s32[7]{0:T(128)} %concatenate.44.starts_ref, bf16[128,1024]{1,0:T(8,128)(2,1)} %get-tuple-element.112.n_ref.n0_ref, bf16[128,1024]{1,0:T(8,128)(2,1)} %bitcast.29.g_ref.g0_ref, ...), custom_call_target="tpu_custom_call" | custom-call | flops 14949999616 | bytes 47970000 | tf_op jit(solution)/shard_map/dense_layer/pallas_call | solution.py:505
  160.1 9.9 %dense_layer.3 = (bf16[128,5248]{1,0:T(8,128)(2,1)}, f32[128,1024]{1,0:T(8,128)}, bf16[128,1024]{1,0:T(8,128)(2,1)}, f32[128,1024]{1,0:T(8,128)}, bf16[128,1024]{1,0:T(8,128)(2,1)}) custom-call(s32[7]{0:T(128)} %concatenate.44.starts_ref, bf16[128,1024]{1,0:T(8,128)(2,1)} %copy-done.36, bf16[128,1024]{1,0:T(8,128)(2,1)} %copy-done.35, bf16[512,2816]{1,0:T(8,128)(2,1)} %wg.3, ...), custom_call_target="tpu_custom_call" | custom-call | flops 14949999616 | bytes 47970000 | tf_op jit(solution)/shard_map/dense_layer/pallas_call | solution.py:505
  172.3 6.7 %collective-permute-done.22.more_ref = bf16[128,1024]{1,0:T(8,128)(2,1)S(1)} collective-permute-done((bf16[128,1024]{1,0:T(8,128)(2,1)}, bf16[128,1024]{1,0:T(8,128)(2,1)S(1)}, u32[]{:S(2)}, u32[]{:S(2)}) %collective-permute-start.22) | collective-permute-done | bytes 262176 | tf_op jit(solution)/shard_map/ppermute | solution.py:767
  181.2 7.1 %dense_weight.1 = (bf16[4,704,128]{2,1,0:T(8,128)(2,1)}, bf16[4,704,128]{2,1,0:T(8,128)(2,1)}, bf16[4,704,128]{2,1,0:T(8,128)(2,1)}, bf16[4,704,128]{2,1,0:T(8,1...) custom-call(s32[3]{0:T(128)} %pad_add_fusion.1.where_ref, ...), custom_call_target="tpu_custom_call" | custom-call | flops 8049999872 | bytes 25830000 | tf_op jit(solution)/shard_map/dense_weight/pallas_call | solution.py:606
  191.4 16.9 %cross_backward.1 = (bf16[128,2048]{1,0:T(8,128)(2,1)}, f32[128,1024]{1,0:T(8,128)}, bf16[8,16,2,32,128]{4,3,2,1,0:T(8,128)(2,1)}, bf16[8,16,2,32,128]{4,3,2,1,0:T(8,128)(2,1)}, f32[1,1024]{1,0:T(1,128)}) custom-call(s32[5]{0:T(128)} %stack.135.starts_ref, s32[9]{0:T(128)} %pad_add_fusion.slots_ref, bf16[128,1024]{1,0:T(8,128)(2,1)} %bitcast.29.g_ref.g0_ref, ...), custom_call_target="tpu_custom_call" | custom-call | flops 17250000896 | bytes 55350000 | tf_op jit(solution)/shard_map/cross_backward/pallas_call | solution.py:1004
  209.3 6.1 %mid_backward.1 = (f32[128,1024]{1,0:T(8,128)}, bf16[128,1024]{1,0:T(8,128)(2,1)}, bf16[16,64,128]{2,1,0:T(8,128)(2,1)}, f32[1,1024]{1,0:T(1,128)}) custom-call(s32[5]{0:T(128)} %stack.135.starts_ref, bf16[128,2048]{1,0:T(8,128)(2,1)} %get-tuple-element.118.right_ref, f32[128,1024]{1,0:T(8,128)} %get-tuple-element.122.gx2_ref, ...), custom_call_target="tpu_custom_call" | custom-call | flops 6899999744 | bytes 22140000 | tf_op jit(solution)/shard_map/mid_backward/pallas_call | solution.py:1022
  221.9 3.5 all-to-all-start.1
  225.7 8.9 %collective-permute-done.46 = bf16[2,704,128]{2,1,0:T(8,128)(2,1)} collective-permute-done((bf16[2,704,128]{2,1,0:T(8,128)(2,1)}, bf16[2,704,128]{2,1,0:T(8,128)(2,1)}, u32[]{:S(2)}, u32[]{:S(2)}) %collective-permute-start.46) | collective-permute-done | bytes 360480 | tf_op jit(solution)/shard_map/ppermute | solution.py:764
  242.1 9.6 %self_backward.1 = (bf16[1024,384]{1,0:T(8,128)(2,1)}, f32[256,1024]{1,0:T(8,128)}) custom-call(bf16[1024,384]{1,0:T(8,128)(2,1)} %get-tuple-element.110.qkv_ref, bf16[1024,128]{1,0:T(8,128)(2,1)} %bitcast.78, f32[256,1024]{1,0:T(8,128)} %bias_table.1.refs_6_.table_ref, s32[2,1024]{1,0:T(2,128)} %reshape.115.refs_7_.doc_row_ref, ...), custom_call_target="tpu_custom_call" | custom-call | flops 11500000256 | bytes 36900000 | tf_op jit(solution)/shard_map/self_backward/pallas_call | solution.py:1046
  251.7 3.8 collective-permute-done.48
  257.1 5.7 %head_weight.1 = bf16[2,768,128]{2,1,0:T(8,128)(2,1)} custom-call(bf16[16,2,64,1024]{3,2,1,0:T(8,128)(2,1)} %get-tuple-element.109.n_ref, bf16[1024,384]{1,0:T(8,128)(2,1)} %get-tuple-element.129.d_ref), custom_call_target="tpu_custom_call" | custom-call | flops 6899999744 | bytes 22140000 | tf_op jit(solution)/shard_map/head_weight/pallas_call | solution.py:1061
  264.9 5.9 %collective-permute-start.49 = (bf16[2,704,128]{2,1,0:T(8,128)(2,1)S(1)}, bf16[2,704,128]{2,1,0:T(8,128)(2,1)S(1)}, u32[]{:S(2)}, u32[]{:S(2)}) collective-permute-start(bf16[2,704,128]{2,1,0:T(8,128)(2,1)S(1)} %slice.244), channel_id=1, source_target_pairs={{0,8},{2,10},{4,12},{6,14},{8,0},{10,2},{12,4},{14,6},{16,24},{18,... | collective-permute-start | bytes 1081352 | tf_op jit(solution)/shard_map/ppermute | solution.py:764
  271.7 4.6 collective-permute-done.45
  277.8 6.3 %collective-permute-done.50 = bf16[1,704,128]{2,1,0:T(8,128)(2,1)S(1)} collective-permute-done((bf16[1,704,128]{2,1,0:T(8,128)(2,1)S(1)}, bf16[1,704,128]{2,1,0:T(8,128)(2,1)S(1)}, u32[]{:S(2)}, u32[]{:S(2)}) %collective-permute-start.50) | collective-permute-done | bytes 180256 | tf_op jit(solution)/shard_map/ppermute | solution.py:764
  285.4 4.9 token_weight.1
  290.3 2.6 convert_add_fusion
  294.0 31.8 %collective-permute-done.36 = bf16[4,16,2,32,128]{4,3,2,1,0:T(8,128)(2,1)S(1)} collective-permute-done((bf16[4,16,2,32,128]{4,3,2,1,0:T(8,128)(2,1)S(1)}, bf16[4,16,2,32,128]{4,3,2,1,0:T(8,128)(2,1)S(1)}, u32[]{:S(2)}, u32[]{:S(2)}) %collective-permute-start.36) | collective-permute-done | bytes 1048608 | tf_op jit(solution)/shard_map/ppermute | solution.py:764
  329.0 33.6 %collective-permute-done.37 = bf16[2,16,2,32,128]{4,3,2,1,0:T(8,128)(2,1)S(1)} collective-permute-done((bf16[2,16,2,32,128]{4,3,2,1,0:T(8,128)(2,1)S(1)}, bf16[2,16,2,32,128]{4,3,2,1,0:T(8,128)(2,1)S(1)}, u32[]{:S(2)}, u32[]{:S(2)}) %collective-permute-start.37) | collective-permute-done | bytes 524320 | tf_op jit(solution)/shard_map/ppermute | solution.py:764
  362.8 2.3 collective-permute-start.38
  365.1 18.0 %collective-permute-done.38 = bf16[1,16,2,32,128]{4,3,2,1,0:T(8,128)(2,1)S(1)} collective-permute-done((bf16[1,16,2,32,128]{4,3,2,1,0:T(8,128)(2,1)S(1)}, bf16[1,16,2,32,128]{4,3,2,1,0:T(8,128)(2,1)S(1)}, u32[]{:S(2)}, u32[]{:S(2)}) %collective-permute-start.38) | collective-permute-done | bytes 262176 | tf_op jit(solution)/shard_map/ppermute | solution.py:764
  384.1 6.4 %collective-permute-start.53 = (bf16[2,768,128]{2,1,0:T(8,128)(2,1)S(1)}, bf16[2,768,128]{2,1,0:T(8,128)(2,1)S(1)}, u32[]{:S(2)}, u32[]{:S(2)}) collective-permute-start(bf16[2,768,128]{2,1,0:T(8,128)(2,1)S(1)} %slice.243), channel_id=1, source_target_pairs={{0,8},{2,10},{4,12},{6,14},{8,0},{10,2},{12,4},{14,6},{16,24},{18,... | collective-permute-start | bytes 1179656 | tf_op jit(solution)/shard_map/ppermute | solution.py:764
  390.5 3.1 cross_head_weight.1
  395.9 11.3 %collective-permute-done.53 = bf16[2,768,128]{2,1,0:T(8,128)(2,1)S(1)} collective-permute-done((bf16[2,768,128]{2,1,0:T(8,128)(2,1)S(1)}, bf16[2,768,128]{2,1,0:T(8,128)(2,1)S(1)}, u32[]{:S(2)}, u32[]{:S(2)}) %collective-permute-start.53) | collective-permute-done | bytes 393248 | tf_op jit(solution)/shard_map/ppermute | solution.py:764
  409.1 10.2 %collective-permute-done.54 = bf16[1,768,128]{2,1,0:T(8,128)(2,1)S(1)} collective-permute-done((bf16[1,768,128]{2,1,0:T(8,128)(2,1)S(1)}, bf16[1,768,128]{2,1,0:T(8,128)(2,1)S(1)}, u32[]{:S(2)}, u32[]{:S(2)}) %collective-permute-start.54) | collective-permute-done | bytes 196640 | tf_op jit(solution)/shard_map/ppermute | solution.py:764
  422.2 34.0 %collective-permute-done.33.refs_0_ = bf16[3,256,1024]{2,1,0:T(8,128)(2,1)S(1)} collective-permute-done((bf16[3,256,1024]{2,1,0:T(8,128)(2,1)S(1)}, bf16[3,256,1024]{2,1,0:T(8,128)(2,1)S(1)}, u32[]{:S(2)}, u32[]{:S(2)}) %collective-permute-start.33) | collective-permute-done | bytes 1572896 | tf_op jit(solution)/shard_map/ppermute | solution.py:767
  456.2 4.9 all-to-all-start.2
  461.7 7.4 %bucket_sums.1 = f32[32,128]{1,0:T(8,128)} custom-call(s32[32]{0:T(128)} %convert_reduce_fusion.edge_ref, f32[256,1024]{1,0:T(8,128)} %get-tuple-element.139.grad_ref), custom_call_target="tpu_custom_call" | custom-call | flops 8049999872 | bytes 25830000 | tf_op jit(solution)/shard_map/bucket_sums/pallas_call | solution.py:137
  470.1 16.7 %all-to-all-done.2.d_ref = bf16[16,64,384]{2,1,0:T(8,128)(2,1)S(1)} async-done(((bf16[16,64,384]{2,1,0:T(8,128)(2,1)}), bf16[16,64,384]{2,1,0:T(8,128)(2,1)S(1)}, u32[]{:S(2)}, u32[]{:S(2)}) %all-to-all-start.2) | async-done | bytes 786464 | tf_op jit(solution)/shard_map/all_to_all | solution.py:1095
  487.7 6.6 %input_grad.1 = (f32[128,1024]{1,0:T(8,128)}, f32[1,1024]{1,0:T(1,128)}) custom-call(s32[3]{0:T(128)} %pad_add_fusion.2.starts_ref, bf16[16,64,384]{2,1,0:T(8,128)(2,1)} %copy-done.6, bf16[2,64,1024]{2,1,0:T(8,128)(2,1)} %bitcast.84, f32[3,1024]{1,0:T(4,128)} %copy-done.23, f32[128,1024]{1,0:T(8,128)} %get-tuple-element.132.gx1_ref, bf16[512,1024]{1,0:T(8,128)(2,1)} %wq.5, ...), custom_call_target="tpu_custom_call" | custom-call | flops 8049999872 | bytes 25830000 | tf_op jit(solution)/shard_map/input_grad/pallas_call | solution.py:1096
  499.6 6.0 %all-to-all-start.3 = ((bf16[16,64,128]{2,1,0:T(8,128)(2,1)}), bf16[16,64,128]{2,1,0:T(8,128)(2,1)S(1)}, u32[]{:S(2)}, u32[]{:S(2)}) async-start(bf16[16,64,128]{2,1,0:T(8,128)(2,1)} %bitcast.45), calls=%async_computation.3 | async-start | bytes 524288 | tf_op jit(solution)/shard_map/all_to_all | solution.py:1133
  508.3 2.2 collective-permute-done.41
  514.3 2.5 collective-permute-start.43
  517.5 5.4 encoder_grad.1
  524.3 13.3 %first_spread.1 = (f32[2,4,64,2816]{3,2,1,0:T(8,128)}, f32[2,4,64,2816]{3,2,1,0:T(8,128)}, f32[1408,1024]{1,0:T(8,128)}, f32[512,1024]{1,0:T(8,128)}, f32[512,1024]{1,0:T(8,128)}, /*index=5*/f32[512,1024]{1,0:T(8,128)}) custom-call(s32[3]{0:T(128)} %pad_add_fusion.1.where_ref, bf16[16,2880,128]{2,1,0:T(8,128)(2,1)} %all-gather.5.cloned.1.call-done.in_ref), custom_call_target="tpu_custom_call" | custom-call | flops 13799999488 | bytes 44280000 | tf_op jit(solution)/shard_map/first_spread/pallas_call | solution.py:683
  537.6 7.7 %second_spread.1 = (f32[2,4,64,1024]{3,2,1,0:T(8,128)}, f32[2,4,64,1024]{3,2,1,0:T(8,128)}, f32[2,4,64,1024]{3,2,1,0:T(8,128)}, f32[512,1024]{1,0:T(8,128)}, f32[512,1024]{1,0:T(8,128)}) custom-call(s32[3]{0:T(128)} %pad_add_fusion.1.where_ref, bf16[16,1280,128]{2,1,0:T(8,128)(2,1)} %all-gather.7.cloned.1.call-done.in_ref), custom_call_target="tpu_custom_call" | custom-call | flops 9200000000 | bytes 29520000 | tf_op jit(solution)/shard_map/second_spread/pallas_call | solution.py:683
  (274 shorter events, 105.1 us)
Async XLA Ops:
  7.2 110.1 %all-gather.9.cloned.1.call-start = ((), (), s32[]{:S(2)}) async-start(), calls=%async_computation.6 | async-start | bytes 2228224 | tf_op jit(solution)/shard_map/all_gather | solution.py:814
  7.2 27.6 %collective-permute-start = (bf16[2,64,1024]{2,1,0:T(8,128)(2,1)}, bf16[2,64,1024]{2,1,0:T(8,128)(2,1)S(1)}, u32[]{:S(2)}, u32[]{:S(2)}) collective-permute-start(bf16[2,64,1024]{2,1,0:T(8,128)(2,1)} %bitcast.80), channel_id=1, source_target_pairs={{0,16},{2,18},{4,20},{6,22},{8,24},{10,26},{12,28},{14,30},{16,0},... | collective-permute-start | bytes 786440 | tf_op jit(solution)/shard_map/ppermute | solution.py:764
  11.3 27.0 %collective-permute-start.1 = (bf16[2,64,1024]{2,1,0:T(8,128)(2,1)}, bf16[2,64,1024]{2,1,0:T(8,128)(2,1)S(1)}, u32[]{:S(2)}, u32[]{:S(2)}) collective-permute-start(bf16[2,64,1024]{2,1,0:T(8,128)(2,1)} %bitcast.81), channel_id=1, source_target_pairs={{0,8},{2,10},{4,12},{6,14},{8,0},{10,2},{12,4},{14,6},{16,24},{18,... | collective-permute-start | bytes 786440 | tf_op jit(solution)/shard_map/ppermute | solution.py:764
  12.9 35.6 %collective-permute-start.3 = (bf16[2,64,1024]{2,1,0:T(8,128)(2,1)}, bf16[2,64,1024]{2,1,0:T(8,128)(2,1)S(1)}, u32[]{:S(2)}, u32[]{:S(2)}) collective-permute-start(bf16[2,64,1024]{2,1,0:T(8,128)(2,1)} %bitcast.82), channel_id=1, source_target_pairs={{0,4},{2,6},{4,0},{6,2},{8,12},{10,14},{12,8},{14,10},{16,20},{18,... | collective-permute-start | bytes 786440 | tf_op jit(solution)/shard_map/ppermute | solution.py:764
  17.2 18.0 %collective-permute-start.8 = (bf16[4,512]{1,0:T(4,128)(2,1)S(1)}, bf16[4,512]{1,0:T(4,128)(2,1)S(1)}, u32[]{:S(2)}, u32[]{:S(2)}) collective-permute-start(bf16[4,512]{1,0:T(4,128)(2,1)S(1)} %fusion.6), channel_id=1, source_target_pairs={{0,1},{1,0},{2,3},{3,2},{4,5},{5,4},{6,7},{7,6},{8,9},{9,8},{10,11... | collective-permute-start | bytes 12296 | tf_op jit(solution)/shard_map/ppermute | solution.py:767
  21.1 15.1 %collective-permute-start.10 = (bf16[512,192]{1,0:T(8,128)(2,1)S(1)}, bf16[512,192]{1,0:T(8,128)(2,1)S(1)}, u32[]{:S(2)}, u32[]{:S(2)}) collective-permute-start(bf16[512,192]{1,0:T(8,128)(2,1)S(1)} %pad_maximum_fusion.7), channel_id=1, source_target_pairs={{0,1},{1,0},{2,3},{3,2},{4,5},{5,4},{6,7},{7,6},{8,9},{9,8},{10,11... | collective-permute-start | bytes 589832 | tf_op jit(solution)/shard_map/ppermute | solution.py:767
  36.3 29.1 %collective-permute-start.11 = (bf16[5,128,1024]{2,1,0:T(8,128)(2,1)}, bf16[5,128,1024]{2,1,0:T(8,128)(2,1)}, u32[]{:S(2)}, u32[]{:S(2)}) collective-permute-start(bf16[5,128,1024]{2,1,0:T(8,128)(2,1)} %bitcast_dynamic-update-slice_fusion), channel_id=1, source_target_pairs={{0,1},{1,0},{2,3},{3,2},{4,5},{5,4},{6,7},{7,6},{8,9},{9,8},{10,11... | collective-permute-start | bytes 3932168 | tf_op jit(solution)/shard_map/ppermute | solution.py:767
  37.8 20.1 %collective-permute-start.4 = (bf16[2,64,1024]{2,1,0:T(8,128)(2,1)S(1)}, bf16[2,64,1024]{2,1,0:T(8,128)(2,1)S(1)}, u32[]{:S(2)}, u32[]{:S(2)}) collective-permute-start(bf16[2,64,1024]{2,1,0:T(8,128)(2,1)S(1)} %collective-permute-done), channel_id=1, source_target_pairs={{0,4},{2,6},{4,0},{6,2},{8,12},{10,14},{12,8},{14,10},{16,20},{18,... | collective-permute-start | bytes 786440 | tf_op jit(solution)/shard_map/ppermute | solution.py:764
  38.3 19.6 %collective-permute-start.5 = (bf16[2,64,1024]{2,1,0:T(8,128)(2,1)S(1)}, bf16[2,64,1024]{2,1,0:T(8,128)(2,1)S(1)}, u32[]{:S(2)}, u32[]{:S(2)}) collective-permute-start(bf16[2,64,1024]{2,1,0:T(8,128)(2,1)S(1)} %collective-permute-done.1), channel_id=1, source_target_pairs={{0,4},{2,6},{4,0},{6,2},{8,12},{10,14},{12,8},{14,10},{16,20},{18,... | collective-permute-start | bytes 786440 | tf_op jit(solution)/shard_map/ppermute | solution.py:764
  42.8 17.9 %collective-permute-start.6 = (bf16[2,64,1024]{2,1,0:T(8,128)(2,1)S(1)}, bf16[2,64,1024]{2,1,0:T(8,128)(2,1)S(1)}, u32[]{:S(2)}, u32[]{:S(2)}) collective-permute-start(bf16[2,64,1024]{2,1,0:T(8,128)(2,1)S(1)} %collective-permute-done.2), channel_id=1, source_target_pairs={{0,4},{2,6},{4,0},{6,2},{8,12},{10,14},{12,8},{14,10},{16,20},{18,... | collective-permute-start | bytes 786440 | tf_op jit(solution)/shard_map/ppermute | solution.py:764
  48.5 20.4 %collective-permute-start.7 = (bf16[4,2,64,1024]{3,2,1,0:T(8,128)(2,1)S(1)}, bf16[4,2,64,1024]{3,2,1,0:T(8,128)(2,1)S(1)}, u32[]{:S(2)}, u32[]{:S(2)}) collective-permute-start(bf16[4,2,64,1024]{3,2,1,0:T(8,128)(2,1)S(1)} %pad_maximum_fusion.1.refs_0_), channel_id=1, source_target_pairs={{0,2},{2,0},{4,6},{6,4},{8,10},{10,8},{12,14},{14,12},{16,18},{18,... | collective-permute-start | bytes 3145736 | tf_op jit(solution)/shard_map/ppermute | solution.py:764
  65.4 28.7 %collective-permute-start.12 = (bf16[5,128,1024]{2,1,0:T(8,128)(2,1)}, bf16[5,128,1024]{2,1,0:T(8,128)(2,1)S(1)}, u32[]{:S(2)}, u32[]{:S(2)}) collective-permute-start(bf16[5,128,1024]{2,1,0:T(8,128)(2,1)} %collective-permute-done.11.refs_0_), channel_id=1, source_target_pairs={{0,4},{2,6},{4,0},{6,2},{8,12},{10,14},{12,8},{14,10},{16,20},{18,... | collective-permute-start | bytes 3932168 | tf_op jit(solution)/shard_map/ppermute | solution.py:764
  67.3 26.8 %collective-permute-start.15 = (bf16[2,128,1408]{2,1,0:T(8,128)(2,1)S(1)}, bf16[2,128,1408]{2,1,0:T(8,128)(2,1)S(1)}, u32[]{:S(2)}, u32[]{:S(2)}) collective-permute-start(bf16[2,128,1408]{2,1,0:T(8,128)(2,1)S(1)} %pad_maximum_fusion.5), channel_id=1, source_target_pairs={{0,1},{1,0},{2,3},{3,2},{4,5},{5,4},{6,7},{7,6},{8,9},{9,8},{10,11... | collective-permute-start | bytes 2162696 | tf_op jit(solution)/shard_map/ppermute | solution.py:767
  68.9 48.4 %collective-permute-start.13 = (bf16[5,128,1024]{2,1,0:T(8,128)(2,1)}, bf16[5,128,1024]{2,1,0:T(8,128)(2,1)}, u32[]{:S(2)}, u32[]{:S(2)}) collective-permute-start(bf16[5,128,1024]{2,1,0:T(8,128)(2,1)} %collective-permute-done.11.refs_0_), channel_id=1, source_target_pairs={{0,2},{2,0},{4,6},{6,4},{8,10},{10,8},{12,14},{14,12},{16,18},{18,... | collective-permute-start | bytes 3932168 | tf_op jit(solution)/shard_map/ppermute | solution.py:764
  94.1 23.2 %collective-permute-start.14 = (bf16[5,128,1024]{2,1,0:T(8,128)(2,1)S(1)}, bf16[5,128,1024]{2,1,0:T(8,128)(2,1)}, u32[]{:S(2)}, u32[]{:S(2)}) collective-permute-start(bf16[5,128,1024]{2,1,0:T(8,128)(2,1)S(1)} %collective-permute-done.12.refs_1_), channel_id=1, source_target_pairs={{0,2},{2,0},{4,6},{6,4},{8,10},{10,8},{12,14},{14,12},{16,18},{18,... | collective-permute-start | bytes 3932168 | tf_op jit(solution)/shard_map/ppermute | solution.py:764
  94.1 22.6 %collective-permute-start.16 = (bf16[2,128,1408]{2,1,0:T(8,128)(2,1)S(1)}, bf16[2,128,1408]{2,1,0:T(8,128)(2,1)}, u32[]{:S(2)}, u32[]{:S(2)}) collective-permute-start(bf16[2,128,1408]{2,1,0:T(8,128)(2,1)S(1)} %collective-permute-done.15.refs_0_), channel_id=1, source_target_pairs={{0,8},{2,10},{4,12},{6,14},{8,0},{10,2},{12,4},{14,6},{16,24},{18,... | collective-permute-start | bytes 2162696 | tf_op jit(solution)/shard_map/ppermute | solution.py:764
  95.8 21.0 %all-to-all-start = ((bf16[16,64,128]{2,1,0:T(8,128)(2,1)}), bf16[16,64,128]{2,1,0:T(8,128)(2,1)S(1)}, u32[]{:S(2)}, u32[]{:S(2)}) async-start(bf16[16,64,128]{2,1,0:T(8,128)(2,1)} %bitcast.77), calls=%async_computation | async-start | bytes 524288 | tf_op jit(solution)/shard_map/all_to_all | solution.py:908
  100.7 58.7 %collective-permute-start.21 = (bf16[128,1024]{1,0:T(8,128)(2,1)}, bf16[128,1024]{1,0:T(8,128)(2,1)S(1)}, u32[]{:S(2)}, u32[]{:S(2)}) collective-permute-start(bf16[128,1024]{1,0:T(8,128)(2,1)} %bitcast.29.g_ref.g0_ref), channel_id=1, source_target_pairs={{0,1},{1,0},{2,3},{3,2},{4,5},{5,4},{6,7},{7,6},{8,9},{9,8},{10,11... | collective-permute-start | bytes 786440 | tf_op jit(solution)/shard_map/ppermute | solution.py:767
  116.8 31.4 %collective-permute-start.17 = (bf16[2,128,1408]{2,1,0:T(8,128)(2,1)S(1)}, bf16[2,128,1408]{2,1,0:T(8,128)(2,1)}, u32[]{:S(2)}, u32[]{:S(2)}) collective-permute-start(bf16[2,128,1408]{2,1,0:T(8,128)(2,1)S(1)} %collective-permute-done.15.refs_0_), channel_id=1, source_target_pairs={{0,2},{2,0},{4,6},{6,4},{8,10},{10,8},{12,14},{14,12},{16,18},{18,... | collective-permute-start | bytes 2162696 | tf_op jit(solution)/shard_map/ppermute | solution.py:764
  116.8 31.4 %collective-permute-start.18 = (bf16[2,128,1408]{2,1,0:T(8,128)(2,1)}, bf16[2,128,1408]{2,1,0:T(8,128)(2,1)}, u32[]{:S(2)}, u32[]{:S(2)}) collective-permute-start(bf16[2,128,1408]{2,1,0:T(8,128)(2,1)} %collective-permute-done.16.refs_1_), channel_id=1, source_target_pairs={{0,2},{2,0},{4,6},{6,4},{8,10},{10,8},{12,14},{14,12},{16,18},{18,... | collective-permute-start | bytes 2162696 | tf_op jit(solution)/shard_map/ppermute | solution.py:764
  142.4 15.7 %collective-permute-start.19 = (bf16[128,1024]{1,0:T(8,128)(2,1)}, bf16[128,1024]{1,0:T(8,128)(2,1)S(1)}, u32[]{:S(2)}, u32[]{:S(2)}) collective-permute-start(bf16[128,1024]{1,0:T(8,128)(2,1)} %get-tuple-element.112.n_ref.n0_ref), channel_id=1, source_target_pairs={{0,1},{1,0},{2,3},{3,2},{4,5},{5,4},{6,7},{7,6},{8,9},{9,8},{10,11... | collective-permute-start | bytes 786440 | tf_op jit(solution)/shard_map/ppermute | solution.py:767
  158.1 20.9 %collective-permute-start.23 = (bf16[128,5248]{1,0:T(8,128)(2,1)}, bf16[128,5248]{1,0:T(8,128)(2,1)S(1)}, u32[]{:S(2)}, u32[]{:S(2)}) collective-permute-start(bf16[128,5248]{1,0:T(8,128)(2,1)} %get-tuple-element.113.own0_ref), channel_id=1, source_target_pairs={{0,2},{2,0},{4,6},{6,4},{8,10},{10,8},{12,14},{14,12},{16,18},{18,... | collective-permute-start | bytes 4030472 | tf_op jit(solution)/shard_map/ppermute | solution.py:764
  188.3 20.0 %collective-permute-start.25 = (bf16[4,704,128]{2,1,0:T(8,128)(2,1)}, bf16[4,704,128]{2,1,0:T(8,128)(2,1)S(1)}, u32[]{:S(2)}, u32[]{:S(2)}) collective-permute-start(bf16[4,704,128]{2,1,0:T(8,128)(2,1)} %get-tuple-element.115), channel_id=1, source_target_pairs={{0,8},{2,10},{4,12},{6,14},{8,0},{10,2},{12,4},{14,6},{16,24},{18,... | collective-permute-start | bytes 2162696 | tf_op jit(solution)/shard_map/ppermute | solution.py:764
  190.0 18.3 %collective-permute-start.26 = (bf16[4,704,128]{2,1,0:T(8,128)(2,1)}, bf16[4,704,128]{2,1,0:T(8,128)(2,1)S(1)}, u32[]{:S(2)}, u32[]{:S(2)}) collective-permute-start(bf16[4,704,128]{2,1,0:T(8,128)(2,1)} %get-tuple-element.120), channel_id=1, source_target_pairs={{0,4},{2,6},{4,0},{6,2},{8,12},{10,14},{12,8},{14,10},{16,20},{18,... | collective-permute-start | bytes 2162696 | tf_op jit(solution)/shard_map/ppermute | solution.py:764
  190.3 18.0 %collective-permute-start.27 = (bf16[4,704,128]{2,1,0:T(8,128)(2,1)}, bf16[4,704,128]{2,1,0:T(8,128)(2,1)}, u32[]{:S(2)}, u32[]{:S(2)}) collective-permute-start(bf16[4,704,128]{2,1,0:T(8,128)(2,1)} %get-tuple-element.121), channel_id=1, source_target_pairs={{0,1},{1,0},{2,3},{3,2},{4,5},{5,4},{6,7},{7,6},{8,9},{9,8},{10,11... | collective-permute-start | bytes 2162696 | tf_op jit(solution)/shard_map/ppermute | solution.py:767
  208.3 48.5 %collective-permute-start.31 = (bf16[8,16,2,32,128]{4,3,2,1,0:T(8,128)(2,1)}, bf16[8,16,2,32,128]{4,3,2,1,0:T(8,128)(2,1)}, u32[]{:S(2)}, u32[]{:S(2)}) collective-permute-start(bf16[8,16,2,32,128]{4,3,2,1,0:T(8,128)(2,1)} %get-tuple-element.128), channel_id=1, source_target_pairs={{0,2},{2,0},{4,6},{6,4},{8,10},{10,8},{12,14},{14,12},{16,18},{18,... | collective-permute-start | bytes 6291464 | tf_op jit(solution)/shard_map/ppermute | solution.py:764
  215.4 19.1 %collective-permute-start.46 = (bf16[2,704,128]{2,1,0:T(8,128)(2,1)}, bf16[2,704,128]{2,1,0:T(8,128)(2,1)}, u32[]{:S(2)}, u32[]{:S(2)}) collective-permute-start(bf16[2,704,128]{2,1,0:T(8,128)(2,1)} %slice.245), channel_id=1, source_target_pairs={{0,8},{2,10},{4,12},{6,14},{8,0},{10,2},{12,4},{14,6},{16,24},{18,... | collective-permute-start | bytes 1081352 | tf_op jit(solution)/shard_map/ppermute | solution.py:764
  217.7 21.2 %collective-permute-start.44 = (bf16[2,704,128]{2,1,0:T(8,128)(2,1)}, bf16[2,704,128]{2,1,0:T(8,128)(2,1)S(1)}, u32[]{:S(2)}, u32[]{:S(2)}) collective-permute-start(bf16[2,704,128]{2,1,0:T(8,128)(2,1)} %slice.246), channel_id=1, source_target_pairs={{0,16},{2,18},{4,20},{6,22},{8,24},{10,26},{12,28},{14,30},{16,0},... | collective-permute-start | bytes 1081352 | tf_op jit(solution)/shard_map/ppermute | solution.py:764
  219.9 36.9 %collective-permute-start.28 = (bf16[128,2048]{1,0:T(8,128)(2,1)}, bf16[128,2048]{1,0:T(8,128)(2,1)}, u32[]{:S(2)}, u32[]{:S(2)}) collective-permute-start(bf16[128,2048]{1,0:T(8,128)(2,1)} %get-tuple-element.118.right_ref), channel_id=1, source_target_pairs={{0,1},{1,0},{2,3},{3,2},{4,5},{5,4},{6,7},{7,6},{8,9},{9,8},{10,11... | collective-permute-start | bytes 1572872 | tf_op jit(solution)/shard_map/ppermute | solution.py:767
  220.8 30.9 %collective-permute-start.30 = (bf16[4,704,128]{2,1,0:T(8,128)(2,1)}, bf16[4,704,128]{2,1,0:T(8,128)(2,1)}, u32[]{:S(2)}, u32[]{:S(2)}) collective-permute-start(bf16[4,704,128]{2,1,0:T(8,128)(2,1)} %get-tuple-element.127), channel_id=1, source_target_pairs={{0,1},{1,0},{2,3},{3,2},{4,5},{5,4},{6,7},{7,6},{8,9},{9,8},{10,11... | collective-permute-start | bytes 2162696 | tf_op jit(solution)/shard_map/ppermute | solution.py:767
  221.9 19.5 %all-to-all-start.1 = ((bf16[16,64,128]{2,1,0:T(8,128)(2,1)}), bf16[16,64,128]{2,1,0:T(8,128)(2,1)S(1)}, u32[]{:S(2)}, u32[]{:S(2)}) async-start(bf16[16,64,128]{2,1,0:T(8,128)(2,1)} %get-tuple-element.124), calls=%async_computation.1 | async-start | bytes 524288 | tf_op jit(solution)/shard_map/all_to_all | solution.py:1037
  225.5 193.9 %all-gather.5.cloned.1.call-start = ((), (), s32[]{:S(2)}) async-start(), calls=%async_computation.4 | async-start | bytes 12533760 | tf_op jit(solution)/shard_map/all_gather | solution.py:1153
  234.5 22.3 %collective-permute-start.29 = (bf16[128,1024]{1,0:T(8,128)(2,1)}, bf16[128,1024]{1,0:T(8,128)(2,1)}, u32[]{:S(2)}, u32[]{:S(2)}) collective-permute-start(bf16[128,1024]{1,0:T(8,128)(2,1)} %get-tuple-element.126.last_ref), channel_id=1, source_target_pairs={{0,1},{1,0},{2,3},{3,2},{4,5},{5,4},{6,7},{7,6},{8,9},{9,8},{10,11... | collective-permute-start | bytes 786440 | tf_op jit(solution)/shard_map/ppermute | solution.py:767
  239.0 16.5 %collective-permute-start.48 = (bf16[4,704,128]{2,1,0:T(8,128)(2,1)}, bf16[4,704,128]{2,1,0:T(8,128)(2,1)S(1)}, u32[]{:S(2)}, u32[]{:S(2)}) collective-permute-start(bf16[4,704,128]{2,1,0:T(8,128)(2,1)} %collective-permute-done.27), channel_id=1, source_target_pairs={{0,4},{2,6},{4,0},{6,2},{8,12},{10,14},{12,8},{14,10},{16,20},{18,... | collective-permute-start | bytes 2162696 | tf_op jit(solution)/shard_map/ppermute | solution.py:764
  256.9 14.7 %collective-permute-start.47 = (bf16[1,704,128]{2,1,0:T(8,128)(2,1)S(1)}, bf16[1,704,128]{2,1,0:T(8,128)(2,1)S(1)}, u32[]{:S(2)}, u32[]{:S(2)}) collective-permute-start(bf16[1,704,128]{2,1,0:T(8,128)(2,1)S(1)} %copy-done.20), channel_id=1, source_target_pairs={{0,16},{2,18},{4,20},{6,22},{8,24},{10,26},{12,28},{14,30},{16,0},... | collective-permute-start | bytes 540680 | tf_op jit(solution)/shard_map/ppermute | solution.py:764
  263.8 14.0 %collective-permute-start.32 = (bf16[1,768,128]{2,1,0:T(8,128)(2,1)S(1)}, bf16[1,768,128]{2,1,0:T(8,128)(2,1)S(1)}, u32[]{:S(2)}, u32[]{:S(2)}) collective-permute-start(bf16[1,768,128]{2,1,0:T(8,128)(2,1)S(1)} %constant_dynamic-slice_fusion.4), channel_id=1, source_target_pairs={{0,1},{1,0},{2,3},{3,2},{4,5},{5,4},{6,7},{7,6},{8,9},{9,8},{10,11... | collective-permute-start | bytes 589832 | tf_op jit(solution)/shard_map/ppermute | solution.py:767
  285.1 252.5 %all-gather.7.cloned.1.call-start = ((), (), s32[]{:S(2)}) async-start(), calls=%async_computation.5 | async-start | bytes 5570560 | tf_op jit(solution)/shard_map/all_gather | solution.py:1153
  290.3 37.6 %collective-permute-start.51 = (bf16[8,768,128]{2,1,0:T(8,128)(2,1)}, bf16[8,768,128]{2,1,0:T(8,128)(2,1)S(1)}, u32[]{:S(2)}, u32[]{:S(2)}) collective-permute-start(bf16[8,768,128]{2,1,0:T(8,128)(2,1)} %get-tuple-element.154), channel_id=1, source_target_pairs={{0,2},{2,0},{4,6},{6,4},{8,10},{10,8},{12,14},{14,12},{16,18},{18,... | collective-permute-start | bytes 4718600 | tf_op jit(solution)/shard_map/ppermute | solution.py:764
  293.2 32.6 %collective-permute-start.36 = (bf16[4,16,2,32,128]{4,3,2,1,0:T(8,128)(2,1)S(1)}, bf16[4,16,2,32,128]{4,3,2,1,0:T(8,128)(2,1)S(1)}, u32[]{:S(2)}, u32[]{:S(2)}) collective-permute-start(bf16[4,16,2,32,128]{4,3,2,1,0:T(8,128)(2,1)S(1)} %slice.240), channel_id=1, source_target_pairs={{0,4},{2,6},{4,0},{6,2},{8,12},{10,14},{12,8},{14,10},{16,20},{18,... | collective-permute-start | bytes 3145736 | tf_op jit(solution)/shard_map/ppermute | solution.py:764
  326.4 36.2 %collective-permute-start.37 = (bf16[2,16,2,32,128]{4,3,2,1,0:T(8,128)(2,1)S(1)}, bf16[2,16,2,32,128]{4,3,2,1,0:T(8,128)(2,1)S(1)}, u32[]{:S(2)}, u32[]{:S(2)}) collective-permute-start(bf16[2,16,2,32,128]{4,3,2,1,0:T(8,128)(2,1)S(1)} %slice.242), channel_id=1, source_target_pairs={{0,8},{2,10},{4,12},{6,14},{8,0},{10,2},{12,4},{14,6},{16,24},{18,... | collective-permute-start | bytes 1572872 | tf_op jit(solution)/shard_map/ppermute | solution.py:764
  328.4 55.5 %collective-permute-start.52 = (bf16[4,768,128]{2,1,0:T(8,128)(2,1)S(1)}, bf16[4,768,128]{2,1,0:T(8,128)(2,1)S(1)}, u32[]{:S(2)}, u32[]{:S(2)}) collective-permute-start(bf16[4,768,128]{2,1,0:T(8,128)(2,1)S(1)} %slice.241), channel_id=1, source_target_pairs={{0,4},{2,6},{4,0},{6,2},{8,12},{10,14},{12,8},{14,10},{16,20},{18,... | collective-permute-start | bytes 2359304 | tf_op jit(solution)/shard_map/ppermute | solution.py:764
  362.8 20.3 %collective-permute-start.38 = (bf16[1,16,2,32,128]{4,3,2,1,0:T(8,128)(2,1)S(1)}, bf16[1,16,2,32,128]{4,3,2,1,0:T(8,128)(2,1)S(1)}, u32[]{:S(2)}, u32[]{:S(2)}) collective-permute-start(bf16[1,16,2,32,128]{4,3,2,1,0:T(8,128)(2,1)S(1)} %slice.247), channel_id=1, source_target_pairs={{0,16},{2,18},{4,20},{6,22},{8,24},{10,26},{12,28},{14,30},{16,0},... | collective-permute-start | bytes 786440 | tf_op jit(solution)/shard_map/ppermute | solution.py:764
  384.1 23.1 %collective-permute-start.53 = (bf16[2,768,128]{2,1,0:T(8,128)(2,1)S(1)}, bf16[2,768,128]{2,1,0:T(8,128)(2,1)S(1)}, u32[]{:S(2)}, u32[]{:S(2)}) collective-permute-start(bf16[2,768,128]{2,1,0:T(8,128)(2,1)S(1)} %slice.243), channel_id=1, source_target_pairs={{0,8},{2,10},{4,12},{6,14},{8,0},{10,2},{12,4},{14,6},{16,24},{18,... | collective-permute-start | bytes 1179656 | tf_op jit(solution)/shard_map/ppermute | solution.py:764
  394.6 14.5 %collective-permute-start.55 = (bf16[1,512,128]{2,1,0:T(8,128)(2,1)S(1)}, bf16[1,512,128]{2,1,0:T(8,128)(2,1)S(1)}, u32[]{:S(2)}, u32[]{:S(2)}) collective-permute-start(bf16[1,512,128]{2,1,0:T(8,128)(2,1)S(1)} %constant_dynamic-slice_fusion.3), channel_id=1, source_target_pairs={{0,1},{1,0},{2,3},{3,2},{4,5},{5,4},{6,7},{7,6},{8,9},{9,8},{10,11... | collective-permute-start | bytes 393224 | tf_op jit(solution)/shard_map/ppermute | solution.py:767
  420.5 35.6 %collective-permute-start.33 = (bf16[3,256,1024]{2,1,0:T(8,128)(2,1)S(1)}, bf16[3,256,1024]{2,1,0:T(8,128)(2,1)S(1)}, u32[]{:S(2)}, u32[]{:S(2)}) collective-permute-start(bf16[3,256,1024]{2,1,0:T(8,128)(2,1)S(1)} %pad_maximum_fusion), channel_id=1, source_target_pairs={{0,1},{1,0},{2,3},{3,2},{4,5},{5,4},{6,7},{7,6},{8,9},{9,8},{10,11... | collective-permute-start | bytes 4718600 | tf_op jit(solution)/shard_map/ppermute | solution.py:767
  456.2 30.6 %all-to-all-start.2 = ((bf16[16,64,384]{2,1,0:T(8,128)(2,1)}), bf16[16,64,384]{2,1,0:T(8,128)(2,1)S(1)}, u32[]{:S(2)}, u32[]{:S(2)}) async-start(bf16[16,64,384]{2,1,0:T(8,128)(2,1)} %bitcast.42), calls=%async_computation.2 | async-start | bytes 1572864 | tf_op jit(solution)/shard_map/all_to_all | solution.py:1095
  496.6 15.5 %collective-permute-start.34 = (bf16[128,1024]{1,0:T(8,128)(2,1)S(1)}, bf16[128,1024]{1,0:T(8,128)(2,1)S(1)}, u32[]{:S(2)}, u32[]{:S(2)}) collective-permute-start(bf16[128,1024]{1,0:T(8,128)(2,1)S(1)} %copy-done.34), channel_id=1, source_target_pairs={{0,1},{1,0},{2,3},{3,2},{4,5},{5,4},{6,7},{7,6},{8,9},{9,8},{10,11... | collective-permute-start | bytes 786440 | tf_op jit(solution)/shard_map/ppermute | solution.py:767
  499.6 17.2 %all-to-all-start.3 = ((bf16[16,64,128]{2,1,0:T(8,128)(2,1)}), bf16[16,64,128]{2,1,0:T(8,128)(2,1)S(1)}, u32[]{:S(2)}, u32[]{:S(2)}) async-start(bf16[16,64,128]{2,1,0:T(8,128)(2,1)} %bitcast.45), calls=%async_computation.3 | async-start | bytes 524288 | tf_op jit(solution)/shard_map/all_to_all | solution.py:1133
  (54 other events, 462.9 us)
Sparse Core Ops, SparseCore 0:
  21.8 43.2 all-gather.8
  285.2 119.3 all-gather.4
  420.3 66.6 all-gather.6

commit v5 on v4

--- a/solution.py
+++ b/solution.py
@@ -163,6 +163,41 @@
             out_ref[...] = total
         else:
             out_ref[:, aligned(starts_ref[place], rows)] = total
+
+
+def pack_kernel(counts, where_ref, *refs):
+    total = sum(counts)
+    weights, outs, sem = refs[:total], refs[total:-1], refs[-1]
+    copies = []
+    for place, w_ref in enumerate(weights):
+        kind = 0 if place < counts[0] else 1
+        out_ref = outs[kind].at[place - kind * counts[0]]
+        rows, cols = outs[kind].shape[1:]
+        source = w_ref.at[aligned(where_ref[kind], rows), :]
+        if kind:
+            source = w_ref.at[aligned(where_ref[kind], rows), aligned(where_ref[2], cols)]
+        copies.append(pltpu.make_async_copy(source, out_ref, sem.at[place]))
+    for copy in copies:
+        copy.start()
+    for copy in copies:
+        copy.wait()
+
+
+def pack(where, first, second, rows, cols):
+    anywhere = pl.BlockSpec(memory_space=pl.ANY)
+    counts = (len(first), len(second))
+    return pl.pallas_call(
+        functools.partial(pack_kernel, counts),
+        out_shape=[
+            jax.ShapeDtypeStruct((counts[0], rows, first[0].shape[1]), BF16),
+            jax.ShapeDtypeStruct((counts[1], rows, cols), BF16),
+        ],
+        in_specs=[smem()] + [anywhere] * sum(counts),
+        out_specs=[anywhere] * 2,
+        scratch_shapes=[pltpu.SemaphoreType.DMA((sum(counts),))],
+        cost_estimate=cost(2),
+        name="pack",
+    )(where, *first, *second)
 
 
 def pieces_of(own_ref, more, index):
@@ -312,7 +347,7 @@
 
 def mid_forward_kernel(split, starts_ref, o1_ref, x_ref, gain_ref, ke_ref, ve_ref, wo, wq, wc, *refs):
     more = refs[:split]
-    left_ref, x1_ref, q2_ref, x2_ref, n3_ref, o1c_ref, n2_ref, o2_ref = refs[split:]
+    left_ref, x1_ref, q2_ref, x2_ref, n3_ref, sent_ref, o1c_ref, n2_ref, o2_ref = refs[split:]
     heads, rows, _ = o1_ref.shape
     width = x_ref.shape[-1]
     for pair in range(heads // 2):
@@ -342,6 +377,10 @@
     left_ref[0] = o2_ref[...]
     left_ref[1] = n2_ref[...]
     left_ref[2] = o1c_ref[...]
+    if split:
+        span = sent_ref.shape[2]
+        for kind in range(3):
+            sent_ref[kind] = left_ref[kind, :, aligned(span - starts_ref[0], span)]
 
 
 def cross_backward_kernel(
@@ -631,13 +670,18 @@
     head_rows(in_ref, at + span, half, ((v_ref, slice(0, half)), (v_ref, slice(half, span))))
 
 
-def first_spread_kernel(where_ref, in_ref, gate_ref, up_ref, down_ref, q_ref, k_ref, v_ref):
+def spread_kernel(where_ref, in_ref, gate_ref, up_ref, down_ref, q_ref, k_ref, v_ref, *out_refs):
     shard = where_ref[1]
     hidden = gate_ref.shape[3] // 2
     rows = gate_ref.shape[2] // 2
     at = rows * hidden // 128
     tall = down_ref.shape[0] // 2
     half = down_ref.shape[1] // 2
+    span = q_ref.shape[0]
+    kinds = len(out_refs) - 2
+    width = out_refs[0].shape[3]
+    base = 6 * at + 3 * span // 2
+    step = rows * width // 128
     for piece in range(4):
         chip, core = piece // 2, piece % 2
         place = slice(chip * rows, (chip + 1) * rows)
@@ -648,24 +692,15 @@
                 out_ref[core, 0, place, lanes] = chunk
         chunk = take_chunk(in_ref, piece, 2 * at, tall, half)
         down_ref[chip * tall : (chip + 1) * tall, core * half : (core + 1) * half] = chunk
+        for kind in range(kinds):
+            chunk = take_chunk(in_ref, piece, base + kind * step, rows, width)
+            out_refs[kind][core, 0, place, :] = chunk
     head_spread(in_ref, 6 * at, q_ref, k_ref, v_ref)
-
-
-def second_spread_kernel(where_ref, in_ref, *out_refs):
-    kinds = len(out_refs) - 2
     k_ref, v_ref = out_refs[kinds:]
-    rows, width = out_refs[0].shape[2] // 2, out_refs[0].shape[3]
-    at = rows * width // 128
-    for piece in range(4):
-        chip, core = piece // 2, piece % 2
-        for kind in range(kinds):
-            chunk = take_chunk(in_ref, piece, kind * at, rows, width)
-            out_refs[kind][core, 0, chip * rows : (chip + 1) * rows, :] = chunk
-    span = k_ref.shape[0]
-    head_rows(in_ref, kinds * at, span, ((k_ref, slice(None)), (v_ref, slice(None))))
-
-
-def spread(kernel, where, pieces, outs, length, name):
+    head_rows(in_ref, base + kinds * step, span, ((k_ref, slice(None)), (v_ref, slice(None))))
+
+
+def spread(where, pieces, outs):
     count, total, _ = pieces.shape
     steps = count // 4
     specs, shapes = [], []
@@ -681,7 +716,7 @@
             shapes.append((rows, cols))
             specs.append(pl.BlockSpec((rows, cols // steps), lambda q, where: (0, q)))
     made = pl.pallas_call(
-        kernel,
+        spread_kernel,
         grid_spec=pltpu.PrefetchScalarGridSpec(
             num_scalar_prefetch=1,
             grid=(steps,),
@@ -690,8 +725,8 @@
         ),
         out_shape=[jax.ShapeDtypeStruct(shape, F32) for shape in shapes],
         compiler_params=params(),
-        cost_estimate=cost(length),
-        name=name,
+        cost_estimate=cost(20),
+        name="spread",
     )(where, pieces)
     return [array.reshape(shape) for array, (shape, _) in zip(made, outs)]
 
@@ -841,24 +876,16 @@
         starts = quarter_starts(near_bit)
         kv_own = (key_cross, value_cross)
         near_own = (output_self, query_cross, output_cross)
-        near_sent = jnp.stack(
-            [
-                lax.dynamic_slice_in_dim(w, quarter(near_bit) * (half // 2), half // 2, axis=0)
-                for w in near_own + kv_own
-            ]
-        )
-        near_got = swap_fs(after(near_sent, small_got, head_got))
+        picked = [quarter(near_bit) * (half // 2), quarter(dense_bit) * (half // 2)]
+        near_sent, theirs = pack(
+            jnp.stack(picked + [(1 - shard) * hidden]).astype(jnp.int32),
+            near_own + kv_own,
+            (dense_gate, dense_up),
+            half // 2,
+            hidden,
+        )
+        near_got = swap_fs(near_sent)
         near_far = swap_dp(near_got, near_bit)
-        theirs = jnp.stack(
-            [
-                lax.dynamic_slice(
-                    w,
-                    (quarter(dense_bit) * (half // 2), (1 - shard) * hidden),
-                    (half // 2, hidden),
-                )
-                for w in (dense_gate, dense_up)
-            ]
-        )
         dense_got = swap_fs(after(theirs, near_got))
         dense_own = (dense_gate, dense_up)
         which = jnp.stack([shard, core]).astype(jnp.int32)
@@ -915,13 +942,18 @@
 
     row32 = jax.ShapeDtypeStruct((tokens, width), F32)
     row16 = jax.ShapeDtypeStruct((tokens, width), BF16)
-    left, x1, q2, x2, n3 = pl.pallas_call(
+    left, x1, q2, x2, n3, left_sent = pl.pallas_call(
         functools.partial(mid_forward_kernel, len(near_more)),
         out_shape=[
-            jax.ShapeDtypeStruct((3, tokens, width), BF16), row32, row16, row32, row16
+            jax.ShapeDtypeStruct((3, tokens, width), BF16),
+            row32,
+            row16,
+            row32,
+            row16,
+            jax.ShapeDtypeStruct((3, tokens, span), BF16),
         ],
         in_specs=[smem()] + [vmem()] * (8 + len(near_more)),
-        out_specs=[vmem()] * 5,
+        out_specs=[vmem()] * 6,
         scratch_shapes=[pltpu.VMEM((tokens, width), BF16)] * 3,
         compiler_params=params(),
         cost_estimate=cost(12),
@@ -938,8 +970,7 @@
         g_rows = g.reshape(tokens, width)
         g_got = swap_fs(after(g_rows, dense_got))
         n_got = swap_fs(n3)
-        views = left.reshape(3, tokens, 2, span)
-        left_got = swap_fs(lax.dynamic_index_in_dim(views, 1 - shard, 2, keepdims=False))
+        left_got = swap_fs(left_sent)
         back, y32, _, dn3, _ = dense_layer(
             dense_starts, n3, g_rows, *dense_own, dense_down, dense_more, tokens
         )
@@ -993,7 +1024,7 @@
         )
         dn3_more = after(dn3_more, own_sent)
         own_got, down_got = swap_dp(own_sent, z_order[0]), swap_dp(down_sent, x_order[0])
-        far_got, far_kept = swap_fs(far_sent), swap_fs(far_kept)
+        far_got = swap_fs(far_sent)
 
     straight = chunked
     if straight:
@@ -1039,9 +1070,12 @@
     ).reshape(length, 128)
 
     if chunked:
-        right_got, last_got = swap_fs(right), swap_fs(last)
+        right_got, last_got = swap_fs(after(right, do1_heads)), swap_fs(last)
+        far_kept = swap_fs(after(far_kept, right_got, last_got))
         if straight:
-            dkv_got = swap_dp(dkv_sent, 1)
+            dkv_got = swap_dp(after(dkv_sent, do1_heads), 1)
+            dkv_total = dkv_kept.astype(F32) + dkv_got.astype(F32)
+            dkv_far = swap_dp(dkv_total[chips // 2 :].astype(BF16), x_order[0])
 
     dqkv, table_grad = pl.pallas_call(
         self_backward_kernel,
@@ -1057,7 +1091,7 @@
         name="self_backward",
     )(qkv, do1, table, doc_row, doc_col)
     if chunked:
-        dqkv = after(dqkv, right_got, last_got, far_kept, dkv_got)
+        dqkv = after(dqkv, right_got, last_got, dkv_far)
     head_grad = pl.pallas_call(
         head_weight_kernel,
         out_shape=jax.ShapeDtypeStruct((fs, span * 3 // 2, 128), BF16),
@@ -1108,7 +1142,7 @@
     )(half_starts, own_d, x, gains, gx1, *first_own, *first_more)
 
     if straight:
-        dkv = reduce_chips(dkv_kept, dkv_got, [1] + x_order).reshape(-1, 128)
+        dkv = reduce_chips(dkv_total[: chips // 2], dkv_far).reshape(-1, 128)
     else:
         dkv = jnp.stack([dkv_kept, dkv_sent], axis=1).reshape(heads * copies, -1, 128)
         dkv = lax.psum_scatter(dkv, "dp", scatter_dimension=0, tiled=True)[0]
@@ -1143,17 +1177,18 @@
     )(starts, own_dkv, *kv_own, *kv_more)
 
     if chunked:
-        own_sum = reduce_chips(own_kept, own_got, z_order, (do1_heads, dqkv))
-        down_sum = reduce_chips(down_kept, down_got, x_order, (do1_heads, dqkv))
-        far_got = swap_dp(after(far_got, do1_heads), x_order[0])
-        far_sum = reduce_chips(far_kept, far_got, x_order, (dqkv, head_grad))
-        token_sum = reduce_chips(token_kept, token_got, [1] + x_order)
-
-        def gather(*values):
-            return lax.all_gather(jnp.concatenate(values, axis=1), "dp", axis=0, tiled=True)
-
+        sums = (
+            reduce_chips(own_kept, own_got, z_order, (do1, dqkv)),
+            reduce_chips(down_kept, down_got, x_order, (do1, dqkv)),
+            reduce_chips(
+                far_kept, swap_dp(after(far_got, do1), x_order[0]), x_order, (dqkv, head_grad)
+            ),
+            head_sum,
+            reduce_chips(token_kept, token_got, [1] + x_order),
+            cross_sum,
+        )
+        pieces = lax.all_gather(jnp.concatenate(sums, axis=1), "dp", axis=0, tiled=True)
         square, wide = (span, width), (span, fs * hidden)
-        first_pieces = gather(own_sum, down_sum, far_sum, head_sum)
         (
             grad_dense_gate,
             grad_dense_up,
@@ -1161,27 +1196,19 @@
             grad_query_self,
             grad_key_self,
             grad_value_self,
-        ) = spread(
-            first_spread_kernel,
-            where,
-            first_pieces,
-            [(wide, "core"), (wide, "core"), ((hidden, width), "chip")] + [(square, "head")] * 3,
-            12,
-            "first_spread",
-        )
-        (
             grad_output_cross,
             grad_query_cross,
             grad_output_self,
             grad_key_cross,
             grad_value_cross,
         ) = spread(
-            second_spread_kernel,
             where,
-            gather(after(token_sum, first_pieces), cross_sum),
-            [(square, "core")] * 3 + [(square, "head")] * 2,
-            8,
-            "second_spread",
+            pieces,
+            [(wide, "core")] * 2
+            + [((hidden, width), "chip")]
+            + [(square, "head")] * 3
+            + [(square, "core")] * 3
+            + [(square, "head")] * 2,
         )
     else:
 

time: 562 us -> 530 us (0.943)
  waiting for transfers between devices: 241 us -> 175 us
  Pallas kernels: 155 us -> 215 us
  starting transfers between devices: 85.3 us -> 68.2 us
  local copies, waits for them, and re-layouts: 37 us -> 27.2 us
    ppermute x39, waiting for transfers between devices: 162 us -> 75.9 us  [swap_dp(): return lax.ppermute(values, 'dp', [(j, j ^ bit) for j in range(dp)])]
    pallas_call x2, Pallas kernels: 21.1 us -> 80.9 us  [the longest x1 63.5 us: pack(): pl.pallas_call(functools.partial(pack_kernel, counts), out_shape=[jax.Sha...]
    ppermute x39, starting transfers between devices: 47.2 us -> 36.8 us  [swap_dp(): return lax.ppermute(values, 'dp', [(j, j ^ bit) for j in range(dp)])]
    ppermute x17, waiting for transfers between devices: 46.2 us -> 53.3 us  [swap_fs(): return lax.ppermute(values, 'fsdp', [(j, 1 - j) for j in range(2)])]
    all_to_all x1, waiting for transfers between devices: 0.01 us -> 6.14 us  [per_device(): own_dkv = lax.all_to_all(own_dkv, 'dp', 0, 0, tiled=True)[::copies]]
    all_to_all x1, waiting for transfers between devices: 16.7 us -> 22.4 us  [per_device(): lax.all_to_all(dqkv.reshape(dp, rows, 384), 'dp', 0, 0, tiled=True)]
    unnamed x83 -> x88, local copies, waits for them, and re-layouts: 14 us -> 11 us
  transfers between devices with their start and end apart: 63 -> 62, of which waited for: 25 -> 24; matrix products, arithmetic and copies ran while one was open for 9% -> 7% of each run, Pallas kernels for 25% -> 35%
where the time goes in v5:
time: 530 us; the launch traced here: 520 us
  Pallas kernels  215 us (41%)
  waiting for transfers between devices  175 us (33%)
  starting transfers between devices  68.2 us (13%)
  local copies, waits for them, and re-layouts  27.2 us (5%)
  other arithmetic  19.4 us (4%)
  between operations  15.1 us (3%)
    ppermute x39, waiting for transfers between devices, swap_dp(): return lax.ppermute(values, 'dp', [(j, j ^ bit) for j in range(dp)])  75.9 us
    pallas_call x1, Pallas kernels, pack(): pl.pallas_call(functools.partial(pack_kernel, counts), out_shape=[jax.Sha...  63.5 us
    ppermute x17, waiting for transfers between devices, swap_fs(): return lax.ppermute(values, 'fsdp', [(j, 1 - j) for j in range(2)])  53.3 us
    ppermute x39, starting transfers between devices, swap_dp(): return lax.ppermute(values, 'dp', [(j, j ^ bit) for j in range(dp)])  36.8 us
    all_to_all x1, waiting for transfers between devices, per_device(): lax.all_to_all(dqkv.reshape(dp, rows, 384), 'dp', 0, 0, tiled=True)  22.4 us
    pallas_call x2, Pallas kernels, dense_layer(): pl.pallas_call(functools.partial(dense_kernel, len(more)), grid_spec=pltp...  19.9 us
    pallas_call x1, Pallas kernels, spread(): pl.pallas_call(spread_kernel, grid_spec=pltpu.PrefetchScalarGridSpec(num_...  17.4 us
    all_to_all x1, waiting for transfers between devices, per_device(): lax.all_to_all(mixed.reshape(dp, rows, 128), 'dp', 0, 0, tiled=True)  17 us
  transfers between devices with their start and end apart: 62, of which 24 were waited for; matrix products, arithmetic and copies ran while one was open for 7% of the time, Pallas kernels for 35%

profile of v5, /device:TPU:0, one launch (start us, length us, event | category | flops | bytes accessed | tf_op | source)
XLA Modules:
  0.0 520.0 jit_solution(1338889936037158322)
XLA Ops:
  7.2 3.0 collective-permute-start.3
  11.8 2.6 collective-permute-start
  19.4 63.5 %pack.1 = (bf16[5,128,1024]{2,1,0:T(8,128)(2,1)}, bf16[2,128,1408]{2,1,0:T(8,128)(2,1)}) custom-call(s32[3]{0:T(128)} %pad_add_fusion.where_ref, bf16[512,1024]{1,0:T(8,128)(2,1)} %wo.3, bf16[512,1024]{1,0:T(8,128)(2,1)} %wq.4, bf16[512,1024]{1,0:T(8,128)(2,1)} %wc.3, bf16[512,1024]{1,0:T(8,128)(2,1)} %wk.3, bf16[512,1024]{1,0:T(8,128)(2,1)} %wv.3, ...), custom_call_target="tpu_custom_call" | custom-call | flops 2300000000 | bytes 7380000 | tf_op jit(solution)/shard_map/pack/pallas_call | solution.py:189
  90.0 3.2 collective-permute-done.2
  93.7 4.4 bias_table.1.refs_6_.table_ref
  99.8 3.0 collective-permute-done.5
  102.8 2.8 collective-permute-done.6
  110.9 7.3 %collective-permute-done.10 = bf16[512,192]{1,0:T(8,128)(2,1)S(1)} collective-permute-done((bf16[512,192]{1,0:T(8,128)(2,1)S(1)}, bf16[512,192]{1,0:T(8,128)(2,1)S(1)}, u32[]{:S(2)}, u32[]{:S(2)}) %collective-permute-start.10) | collective-permute-done | bytes 196640 | tf_op jit(solution)/shard_map/ppermute | solution.py:802
  121.4 11.7 %self_forward.1 = (bf16[16,2,64,1024]{3,2,1,0:T(8,128)(2,1)}, bf16[1024,384]{1,0:T(8,128)(2,1)}, bf16[1024,128]{1,0:T(8,128)(2,1)}) custom-call(s32[16]{0:T(128)} %broadcast_xor_fusion.source_ref, bf16[4,2,64,1024]{3,2,1,0:T(8,128)(2,1)} %copy-done.5, bf16[4,2,64,1024]{3,2,1,0:T(8,128)(2,1)} %copy-done.6, ...), custom_call_target="tpu_custom_call" | custom-call | flops 13799999488 | bytes 44280000 | tf_op jit(solution)/shard_map/self_forward/pallas_call | solution.py:922
  133.1 14.6 %collective-permute-done.12.refs_1_ = bf16[5,128,1024]{2,1,0:T(8,128)(2,1)} collective-permute-done((bf16[5,128,1024]{2,1,0:T(8,128)(2,1)}, bf16[5,128,1024]{2,1,0:T(8,128)(2,1)}, u32[]{:S(2)}, u32[]{:S(2)}) %collective-permute-start.12) | collective-permute-done | bytes 1310752 | tf_op jit(solution)/shard_map/ppermute | solution.py:799
  148.2 3.5 all-to-all-start
  153.6 17.0 %all-to-all-done.o1_ref = bf16[16,64,128]{2,1,0:T(8,128)(2,1)S(1)} async-done(((bf16[16,64,128]{2,1,0:T(8,128)(2,1)}), bf16[16,64,128]{2,1,0:T(8,128)(2,1)S(1)}, u32[]{:S(2)}, u32[]{:S(2)}) %all-to-all-start) | async-done | bytes 262176 | tf_op jit(solution)/shard_map/all_to_all | solution.py:935
  172.1 11.9 %cross_kv.1 = (bf16[2,512,1024]{2,1,0:T(8,128)(2,1)}, bf16[2,512,1024]{2,1,0:T(8,128)(2,1)}) custom-call(s32[5]{0:T(128)} %stack.120.starts_ref, bf16[16,2,32,1024]{3,2,1,0:T(8,128)(2,1)} %bitcast.83, bf16[512,1024]{1,0:T(8,128)(2,1)} %wk.3, bf16[512,1024]{1,0:T(8,128)(2,1)} %wv.3, bf16[5,128,1024]{2,1,0:T(8,128)(2,1)} %collective-permute-done.11.refs_0_, ...), custom_call_target="tpu_custom_call" | custom-call | flops 9200000000 | bytes 29520000 | tf_op jit(solution)/shard_map/cross_kv/pallas_call | solution.py:332
  184.0 13.3 %mid_forward.1 = (bf16[3,128,1024]{2,1,0:T(8,128)(2,1)}, f32[128,1024]{1,0:T(8,128)}, bf16[128,1024]{1,0:T(8,128)(2,1)}, f32[128,1024]{1,0:T(8,128)}, bf16[128,1...) custom-call(s32[5]{0:T(128)} %stack.120.starts_ref, bf16[16,64,128]{2,1,0:T(8,128)(2,1)} %copy-done.18, ...), custom_call_target="tpu_custom_call" | custom-call | flops 13799999488 | bytes 44280000 | tf_op jit(solution)/shard_map/mid_forward/pallas_call | solution.py:945
  200.2 9.9 %dense_layer.2 = (bf16[128,5248]{1,0:T(8,128)(2,1)}, f32[128,1024]{1,0:T(8,128)}, bf16[128,1024]{1,0:T(8,128)(2,1)}, f32[128,1024]{1,0:T(8,128)}, bf16[128,1024]{1,0:T(8,128)(2,1)}) custom-call(s32[7]{0:T(128)} %concatenate.41.starts_ref, bf16[128,1024]{1,0:T(8,128)(2,1)} %get-tuple-element.117.n_ref.n0_ref, bf16[128,1024]{1,0:T(8,128)(2,1)} %bitcast.86, ...), custom_call_target="tpu_custom_call" | custom-call | flops 14949999616 | bytes 47970000 | tf_op jit(solution)/shard_map/dense_layer/pallas_call | solution.py:544
  210.2 4.1 collective-permute-done.20.left_more_ref
  215.1 9.9 %dense_layer.3 = (bf16[128,5248]{1,0:T(8,128)(2,1)}, f32[128,1024]{1,0:T(8,128)}, bf16[128,1024]{1,0:T(8,128)(2,1)}, f32[128,1024]{1,0:T(8,128)}, bf16[128,1024]{1,0:T(8,128)(2,1)}) custom-call(s32[7]{0:T(128)} %concatenate.41.starts_ref, bf16[128,1024]{1,0:T(8,128)(2,1)} %copy-done.41, bf16[128,1024]{1,0:T(8,128)(2,1)} %copy-done.40, bf16[512,2816]{1,0:T(8,128)(2,1)} %wg.3, ...), custom_call_target="tpu_custom_call" | custom-call | flops 14949999616 | bytes 47970000 | tf_op jit(solution)/shard_map/dense_layer/pallas_call | solution.py:544
  227.1 7.1 %collective-permute-done.22.more_ref = bf16[128,1024]{1,0:T(8,128)(2,1)S(1)} collective-permute-done((bf16[128,1024]{1,0:T(8,128)(2,1)}, bf16[128,1024]{1,0:T(8,128)(2,1)S(1)}, u32[]{:S(2)}, u32[]{:S(2)}) %collective-permute-start.22) | collective-permute-done | bytes 262176 | tf_op jit(solution)/shard_map/ppermute | solution.py:802
  236.3 7.1 %dense_weight.1 = (bf16[4,704,128]{2,1,0:T(8,128)(2,1)}, bf16[4,704,128]{2,1,0:T(8,128)(2,1)}, bf16[4,704,128]{2,1,0:T(8,128)(2,1)}, bf16[4,704,128]{2,1,0:T(8,1...) custom-call(s32[3]{0:T(128)} %pad_add_fusion.2.where_ref, ...), custom_call_target="tpu_custom_call" | custom-call | flops 8049999872 | bytes 25830000 | tf_op jit(solution)/shard_map/dense_weight/pallas_call | solution.py:645
  245.5 16.5 %cross_backward.1 = (bf16[128,2048]{1,0:T(8,128)(2,1)}, f32[128,1024]{1,0:T(8,128)}, bf16[8,16,2,32,128]{4,3,2,1,0:T(8,128)(2,1)}, bf16[8,16,2,32,128]{4,3,2,1,0:T(8,128)(2,1)}, f32[1,1024]{1,0:T(1,128)}) custom-call(s32[5]{0:T(128)} %stack.120.starts_ref, s32[9]{0:T(128)} %pad_add_fusion.1.slots_ref, bf16[128,1024]{1,0:T(8,128)(2,1)} %bitcast.88, ...), custom_call_target="tpu_custom_call" | custom-call | flops 17250000896 | bytes 55350000 | tf_op jit(solution)/shard_map/cross_backward/pallas_call | solution.py:1035
  262.6 7.0 %mid_backward.1 = (f32[128,1024]{1,0:T(8,128)}, bf16[128,1024]{1,0:T(8,128)(2,1)}, bf16[16,64,128]{2,1,0:T(8,128)(2,1)}, f32[1,1024]{1,0:T(1,128)}) custom-call(s32[5]{0:T(128)} %stack.120.starts_ref, bf16[128,2048]{1,0:T(8,128)(2,1)} %get-tuple-element.131.right_ref, f32[128,1024]{1,0:T(8,128)} %get-tuple-element.127.gx2_ref, ...), custom_call_target="tpu_custom_call" | custom-call | flops 6899999744 | bytes 22140000 | tf_op jit(solution)/shard_map/mid_backward/pallas_call | solution.py:1053
  269.7 3.9 all-to-all-start.1
  277.7 2.5 convert_add_fusion
  286.1 9.7 %self_backward.1 = (bf16[1024,384]{1,0:T(8,128)(2,1)}, f32[256,1024]{1,0:T(8,128)}) custom-call(bf16[1024,384]{1,0:T(8,128)(2,1)} %get-tuple-element.115.qkv_ref, bf16[1024,128]{1,0:T(8,128)(2,1)} %bitcast.63, f32[256,1024]{1,0:T(8,128)} %bias_table.1.refs_6_.table_ref, s32[2,1024]{1,0:T(2,128)} %reshape.112.refs_7_.doc_row_ref, ...), custom_call_target="tpu_custom_call" | custom-call | flops 11500000256 | bytes 36900000 | tf_op jit(solution)/shard_map/self_backward/pallas_call | solution.py:1080
  297.3 2.4 collective-permute-start.43
  301.4 8.4 %collective-permute-done.31 = bf16[4,16,2,32,128]{4,3,2,1,0:T(8,128)(2,1)} collective-permute-done((bf16[4,16,2,32,128]{4,3,2,1,0:T(8,128)(2,1)}, bf16[4,16,2,32,128]{4,3,2,1,0:T(8,128)(2,1)}, u32[]{:S(2)}, u32[]{:S(2)}) %collective-permute-start.31) | collective-permute-done | bytes 1048608 | tf_op jit(solution)/shard_map/ppermute | solution.py:799
  309.8 5.6 %head_weight.1 = bf16[2,768,128]{2,1,0:T(8,128)(2,1)} custom-call(bf16[16,2,64,1024]{3,2,1,0:T(8,128)(2,1)} %get-tuple-element.114.n_ref, bf16[1024,384]{1,0:T(8,128)(2,1)} %get-tuple-element.136.d_ref), custom_call_target="tpu_custom_call" | custom-call | flops 6899999744 | bytes 22140000 | tf_op jit(solution)/shard_map/head_weight/pallas_call | solution.py:1095
  315.5 4.8 token_weight.1
  320.6 3.4 collective-permute-done.48
  326.0 2.4 collective-permute-start.46
  336.9 5.4 %collective-permute-done.49 = bf16[2,704,128]{2,1,0:T(8,128)(2,1)S(1)} collective-permute-done((bf16[2,704,128]{2,1,0:T(8,128)(2,1)S(1)}, bf16[2,704,128]{2,1,0:T(8,128)(2,1)S(1)}, u32[]{:S(2)}, u32[]{:S(2)}) %collective-permute-start.49) | collective-permute-done | bytes 360480 | tf_op jit(solution)/shard_map/ppermute | solution.py:799
  342.4 2.8 collective-permute-start.50
  345.2 10.5 %collective-permute-done.36 = bf16[2,16,2,32,128]{4,3,2,1,0:T(8,128)(2,1)S(1)} collective-permute-done((bf16[2,16,2,32,128]{4,3,2,1,0:T(8,128)(2,1)S(1)}, bf16[2,16,2,32,128]{4,3,2,1,0:T(8,128)(2,1)S(1)}, u32[]{:S(2)}, u32[]{:S(2)}) %collective-permute-start.36) | collective-permute-done | bytes 524320 | tf_op jit(solution)/shard_map/ppermute | solution.py:799
  356.9 2.5 collective-permute-start.53
  359.5 9.1 %collective-permute-done.37 = bf16[1,16,2,32,128]{4,3,2,1,0:T(8,128)(2,1)S(1)} collective-permute-done((bf16[1,16,2,32,128]{4,3,2,1,0:T(8,128)(2,1)S(1)}, bf16[1,16,2,32,128]{4,3,2,1,0:T(8,128)(2,1)S(1)}, u32[]{:S(2)}, u32[]{:S(2)}) %collective-permute-start.37) | collective-permute-done | bytes 262176 | tf_op jit(solution)/shard_map/ppermute | solution.py:799
  369.4 2.6 collective-permute-done.53
  372.1 3.1 cross_head_weight.1
  377.1 3.8 collective-permute-done.54
  385.7 34.0 %collective-permute-done.33.refs_0_ = bf16[3,256,1024]{2,1,0:T(8,128)(2,1)S(1)} collective-permute-done((bf16[3,256,1024]{2,1,0:T(8,128)(2,1)S(1)}, bf16[3,256,1024]{2,1,0:T(8,128)(2,1)S(1)}, u32[]{:S(2)}, u32[]{:S(2)}) %collective-permute-start.33) | collective-permute-done | bytes 1572896 | tf_op jit(solution)/shard_map/ppermute | solution.py:802
  419.7 3.6 all-to-all-start.2
  424.0 7.4 %bucket_sums.1 = f32[32,128]{1,0:T(8,128)} custom-call(s32[32]{0:T(128)} %convert_reduce_fusion.edge_ref, f32[256,1024]{1,0:T(8,128)} %get-tuple-element.145.grad_ref), custom_call_target="tpu_custom_call" | custom-call | flops 8049999872 | bytes 25830000 | tf_op jit(solution)/shard_map/bucket_sums/pallas_call | solution.py:137
  432.3 22.4 %all-to-all-done.2.d_ref = bf16[16,64,384]{2,1,0:T(8,128)(2,1)S(1)} async-done(((bf16[16,64,384]{2,1,0:T(8,128)(2,1)}), bf16[16,64,384]{2,1,0:T(8,128)(2,1)S(1)}, u32[]{:S(2)}, u32[]{:S(2)}) %all-to-all-start.2) | async-done | bytes 786464 | tf_op jit(solution)/shard_map/all_to_all | solution.py:1129
  455.6 6.7 %input_grad.1 = (f32[128,1024]{1,0:T(8,128)}, f32[1,1024]{1,0:T(1,128)}) custom-call(s32[3]{0:T(128)} %pad_add_fusion.3.starts_ref, bf16[16,64,384]{2,1,0:T(8,128)(2,1)} %copy-done.7, bf16[2,64,1024]{2,1,0:T(8,128)(2,1)} %bitcast.69, f32[3,1024]{1,0:T(4,128)} %copy-done.25, f32[128,1024]{1,0:T(8,128)} %get-tuple-element.139.gx1_ref, bf16[512,1024]{1,0:T(8,128)(2,1)} %wq.5, ...), custom_call_target="tpu_custom_call" | custom-call | flops 8049999872 | bytes 25830000 | tf_op jit(solution)/shard_map/input_grad/pallas_call | solution.py:1130
  464.7 3.5 all-to-all-start.3
  476.8 6.1 %all-to-all-done.3.d_ref = bf16[16,64,128]{2,1,0:T(8,128)(2,1)S(1)} async-done(((bf16[16,64,128]{2,1,0:T(8,128)(2,1)}), bf16[16,64,128]{2,1,0:T(8,128)(2,1)S(1)}, u32[]{:S(2)}, u32[]{:S(2)}) %all-to-all-start.3) | async-done | bytes 262176 | tf_op jit(solution)/shard_map/all_to_all | solution.py:1167
  483.7 5.5 %encoder_grad.1 = f32[64,1024]{1,0:T(8,128)} custom-call(s32[5]{0:T(128)} %stack.120.starts_ref, bf16[16,64,128]{2,1,0:T(8,128)(2,1)} %copy-done.19, bf16[512,1024]{1,0:T(8,128)(2,1)} %wk.3, bf16[512,1024]{1,0:T(8,128)(2,1)} %wv.3, bf16[5,128,1024]{2,1,0:T(8,128)(2,1)} %collective-permute-done.11.refs_0_, ...), custom_call_target="tpu_custom_call" | custom-call | flops 4600000000 | bytes 14760000 | tf_op jit(solution)/shard_map/encoder_grad/pallas_call | solution.py:1168
  490.1 4.1 collective-permute-done.42
  495.6 17.4 %spread.1 = (f32[2,4,64,2816]{3,2,1,0:T(8,128)}, f32[2,4,64,2816]{3,2,1,0:T(8,128)}, f32[1408,1024]{1,0:T(8,128)}, f32[512,1024]{1,0:T(8,128)}, f32[512,1024]{1,...) custom-call(s32[3]{0:T(128)} %pad_add_fusion.2.where_ref, ...), custom_call_target="tpu_custom_call" | custom-call | flops 23000000512 | bytes 73800000 | tf_op jit(solution)/shard_map/spread/pallas_call | solution.py:718
  (270 shorter events, 87.9 us)
Async XLA Ops:
  7.2 163.9 %all-gather.6.cloned.1.call-start = ((), (), s32[]{:S(2)}) async-start(), calls=%async_computation.5 | async-start | bytes 2228224 | tf_op jit(solution)/shard_map/all_gather | solution.py:849
  7.2 91.0 %collective-permute-start.3 = (bf16[2,64,1024]{2,1,0:T(8,128)(2,1)}, bf16[2,64,1024]{2,1,0:T(8,128)(2,1)S(1)}, u32[]{:S(2)}, u32[]{:S(2)}) collective-permute-start(bf16[2,64,1024]{2,1,0:T(8,128)(2,1)} %bitcast.65), channel_id=1, source_target_pairs={{0,4},{2,6},{4,0},{6,2},{8,12},{10,14},{12,8},{14,10},{16,20},{18,... | collective-permute-start | bytes 786440 | tf_op jit(solution)/shard_map/ppermute | solution.py:799
  10.2 78.2 %collective-permute-start.1 = (bf16[2,64,1024]{2,1,0:T(8,128)(2,1)}, bf16[2,64,1024]{2,1,0:T(8,128)(2,1)S(1)}, u32[]{:S(2)}, u32[]{:S(2)}) collective-permute-start(bf16[2,64,1024]{2,1,0:T(8,128)(2,1)} %bitcast.66), channel_id=1, source_target_pairs={{0,8},{2,10},{4,12},{6,14},{8,0},{10,2},{12,4},{14,6},{16,24},{18,... | collective-permute-start | bytes 786440 | tf_op jit(solution)/shard_map/ppermute | solution.py:799
  11.8 74.7 %collective-permute-start = (bf16[2,64,1024]{2,1,0:T(8,128)(2,1)}, bf16[2,64,1024]{2,1,0:T(8,128)(2,1)S(1)}, u32[]{:S(2)}, u32[]{:S(2)}) collective-permute-start(bf16[2,64,1024]{2,1,0:T(8,128)(2,1)} %bitcast.67), channel_id=1, source_target_pairs={{0,16},{2,18},{4,20},{6,22},{8,24},{10,26},{12,28},{14,30},{16,0},... | collective-permute-start | bytes 786440 | tf_op jit(solution)/shard_map/ppermute | solution.py:799
  17.3 69.7 %collective-permute-start.8 = (bf16[4,512]{1,0:T(4,128)(2,1)S(1)}, bf16[4,512]{1,0:T(4,128)(2,1)S(1)}, u32[]{:S(2)}, u32[]{:S(2)}) collective-permute-start(bf16[4,512]{1,0:T(4,128)(2,1)S(1)} %fusion.11), channel_id=1, source_target_pairs={{0,1},{1,0},{2,3},{3,2},{4,5},{5,4},{6,7},{7,6},{8,9},{9,8},{10,11... | collective-permute-start | bytes 12296 | tf_op jit(solution)/shard_map/ppermute | solution.py:802
  83.0 35.9 %collective-permute-start.11 = (bf16[5,128,1024]{2,1,0:T(8,128)(2,1)}, bf16[5,128,1024]{2,1,0:T(8,128)(2,1)}, u32[]{:S(2)}, u32[]{:S(2)}) collective-permute-start(bf16[5,128,1024]{2,1,0:T(8,128)(2,1)} %get-tuple-element.97), channel_id=1, source_target_pairs={{0,1},{1,0},{2,3},{3,2},{4,5},{5,4},{6,7},{7,6},{8,9},{9,8},{10,11... | collective-permute-start | bytes 3932168 | tf_op jit(solution)/shard_map/ppermute | solution.py:802
  87.9 14.9 %collective-permute-start.4 = (bf16[2,64,1024]{2,1,0:T(8,128)(2,1)S(1)}, bf16[2,64,1024]{2,1,0:T(8,128)(2,1)S(1)}, u32[]{:S(2)}, u32[]{:S(2)}) collective-permute-start(bf16[2,64,1024]{2,1,0:T(8,128)(2,1)S(1)} %collective-permute-done), channel_id=1, source_target_pairs={{0,4},{2,6},{4,0},{6,2},{8,12},{10,14},{12,8},{14,10},{16,20},{18,... | collective-permute-start | bytes 786440 | tf_op jit(solution)/shard_map/ppermute | solution.py:799
  88.5 14.4 %collective-permute-start.5 = (bf16[2,64,1024]{2,1,0:T(8,128)(2,1)S(1)}, bf16[2,64,1024]{2,1,0:T(8,128)(2,1)}, u32[]{:S(2)}, u32[]{:S(2)}) collective-permute-start(bf16[2,64,1024]{2,1,0:T(8,128)(2,1)S(1)} %collective-permute-done.1), channel_id=1, source_target_pairs={{0,4},{2,6},{4,0},{6,2},{8,12},{10,14},{12,8},{14,10},{16,20},{18,... | collective-permute-start | bytes 786440 | tf_op jit(solution)/shard_map/ppermute | solution.py:799
  98.2 20.0 %collective-permute-start.10 = (bf16[512,192]{1,0:T(8,128)(2,1)S(1)}, bf16[512,192]{1,0:T(8,128)(2,1)S(1)}, u32[]{:S(2)}, u32[]{:S(2)}) collective-permute-start(bf16[512,192]{1,0:T(8,128)(2,1)S(1)} %pad_maximum_fusion.4), channel_id=1, source_target_pairs={{0,1},{1,0},{2,3},{3,2},{4,5},{5,4},{6,7},{7,6},{8,9},{9,8},{10,11... | collective-permute-start | bytes 589832 | tf_op jit(solution)/shard_map/ppermute | solution.py:802
  102.8 18.5 %collective-permute-start.7 = (bf16[4,2,64,1024]{3,2,1,0:T(8,128)(2,1)S(1)}, bf16[4,2,64,1024]{3,2,1,0:T(8,128)(2,1)}, u32[]{:S(2)}, u32[]{:S(2)}) collective-permute-start(bf16[4,2,64,1024]{3,2,1,0:T(8,128)(2,1)S(1)} %pad_maximum_fusion.1.refs_0_), channel_id=1, source_target_pairs={{0,2},{2,0},{4,6},{6,4},{8,10},{10,8},{12,14},{14,12},{16,18},{18,... | collective-permute-start | bytes 3145736 | tf_op jit(solution)/shard_map/ppermute | solution.py:799
  106.9 14.5 %collective-permute-start.9 = (bf16[4,2,64,1024]{3,2,1,0:T(8,128)(2,1)S(1)}, bf16[4,2,64,1024]{3,2,1,0:T(8,128)(2,1)}, u32[]{:S(2)}, u32[]{:S(2)}) collective-permute-start(bf16[4,2,64,1024]{3,2,1,0:T(8,128)(2,1)S(1)} %pad_maximum_fusion.2.refs_1_), channel_id=1, source_target_pairs={{0,2},{2,0},{4,6},{6,4},{8,10},{10,8},{12,14},{14,12},{16,18},{18,... | collective-permute-start | bytes 3145736 | tf_op jit(solution)/shard_map/ppermute | solution.py:799
  118.8 28.9 %collective-permute-start.12 = (bf16[5,128,1024]{2,1,0:T(8,128)(2,1)}, bf16[5,128,1024]{2,1,0:T(8,128)(2,1)}, u32[]{:S(2)}, u32[]{:S(2)}) collective-permute-start(bf16[5,128,1024]{2,1,0:T(8,128)(2,1)} %collective-permute-done.11.refs_0_), channel_id=1, source_target_pairs={{0,4},{2,6},{4,0},{6,2},{8,12},{10,14},{12,8},{14,10},{16,20},{18,... | collective-permute-start | bytes 3932168 | tf_op jit(solution)/shard_map/ppermute | solution.py:799
  120.9 26.8 %collective-permute-start.15 = (bf16[2,128,1408]{2,1,0:T(8,128)(2,1)S(1)}, bf16[2,128,1408]{2,1,0:T(8,128)(2,1)}, u32[]{:S(2)}, u32[]{:S(2)}) collective-permute-start(bf16[2,128,1408]{2,1,0:T(8,128)(2,1)S(1)} %copy-done.32), channel_id=1, source_target_pairs={{0,1},{1,0},{2,3},{3,2},{4,5},{5,4},{6,7},{7,6},{8,9},{9,8},{10,11... | collective-permute-start | bytes 2162696 | tf_op jit(solution)/shard_map/ppermute | solution.py:802
  121.4 49.7 %collective-permute-start.13 = (bf16[5,128,1024]{2,1,0:T(8,128)(2,1)}, bf16[5,128,1024]{2,1,0:T(8,128)(2,1)}, u32[]{:S(2)}, u32[]{:S(2)}) collective-permute-start(bf16[5,128,1024]{2,1,0:T(8,128)(2,1)} %collective-permute-done.11.refs_0_), channel_id=1, source_target_pairs={{0,2},{2,0},{4,6},{6,4},{8,10},{10,8},{12,14},{14,12},{16,18},{18,... | collective-permute-start | bytes 3932168 | tf_op jit(solution)/shard_map/ppermute | solution.py:799
  147.7 23.4 %collective-permute-start.14 = (bf16[5,128,1024]{2,1,0:T(8,128)(2,1)}, bf16[5,128,1024]{2,1,0:T(8,128)(2,1)S(1)}, u32[]{:S(2)}, u32[]{:S(2)}) collective-permute-start(bf16[5,128,1024]{2,1,0:T(8,128)(2,1)} %collective-permute-done.12.refs_1_), channel_id=1, source_target_pairs={{0,2},{2,0},{4,6},{6,4},{8,10},{10,8},{12,14},{14,12},{16,18},{18,... | collective-permute-start | bytes 3932168 | tf_op jit(solution)/shard_map/ppermute | solution.py:799
  147.7 22.8 %collective-permute-start.16 = (bf16[2,128,1408]{2,1,0:T(8,128)(2,1)}, bf16[2,128,1408]{2,1,0:T(8,128)(2,1)S(1)}, u32[]{:S(2)}, u32[]{:S(2)}) collective-permute-start(bf16[2,128,1408]{2,1,0:T(8,128)(2,1)} %collective-permute-done.15.refs_0_), channel_id=1, source_target_pairs={{0,8},{2,10},{4,12},{6,14},{8,0},{10,2},{12,4},{14,6},{16,24},{18,... | collective-permute-start | bytes 2162696 | tf_op jit(solution)/shard_map/ppermute | solution.py:799
  148.2 22.4 %all-to-all-start = ((bf16[16,64,128]{2,1,0:T(8,128)(2,1)}), bf16[16,64,128]{2,1,0:T(8,128)(2,1)S(1)}, u32[]{:S(2)}, u32[]{:S(2)}) async-start(bf16[16,64,128]{2,1,0:T(8,128)(2,1)} %bitcast.62), calls=%async_computation | async-start | bytes 524288 | tf_op jit(solution)/shard_map/all_to_all | solution.py:935
  153.1 61.3 %collective-permute-start.21 = (bf16[128,1024]{1,0:T(8,128)(2,1)}, bf16[128,1024]{1,0:T(8,128)(2,1)S(1)}, u32[]{:S(2)}, u32[]{:S(2)}) collective-permute-start(bf16[128,1024]{1,0:T(8,128)(2,1)} %bitcast.85), channel_id=1, source_target_pairs={{0,1},{1,0},{2,3},{3,2},{4,5},{5,4},{6,7},{7,6},{8,9},{9,8},{10,11... | collective-permute-start | bytes 786440 | tf_op jit(solution)/shard_map/ppermute | solution.py:802
  170.5 28.8 %collective-permute-start.17 = (bf16[2,128,1408]{2,1,0:T(8,128)(2,1)}, bf16[2,128,1408]{2,1,0:T(8,128)(2,1)S(1)}, u32[]{:S(2)}, u32[]{:S(2)}) collective-permute-start(bf16[2,128,1408]{2,1,0:T(8,128)(2,1)} %collective-permute-done.15.refs_0_), channel_id=1, source_target_pairs={{0,2},{2,0},{4,6},{6,4},{8,10},{10,8},{12,14},{14,12},{16,18},{18,... | collective-permute-start | bytes 2162696 | tf_op jit(solution)/shard_map/ppermute | solution.py:799
  170.5 28.8 %collective-permute-start.18 = (bf16[2,128,1408]{2,1,0:T(8,128)(2,1)S(1)}, bf16[2,128,1408]{2,1,0:T(8,128)(2,1)}, u32[]{:S(2)}, u32[]{:S(2)}) collective-permute-start(bf16[2,128,1408]{2,1,0:T(8,128)(2,1)S(1)} %collective-permute-done.16.refs_1_), channel_id=1, source_target_pairs={{0,2},{2,0},{4,6},{6,4},{8,10},{10,8},{12,14},{14,12},{16,18},{18,... | collective-permute-start | bytes 2162696 | tf_op jit(solution)/shard_map/ppermute | solution.py:799
  197.3 12.9 %collective-permute-start.19 = (bf16[128,1024]{1,0:T(8,128)(2,1)}, bf16[128,1024]{1,0:T(8,128)(2,1)S(1)}, u32[]{:S(2)}, u32[]{:S(2)}) collective-permute-start(bf16[128,1024]{1,0:T(8,128)(2,1)} %get-tuple-element.117.n_ref.n0_ref), channel_id=1, source_target_pairs={{0,1},{1,0},{2,3},{3,2},{4,5},{5,4},{6,7},{7,6},{8,9},{9,8},{10,11... | collective-permute-start | bytes 786440 | tf_op jit(solution)/shard_map/ppermute | solution.py:802
  197.8 16.5 %collective-permute-start.20 = (bf16[3,128,512]{2,1,0:T(8,128)(2,1)}, bf16[3,128,512]{2,1,0:T(8,128)(2,1)S(1)}, u32[]{:S(2)}, u32[]{:S(2)}) collective-permute-start(bf16[3,128,512]{2,1,0:T(8,128)(2,1)} %get-tuple-element.110), channel_id=1, source_target_pairs={{0,1},{1,0},{2,3},{3,2},{4,5},{5,4},{6,7},{7,6},{8,9},{9,8},{10,11... | collective-permute-start | bytes 1179656 | tf_op jit(solution)/shard_map/ppermute | solution.py:802
  210.2 24.0 %collective-permute-start.23 = (bf16[128,5248]{1,0:T(8,128)(2,1)}, bf16[128,5248]{1,0:T(8,128)(2,1)S(1)}, u32[]{:S(2)}, u32[]{:S(2)}) collective-permute-start(bf16[128,5248]{1,0:T(8,128)(2,1)} %get-tuple-element.118.own0_ref), channel_id=1, source_target_pairs={{0,2},{2,0},{4,6},{6,4},{8,10},{10,8},{12,14},{14,12},{16,18},{18,... | collective-permute-start | bytes 4030472 | tf_op jit(solution)/shard_map/ppermute | solution.py:799
  243.4 19.1 %collective-permute-start.25 = (bf16[4,704,128]{2,1,0:T(8,128)(2,1)}, bf16[4,704,128]{2,1,0:T(8,128)(2,1)S(1)}, u32[]{:S(2)}, u32[]{:S(2)}) collective-permute-start(bf16[4,704,128]{2,1,0:T(8,128)(2,1)} %get-tuple-element.120), channel_id=1, source_target_pairs={{0,8},{2,10},{4,12},{6,14},{8,0},{10,2},{12,4},{14,6},{16,24},{18,... | collective-permute-start | bytes 2162696 | tf_op jit(solution)/shard_map/ppermute | solution.py:799
  244.1 17.9 %collective-permute-start.26 = (bf16[4,704,128]{2,1,0:T(8,128)(2,1)}, bf16[4,704,128]{2,1,0:T(8,128)(2,1)S(1)}, u32[]{:S(2)}, u32[]{:S(2)}) collective-permute-start(bf16[4,704,128]{2,1,0:T(8,128)(2,1)} %get-tuple-element.125), channel_id=1, source_target_pairs={{0,4},{2,6},{4,0},{6,2},{8,12},{10,14},{12,8},{14,10},{16,20},{18,... | collective-permute-start | bytes 2162696 | tf_op jit(solution)/shard_map/ppermute | solution.py:799
  244.9 17.6 %collective-permute-start.27 = (bf16[4,704,128]{2,1,0:T(8,128)(2,1)}, bf16[4,704,128]{2,1,0:T(8,128)(2,1)S(1)}, u32[]{:S(2)}, u32[]{:S(2)}) collective-permute-start(bf16[4,704,128]{2,1,0:T(8,128)(2,1)} %get-tuple-element.126), channel_id=1, source_target_pairs={{0,1},{1,0},{2,3},{3,2},{4,5},{5,4},{6,7},{7,6},{8,9},{9,8},{10,11... | collective-permute-start | bytes 2162696 | tf_op jit(solution)/shard_map/ppermute | solution.py:802
  269.7 15.7 %all-to-all-start.1 = ((bf16[16,64,128]{2,1,0:T(8,128)(2,1)}), bf16[16,64,128]{2,1,0:T(8,128)(2,1)S(1)}, u32[]{:S(2)}, u32[]{:S(2)}) async-start(bf16[16,64,128]{2,1,0:T(8,128)(2,1)} %get-tuple-element.129), calls=%async_computation.1 | async-start | bytes 524288 | tf_op jit(solution)/shard_map/all_to_all | solution.py:1068
  273.6 222.0 %all-gather.4.cloned.1.call-start = ((), (), s32[]{:S(2)}) async-start(), calls=%async_computation.4 | async-start | bytes 18104320 | tf_op jit(solution)/shard_map/all_gather | solution.py:1190
  273.9 25.8 %collective-permute-start.29 = (bf16[128,1024]{1,0:T(8,128)(2,1)}, bf16[128,1024]{1,0:T(8,128)(2,1)}, u32[]{:S(2)}, u32[]{:S(2)}) collective-permute-start(bf16[128,1024]{1,0:T(8,128)(2,1)} %get-tuple-element.132.last_ref), channel_id=1, source_target_pairs={{0,1},{1,0},{2,3},{3,2},{4,5},{5,4},{6,7},{7,6},{8,9},{9,8},{10,11... | collective-permute-start | bytes 786440 | tf_op jit(solution)/shard_map/ppermute | solution.py:802
  275.1 25.1 %collective-permute-start.28 = (bf16[128,2048]{1,0:T(8,128)(2,1)}, bf16[128,2048]{1,0:T(8,128)(2,1)}, u32[]{:S(2)}, u32[]{:S(2)}) collective-permute-start(bf16[128,2048]{1,0:T(8,128)(2,1)} %get-tuple-element.131.right_ref), channel_id=1, source_target_pairs={{0,1},{1,0},{2,3},{3,2},{4,5},{5,4},{6,7},{7,6},{8,9},{9,8},{10,11... | collective-permute-start | bytes 1572872 | tf_op jit(solution)/shard_map/ppermute | solution.py:802
  283.5 26.4 %collective-permute-start.31 = (bf16[4,16,2,32,128]{4,3,2,1,0:T(8,128)(2,1)}, bf16[4,16,2,32,128]{4,3,2,1,0:T(8,128)(2,1)}, u32[]{:S(2)}, u32[]{:S(2)}) collective-permute-start(bf16[4,16,2,32,128]{4,3,2,1,0:T(8,128)(2,1)} %slice.248), channel_id=1, source_target_pairs={{0,4},{2,6},{4,0},{6,2},{8,12},{10,14},{12,8},{14,10},{16,20},{18,... | collective-permute-start | bytes 3145736 | tf_op jit(solution)/shard_map/ppermute | solution.py:799
  295.8 24.4 %collective-permute-start.45 = (bf16[2,704,128]{2,1,0:T(8,128)(2,1)S(1)}, bf16[2,704,128]{2,1,0:T(8,128)(2,1)S(1)}, u32[]{:S(2)}, u32[]{:S(2)}) collective-permute-start(bf16[2,704,128]{2,1,0:T(8,128)(2,1)S(1)} %slice.253), channel_id=1, source_target_pairs={{0,8},{2,10},{4,12},{6,14},{8,0},{10,2},{12,4},{14,6},{16,24},{18,... | collective-permute-start | bytes 1081352 | tf_op jit(solution)/shard_map/ppermute | solution.py:799
  297.3 23.1 %collective-permute-start.43 = (bf16[2,704,128]{2,1,0:T(8,128)(2,1)S(1)}, bf16[2,704,128]{2,1,0:T(8,128)(2,1)S(1)}, u32[]{:S(2)}, u32[]{:S(2)}) collective-permute-start(bf16[2,704,128]{2,1,0:T(8,128)(2,1)S(1)} %copy-done.17), channel_id=1, source_target_pairs={{0,16},{2,18},{4,20},{6,22},{8,24},{10,26},{12,28},{14,30},{16,0},... | collective-permute-start | bytes 1081352 | tf_op jit(solution)/shard_map/ppermute | solution.py:799
  299.6 24.4 %collective-permute-start.48 = (bf16[4,704,128]{2,1,0:T(8,128)(2,1)S(1)}, bf16[4,704,128]{2,1,0:T(8,128)(2,1)S(1)}, u32[]{:S(2)}, u32[]{:S(2)}) collective-permute-start(bf16[4,704,128]{2,1,0:T(8,128)(2,1)S(1)} %copy-done.35), channel_id=1, source_target_pairs={{0,4},{2,6},{4,0},{6,2},{8,12},{10,14},{12,8},{14,10},{16,20},{18,... | collective-permute-start | bytes 2162696 | tf_op jit(solution)/shard_map/ppermute | solution.py:799
  300.2 23.8 %collective-permute-start.47 = (bf16[4,704,128]{2,1,0:T(8,128)(2,1)S(1)}, bf16[4,704,128]{2,1,0:T(8,128)(2,1)S(1)}, u32[]{:S(2)}, u32[]{:S(2)}) collective-permute-start(bf16[4,704,128]{2,1,0:T(8,128)(2,1)S(1)} %copy-done.33), channel_id=1, source_target_pairs={{0,1},{1,0},{2,3},{3,2},{4,5},{5,4},{6,7},{7,6},{8,9},{9,8},{10,11... | collective-permute-start | bytes 2162696 | tf_op jit(solution)/shard_map/ppermute | solution.py:802
  320.2 15.5 %collective-permute-start.51 = (bf16[8,768,128]{2,1,0:T(8,128)(2,1)}, bf16[8,768,128]{2,1,0:T(8,128)(2,1)S(1)}, u32[]{:S(2)}, u32[]{:S(2)}) collective-permute-start(bf16[8,768,128]{2,1,0:T(8,128)(2,1)} %get-tuple-element.160), channel_id=1, source_target_pairs={{0,2},{2,0},{4,6},{6,4},{8,10},{10,8},{12,14},{14,12},{16,18},{18,... | collective-permute-start | bytes 4718600 | tf_op jit(solution)/shard_map/ppermute | solution.py:799
  328.4 31.1 %collective-permute-start.32 = (bf16[1,768,128]{2,1,0:T(8,128)(2,1)S(1)}, bf16[1,768,128]{2,1,0:T(8,128)(2,1)S(1)}, u32[]{:S(2)}, u32[]{:S(2)}) collective-permute-start(bf16[1,768,128]{2,1,0:T(8,128)(2,1)S(1)} %constant_dynamic-slice_fusion.3), channel_id=1, source_target_pairs={{0,1},{1,0},{2,3},{3,2},{4,5},{5,4},{6,7},{7,6},{8,9},{9,8},{10,11... | collective-permute-start | bytes 589832 | tf_op jit(solution)/shard_map/ppermute | solution.py:802
  329.6 12.7 %collective-permute-start.49 = (bf16[2,704,128]{2,1,0:T(8,128)(2,1)S(1)}, bf16[2,704,128]{2,1,0:T(8,128)(2,1)S(1)}, u32[]{:S(2)}, u32[]{:S(2)}) collective-permute-start(bf16[2,704,128]{2,1,0:T(8,128)(2,1)S(1)} %slice.252), channel_id=1, source_target_pairs={{0,8},{2,10},{4,12},{6,14},{8,0},{10,2},{12,4},{14,6},{16,24},{18,... | collective-permute-start | bytes 1081352 | tf_op jit(solution)/shard_map/ppermute | solution.py:799
  332.9 22.8 %collective-permute-start.36 = (bf16[2,16,2,32,128]{4,3,2,1,0:T(8,128)(2,1)S(1)}, bf16[2,16,2,32,128]{4,3,2,1,0:T(8,128)(2,1)S(1)}, u32[]{:S(2)}, u32[]{:S(2)}) collective-permute-start(bf16[2,16,2,32,128]{4,3,2,1,0:T(8,128)(2,1)S(1)} %slice.250), channel_id=1, source_target_pairs={{0,8},{2,10},{4,12},{6,14},{8,0},{10,2},{12,4},{14,6},{16,24},{18,... | collective-permute-start | bytes 1572872 | tf_op jit(solution)/shard_map/ppermute | solution.py:799
  336.1 20.5 %collective-permute-start.52 = (bf16[4,768,128]{2,1,0:T(8,128)(2,1)S(1)}, bf16[4,768,128]{2,1,0:T(8,128)(2,1)S(1)}, u32[]{:S(2)}, u32[]{:S(2)}) collective-permute-start(bf16[4,768,128]{2,1,0:T(8,128)(2,1)S(1)} %slice.249), channel_id=1, source_target_pairs={{0,4},{2,6},{4,0},{6,2},{8,12},{10,14},{12,8},{14,10},{16,20},{18,... | collective-permute-start | bytes 2359304 | tf_op jit(solution)/shard_map/ppermute | solution.py:799
  342.4 14.1 %collective-permute-start.50 = (bf16[1,704,128]{2,1,0:T(8,128)(2,1)S(1)}, bf16[1,704,128]{2,1,0:T(8,128)(2,1)S(1)}, u32[]{:S(2)}, u32[]{:S(2)}) collective-permute-start(bf16[1,704,128]{2,1,0:T(8,128)(2,1)S(1)} %slice.257), channel_id=1, source_target_pairs={{0,16},{2,18},{4,20},{6,22},{8,24},{10,26},{12,28},{14,30},{16,0},... | collective-permute-start | bytes 540680 | tf_op jit(solution)/shard_map/ppermute | solution.py:799
  356.0 12.6 %collective-permute-start.37 = (bf16[1,16,2,32,128]{4,3,2,1,0:T(8,128)(2,1)S(1)}, bf16[1,16,2,32,128]{4,3,2,1,0:T(8,128)(2,1)S(1)}, u32[]{:S(2)}, u32[]{:S(2)}) collective-permute-start(bf16[1,16,2,32,128]{4,3,2,1,0:T(8,128)(2,1)S(1)} %slice.255), channel_id=1, source_target_pairs={{0,16},{2,18},{4,20},{6,22},{8,24},{10,26},{12,28},{14,30},{16,0},... | collective-permute-start | bytes 786440 | tf_op jit(solution)/shard_map/ppermute | solution.py:799
  356.9 15.1 %collective-permute-start.53 = (bf16[2,768,128]{2,1,0:T(8,128)(2,1)S(1)}, bf16[2,768,128]{2,1,0:T(8,128)(2,1)S(1)}, u32[]{:S(2)}, u32[]{:S(2)}) collective-permute-start(bf16[2,768,128]{2,1,0:T(8,128)(2,1)S(1)} %slice.251), channel_id=1, source_target_pairs={{0,8},{2,10},{4,12},{6,14},{8,0},{10,2},{12,4},{14,6},{16,24},{18,... | collective-permute-start | bytes 1179656 | tf_op jit(solution)/shard_map/ppermute | solution.py:799
  384.5 35.2 %collective-permute-start.33 = (bf16[3,256,1024]{2,1,0:T(8,128)(2,1)S(1)}, bf16[3,256,1024]{2,1,0:T(8,128)(2,1)S(1)}, u32[]{:S(2)}, u32[]{:S(2)}) collective-permute-start(bf16[3,256,1024]{2,1,0:T(8,128)(2,1)S(1)} %pad_maximum_fusion), channel_id=1, source_target_pairs={{0,1},{1,0},{2,3},{3,2},{4,5},{5,4},{6,7},{7,6},{8,9},{9,8},{10,11... | collective-permute-start | bytes 4718600 | tf_op jit(solution)/shard_map/ppermute | solution.py:802
  419.7 35.0 %all-to-all-start.2 = ((bf16[16,64,384]{2,1,0:T(8,128)(2,1)}), bf16[16,64,384]{2,1,0:T(8,128)(2,1)S(1)}, u32[]{:S(2)}, u32[]{:S(2)}) async-start(bf16[16,64,384]{2,1,0:T(8,128)(2,1)} %bitcast.37), calls=%async_computation.2 | async-start | bytes 1572864 | tf_op jit(solution)/shard_map/all_to_all | solution.py:1129
  464.7 18.3 %all-to-all-start.3 = ((bf16[16,64,128]{2,1,0:T(8,128)(2,1)}), bf16[16,64,128]{2,1,0:T(8,128)(2,1)S(1)}, u32[]{:S(2)}, u32[]{:S(2)}) async-start(bf16[16,64,128]{2,1,0:T(8,128)(2,1)} %bitcast.40), calls=%async_computation.3 | async-start | bytes 524288 | tf_op jit(solution)/shard_map/all_to_all | solution.py:1167
  472.8 16.5 %collective-permute-start.34 = (bf16[128,1024]{1,0:T(8,128)(2,1)S(1)}, bf16[128,1024]{1,0:T(8,128)(2,1)S(1)}, u32[]{:S(2)}, u32[]{:S(2)}) collective-permute-start(bf16[128,1024]{1,0:T(8,128)(2,1)S(1)} %copy-done.39), channel_id=1, source_target_pairs={{0,1},{1,0},{2,3},{3,2},{4,5},{5,4},{6,7},{7,6},{8,9},{9,8},{10,11... | collective-permute-start | bytes 786440 | tf_op jit(solution)/shard_map/ppermute | solution.py:802
  475.2 14.0 %collective-permute-start.41 = (f32[4,1024]{1,0:T(4,128)S(1)}, f32[4,1024]{1,0:T(4,128)S(1)}, u32[]{:S(2)}, u32[]{:S(2)}) collective-permute-start(f32[4,1024]{1,0:T(4,128)S(1)} %add.235), channel_id=1, source_target_pairs={{0,8},{2,10},{4,12},{6,14},{8,0},{10,2},{12,4},{14,6},{16,24},{18,... | collective-permute-start | bytes 49160 | tf_op jit(solution)/shard_map/ppermute | solution.py:799
  (58 other events, 468.3 us)
Sparse Core Ops, SparseCore 0:
  14.5 40.4 all-gather.5
  383.3 106.4 all-gather.3

commit v6 on v5

--- a/solution.py
+++ b/solution.py
@@ -167,35 +167,34 @@
 
 def pack_kernel(counts, where_ref, *refs):
     total = sum(counts)
-    weights, outs, sem = refs[:total], refs[total:-1], refs[-1]
-    copies = []
-    for place, w_ref in enumerate(weights):
-        kind = 0 if place < counts[0] else 1
-        out_ref = outs[kind].at[place - kind * counts[0]]
-        rows, cols = outs[kind].shape[1:]
-        source = w_ref.at[aligned(where_ref[kind], rows), :]
-        if kind:
-            source = w_ref.at[aligned(where_ref[kind], rows), aligned(where_ref[2], cols)]
-        copies.append(pltpu.make_async_copy(source, out_ref, sem.at[place]))
-    for copy in copies:
-        copy.start()
-    for copy in copies:
-        copy.wait()
+    first_ref, second_ref = refs[total:]
+    for place in range(counts[0]):
+        first_ref[place] = refs[place][...]
+    for place in range(counts[1]):
+        second_ref[place] = refs[counts[0] + place][...]
 
 
 def pack(where, first, second, rows, cols):
-    anywhere = pl.BlockSpec(memory_space=pl.ANY)
+    width = first[0].shape[1]
     counts = (len(first), len(second))
     return pl.pallas_call(
         functools.partial(pack_kernel, counts),
+        grid_spec=pltpu.PrefetchScalarGridSpec(
+            num_scalar_prefetch=1,
+            grid=(1,),
+            in_specs=[pl.BlockSpec((rows, width), lambda i, where: (where[0], 0))] * counts[0]
+            + [pl.BlockSpec((rows, cols), lambda i, where: (where[1], where[2]))] * counts[1],
+            out_specs=[
+                pl.BlockSpec((counts[0], rows, width), lambda i, where: (0, 0, 0)),
+                pl.BlockSpec((counts[1], rows, cols), lambda i, where: (0, 0, 0)),
+            ],
+        ),
         out_shape=[
-            jax.ShapeDtypeStruct((counts[0], rows, first[0].shape[1]), BF16),
+            jax.ShapeDtypeStruct((counts[0], rows, width), BF16),
             jax.ShapeDtypeStruct((counts[1], rows, cols), BF16),
         ],
-        in_specs=[smem()] + [anywhere] * sum(counts),
-        out_specs=[anywhere] * 2,
-        scratch_shapes=[pltpu.SemaphoreType.DMA((sum(counts),))],
-        cost_estimate=cost(2),
+        compiler_params=params(),
+        cost_estimate=cost(3),
         name="pack",
     )(where, *first, *second)
 
@@ -876,9 +875,8 @@
         starts = quarter_starts(near_bit)
         kv_own = (key_cross, value_cross)
         near_own = (output_self, query_cross, output_cross)
-        picked = [quarter(near_bit) * (half // 2), quarter(dense_bit) * (half // 2)]
         near_sent, theirs = pack(
-            jnp.stack(picked + [(1 - shard) * hidden]).astype(jnp.int32),
+            jnp.stack([quarter(near_bit), quarter(dense_bit), 1 - shard]).astype(jnp.int32),
             near_own + kv_own,
             (dense_gate, dense_up),
             half // 2,
@@ -932,6 +930,8 @@
         cost_estimate=cost(12),
         name="self_forward",
     )(source, *x_groups, gains[0:1], head_w, table, doc_row, doc_col)
+    if paired:
+        mixed = after(mixed, dense_got)
     o1_heads = lax.all_to_all(mixed.reshape(dp, rows, 128), "dp", 0, 0, tiled=True)[::copies]
 
     if paired:
@@ -964,8 +964,8 @@
         dense_more = (
             dense_got,
             dense_far,
-            swap_dp(after(dense_got, o1_heads), 1),
-            swap_dp(after(dense_far, o1_heads), 1),
+            swap_dp(after(dense_got, ke), 1),
+            swap_dp(after(dense_far, ke), 1),
         )
         g_rows = g.reshape(tokens, width)
         g_got = swap_fs(after(g_rows, dense_got))
@@ -985,7 +985,7 @@
             tokens,
         )
         back_got_mate = swap_dp(back_got, 1)
-        dn3_more = swap_fs(d16)
+        dn3_more = swap_fs(after(d16, back_mate))
     else:
         n_group = both_tokens(n3)
         back, _, y16, _, d16 = dense_layer(
@@ -1076,6 +1076,8 @@
             dkv_got = swap_dp(after(dkv_sent, do1_heads), 1)
             dkv_total = dkv_kept.astype(F32) + dkv_got.astype(F32)
             dkv_far = swap_dp(dkv_total[chips // 2 :].astype(BF16), x_order[0])
+        far_x = swap_dp(far_got, x_order[0])
+        do1 = after(do1, far_x, dkv_got)
 
     dqkv, table_grad = pl.pallas_call(
         self_backward_kernel,
@@ -1092,6 +1094,19 @@
     )(qkv, do1, table, doc_row, doc_col)
     if chunked:
         dqkv = after(dqkv, right_got, last_got, dkv_far)
+    if chunked:
+        token_kept, token_sent = chunk_weights(
+            functools.partial(token_weight_kernel, masks[1]),
+            where,
+            (left, left_got, right, right_got, last, last_got),
+            (3 * half // chips * width // 128,),
+            chips,
+            [pltpu.VMEM((span, width), F32)],
+            6,
+            "token_weight",
+        )
+        token_got = swap_dp(token_sent, 1)
+        dqkv = after(dqkv, token_kept)
     head_grad = pl.pallas_call(
         head_weight_kernel,
         out_shape=jax.ShapeDtypeStruct((fs, span * 3 // 2, 128), BF16),
@@ -1109,18 +1124,7 @@
         return lax.psum_scatter(values, "fsdp", scatter_dimension=0, tiled=True)
 
     head_sum = sum_shards(head_grad)
-    if chunked:
-        token_kept, token_sent = chunk_weights(
-            functools.partial(token_weight_kernel, masks[0]),
-            where,
-            (after(left, head_grad), left_got, right, right_got, last, last_got),
-            (3 * half // chips * width // 128,),
-            chips,
-            [pltpu.VMEM((span, width), F32)],
-            6,
-            "token_weight",
-        )
-        token_got = swap_dp(token_sent, 1)
+
     if paired:
         first_own = (query_self, key_self, value_self)
         first_more = both_halves(after(half_rows(first_own), head_sum))
@@ -1180,11 +1184,9 @@
         sums = (
             reduce_chips(own_kept, own_got, z_order, (do1, dqkv)),
             reduce_chips(down_kept, down_got, x_order, (do1, dqkv)),
-            reduce_chips(
-                far_kept, swap_dp(after(far_got, do1), x_order[0]), x_order, (dqkv, head_grad)
-            ),
+            reduce_chips(far_kept, far_x, x_order, (dqkv, head_grad)),
             head_sum,
-            reduce_chips(token_kept, token_got, [1] + x_order),
+            reduce_chips(token_kept, token_got, [1] + z_order),
             cross_sum,
         )
         pieces = lax.all_gather(jnp.concatenate(sums, axis=1), "dp", axis=0, tiled=True)

time: 530 us -> 512 us (0.966)
  Pallas kernels: 215 us -> 155 us
  waiting for transfers between devices: 175 us -> 194 us
  starting transfers between devices: 68.2 us -> 78.4 us
  other arithmetic: 19.4 us -> 26.2 us
  local copies, waits for them, and re-layouts: 27.2 us -> 32.9 us
    pallas_call x1, Pallas kernels: 63.5 us -> 3.7 us  [pack(): pl.pallas_call(functools.partial(pack_kernel, counts), grid_spec=pltpu.Pr...]
    ppermute x39, waiting for transfers between devices: 75.9 us -> 100 us  [swap_dp(): return lax.ppermute(values, 'dp', [(j, j ^ bit) for j in range(dp)])]
    all_to_all x1, waiting for transfers between devices: 17 us -> 0.01 us  [per_device(): lax.all_to_all(mixed.reshape(dp, rows, 128), 'dp', 0, 0, tiled=True)]
    ppermute x17, waiting for transfers between devices: 53.3 us -> 65 us  [swap_fs(): return lax.ppermute(values, 'fsdp', [(j, 1 - j) for j in range(2)])]
    all_to_all x1, starting transfers between devices: 3.62 us -> 9.47 us  [per_device(): lax.all_to_all(dqkv.reshape(dp, rows, 384), 'dp', 0, 0, tiled=True)]
    unnamed x88 -> x108, local copies, waits for them, and re-layouts: 11 us -> 12.6 us
  transfers between devices with their start and end apart: 62 -> 62, of which waited for: 24 -> 25; matrix products, arithmetic and copies ran while one was open for 7% -> 9% of each run, Pallas kernels for 35% -> 25%
where the time goes in v6:
time: 512 us; the launch traced here: 502 us
  waiting for transfers between devices  194 us (38%)
  Pallas kernels  155 us (30%)
  starting transfers between devices  78.4 us (15%)
  local copies, waits for them, and re-layouts  32.9 us (6%)
  other arithmetic  26.2 us (5%)
  between operations  15.1 us (3%)
    ppermute x39, waiting for transfers between devices, swap_dp(): return lax.ppermute(values, 'dp', [(j, j ^ bit) for j in range(dp)])  100 us
    ppermute x17, waiting for transfers between devices, swap_fs(): return lax.ppermute(values, 'fsdp', [(j, 1 - j) for j in range(2)])  65 us
    ppermute x39, starting transfers between devices, swap_dp(): return lax.ppermute(values, 'dp', [(j, j ^ bit) for j in range(dp)])  34.9 us
    all_to_all x1, waiting for transfers between devices, per_device(): lax.all_to_all(dqkv.reshape(dp, rows, 384), 'dp', 0, 0, tiled=True)  22.5 us
    ppermute x17, starting transfers between devices, swap_fs(): return lax.ppermute(values, 'fsdp', [(j, 1 - j) for j in range(2)])  20.8 us
    pallas_call x2, Pallas kernels, dense_layer(): pl.pallas_call(functools.partial(dense_kernel, len(more)), grid_spec=pltp...  19.9 us
    pallas_call x1, Pallas kernels, spread(): pl.pallas_call(spread_kernel, grid_spec=pltpu.PrefetchScalarGridSpec(num_...  17.4 us
    pallas_call x1, Pallas kernels, per_device(): pl.pallas_call(functools.partial(cross_backward_kernel, len(near_more)),...  16.5 us
  transfers between devices with their start and end apart: 62, of which 25 were waited for; matrix products, arithmetic and copies ran while one was open for 9% of the time, Pallas kernels for 25%

profile of v6, /device:TPU:0, one launch (start us, length us, event | category | flops | bytes accessed | tf_op | source)
XLA Modules:
  0.0 501.8 jit_solution(10949882311755387690)
XLA Ops:
  7.2 3.0 collective-permute-start.3
  11.8 2.6 collective-permute-start
  19.4 3.7 pack.1
  30.4 5.5 %collective-permute-done.2 = bf16[2,64,1024]{2,1,0:T(8,128)(2,1)S(1)} collective-permute-done((bf16[2,64,1024]{2,1,0:T(8,128)(2,1)S(1)}, bf16[2,64,1024]{2,1,0:T(8,128)(2,1)S(1)}, u32[]{:S(2)}, u32[]{:S(2)}) %collective-permute-start.2) | collective-permute-done | bytes 262176 | tf_op jit(solution)/shard_map/ppermute | solution.py:798
  36.5 4.4 bias_table.1.refs_6_.table_ref
  43.3 8.0 %collective-permute-done.6 = bf16[2,64,1024]{2,1,0:T(8,128)(2,1)} collective-permute-done((bf16[2,64,1024]{2,1,0:T(8,128)(2,1)S(1)}, bf16[2,64,1024]{2,1,0:T(8,128)(2,1)}, u32[]{:S(2)}, u32[]{:S(2)}) %collective-permute-start.6) | collective-permute-done | bytes 262176 | tf_op jit(solution)/shard_map/ppermute | solution.py:798
  61.5 11.6 %self_forward.1 = (bf16[16,2,64,1024]{3,2,1,0:T(8,128)(2,1)}, bf16[1024,384]{1,0:T(8,128)(2,1)}, bf16[1024,128]{1,0:T(8,128)(2,1)}) custom-call(s32[16]{0:T(128)} %broadcast_xor_fusion.source_ref, bf16[4,2,64,1024]{3,2,1,0:T(8,128)(2,1)} %copy-done.14, bf16[4,2,64,1024]{3,2,1,0:T(8,128)(2,1)} %copy-done.15, ...), custom_call_target="tpu_custom_call" | custom-call | flops 13799999488 | bytes 44280000 | tf_op jit(solution)/shard_map/self_forward/pallas_call | solution.py:920
  73.1 4.4 collective-permute-done.12.refs_0_
  77.5 11.3 %collective-permute-done.13.refs_1_ = bf16[5,128,1024]{2,1,0:T(8,128)(2,1)} collective-permute-done((bf16[5,128,1024]{2,1,0:T(8,128)(2,1)}, bf16[5,128,1024]{2,1,0:T(8,128)(2,1)}, u32[]{:S(2)}, u32[]{:S(2)}) %collective-permute-start.13) | collective-permute-done | bytes 1310752 | tf_op jit(solution)/shard_map/ppermute | solution.py:798
  90.0 3.5 all-to-all-start
  98.0 11.9 %cross_kv.1 = (bf16[2,512,1024]{2,1,0:T(8,128)(2,1)}, bf16[2,512,1024]{2,1,0:T(8,128)(2,1)}) custom-call(s32[5]{0:T(128)} %stack.120.starts_ref, bf16[16,2,32,1024]{3,2,1,0:T(8,128)(2,1)} %bitcast.83, bf16[512,1024]{1,0:T(8,128)(2,1)} %wk.3, bf16[512,1024]{1,0:T(8,128)(2,1)} %wv.3, bf16[5,128,1024]{2,1,0:T(8,128)(2,1)} %collective-permute-done.11.refs_0_, ...), custom_call_target="tpu_custom_call" | custom-call | flops 9200000000 | bytes 29520000 | tf_op jit(solution)/shard_map/cross_kv/pallas_call | solution.py:331
  109.9 6.4 %collective-permute-done.16.refs_1_ = bf16[2,128,1408]{2,1,0:T(8,128)(2,1)} collective-permute-done((bf16[2,128,1408]{2,1,0:T(8,128)(2,1)S(1)}, bf16[2,128,1408]{2,1,0:T(8,128)(2,1)}, u32[]{:S(2)}, u32[]{:S(2)}) %collective-permute-start.16) | collective-permute-done | bytes 720928 | tf_op jit(solution)/shard_map/ppermute | solution.py:798
  117.5 13.3 %mid_forward.1 = (bf16[3,128,1024]{2,1,0:T(8,128)(2,1)}, f32[128,1024]{1,0:T(8,128)}, bf16[128,1024]{1,0:T(8,128)(2,1)}, f32[128,1024]{1,0:T(8,128)}, bf16[128,1...) custom-call(s32[5]{0:T(128)} %stack.120.starts_ref, bf16[16,64,128]{2,1,0:T(8,128)(2,1)} %copy-done.28, ...), custom_call_target="tpu_custom_call" | custom-call | flops 13799999488 | bytes 44280000 | tf_op jit(solution)/shard_map/mid_forward/pallas_call | solution.py:945
  134.6 10.0 %dense_layer.2 = (bf16[128,5248]{1,0:T(8,128)(2,1)}, f32[128,1024]{1,0:T(8,128)}, bf16[128,1024]{1,0:T(8,128)(2,1)}, f32[128,1024]{1,0:T(8,128)}, bf16[128,1024]{1,0:T(8,128)(2,1)}) custom-call(s32[7]{0:T(128)} %concatenate.41.starts_ref, bf16[128,1024]{1,0:T(8,128)(2,1)} %get-tuple-element.122.n_ref.n0_ref, bf16[128,1024]{1,0:T(8,128)(2,1)} %bitcast.85, ...), custom_call_target="tpu_custom_call" | custom-call | flops 14949999616 | bytes 47970000 | tf_op jit(solution)/shard_map/dense_layer/pallas_call | solution.py:543
  144.6 3.1 collective-permute-done.20.left_more_ref
  148.4 10.0 %dense_layer.3 = (bf16[128,5248]{1,0:T(8,128)(2,1)}, f32[128,1024]{1,0:T(8,128)}, bf16[128,1024]{1,0:T(8,128)(2,1)}, f32[128,1024]{1,0:T(8,128)}, bf16[128,1024]{1,0:T(8,128)(2,1)}) custom-call(s32[7]{0:T(128)} %concatenate.41.starts_ref, bf16[128,1024]{1,0:T(8,128)(2,1)} %copy-done.50, bf16[128,1024]{1,0:T(8,128)(2,1)} %copy-done.49, bf16[512,2816]{1,0:T(8,128)(2,1)} %wg.3, ...), custom_call_target="tpu_custom_call" | custom-call | flops 14949999616 | bytes 47970000 | tf_op jit(solution)/shard_map/dense_layer/pallas_call | solution.py:543
  161.8 5.6 %collective-permute-done.23.more_ref = bf16[128,1024]{1,0:T(8,128)(2,1)S(1)} collective-permute-done((bf16[128,1024]{1,0:T(8,128)(2,1)}, bf16[128,1024]{1,0:T(8,128)(2,1)S(1)}, u32[]{:S(2)}, u32[]{:S(2)}) %collective-permute-start.23) | collective-permute-done | bytes 262176 | tf_op jit(solution)/shard_map/ppermute | solution.py:801
  168.5 7.1 %dense_weight.1 = (bf16[4,704,128]{2,1,0:T(8,128)(2,1)}, bf16[4,704,128]{2,1,0:T(8,128)(2,1)}, bf16[4,704,128]{2,1,0:T(8,128)(2,1)}, bf16[4,704,128]{2,1,0:T(8,1...) custom-call(s32[3]{0:T(128)} %pad_add_fusion.2.where_ref, ...), custom_call_target="tpu_custom_call" | custom-call | flops 8049999872 | bytes 25830000 | tf_op jit(solution)/shard_map/dense_weight/pallas_call | solution.py:644
  179.4 16.5 %cross_backward.1 = (bf16[128,2048]{1,0:T(8,128)(2,1)}, f32[128,1024]{1,0:T(8,128)}, bf16[8,16,2,32,128]{4,3,2,1,0:T(8,128)(2,1)}, bf16[8,16,2,32,128]{4,3,2,1,0:T(8,128)(2,1)}, f32[1,1024]{1,0:T(1,128)}) custom-call(s32[5]{0:T(128)} %stack.120.starts_ref, s32[9]{0:T(128)} %pad_add_fusion.1.slots_ref, bf16[128,1024]{1,0:T(8,128)(2,1)} %bitcast.87, ...), custom_call_target="tpu_custom_call" | custom-call | flops 17250000896 | bytes 55350000 | tf_op jit(solution)/shard_map/cross_backward/pallas_call | solution.py:1035
  195.9 6.7 %mid_backward.1 = (f32[128,1024]{1,0:T(8,128)}, bf16[128,1024]{1,0:T(8,128)(2,1)}, bf16[16,64,128]{2,1,0:T(8,128)(2,1)}, f32[1,1024]{1,0:T(1,128)}) custom-call(s32[5]{0:T(128)} %stack.120.starts_ref, bf16[128,2048]{1,0:T(8,128)(2,1)} %get-tuple-element.138.right_ref, f32[128,1024]{1,0:T(8,128)} %get-tuple-element.131.gx2_ref, ...), custom_call_target="tpu_custom_call" | custom-call | flops 6899999744 | bytes 22140000 | tf_op jit(solution)/shard_map/mid_backward/pallas_call | solution.py:1053
  204.7 15.8 %collective-permute-done.31.last_more_ref = bf16[128,1024]{1,0:T(8,128)(2,1)S(1)} collective-permute-done((bf16[128,1024]{1,0:T(8,128)(2,1)}, bf16[128,1024]{1,0:T(8,128)(2,1)S(1)}, u32[]{:S(2)}, u32[]{:S(2)}) %collective-permute-start.31) | collective-permute-done | bytes 262176 | tf_op jit(solution)/shard_map/ppermute | solution.py:801
  221.4 4.8 token_weight.1
  227.0 5.8 %all-to-all-start.1 = ((bf16[16,64,128]{2,1,0:T(8,128)(2,1)}), bf16[16,64,128]{2,1,0:T(8,128)(2,1)S(1)}, u32[]{:S(2)}, u32[]{:S(2)}) async-start(bf16[16,64,128]{2,1,0:T(8,128)(2,1)} %get-tuple-element.133), calls=%async_computation.1 | async-start | bytes 524288 | tf_op jit(solution)/shard_map/all_to_all | solution.py:1068
  236.4 11.2 %collective-permute-done.28 = bf16[4,704,128]{2,1,0:T(8,128)(2,1)} collective-permute-done((bf16[4,704,128]{2,1,0:T(8,128)(2,1)}, bf16[4,704,128]{2,1,0:T(8,128)(2,1)}, u32[]{:S(2)}, u32[]{:S(2)}) %collective-permute-start.28) | collective-permute-done | bytes 720928 | tf_op jit(solution)/shard_map/ppermute | solution.py:798
  259.3 3.2 convert_add_fusion
  264.2 9.6 %self_backward.1 = (bf16[1024,384]{1,0:T(8,128)(2,1)}, f32[256,1024]{1,0:T(8,128)}) custom-call(bf16[1024,384]{1,0:T(8,128)(2,1)} %get-tuple-element.118.qkv_ref, bf16[1024,128]{1,0:T(8,128)(2,1)} %bitcast.63, f32[256,1024]{1,0:T(8,128)} %bias_table.1.refs_6_.table_ref, s32[2,1024]{1,0:T(2,128)} %reshape.112.refs_7_.doc_row_ref, ...), custom_call_target="tpu_custom_call" | custom-call | flops 11500000256 | bytes 36900000 | tf_op jit(solution)/shard_map/self_backward/pallas_call | solution.py:1082
  273.8 7.8 %collective-permute-done.44 = bf16[2,704,128]{2,1,0:T(8,128)(2,1)S(1)} collective-permute-done((bf16[2,704,128]{2,1,0:T(8,128)(2,1)}, bf16[2,704,128]{2,1,0:T(8,128)(2,1)S(1)}, u32[]{:S(2)}, u32[]{:S(2)}) %collective-permute-start.44) | collective-permute-done | bytes 360480 | tf_op jit(solution)/shard_map/ppermute | solution.py:798
  282.9 5.7 %collective-permute-done.46 = bf16[2,704,128]{2,1,0:T(8,128)(2,1)S(1)} collective-permute-done((bf16[2,704,128]{2,1,0:T(8,128)(2,1)}, bf16[2,704,128]{2,1,0:T(8,128)(2,1)S(1)}, u32[]{:S(2)}, u32[]{:S(2)}) %collective-permute-start.46) | collective-permute-done | bytes 360480 | tf_op jit(solution)/shard_map/ppermute | solution.py:798
  292.1 2.5 collective-permute-start.53
  294.6 5.7 %head_weight.1 = bf16[2,768,128]{2,1,0:T(8,128)(2,1)} custom-call(bf16[16,2,64,1024]{3,2,1,0:T(8,128)(2,1)} %get-tuple-element.117.n_ref, bf16[1024,384]{1,0:T(8,128)(2,1)} %get-tuple-element.144.d_ref), custom_call_target="tpu_custom_call" | custom-call | flops 6899999744 | bytes 22140000 | tf_op jit(solution)/shard_map/head_weight/pallas_call | solution.py:1110
  306.2 9.8 %collective-permute-done.53 = bf16[2,768,128]{2,1,0:T(8,128)(2,1)S(1)} collective-permute-done((bf16[2,768,128]{2,1,0:T(8,128)(2,1)S(1)}, bf16[2,768,128]{2,1,0:T(8,128)(2,1)S(1)}, u32[]{:S(2)}, u32[]{:S(2)}) %collective-permute-start.53) | collective-permute-done | bytes 393248 | tf_op jit(solution)/shard_map/ppermute | solution.py:798
  318.9 7.3 %collective-permute-done.49 = bf16[2,704,128]{2,1,0:T(8,128)(2,1)S(1)} collective-permute-done((bf16[2,704,128]{2,1,0:T(8,128)(2,1)S(1)}, bf16[2,704,128]{2,1,0:T(8,128)(2,1)S(1)}, u32[]{:S(2)}, u32[]{:S(2)}) %collective-permute-start.49) | collective-permute-done | bytes 360480 | tf_op jit(solution)/shard_map/ppermute | solution.py:798
  326.3 2.6 collective-permute-start.50
  328.9 9.3 %collective-permute-done.37 = bf16[2,16,2,32,128]{4,3,2,1,0:T(8,128)(2,1)S(1)} collective-permute-done((bf16[2,16,2,32,128]{4,3,2,1,0:T(8,128)(2,1)S(1)}, bf16[2,16,2,32,128]{4,3,2,1,0:T(8,128)(2,1)S(1)}, u32[]{:S(2)}, u32[]{:S(2)}) %collective-permute-start.37) | collective-permute-done | bytes 524320 | tf_op jit(solution)/shard_map/ppermute | solution.py:798
  339.6 8.9 %collective-permute-done.38 = bf16[1,16,2,32,128]{4,3,2,1,0:T(8,128)(2,1)S(1)} collective-permute-done((bf16[1,16,2,32,128]{4,3,2,1,0:T(8,128)(2,1)S(1)}, bf16[1,16,2,32,128]{4,3,2,1,0:T(8,128)(2,1)S(1)}, u32[]{:S(2)}, u32[]{:S(2)}) %collective-permute-start.38) | collective-permute-done | bytes 262176 | tf_op jit(solution)/shard_map/ppermute | solution.py:798
  349.3 3.1 cross_head_weight.1
  353.3 2.6 collective-permute-start.55
  355.9 2.9 collective-permute-done.55
  364.2 31.4 %collective-permute-done.34.refs_0_ = bf16[3,256,1024]{2,1,0:T(8,128)(2,1)S(1)} collective-permute-done((bf16[3,256,1024]{2,1,0:T(8,128)(2,1)S(1)}, bf16[3,256,1024]{2,1,0:T(8,128)(2,1)S(1)}, u32[]{:S(2)}, u32[]{:S(2)}) %collective-permute-start.34) | collective-permute-done | bytes 1572896 | tf_op jit(solution)/shard_map/ppermute | solution.py:801
  395.7 9.5 %all-to-all-start.2 = ((bf16[16,64,384]{2,1,0:T(8,128)(2,1)}), bf16[16,64,384]{2,1,0:T(8,128)(2,1)S(1)}, u32[]{:S(2)}, u32[]{:S(2)}) async-start(bf16[16,64,384]{2,1,0:T(8,128)(2,1)} %bitcast.37), calls=%async_computation.2 | async-start | bytes 1572864 | tf_op jit(solution)/shard_map/all_to_all | solution.py:1133
  405.8 7.4 %bucket_sums.1 = f32[32,128]{1,0:T(8,128)} custom-call(s32[32]{0:T(128)} %convert_reduce_fusion.edge_ref, f32[256,1024]{1,0:T(8,128)} %get-tuple-element.153.grad_ref), custom_call_target="tpu_custom_call" | custom-call | flops 8049999872 | bytes 25830000 | tf_op jit(solution)/shard_map/bucket_sums/pallas_call | solution.py:137
  414.1 22.5 %all-to-all-done.2.d_ref = bf16[16,64,384]{2,1,0:T(8,128)(2,1)S(1)} async-done(((bf16[16,64,384]{2,1,0:T(8,128)(2,1)}), bf16[16,64,384]{2,1,0:T(8,128)(2,1)S(1)}, u32[]{:S(2)}, u32[]{:S(2)}) %all-to-all-start.2) | async-done | bytes 786464 | tf_op jit(solution)/shard_map/all_to_all | solution.py:1133
  437.5 6.8 %input_grad.1 = (f32[128,1024]{1,0:T(8,128)}, f32[1,1024]{1,0:T(1,128)}) custom-call(s32[3]{0:T(128)} %pad_add_fusion.3.starts_ref, bf16[16,64,384]{2,1,0:T(8,128)(2,1)} %copy-done.16, bf16[2,64,1024]{2,1,0:T(8,128)(2,1)} %bitcast.69, f32[3,1024]{1,0:T(4,128)} %copy-done.33, f32[128,1024]{1,0:T(8,128)} %get-tuple-element.147.gx1_ref, bf16[512,1024]{1,0:T(8,128)(2,1)} %wq.5, ...), custom_call_target="tpu_custom_call" | custom-call | flops 8049999872 | bytes 25830000 | tf_op jit(solution)/shard_map/input_grad/pallas_call | solution.py:1134
  446.5 3.7 all-to-all-start.3
  458.9 6.0 %all-to-all-done.3.d_ref = bf16[16,64,128]{2,1,0:T(8,128)(2,1)S(1)} async-done(((bf16[16,64,128]{2,1,0:T(8,128)(2,1)}), bf16[16,64,128]{2,1,0:T(8,128)(2,1)S(1)}, u32[]{:S(2)}, u32[]{:S(2)}) %all-to-all-start.3) | async-done | bytes 262176 | tf_op jit(solution)/shard_map/all_to_all | solution.py:1171
  465.6 5.5 %encoder_grad.1 = f32[64,1024]{1,0:T(8,128)} custom-call(s32[5]{0:T(128)} %stack.120.starts_ref, bf16[16,64,128]{2,1,0:T(8,128)(2,1)} %copy-done.26, bf16[512,1024]{1,0:T(8,128)(2,1)} %wk.3, bf16[512,1024]{1,0:T(8,128)(2,1)} %wv.3, bf16[5,128,1024]{2,1,0:T(8,128)(2,1)} %collective-permute-done.11.refs_0_, ...), custom_call_target="tpu_custom_call" | custom-call | flops 4600000000 | bytes 14760000 | tf_op jit(solution)/shard_map/encoder_grad/pallas_call | solution.py:1172
  472.0 4.0 collective-permute-done.43
  477.4 17.4 %spread.1 = (f32[2,4,64,2816]{3,2,1,0:T(8,128)}, f32[2,4,64,2816]{3,2,1,0:T(8,128)}, f32[1408,1024]{1,0:T(8,128)}, f32[512,1024]{1,0:T(8,128)}, f32[512,1024]{1,...) custom-call(s32[3]{0:T(128)} %pad_add_fusion.2.where_ref, ...), custom_call_target="tpu_custom_call" | custom-call | flops 23000000512 | bytes 73800000 | tf_op jit(solution)/shard_map/spread/pallas_call | solution.py:717
  (290 shorter events, 105.3 us)
Async XLA Ops:
  7.2 89.8 %all-gather.6.cloned.1.call-start = ((), (), s32[]{:S(2)}) async-start(), calls=%async_computation.5 | async-start | bytes 2228224 | tf_op jit(solution)/shard_map/all_gather | solution.py:848
  7.2 33.9 %collective-permute-start.3 = (bf16[2,64,1024]{2,1,0:T(8,128)(2,1)}, bf16[2,64,1024]{2,1,0:T(8,128)(2,1)S(1)}, u32[]{:S(2)}, u32[]{:S(2)}) collective-permute-start(bf16[2,64,1024]{2,1,0:T(8,128)(2,1)} %bitcast.65), channel_id=1, source_target_pairs={{0,4},{2,6},{4,0},{6,2},{8,12},{10,14},{12,8},{14,10},{16,20},{18,... | collective-permute-start | bytes 786440 | tf_op jit(solution)/shard_map/ppermute | solution.py:798
  10.2 18.6 %collective-permute-start.1 = (bf16[2,64,1024]{2,1,0:T(8,128)(2,1)}, bf16[2,64,1024]{2,1,0:T(8,128)(2,1)S(1)}, u32[]{:S(2)}, u32[]{:S(2)}) collective-permute-start(bf16[2,64,1024]{2,1,0:T(8,128)(2,1)} %bitcast.66), channel_id=1, source_target_pairs={{0,8},{2,10},{4,12},{6,14},{8,0},{10,2},{12,4},{14,6},{16,24},{18,... | collective-permute-start | bytes 786440 | tf_op jit(solution)/shard_map/ppermute | solution.py:798
  11.8 14.8 %collective-permute-start = (bf16[2,64,1024]{2,1,0:T(8,128)(2,1)}, bf16[2,64,1024]{2,1,0:T(8,128)(2,1)S(1)}, u32[]{:S(2)}, u32[]{:S(2)}) collective-permute-start(bf16[2,64,1024]{2,1,0:T(8,128)(2,1)} %bitcast.67), channel_id=1, source_target_pairs={{0,16},{2,18},{4,20},{6,22},{8,24},{10,26},{12,28},{14,30},{16,0},... | collective-permute-start | bytes 786440 | tf_op jit(solution)/shard_map/ppermute | solution.py:798
  23.1 35.8 %collective-permute-start.11 = (bf16[5,128,1024]{2,1,0:T(8,128)(2,1)}, bf16[5,128,1024]{2,1,0:T(8,128)(2,1)}, u32[]{:S(2)}, u32[]{:S(2)}) collective-permute-start(bf16[5,128,1024]{2,1,0:T(8,128)(2,1)} %get-tuple-element.100), channel_id=1, source_target_pairs={{0,1},{1,0},{2,3},{3,2},{4,5},{5,4},{6,7},{7,6},{8,9},{9,8},{10,11... | collective-permute-start | bytes 3932168 | tf_op jit(solution)/shard_map/ppermute | solution.py:801
  28.4 14.9 %collective-permute-start.4 = (bf16[2,64,1024]{2,1,0:T(8,128)(2,1)S(1)}, bf16[2,64,1024]{2,1,0:T(8,128)(2,1)S(1)}, u32[]{:S(2)}, u32[]{:S(2)}) collective-permute-start(bf16[2,64,1024]{2,1,0:T(8,128)(2,1)S(1)} %collective-permute-done), channel_id=1, source_target_pairs={{0,4},{2,6},{4,0},{6,2},{8,12},{10,14},{12,8},{14,10},{16,20},{18,... | collective-permute-start | bytes 786440 | tf_op jit(solution)/shard_map/ppermute | solution.py:798
  28.8 14.5 %collective-permute-start.5 = (bf16[2,64,1024]{2,1,0:T(8,128)(2,1)S(1)}, bf16[2,64,1024]{2,1,0:T(8,128)(2,1)}, u32[]{:S(2)}, u32[]{:S(2)}) collective-permute-start(bf16[2,64,1024]{2,1,0:T(8,128)(2,1)S(1)} %collective-permute-done.1), channel_id=1, source_target_pairs={{0,4},{2,6},{4,0},{6,2},{8,12},{10,14},{12,8},{14,10},{16,20},{18,... | collective-permute-start | bytes 786440 | tf_op jit(solution)/shard_map/ppermute | solution.py:798
  35.9 15.4 %collective-permute-start.6 = (bf16[2,64,1024]{2,1,0:T(8,128)(2,1)S(1)}, bf16[2,64,1024]{2,1,0:T(8,128)(2,1)}, u32[]{:S(2)}, u32[]{:S(2)}) collective-permute-start(bf16[2,64,1024]{2,1,0:T(8,128)(2,1)S(1)} %collective-permute-done.2), channel_id=1, source_target_pairs={{0,4},{2,6},{4,0},{6,2},{8,12},{10,14},{12,8},{14,10},{16,20},{18,... | collective-permute-start | bytes 786440 | tf_op jit(solution)/shard_map/ppermute | solution.py:798
  41.1 17.2 %collective-permute-start.10 = (bf16[512,192]{1,0:T(8,128)(2,1)S(1)}, bf16[512,192]{1,0:T(8,128)(2,1)S(1)}, u32[]{:S(2)}, u32[]{:S(2)}) collective-permute-start(bf16[512,192]{1,0:T(8,128)(2,1)S(1)} %pad_maximum_fusion.4), channel_id=1, source_target_pairs={{0,1},{1,0},{2,3},{3,2},{4,5},{5,4},{6,7},{7,6},{8,9},{9,8},{10,11... | collective-permute-start | bytes 589832 | tf_op jit(solution)/shard_map/ppermute | solution.py:801
  43.3 18.2 %collective-permute-start.7 = (bf16[4,2,64,1024]{3,2,1,0:T(8,128)(2,1)S(1)}, bf16[4,2,64,1024]{3,2,1,0:T(8,128)(2,1)}, u32[]{:S(2)}, u32[]{:S(2)}) collective-permute-start(bf16[4,2,64,1024]{3,2,1,0:T(8,128)(2,1)S(1)} %pad_maximum_fusion.1.refs_0_), channel_id=1, source_target_pairs={{0,2},{2,0},{4,6},{6,4},{8,10},{10,8},{12,14},{14,12},{16,18},{18,... | collective-permute-start | bytes 3145736 | tf_op jit(solution)/shard_map/ppermute | solution.py:798
  58.9 29.8 %collective-permute-start.13 = (bf16[5,128,1024]{2,1,0:T(8,128)(2,1)}, bf16[5,128,1024]{2,1,0:T(8,128)(2,1)}, u32[]{:S(2)}, u32[]{:S(2)}) collective-permute-start(bf16[5,128,1024]{2,1,0:T(8,128)(2,1)} %collective-permute-done.11.refs_0_), channel_id=1, source_target_pairs={{0,4},{2,6},{4,0},{6,2},{8,12},{10,14},{12,8},{14,10},{16,20},{18,... | collective-permute-start | bytes 3932168 | tf_op jit(solution)/shard_map/ppermute | solution.py:798
  60.9 16.5 %collective-permute-start.12 = (bf16[2,128,1408]{2,1,0:T(8,128)(2,1)S(1)}, bf16[2,128,1408]{2,1,0:T(8,128)(2,1)S(1)}, u32[]{:S(2)}, u32[]{:S(2)}) collective-permute-start(bf16[2,128,1408]{2,1,0:T(8,128)(2,1)S(1)} %copy-done.40), channel_id=1, source_target_pairs={{0,1},{1,0},{2,3},{3,2},{4,5},{5,4},{6,7},{7,6},{8,9},{9,8},{10,11... | collective-permute-start | bytes 2162696 | tf_op jit(solution)/shard_map/ppermute | solution.py:801
  61.4 35.5 %collective-permute-start.14 = (bf16[5,128,1024]{2,1,0:T(8,128)(2,1)}, bf16[5,128,1024]{2,1,0:T(8,128)(2,1)}, u32[]{:S(2)}, u32[]{:S(2)}) collective-permute-start(bf16[5,128,1024]{2,1,0:T(8,128)(2,1)} %collective-permute-done.11.refs_0_), channel_id=1, source_target_pairs={{0,2},{2,0},{4,6},{6,4},{8,10},{10,8},{12,14},{14,12},{16,18},{18,... | collective-permute-start | bytes 3932168 | tf_op jit(solution)/shard_map/ppermute | solution.py:798
  90.0 26.9 %all-to-all-start = ((bf16[16,64,128]{2,1,0:T(8,128)(2,1)}), bf16[16,64,128]{2,1,0:T(8,128)(2,1)S(1)}, u32[]{:S(2)}, u32[]{:S(2)}) async-start(bf16[16,64,128]{2,1,0:T(8,128)(2,1)} %bitcast.62), calls=%async_computation | async-start | bytes 524288 | tf_op jit(solution)/shard_map/all_to_all | solution.py:935
  93.5 54.1 %collective-permute-start.21 = (bf16[128,1024]{1,0:T(8,128)(2,1)S(1)}, bf16[128,1024]{1,0:T(8,128)(2,1)S(1)}, u32[]{:S(2)}, u32[]{:S(2)}) collective-permute-start(bf16[128,1024]{1,0:T(8,128)(2,1)S(1)} %bitcast.88), channel_id=1, source_target_pairs={{0,1},{1,0},{2,3},{3,2},{4,5},{5,4},{6,7},{7,6},{8,9},{9,8},{10,11... | collective-permute-start | bytes 786440 | tf_op jit(solution)/shard_map/ppermute | solution.py:801
  95.1 21.2 %collective-permute-start.16 = (bf16[2,128,1408]{2,1,0:T(8,128)(2,1)S(1)}, bf16[2,128,1408]{2,1,0:T(8,128)(2,1)}, u32[]{:S(2)}, u32[]{:S(2)}) collective-permute-start(bf16[2,128,1408]{2,1,0:T(8,128)(2,1)S(1)} %collective-permute-done.12.refs_0_), channel_id=1, source_target_pairs={{0,8},{2,10},{4,12},{6,14},{8,0},{10,2},{12,4},{14,6},{16,24},{18,... | collective-permute-start | bytes 2162696 | tf_op jit(solution)/shard_map/ppermute | solution.py:798
  116.3 16.5 %collective-permute-start.17 = (bf16[2,128,1408]{2,1,0:T(8,128)(2,1)S(1)}, bf16[2,128,1408]{2,1,0:T(8,128)(2,1)S(1)}, u32[]{:S(2)}, u32[]{:S(2)}) collective-permute-start(bf16[2,128,1408]{2,1,0:T(8,128)(2,1)S(1)} %collective-permute-done.12.refs_0_), channel_id=1, source_target_pairs={{0,2},{2,0},{4,6},{6,4},{8,10},{10,8},{12,14},{14,12},{16,18},{18,... | collective-permute-start | bytes 2162696 | tf_op jit(solution)/shard_map/ppermute | solution.py:798
  116.3 16.5 %collective-permute-start.18 = (bf16[2,128,1408]{2,1,0:T(8,128)(2,1)}, bf16[2,128,1408]{2,1,0:T(8,128)(2,1)S(1)}, u32[]{:S(2)}, u32[]{:S(2)}) collective-permute-start(bf16[2,128,1408]{2,1,0:T(8,128)(2,1)} %collective-permute-done.16.refs_1_), channel_id=1, source_target_pairs={{0,2},{2,0},{4,6},{6,4},{8,10},{10,8},{12,14},{14,12},{16,18},{18,... | collective-permute-start | bytes 2162696 | tf_op jit(solution)/shard_map/ppermute | solution.py:798
  130.8 13.8 %collective-permute-start.19 = (bf16[128,1024]{1,0:T(8,128)(2,1)}, bf16[128,1024]{1,0:T(8,128)(2,1)S(1)}, u32[]{:S(2)}, u32[]{:S(2)}) collective-permute-start(bf16[128,1024]{1,0:T(8,128)(2,1)} %get-tuple-element.122.n_ref.n0_ref), channel_id=1, source_target_pairs={{0,1},{1,0},{2,3},{3,2},{4,5},{5,4},{6,7},{7,6},{8,9},{9,8},{10,11... | collective-permute-start | bytes 786440 | tf_op jit(solution)/shard_map/ppermute | solution.py:801
  132.3 15.3 %collective-permute-start.20 = (bf16[3,128,512]{2,1,0:T(8,128)(2,1)}, bf16[3,128,512]{2,1,0:T(8,128)(2,1)S(1)}, u32[]{:S(2)}, u32[]{:S(2)}) collective-permute-start(bf16[3,128,512]{2,1,0:T(8,128)(2,1)} %get-tuple-element.113), channel_id=1, source_target_pairs={{0,1},{1,0},{2,3},{3,2},{4,5},{5,4},{6,7},{7,6},{8,9},{9,8},{10,11... | collective-permute-start | bytes 1179656 | tf_op jit(solution)/shard_map/ppermute | solution.py:801
  175.6 20.2 %collective-permute-start.25 = (bf16[4,704,128]{2,1,0:T(8,128)(2,1)}, bf16[4,704,128]{2,1,0:T(8,128)(2,1)S(1)}, u32[]{:S(2)}, u32[]{:S(2)}) collective-permute-start(bf16[4,704,128]{2,1,0:T(8,128)(2,1)} %get-tuple-element.124), channel_id=1, source_target_pairs={{0,8},{2,10},{4,12},{6,14},{8,0},{10,2},{12,4},{14,6},{16,24},{18,... | collective-permute-start | bytes 2162696 | tf_op jit(solution)/shard_map/ppermute | solution.py:798
  176.0 19.8 %collective-permute-start.26 = (bf16[4,704,128]{2,1,0:T(8,128)(2,1)}, bf16[4,704,128]{2,1,0:T(8,128)(2,1)S(1)}, u32[]{:S(2)}, u32[]{:S(2)}) collective-permute-start(bf16[4,704,128]{2,1,0:T(8,128)(2,1)} %get-tuple-element.129), channel_id=1, source_target_pairs={{0,4},{2,6},{4,0},{6,2},{8,12},{10,14},{12,8},{14,10},{16,20},{18,... | collective-permute-start | bytes 2162696 | tf_op jit(solution)/shard_map/ppermute | solution.py:798
  177.7 18.1 %collective-permute-start.27 = (bf16[4,704,128]{2,1,0:T(8,128)(2,1)}, bf16[4,704,128]{2,1,0:T(8,128)(2,1)}, u32[]{:S(2)}, u32[]{:S(2)}) collective-permute-start(bf16[4,704,128]{2,1,0:T(8,128)(2,1)} %get-tuple-element.130), channel_id=1, source_target_pairs={{0,1},{1,0},{2,3},{3,2},{4,5},{5,4},{6,7},{7,6},{8,9},{9,8},{10,11... | collective-permute-start | bytes 2162696 | tf_op jit(solution)/shard_map/ppermute | solution.py:801
  202.6 17.9 %collective-permute-start.30 = (bf16[128,2048]{1,0:T(8,128)(2,1)S(1)}, bf16[128,2048]{1,0:T(8,128)(2,1)S(1)}, u32[]{:S(2)}, u32[]{:S(2)}) collective-permute-start(bf16[128,2048]{1,0:T(8,128)(2,1)S(1)} %copy-done.44), channel_id=1, source_target_pairs={{0,1},{1,0},{2,3},{3,2},{4,5},{5,4},{6,7},{7,6},{8,9},{9,8},{10,11... | collective-permute-start | bytes 1572872 | tf_op jit(solution)/shard_map/ppermute | solution.py:801
  203.0 17.5 %collective-permute-start.31 = (bf16[128,1024]{1,0:T(8,128)(2,1)}, bf16[128,1024]{1,0:T(8,128)(2,1)S(1)}, u32[]{:S(2)}, u32[]{:S(2)}) collective-permute-start(bf16[128,1024]{1,0:T(8,128)(2,1)} %get-tuple-element.139.last_ref), channel_id=1, source_target_pairs={{0,1},{1,0},{2,3},{3,2},{4,5},{5,4},{6,7},{7,6},{8,9},{9,8},{10,11... | collective-permute-start | bytes 786440 | tf_op jit(solution)/shard_map/ppermute | solution.py:801
  204.7 50.9 %collective-permute-start.29 = (bf16[8,16,2,32,128]{4,3,2,1,0:T(8,128)(2,1)}, bf16[8,16,2,32,128]{4,3,2,1,0:T(8,128)(2,1)}, u32[]{:S(2)}, u32[]{:S(2)}) collective-permute-start(bf16[8,16,2,32,128]{4,3,2,1,0:T(8,128)(2,1)} %get-tuple-element.135), channel_id=1, source_target_pairs={{0,2},{2,0},{4,6},{6,4},{8,10},{10,8},{12,14},{14,12},{16,18},{18,... | collective-permute-start | bytes 6291464 | tf_op jit(solution)/shard_map/ppermute | solution.py:798
  226.3 23.7 %collective-permute-start.51 = (bf16[8,768,128]{2,1,0:T(8,128)(2,1)}, bf16[8,768,128]{2,1,0:T(8,128)(2,1)S(1)}, u32[]{:S(2)}, u32[]{:S(2)}) collective-permute-start(bf16[8,768,128]{2,1,0:T(8,128)(2,1)} %get-tuple-element.164), channel_id=1, source_target_pairs={{0,2},{2,0},{4,6},{6,4},{8,10},{10,8},{12,14},{14,12},{16,18},{18,... | collective-permute-start | bytes 4718600 | tf_op jit(solution)/shard_map/ppermute | solution.py:798
  226.3 21.3 %collective-permute-start.28 = (bf16[4,704,128]{2,1,0:T(8,128)(2,1)}, bf16[4,704,128]{2,1,0:T(8,128)(2,1)}, u32[]{:S(2)}, u32[]{:S(2)}) collective-permute-start(bf16[4,704,128]{2,1,0:T(8,128)(2,1)} %collective-permute-done.27), channel_id=1, source_target_pairs={{0,4},{2,6},{4,0},{6,2},{8,12},{10,14},{12,8},{14,10},{16,20},{18,... | collective-permute-start | bytes 2162696 | tf_op jit(solution)/shard_map/ppermute | solution.py:798
  226.6 21.0 %collective-permute-start.48 = (bf16[4,704,128]{2,1,0:T(8,128)(2,1)}, bf16[4,704,128]{2,1,0:T(8,128)(2,1)}, u32[]{:S(2)}, u32[]{:S(2)}) collective-permute-start(bf16[4,704,128]{2,1,0:T(8,128)(2,1)} %get-tuple-element.161), channel_id=1, source_target_pairs={{0,1},{1,0},{2,3},{3,2},{4,5},{5,4},{6,7},{7,6},{8,9},{9,8},{10,11... | collective-permute-start | bytes 2162696 | tf_op jit(solution)/shard_map/ppermute | solution.py:801
  227.0 28.6 %all-to-all-start.1 = ((bf16[16,64,128]{2,1,0:T(8,128)(2,1)}), bf16[16,64,128]{2,1,0:T(8,128)(2,1)S(1)}, u32[]{:S(2)}, u32[]{:S(2)}) async-start(bf16[16,64,128]{2,1,0:T(8,128)(2,1)} %get-tuple-element.133), calls=%async_computation.1 | async-start | bytes 524288 | tf_op jit(solution)/shard_map/all_to_all | solution.py:1068
  232.9 244.5 %all-gather.4.cloned.1.call-start = ((), (), s32[]{:S(2)}) async-start(), calls=%async_computation.4 | async-start | bytes 18104320 | tf_op jit(solution)/shard_map/all_gather | solution.py:1192
  254.1 35.5 %collective-permute-start.52 = (bf16[4,768,128]{2,1,0:T(8,128)(2,1)}, bf16[4,768,128]{2,1,0:T(8,128)(2,1)}, u32[]{:S(2)}, u32[]{:S(2)}) collective-permute-start(bf16[4,768,128]{2,1,0:T(8,128)(2,1)} %slice.249), channel_id=1, source_target_pairs={{0,8},{2,10},{4,12},{6,14},{8,0},{10,2},{12,4},{14,6},{16,24},{18,... | collective-permute-start | bytes 2359304 | tf_op jit(solution)/shard_map/ppermute | solution.py:798
  256.3 25.3 %collective-permute-start.44 = (bf16[2,704,128]{2,1,0:T(8,128)(2,1)}, bf16[2,704,128]{2,1,0:T(8,128)(2,1)S(1)}, u32[]{:S(2)}, u32[]{:S(2)}) collective-permute-start(bf16[2,704,128]{2,1,0:T(8,128)(2,1)} %slice.254), channel_id=1, source_target_pairs={{0,16},{2,18},{4,20},{6,22},{8,24},{10,26},{12,28},{14,30},{16,0},... | collective-permute-start | bytes 1081352 | tf_op jit(solution)/shard_map/ppermute | solution.py:798
  258.8 29.9 %collective-permute-start.46 = (bf16[2,704,128]{2,1,0:T(8,128)(2,1)}, bf16[2,704,128]{2,1,0:T(8,128)(2,1)S(1)}, u32[]{:S(2)}, u32[]{:S(2)}) collective-permute-start(bf16[2,704,128]{2,1,0:T(8,128)(2,1)} %slice.253), channel_id=1, source_target_pairs={{0,8},{2,10},{4,12},{6,14},{8,0},{10,2},{12,4},{14,6},{16,24},{18,... | collective-permute-start | bytes 1081352 | tf_op jit(solution)/shard_map/ppermute | solution.py:798
  263.7 30.9 %collective-permute-start.32 = (bf16[4,16,2,32,128]{4,3,2,1,0:T(8,128)(2,1)}, bf16[4,16,2,32,128]{4,3,2,1,0:T(8,128)(2,1)}, u32[]{:S(2)}, u32[]{:S(2)}) collective-permute-start(bf16[4,16,2,32,128]{4,3,2,1,0:T(8,128)(2,1)} %slice.248), channel_id=1, source_target_pairs={{0,4},{2,6},{4,0},{6,2},{8,12},{10,14},{12,8},{14,10},{16,20},{18,... | collective-permute-start | bytes 3145736 | tf_op jit(solution)/shard_map/ppermute | solution.py:798
  292.1 24.0 %collective-permute-start.53 = (bf16[2,768,128]{2,1,0:T(8,128)(2,1)S(1)}, bf16[2,768,128]{2,1,0:T(8,128)(2,1)S(1)}, u32[]{:S(2)}, u32[]{:S(2)}) collective-permute-start(bf16[2,768,128]{2,1,0:T(8,128)(2,1)S(1)} %slice.251), channel_id=1, source_target_pairs={{0,16},{2,18},{4,20},{6,22},{8,24},{10,26},{12,28},{14,30},{16,0},... | collective-permute-start | bytes 1179656 | tf_op jit(solution)/shard_map/ppermute | solution.py:798
  300.3 15.9 %collective-permute-start.45 = (bf16[1,704,128]{2,1,0:T(8,128)(2,1)S(1)}, bf16[1,704,128]{2,1,0:T(8,128)(2,1)S(1)}, u32[]{:S(2)}, u32[]{:S(2)}) collective-permute-start(bf16[1,704,128]{2,1,0:T(8,128)(2,1)S(1)} %slice.259), channel_id=1, source_target_pairs={{0,4},{2,6},{4,0},{6,2},{8,12},{10,14},{12,8},{14,10},{16,20},{18,... | collective-permute-start | bytes 540680 | tf_op jit(solution)/shard_map/ppermute | solution.py:798
  300.8 18.0 %collective-permute-start.47 = (bf16[1,704,128]{2,1,0:T(8,128)(2,1)}, bf16[1,704,128]{2,1,0:T(8,128)(2,1)S(1)}, u32[]{:S(2)}, u32[]{:S(2)}) collective-permute-start(bf16[1,704,128]{2,1,0:T(8,128)(2,1)} %slice.258), channel_id=1, source_target_pairs={{0,16},{2,18},{4,20},{6,22},{8,24},{10,26},{12,28},{14,30},{16,0},... | collective-permute-start | bytes 540680 | tf_op jit(solution)/shard_map/ppermute | solution.py:798
  302.1 37.4 %collective-permute-start.33 = (bf16[1,768,128]{2,1,0:T(8,128)(2,1)S(1)}, bf16[1,768,128]{2,1,0:T(8,128)(2,1)S(1)}, u32[]{:S(2)}, u32[]{:S(2)}) collective-permute-start(bf16[1,768,128]{2,1,0:T(8,128)(2,1)S(1)} %constant_dynamic-slice_fusion.3), channel_id=1, source_target_pairs={{0,1},{1,0},{2,3},{3,2},{4,5},{5,4},{6,7},{7,6},{8,9},{9,8},{10,11... | collective-permute-start | bytes 589832 | tf_op jit(solution)/shard_map/ppermute | solution.py:801
  302.6 23.6 %collective-permute-start.49 = (bf16[2,704,128]{2,1,0:T(8,128)(2,1)S(1)}, bf16[2,704,128]{2,1,0:T(8,128)(2,1)S(1)}, u32[]{:S(2)}, u32[]{:S(2)}) collective-permute-start(bf16[2,704,128]{2,1,0:T(8,128)(2,1)S(1)} %copy-done.25), channel_id=1, source_target_pairs={{0,8},{2,10},{4,12},{6,14},{8,0},{10,2},{12,4},{14,6},{16,24},{18,... | collective-permute-start | bytes 1081352 | tf_op jit(solution)/shard_map/ppermute | solution.py:798
  316.1 22.2 %collective-permute-start.37 = (bf16[2,16,2,32,128]{4,3,2,1,0:T(8,128)(2,1)S(1)}, bf16[2,16,2,32,128]{4,3,2,1,0:T(8,128)(2,1)S(1)}, u32[]{:S(2)}, u32[]{:S(2)}) collective-permute-start(bf16[2,16,2,32,128]{4,3,2,1,0:T(8,128)(2,1)S(1)} %slice.250), channel_id=1, source_target_pairs={{0,8},{2,10},{4,12},{6,14},{8,0},{10,2},{12,4},{14,6},{16,24},{18,... | collective-permute-start | bytes 1572872 | tf_op jit(solution)/shard_map/ppermute | solution.py:798
  316.2 39.7 %collective-permute-start.54 = (bf16[1,768,128]{2,1,0:T(8,128)(2,1)S(1)}, bf16[1,768,128]{2,1,0:T(8,128)(2,1)S(1)}, u32[]{:S(2)}, u32[]{:S(2)}) collective-permute-start(bf16[1,768,128]{2,1,0:T(8,128)(2,1)S(1)} %slice.256), channel_id=1, source_target_pairs={{0,4},{2,6},{4,0},{6,2},{8,12},{10,14},{12,8},{14,10},{16,20},{18,... | collective-permute-start | bytes 589832 | tf_op jit(solution)/shard_map/ppermute | solution.py:798
  326.3 13.1 %collective-permute-start.50 = (bf16[1,704,128]{2,1,0:T(8,128)(2,1)S(1)}, bf16[1,704,128]{2,1,0:T(8,128)(2,1)S(1)}, u32[]{:S(2)}, u32[]{:S(2)}) collective-permute-start(bf16[1,704,128]{2,1,0:T(8,128)(2,1)S(1)} %slice.257), channel_id=1, source_target_pairs={{0,16},{2,18},{4,20},{6,22},{8,24},{10,26},{12,28},{14,30},{16,0},... | collective-permute-start | bytes 540680 | tf_op jit(solution)/shard_map/ppermute | solution.py:798
  362.2 33.5 %collective-permute-start.34 = (bf16[3,256,1024]{2,1,0:T(8,128)(2,1)S(1)}, bf16[3,256,1024]{2,1,0:T(8,128)(2,1)S(1)}, u32[]{:S(2)}, u32[]{:S(2)}) collective-permute-start(bf16[3,256,1024]{2,1,0:T(8,128)(2,1)S(1)} %pad_maximum_fusion), channel_id=1, source_target_pairs={{0,1},{1,0},{2,3},{3,2},{4,5},{5,4},{6,7},{7,6},{8,9},{9,8},{10,11... | collective-permute-start | bytes 4718600 | tf_op jit(solution)/shard_map/ppermute | solution.py:801
  395.7 40.9 %all-to-all-start.2 = ((bf16[16,64,384]{2,1,0:T(8,128)(2,1)}), bf16[16,64,384]{2,1,0:T(8,128)(2,1)S(1)}, u32[]{:S(2)}, u32[]{:S(2)}) async-start(bf16[16,64,384]{2,1,0:T(8,128)(2,1)} %bitcast.37), calls=%async_computation.2 | async-start | bytes 1572864 | tf_op jit(solution)/shard_map/all_to_all | solution.py:1133
  446.5 18.5 %all-to-all-start.3 = ((bf16[16,64,128]{2,1,0:T(8,128)(2,1)}), bf16[16,64,128]{2,1,0:T(8,128)(2,1)S(1)}, u32[]{:S(2)}, u32[]{:S(2)}) async-start(bf16[16,64,128]{2,1,0:T(8,128)(2,1)} %bitcast.40), calls=%async_computation.3 | async-start | bytes 524288 | tf_op jit(solution)/shard_map/all_to_all | solution.py:1171
  454.9 16.3 %collective-permute-start.35 = (bf16[128,1024]{1,0:T(8,128)(2,1)S(1)}, bf16[128,1024]{1,0:T(8,128)(2,1)S(1)}, u32[]{:S(2)}, u32[]{:S(2)}) collective-permute-start(bf16[128,1024]{1,0:T(8,128)(2,1)S(1)} %copy-done.48), channel_id=1, source_target_pairs={{0,1},{1,0},{2,3},{3,2},{4,5},{5,4},{6,7},{7,6},{8,9},{9,8},{10,11... | collective-permute-start | bytes 786440 | tf_op jit(solution)/shard_map/ppermute | solution.py:801
  457.2 13.9 %collective-permute-start.42 = (f32[4,1024]{1,0:T(4,128)S(1)}, f32[4,1024]{1,0:T(4,128)S(1)}, u32[]{:S(2)}, u32[]{:S(2)}) collective-permute-start(f32[4,1024]{1,0:T(4,128)S(1)} %add.235), channel_id=1, source_target_pairs={{0,8},{2,10},{4,12},{6,14},{8,0},{10,2},{12,4},{14,6},{16,24},{18,... | collective-permute-start | bytes 49160 | tf_op jit(solution)/shard_map/ppermute | solution.py:798
  (68 other events, 548.9 us)
Sparse Core Ops, SparseCore 0:
  14.5 43.2 all-gather.5
  360.9 110.0 all-gather.3
